TPU v7x, 32 devices: a whole 2x2x4 slice. The times are simulated.
32 devices in a mesh: seq: 4 (over y, core), dp: 8 (over z, x).
Axes of the slice: x: 2, y: 2, z: 4, core: 2. Of those that a mesh axis runs over, the one named last changes fastest.
Arguments:
- tokens: bfloat16 [16, 1024, 1024], P('dp', 'seq'), may hold values from -6 to 6
- attn_gain: float32 [1024], P('dp'), may hold values from 0.5 to 1.5
- query_weight: float32 [1024, 1024], P('dp'), may hold values from -0.1875 to 0.1875
- latent_weight: float32 [1024, 512], P('dp'), may hold values from -0.1875 to 0.1875
- key_expand: float32 [256, 1024], P(None, 'dp'), may hold values from -0.375 to 0.375
- value_expand: float32 [256, 1024], P(None, 'dp'), may hold values from -0.375 to 0.375
- output_weight: float32 [1024, 1024], P('dp'), may hold values from -1.5 to 1.5
- mlp_gain: float32 [1024], P('dp'), may hold values from 0.5 to 1.5
- gate_weight: float32 [1024, 2816], P('dp'), may hold values from -0.1875 to 0.1875
- up_weight: float32 [1024, 2816], P('dp'), may hold values from -0.1875 to 0.1875
- down_weight: float32 [2816, 1024], P('dp'), may hold values from -0.109375 to 0.109375
- cotangent: bfloat16 [16, 1024, 1024], P('dp', 'seq'), may hold values from -6 to 6
- lengths: int32 [16, 2], P('dp'), may hold values from 0 to 1024, as said below
Outputs:
- layer_out: bfloat16 [16, 1024, 1024], P('dp', 'seq')
- grad_tokens: float32 [16, 1024, 1024], P('dp', 'seq')
- grad_attn_gain: float32 [1024], P('dp')
- grad_query: float32 [1024, 1024], P('dp')
- grad_latent: float32 [1024, 512], P('dp')
- grad_key_expand: float32 [256, 1024], P(None, 'dp')
- grad_value_expand: float32 [256, 1024], P(None, 'dp')
- grad_output: float32 [1024, 1024], P('dp')
- grad_mlp_gain: float32 [1024], P('dp')
- grad_gate: float32 [1024, 2816], P('dp')
- grad_up: float32 [1024, 2816], P('dp')
- grad_down: float32 [2816, 1024], P('dp')
Inputs may be any that keep to these rules, and one draw needn't show every extreme that they name: Among each device's 2 rows (rows k * 2 to (k + 1) * 2 - 1) one, drawn from the seed, holds a single sequence: lengths 1024 and 0. Every other row holds two sequences: a first one of 256 to 768 positions and a second one of the rest. The two entries of a row sum to 1024.
All inputs are finite; a program needn't handle non-finite values.
Results may differ from a plain program's by a relative error of at most 0.023.
Values may be sent and summed in bfloat16 or wider, within the bound.
No kernel may reach another device: no remote copies, remote signals or barrier semaphores. Data moves between devices by JAX's collectives and lax.ppermute only.
A program may use at most 192 MiB of HBM per device.

v0:
```python
import jax
import jax.numpy as jnp
from jax import lax
from jax.sharding import PartitionSpec as P

D = 1024
H = 16
HD = 64
KVH = 2
LAT = 256


EPS = 1e-06


def norm_rows(values, gain):
    return values * lax.rsqrt(jnp.mean(values * values, axis=-1, keepdims=True) + EPS) * gain


def expand(latent, weight):
    shaped = latent.reshape(latent.shape[:-1] + (KVH, LAT))
    table = weight.reshape(LAT, KVH, D // KVH)
    result = jnp.einsum("bngl,lgj->bngj", shaped, table, preferred_element_type=jnp.float32)
    return result.reshape(latent.shape[:-1] + (D,)).astype(jnp.bfloat16)


def contract_back(grad, weight):
    shaped = grad.reshape(grad.shape[:-1] + (KVH, D // KVH))
    table = weight.reshape(LAT, KVH, D // KVH)
    result = jnp.einsum("bngj,lgj->bngl", shaped, table, preferred_element_type=jnp.float32)
    return result.reshape(grad.shape[:-1] + (KVH * LAT,))


def weight_term(piece, grad):
    shaped = piece.reshape(piece.shape[:-1] + (KVH, LAT))
    grads = grad.reshape(grad.shape[:-1] + (KVH, D // KVH))
    return jnp.einsum("bngl,bngj->lgj", shaped, grads, preferred_element_type=jnp.float32).reshape(
        LAT, D
    )


def visible(query_pos, key_pos, firsts):
    query_doc = query_pos[None, :] >= firsts[:, None]
    key_doc = key_pos[None, :] >= firsts[:, None]
    causal = key_pos[None, None, :] <= query_pos[None, :, None]
    return causal & (key_doc[:, None, :] == query_doc[:, :, None])


def by_blocks(step, width, carry, piece):
    count = piece.shape[1]

    def inner(index, state):
        part = lax.dynamic_slice_in_dim(piece, index * width, width, 1)
        return step(state, part, index * width)

    return lax.fori_loop(0, count // width, inner, carry)


def per_device(
    tokens,
    attn_gain,
    query_weight,
    latent_weight,
    key_expand,
    value_expand,
    output_weight,
    mlp_gain,
    gate_weight,
    up_weight,
    down_weight,
    cotangent,
    lengths,
):
    low_type = jnp.bfloat16
    gathered = (
        lax.all_gather(attn_gain.astype(low_type), "dp", axis=0, tiled=True),
        lax.all_gather(query_weight.astype(low_type), "dp", axis=0, tiled=True),
        lax.all_gather(latent_weight.astype(low_type), "dp", axis=0, tiled=True),
        lax.all_gather(key_expand.astype(low_type), "dp", axis=1, tiled=True),
        lax.all_gather(value_expand.astype(low_type), "dp", axis=1, tiled=True),
        lax.all_gather(output_weight.astype(low_type), "dp", axis=0, tiled=True),
        lax.all_gather(mlp_gain.astype(low_type), "dp", axis=0, tiled=True),
        lax.all_gather(gate_weight.astype(low_type), "dp", axis=0, tiled=True),
        lax.all_gather(up_weight.astype(low_type), "dp", axis=0, tiled=True),
        lax.all_gather(down_weight.astype(low_type), "dp", axis=0, tiled=True),
    )
    gain_first, query_full, latent_full, key_full, value_full = (
        gathered[0],
        gathered[1],
        gathered[2],
        gathered[3],
        gathered[4],
    )
    output_full, gain_second, gate_full, upward_full, down_full = (
        gathered[5],
        gathered[6],
        gathered[7],
        gathered[8],
        gathered[9],
    )
    batch, length, width = tokens.shape
    row_length = length * lax.axis_size("seq")
    scale = HD ** (-0.5)
    firsts = lengths[:, 0]
    query_pos = lax.axis_index("seq") * length + jnp.arange(length, dtype=jnp.int32)
    inputs = tokens.astype(jnp.float32)
    normed_first, pull_first = jax.vjp(norm_rows, inputs, gain_first.astype(jnp.float32))
    first_low = normed_first.astype(low_type)
    query_low = jnp.dot(first_low, query_full, preferred_element_type=jnp.float32).astype(low_type)
    latent_low = jnp.dot(first_low, latent_full, preferred_element_type=jnp.float32).astype(
        low_type
    )
    query_heads = query_low.reshape(batch, length, H, HD)

    def forward_step(carry, piece, start):
        peak, total, accum, exact = carry
        count = piece.shape[1]
        keys = expand(piece, key_full).reshape(batch, count, H, HD)
        values = expand(piece, value_full).reshape(batch, count, H, HD)
        scores = (
            jnp.einsum("bqhd,bkhd->bhqk", query_heads, keys, preferred_element_type=jnp.float32)
            * scale
        )
        allowed = visible(query_pos, start + jnp.arange(count, dtype=jnp.int32), firsts)[:, None]
        scores = jnp.where(allowed, scores, -1e30)
        new_peak = jnp.maximum(peak, jnp.max(scores, axis=-1))
        weights = jnp.where(allowed, jnp.exp(scores - new_peak[..., None]), 0.0)
        factor = jnp.exp(peak - new_peak)
        total = total * factor + jnp.sum(weights, axis=-1)
        accum = accum * factor[..., None] + jnp.einsum(
            "bhqk,bkhd->bhqd", weights.astype(low_type), values, preferred_element_type=jnp.float32
        )
        exact = exact * factor[..., None] + jnp.einsum(
            "bhqk,bkhd->bhqd",
            weights,
            values.astype(jnp.float32),
            preferred_element_type=jnp.float32,
        )
        return (new_peak, total, accum, exact)

    start_state = (
        jnp.full((batch, H, length), -1e30, jnp.float32),
        jnp.zeros((batch, H, length), jnp.float32),
        jnp.zeros((batch, H, length, HD), jnp.float32),
        jnp.zeros((batch, H, length, HD), jnp.float32),
    )
    peak, total, accum, exact = by_blocks(
        forward_step, length, start_state, lax.all_gather(latent_low, "seq", axis=1, tiled=True)
    )
    attended = accum / total[..., None]
    attended_exact = exact / total[..., None]
    attended_low = (
        jnp.transpose(attended, (0, 2, 1, 3)).reshape(batch, length, width).astype(low_type)
    )
    middle = inputs + jnp.dot(attended_low, output_full, preferred_element_type=jnp.float32)
    normed_second, pull_second = jax.vjp(norm_rows, middle, gain_second.astype(jnp.float32))
    second_low = normed_second.astype(low_type)
    gate_values = jnp.dot(second_low, gate_full, preferred_element_type=jnp.float32)
    upward_values = jnp.dot(second_low, upward_full, preferred_element_type=jnp.float32)
    hidden, pull_hidden = jax.vjp(
        lambda left, right: jax.nn.silu(left) * right, gate_values, upward_values
    )
    hidden_low = hidden.astype(low_type)
    output = middle + jnp.dot(hidden_low, down_full, preferred_element_type=jnp.float32)
    layer_out = output.astype(low_type)
    grad_down = jnp.einsum("bsf,bsd->fd", hidden_low, cotangent, preferred_element_type=jnp.float32)
    grad_hidden = jnp.einsum(
        "bsd,fd->bsf", cotangent, down_full, preferred_element_type=jnp.float32
    )
    grad_gate_values, grad_upward_values = pull_hidden(grad_hidden)
    gate_low = grad_gate_values.astype(low_type)
    upward_low = grad_upward_values.astype(low_type)
    grad_gate = jnp.einsum("bsd,bsf->df", second_low, gate_low, preferred_element_type=jnp.float32)
    grad_upward = jnp.einsum(
        "bsd,bsf->df", second_low, upward_low, preferred_element_type=jnp.float32
    )
    grad_second = jnp.einsum(
        "bsf,df->bsd", gate_low, gate_full, preferred_element_type=jnp.float32
    ) + jnp.einsum("bsf,df->bsd", upward_low, upward_full, preferred_element_type=jnp.float32)
    grad_middle_norm, grad_gain_second = pull_second(grad_second)
    grad_middle = cotangent.astype(jnp.float32) + grad_middle_norm
    middle_low = grad_middle.astype(low_type)
    grad_output = jnp.einsum(
        "bsd,bse->de", attended_low, middle_low, preferred_element_type=jnp.float32
    )
    grad_attended = jnp.einsum(
        "bse,de->bsd", middle_low, output_full, preferred_element_type=jnp.float32
    )
    grad_heads = grad_attended.astype(low_type).reshape(batch, length, H, HD)
    delta = jnp.sum(
        jnp.transpose(grad_heads.astype(jnp.float32), (0, 2, 1, 3)) * attended_exact, axis=-1
    )
    logsum = peak + jnp.log(total)

    def backward_step(carry, piece, start):
        query_acc, key_grad_w, value_grad_w, latent_grads = carry
        count = piece.shape[1]
        keys = expand(piece, key_full).reshape(batch, count, H, HD)
        values = expand(piece, value_full).reshape(batch, count, H, HD)
        scores = (
            jnp.einsum("bqhd,bkhd->bhqk", query_heads, keys, preferred_element_type=jnp.float32)
            * scale
        )
        allowed = visible(query_pos, start + jnp.arange(count, dtype=jnp.int32), firsts)[:, None]
        probs = jnp.where(allowed, jnp.exp(scores - logsum[..., None]), 0.0)
        grad_probs = jnp.einsum(
            "bqhd,bkhd->bhqk", grad_heads, values, preferred_element_type=jnp.float32
        )
        grad_scores = (probs * (grad_probs - delta[..., None])).astype(low_type)
        query_acc = (
            query_acc
            + jnp.einsum("bhqk,bkhd->bqhd", grad_scores, keys, preferred_element_type=jnp.float32)
            * scale
        )
        key_grad = (
            jnp.einsum(
                "bhqk,bqhd->bkhd", grad_scores, query_heads, preferred_element_type=jnp.float32
            ).reshape(batch, count, width)
            * scale
        ).astype(low_type)
        value_grad = (
            jnp.einsum(
                "bhqk,bqhd->bkhd",
                probs.astype(low_type),
                grad_heads,
                preferred_element_type=jnp.float32,
            )
            .reshape(batch, count, width)
            .astype(low_type)
        )
        latent_grad = contract_back(key_grad, key_full) + contract_back(value_grad, value_full)
        key_grad_w = key_grad_w + weight_term(piece, key_grad)
        value_grad_w = value_grad_w + weight_term(piece, value_grad)
        latent_grads = lax.dynamic_update_slice_in_dim(latent_grads, latent_grad, start, 1)
        return (query_acc, key_grad_w, value_grad_w, latent_grads)

    back_state = (
        jnp.zeros((batch, length, H, HD), jnp.float32),
        jnp.zeros((LAT, width), jnp.float32),
        jnp.zeros((LAT, width), jnp.float32),
        jnp.zeros((batch, row_length, KVH * LAT), jnp.float32),
    )
    query_acc, grad_key_w, grad_value_w, latent_grads = by_blocks(
        backward_step, length, back_state, lax.all_gather(latent_low, "seq", axis=1, tiled=True)
    )
    grad_query_low = query_acc.reshape(batch, length, width).astype(low_type)
    latent_share = lax.psum_scatter(
        latent_grads.astype(jnp.bfloat16), "seq", scatter_dimension=1, tiled=True
    ).astype(jnp.float32)
    grad_latent_low = latent_share.astype(low_type)
    grad_query_w = jnp.einsum(
        "bsd,bse->de", first_low, grad_query_low, preferred_element_type=jnp.float32
    )
    grad_latent_w = jnp.einsum(
        "bsd,bsl->dl", first_low, grad_latent_low, preferred_element_type=jnp.float32
    )
    grad_first = jnp.einsum(
        "bse,de->bsd", grad_query_low, query_full, preferred_element_type=jnp.float32
    ) + jnp.einsum("bsl,dl->bsd", grad_latent_low, latent_full, preferred_element_type=jnp.float32)
    grad_inputs_norm, grad_gain_first = pull_first(grad_first)
    grad_tokens = grad_middle + grad_inputs_norm
    shares = (
        lax.psum_scatter(
            grad_gain_first.astype(jnp.bfloat16), "dp", scatter_dimension=0, tiled=True
        ).astype(jnp.float32),
        lax.psum_scatter(
            grad_query_w.astype(jnp.bfloat16), "dp", scatter_dimension=0, tiled=True
        ).astype(jnp.float32),
        lax.psum_scatter(
            grad_latent_w.astype(jnp.bfloat16), "dp", scatter_dimension=0, tiled=True
        ).astype(jnp.float32),
        lax.psum_scatter(
            grad_key_w.astype(jnp.bfloat16), "dp", scatter_dimension=1, tiled=True
        ).astype(jnp.float32),
        lax.psum_scatter(
            grad_value_w.astype(jnp.bfloat16), "dp", scatter_dimension=1, tiled=True
        ).astype(jnp.float32),
        lax.psum_scatter(
            grad_output.astype(jnp.bfloat16), "dp", scatter_dimension=0, tiled=True
        ).astype(jnp.float32),
        lax.psum_scatter(
            grad_gain_second.astype(jnp.bfloat16), "dp", scatter_dimension=0, tiled=True
        ).astype(jnp.float32),
        lax.psum_scatter(
            grad_gate.astype(jnp.bfloat16), "dp", scatter_dimension=0, tiled=True
        ).astype(jnp.float32),
        lax.psum_scatter(
            grad_upward.astype(jnp.bfloat16), "dp", scatter_dimension=0, tiled=True
        ).astype(jnp.float32),
        lax.psum_scatter(
            grad_down.astype(jnp.bfloat16), "dp", scatter_dimension=0, tiled=True
        ).astype(jnp.float32),
    )
    result = (
        lax.psum(shares[0].astype(jnp.bfloat16), "seq").astype(jnp.float32),
        lax.psum(shares[1].astype(jnp.bfloat16), "seq").astype(jnp.float32),
        lax.psum(shares[2].astype(jnp.bfloat16), "seq").astype(jnp.float32),
        lax.psum(shares[3].astype(jnp.bfloat16), "seq").astype(jnp.float32),
        lax.psum(shares[4].astype(jnp.bfloat16), "seq").astype(jnp.float32),
        lax.psum(shares[5].astype(jnp.bfloat16), "seq").astype(jnp.float32),
        lax.psum(shares[6].astype(jnp.bfloat16), "seq").astype(jnp.float32),
        lax.psum(shares[7].astype(jnp.bfloat16), "seq").astype(jnp.float32),
        lax.psum(shares[8].astype(jnp.bfloat16), "seq").astype(jnp.float32),
        lax.psum(shares[9].astype(jnp.bfloat16), "seq").astype(jnp.float32),
    )
    return (
        layer_out,
        grad_tokens,
        result[0],
        result[1],
        result[2],
        result[3],
        result[4],
        result[5],
        result[6],
        result[7],
        result[8],
        result[9],
    )


def solution(mesh):
    return jax.shard_map(
        per_device,
        mesh=mesh,
        in_specs=(
            P("dp", "seq", None),
            P("dp"),
            P("dp", None),
            P("dp", None),
            P(None, "dp"),
            P(None, "dp"),
            P("dp", None),
            P("dp"),
            P("dp", None),
            P("dp", None),
            P("dp", None),
            P("dp", "seq", None),
            P("dp", None),
        ),
        out_specs=(
            P("dp", "seq", None),
            P("dp", "seq", None),
            P("dp"),
            P("dp", None),
            P("dp", None),
            P(None, "dp"),
            P(None, "dp"),
            P("dp", None),
            P("dp"),
            P("dp", None),
            P("dp", None),
            P("dp", None),
        ),
        check_vma=False,
    )
```

profile of v0, /device:TPU:0, one launch (start us, length us, event | category | flops | bytes accessed | tf_op | source)
XLA Modules:
  0.0 1448.5 jit_solution(16356535630669154323)
XLA Ops:
  11.5 22.2 %all-gather = bf16[8,1,128]{2,1,0:T(2,128)(2,1)S(1)} all-gather(bf16[1,1,128]{2,1,0:T(2,128)(2,1)S(1)} %convert_bitcast_fusion.1), channel_id=1, replica_groups=mesh['seq'=4,'dp'=8] {'dp'}, dimensions={0}, use_global_device_ids=true | all-gather | bytes 2304 | tf_op jit(solution)/shard_map/all_gather | solution.py:76
  34.6 19.1 %all-gather.10.cloned.1.call-done = bf16[1024,512]{1,0:T(8,128)(2,1)} async-done(((bf16[128,512]{1,0:T(8,128)(2,1)}), bf16[1024,512]{1,0:T(8,128)(2,1)}) %all-gather.10.cloned.1.call-update) | async-done | bytes 1048592 | tf_op jit(solution)/shard_map/all_gather | solution.py:78
  62.1 30.5 %all_gather.37 = bf16[256,1024]{1,0:T(8,128)(2,1)S(1)} all-gather(bf16[256,128]{1,0:T(8,128)(2,1)S(1)} %convert_element_type.287), channel_id=1, replica_groups=mesh['seq'=4,'dp'=8] {'dp'}, dimensions={1}, use_global_device_ids=true | all-gather | bytes 589824 | tf_op jit(solution)/shard_map/all_gather | solution.py:79
  93.4 29.7 %all_gather.39 = bf16[256,1024]{1,0:T(8,128)(2,1)S(1)} all-gather(bf16[256,128]{1,0:T(8,128)(2,1)S(1)} %convert_element_type.290), channel_id=1, replica_groups=mesh['seq'=4,'dp'=8] {'dp'}, dimensions={1}, use_global_device_ids=true | all-gather | bytes 589824 | tf_op jit(solution)/shard_map/all_gather | solution.py:80
  125.6 18.6 %all-gather.1 = bf16[8,1,128]{2,1,0:T(2,128)(2,1)S(1)} all-gather(bf16[1,1,128]{2,1,0:T(2,128)(2,1)S(1)} %convert_bitcast_fusion), channel_id=1, replica_groups=mesh['seq'=4,'dp'=8] {'dp'}, dimensions={0}, use_global_device_ids=true | all-gather | bytes 2304 | tf_op jit(solution)/shard_map/all_gather | solution.py:82
  144.2 3.9 fusion.91
  149.6 4.0 copy.124
  153.7 126.6 %while.42 = (s32[]{:T(128)}, f32[2,16,256]{2,1,0:T(8,128)S(1)}, f32[2,16,256]{2,1,0:T(8,128)S(1)}, f32[2,16,256,64]{2,3,1,0:T(8,128)}, f32[2,16,256,64]{2,3,1,0:...) while((s32[]{:T(128)}, f32[2,16,256]{2,1,0:T(8,128)S(1)}, ...), condition=%wide.wide.region_4.5_spmd.clone, body=%wide.wide.region_1.4_spmd.clone.sunk | while | flops 1382393344 | bytes 84222344 | solution.py:56
  158.0 6.0 fusion.249
  164.0 4.5 fusion.250
  170.4 7.2 fusion.254
  177.6 5.8 fusion.253
  189.1 6.0 fusion.249
  195.1 4.6 fusion.250
  201.5 7.9 fusion.254
  209.4 5.8 fusion.253
  220.9 6.0 fusion.249
  226.9 4.5 fusion.250
  233.3 7.9 fusion.254
  241.2 5.9 fusion.253
  252.7 6.0 fusion.249
  258.7 4.5 fusion.250
  265.1 8.1 fusion.254
  273.2 5.8 fusion.253
  288.1 7.9 fusion.60
  296.0 81.5 %all-gather.22.cloned.1.call-done = bf16[2816,1024]{1,0:T(8,128)(2,1)} async-done(((bf16[352,1024]{1,0:T(8,128)(2,1)}), bf16[2816,1024]{1,0:T(8,128)(2,1)}) %all-gather.22.cloned.1.call-update) | async-done | bytes 5767184 | tf_op jit(solution)/shard_map/all_gather | solution.py:85
  377.5 8.6 fusion.54
  386.2 84.4 %all-gather.18.cloned.1.call-done = bf16[1024,2816]{1,0:T(8,128)(2,1)} async-done(((bf16[128,2816]{1,0:T(8,128)(2,1)}), bf16[1024,2816]{1,0:T(8,128)(2,1)}) %all-gather.18.cloned.1.call-update) | async-done | bytes 5767184 | tf_op jit(solution)/shard_map/all_gather | solution.py:83
  470.6 10.6 fusion.53
  481.2 7.3 fusion.58
  488.6 4.0 multiply_reduce_fusion
  501.1 154.6 %while.43 = (s32[]{:T(128)}, f32[2,256,16,64]{1,3,2,0:T(8,128)}, f32[256,1024]{0,1:T(8,128)}, f32[256,1024]{0,1:T(8,128)}, bf16[2,1024,512]{1,2,0:T(8,128)(2,1)}...) while((s32[]{:T(128)}, f32[2,256,16,64]{1,3,2,0:T(8,128)}, ...), condition=%wide.wide.region_9.10_spmd.clone, body=%wide.wide.region_8.9_spmd.clone.sunk | while | flops 2979857920 | bytes 118595960 | solution.py:56
  505.9 4.6 fusion.278
  514.3 6.6 fusion.280
  523.3 5.3 fusion.281
  542.8 4.6 fusion.278
  551.2 6.6 fusion.280
  560.2 5.3 fusion.281
  569.9 3.9 bitcast_add_fusion.8
  581.9 4.6 fusion.278
  590.3 6.6 fusion.280
  599.3 5.3 fusion.281
  609.0 3.9 bitcast_add_fusion.8
  621.1 4.6 fusion.278
  629.4 6.6 fusion.280
  638.5 5.3 fusion.281
  648.1 3.9 bitcast_add_fusion.8
  659.5 4.3 bitcast_convert_fusion.3
  669.7 15.8 %reduce-scatter.14.cloned.1.call-done = bf16[2,256,512]{1,2,0:T(8,128)(2,1)} async-done(((bf16[2,1024,512]{1,2,0:T(8,128)(2,1)}), bf16[2,256,512]{1,2,0:T(8,128)(2,1)}) %reduce-scatter.14.cloned.1.call-update) | async-done | bytes 524304 | tf_op jit(solution)/shard_map/reduce_scatter | solution.py:247
  688.5 6.9 bitcast_convert_fusion.2
  695.4 6.8 bitcast_convert_fusion.1
  703.5 6.9 bitcast_convert_fusion
  712.3 39.5 %reduce-scatter.28.cloned.1.call-done = bf16[128,256]{1,0:T(8,128)(2,1)} async-done(((bf16[1024,256]{1,0:T(8,128)(2,1)}), bf16[128,256]{1,0:T(8,128)(2,1)}) %reduce-scatter.28.cloned.1.call-update) | async-done | bytes 65552
  753.3 63.2 %reduce-scatter.30.cloned.1.call-done = bf16[128,256]{1,0:T(8,128)(2,1)} async-done(((bf16[1024,256]{1,0:T(8,128)(2,1)}), bf16[128,256]{1,0:T(8,128)(2,1)}) %reduce-scatter.30.cloned.1.call-update) | async-done | bytes 65552
  818.1 69.0 %reduce-scatter.20.cloned.1.call-done = bf16[128,1024]{1,0:T(8,128)(2,1)} async-done(((bf16[1024,1024]{1,0:T(8,128)(2,1)}), bf16[128,1024]{1,0:T(8,128)(2,1)}) %reduce-scatter.20.cloned.1.call-update) | async-done | bytes 262160 | tf_op jit(solution)/shard_map/reduce_scatter | solution.py:278
  887.0 70.4 %reduce-scatter.16.cloned.1.call-done = bf16[128,1024]{1,0:T(8,128)(2,1)} async-done(((bf16[1024,1024]{1,0:T(8,128)(2,1)}), bf16[128,1024]{1,0:T(8,128)(2,1)}) %reduce-scatter.16.cloned.1.call-update) | async-done | bytes 262160 | tf_op jit(solution)/shard_map/reduce_scatter | solution.py:266
  957.4 66.9 %reduce-scatter.18.cloned.1.call-done = bf16[128,512]{1,0:T(8,128)(2,1)} async-done(((bf16[1024,512]{1,0:T(8,128)(2,1)}), bf16[128,512]{1,0:T(8,128)(2,1)}) %reduce-scatter.18.cloned.1.call-update) | async-done | bytes 131088 | tf_op jit(solution)/shard_map/reduce_scatter | solution.py:269
  1024.3 112.5 %reduce-scatter.22.cloned.1.call-done = bf16[128,2816]{1,0:T(8,128)(2,1)} async-done(((bf16[1024,2816]{1,0:T(8,128)(2,1)}), bf16[128,2816]{1,0:T(8,128)(2,1)}) %reduce-scatter.22.cloned.1.call-update) | async-done | bytes 720912 | tf_op jit(solution)/shard_map/reduce_scatter | solution.py:284
  1136.9 113.3 %reduce-scatter.24.cloned.1.call-done = bf16[128,2816]{1,0:T(8,128)(2,1)} async-done(((bf16[1024,2816]{1,0:T(8,128)(2,1)}), bf16[128,2816]{1,0:T(8,128)(2,1)}) %reduce-scatter.24.cloned.1.call-update) | async-done | bytes 720912 | tf_op jit(solution)/shard_map/reduce_scatter | solution.py:287
  1250.1 113.3 %reduce-scatter.26.cloned.1.call-done = bf16[352,1024]{1,0:T(8,128)(2,1)} async-done(((bf16[2816,1024]{1,0:T(8,128)(2,1)}), bf16[352,1024]{1,0:T(8,128)(2,1)}) %reduce-scatter.26.cloned.1.call-update) | async-done | bytes 720912 | tf_op jit(solution)/shard_map/reduce_scatter | solution.py:290
  1363.5 7.8 add_convert_fusion
  1374.2 19.8 %all-reduce.2 = (bf16[1024]{0:T(1024)(128)(2,1)S(1)}, bf16[1024]{0:T(1024)(128)(2,1)S(1)}) all-reduce(bf16[1024]{0:T(1024)(128)(2,1)S(1)} %get-tuple-element.603, bf16[1024]{0:T(1024)(128)(2,1)S(1)} %copy-done.49), channel_id=3, replica_groups=mesh['seq'=4,'dp'=8] {'dp'}, use_global_device_ids=true, to_apply=%region_13.14.clone | all-reduce | flops 2048 | bytes 8192
  1394.2 5.6 all-reduce.3
  1404.3 28.8 %all-reduce.7.cloned.1.call-done = (bf16[128,1024]{1,0:T(8,128)(2,1)}, bf16[128,512]{1,0:T(8,128)(2,1)}, bf16[256,128]{1,0:T(8,128)(2,1)}, bf16[256,128]{1,0:T(8...) async-done(((bf16[128,1024]{1,0:T(8,128)(2,1)}, bf16[128,512]{1,0:T(8,128)(2,1)}, ...) | async-done | bytes 2949136 | tf_op jit(solution)/shard_map/psum | solution.py:296
  (398 shorter events, 174.6 us)
Async XLA Ops:
  7.2 26.6 %copy-start.13 = (bf16[2,256,1024]{2,1,0:T(8,128)(2,1)S(1)}, bf16[2,256,1024]{2,1,0:T(8,128)(2,1)}, u32[]{:S(2)}) copy-start(bf16[2,256,1024]{2,1,0:T(8,128)(2,1)} %param.17) | copy-start | bytes 3145732
  7.2 46.5 %all-gather.10.cloned.1.call-start = ((), (), s32[]{:S(2)}) async-start(), calls=%async_computation.9 | async-start | bytes 1179648 | tf_op jit(solution)/shard_map/all_gather | solution.py:78
  9.0 135.3 %all-gather.14.cloned.1.call-start = ((), (), s32[]{:S(2)}) async-start(), calls=%async_computation.11 | async-start | bytes 2359296 | tf_op jit(solution)/shard_map/all_gather | solution.py:77
  10.8 138.8 %all-gather.12.cloned.1.call-start = ((), (), s32[]{:S(2)}) async-start(), calls=%async_computation.10 | async-start | bytes 2621440 | tf_op jit(solution)/shard_map/all_gather | solution.py:148
  33.7 110.5 %copy-start.43 = (f32[8,1,128]{2,1,0:T(1,128)}, f32[8,1,128]{2,1,0:T(1,128)S(1)}, u32[]{:S(2)}) copy-start(f32[8,1,128]{2,1,0:T(1,128)S(1)} %convert_element_type.331) | copy-start | bytes 12292
  34.6 109.6 %copy-start.45 = (f32[2,256]{1,0:T(2,128)}, f32[2,256]{1,0:T(2,128)S(1)}, u32[]{:S(2)}) copy-start(f32[2,256]{1,0:T(2,128)S(1)} %fusion.105) | copy-start | bytes 6148
  56.6 226.6 %all-gather.16.cloned.1.call-start = ((), (), s32[]{:S(2)}) async-start(), calls=%async_computation.12 | async-start | bytes 2359296 | tf_op jit(solution)/shard_map/all_gather | solution.py:81
  57.5 230.6 %all-gather.20.cloned.1.call-start = ((), (), s32[]{:S(2)}) async-start(), calls=%async_computation.14 | async-start | bytes 6488064 | tf_op jit(solution)/shard_map/all_gather | solution.py:84
  58.5 319.0 %all-gather.22.cloned.1.call-start = ((), (), s32[]{:S(2)}) async-start(), calls=%async_computation.15 | async-start | bytes 6488064 | tf_op jit(solution)/shard_map/all_gather | solution.py:85
  61.0 409.6 %all-gather.18.cloned.1.call-start = ((), (), s32[]{:S(2)}) async-start(), calls=%async_computation.13 | async-start | bytes 6488064 | tf_op jit(solution)/shard_map/all_gather | solution.py:83
  62.0 31.4 %copy-start.40 = (f32[256,128]{1,0:T(8,128)S(1)}, f32[256,128]{1,0:T(8,128)}, u32[]{:S(2)}) copy-start(f32[256,128]{1,0:T(8,128)} %param.22) | copy-start | bytes 393220
  62.0 623.5 %reduce-scatter.14.cloned.1.call-start = ((), (), s32[]{:S(2)}) async-start(), calls=%async_computation.16 | async-start | bytes 2621440 | tf_op jit(solution)/shard_map/reduce_scatter | solution.py:247
  92.6 32.9 %copy-start.17 = (bf16[256,1024]{1,0:T(8,128)(2,1)}, bf16[256,1024]{1,0:T(8,128)(2,1)S(1)}, u32[]{:S(2)}) copy-start(bf16[256,1024]{1,0:T(8,128)(2,1)S(1)} %all_gather.37) | copy-start | bytes 1572868
  93.0 32.5 %copy-start.52 = (s32[2,2]{1,0:T(2,128)S(1)}, s32[2,2]{1,0:T(2,128)}, u32[]{:S(2)}) copy-start(s32[2,2]{1,0:T(2,128)} %param.29) | copy-start | bytes 52
  93.0 32.6 %copy-start.53 = (f32[128]{0:T(128)S(1)}, f32[128]{0:T(128)}, u32[]{:S(2)}) copy-start(f32[128]{0:T(128)} %param.24) | copy-start | bytes 1540
  123.2 24.9 %copy-start.18 = (bf16[256,1024]{1,0:T(8,128)(2,1)}, bf16[256,1024]{1,0:T(8,128)(2,1)S(1)}, u32[]{:S(2)}) copy-start(bf16[256,1024]{1,0:T(8,128)(2,1)S(1)} %all_gather.39) | copy-start | bytes 1572868
  164.0 4.6 copy-start.12
  170.4 7.2 copy-start.6
  170.4 7.2 copy-start.20
  177.6 7.2 copy-start.11
  195.1 4.6 copy-start.12
  201.5 7.9 copy-start.6
  201.5 7.9 copy-start.20
  209.4 7.2 copy-start.11
  226.9 4.6 copy-start.12
  233.3 7.9 copy-start.6
  233.3 7.9 copy-start.20
  241.2 7.2 copy-start.11
  258.7 4.6 copy-start.12
  265.1 8.1 copy-start.6
  265.1 8.1 copy-start.20
  273.2 7.1 copy-start.11
  288.1 182.5 %copy-start.28 = (bf16[2,256,1024]{2,1,0:T(8,128)(2,1)}, bf16[2,256,1024]{2,1,0:T(8,128)(2,1)S(1)}, u32[]{:S(2)}) copy-start(bf16[2,256,1024]{2,1,0:T(8,128)(2,1)S(1)} %multiply_convert_fusion.3) | copy-start | bytes 3145732
  481.2 7.4 copy-start.56
  481.2 7.4 copy-start.55
  481.2 7.4 copy-start.8
  481.2 7.4 copy-start.50
  488.6 4.0 copy-start.30
  505.9 4.6 copy-start.2
  523.3 5.3 copy-start.3
  542.8 4.6 copy-start.2
  560.2 5.3 copy-start.3
  569.9 3.9 copy-start.1
  581.9 4.6 copy-start.2
  599.3 5.3 copy-start.3
  609.0 3.9 copy-start.1
  621.1 4.6 copy-start.2
  638.5 5.3 copy-start.3
  648.1 3.9 copy-start.1
  655.8 96.0 %reduce-scatter.28.cloned.1.call-start = ((), (), s32[]{:S(2)}) async-start(), calls=%async_computation.23 | async-start | bytes 589824
  658.2 158.3 %reduce-scatter.30.cloned.1.call-start = ((), (), s32[]{:S(2)}) async-start(), calls=%async_computation.24 | async-start | bytes 589824
  659.5 227.6 %reduce-scatter.20.cloned.1.call-start = ((), (), s32[]{:S(2)}) async-start(), calls=%async_computation.19 | async-start | bytes 2359296 | tf_op jit(solution)/shard_map/reduce_scatter | solution.py:278
  663.8 293.6 %reduce-scatter.16.cloned.1.call-start = ((), (), s32[]{:S(2)}) async-start(), calls=%async_computation.17 | async-start | bytes 2359296 | tf_op jit(solution)/shard_map/reduce_scatter | solution.py:266
  669.7 18.8 %copy-start.29 = (bf16[2,256,1024]{2,1,0:T(8,128)(2,1)S(1)}, bf16[2,256,1024]{2,1,0:T(8,128)(2,1)}, u32[]{:S(2)}) copy-start(bf16[2,256,1024]{2,1,0:T(8,128)(2,1)} %copy-done.28) | copy-start | bytes 3145732
  669.7 354.6 %reduce-scatter.18.cloned.1.call-start = ((), (), s32[]{:S(2)}) async-start(), calls=%async_computation.18 | async-start | bytes 1179648 | tf_op jit(solution)/shard_map/reduce_scatter | solution.py:269
  688.4 448.4 %reduce-scatter.22.cloned.1.call-start = ((), (), s32[]{:S(2)}) async-start(), calls=%async_computation.20 | async-start | bytes 6488064 | tf_op jit(solution)/shard_map/reduce_scatter | solution.py:284
  695.4 554.8 %reduce-scatter.24.cloned.1.call-start = ((), (), s32[]{:S(2)}) async-start(), calls=%async_computation.21 | async-start | bytes 6488064 | tf_op jit(solution)/shard_map/reduce_scatter | solution.py:287
  702.3 661.1 %reduce-scatter.26.cloned.1.call-start = ((), (), s32[]{:S(2)}) async-start(), calls=%async_computation.22 | async-start | bytes 6488064 | tf_op jit(solution)/shard_map/reduce_scatter | solution.py:290
  710.4 653.0 %copy-start.9 = (f32[2,256,1024]{2,1,0:T(8,128)S(1)}, f32[2,256,1024]{2,1,0:T(8,128)}, u32[]{:S(2)}) copy-start(f32[2,256,1024]{2,1,0:T(8,128)} %copy-done.7) | copy-start | bytes 6291460
  710.4 722.7 %all-reduce.7.cloned.1.call-start = ((), (), s32[]{:S(2)}) async-start(), calls=%async_computation.25 | async-start | bytes 5898240 | tf_op jit(solution)/shard_map/psum | solution.py:296
  1363.4 7.8 copy-start.27
  1363.5 7.8 copy-start.51
  1373.0 27.9 %copy-start.48 = (f32[2,256]{1,0:T(2,128)S(1)}, f32[2,256]{1,0:T(2,128)}, u32[]{:S(2)}) copy-start(f32[2,256]{1,0:T(2,128)} %copy-done.47) | copy-start | bytes 6148
  1436.7 4.4 copy-start.41
  (40 other events, 80.9 us)
Sparse Core Ops, SparseCore 0:
  10.7 42.9 all-gather.9
  56.4 55.8 all-gather.13
  114.5 25.0 all-gather.11
  141.5 49.2 all-gather.15
  192.9 91.1 all-gather.19
  286.6 90.8 all-gather.21
  379.7 90.8 all-gather.17
  655.9 29.5 reduce-scatter.13
  689.8 61.9 reduce-scatter.27
  755.5 60.9 reduce-scatter.29
  820.4 66.5 reduce-scatter.19
  890.8 66.5 reduce-scatter.15
  961.8 62.4 reduce-scatter.17
  1027.8 109.0 reduce-scatter.21
  1140.4 109.7 reduce-scatter.23
  1253.6 109.7 reduce-scatter.25
  1366.7 66.3 all-reduce.6
where the time goes:
time: 1450 us
  waiting for transfers between devices  878 us (61%)
  matrix products  289 us (20%)
  blocking collectives  127 us (9%)
  local copies, waits for them, and re-layouts  71 us (5%)
  other arithmetic  66.6 us (5%)
  between operations  15.4 us (1%)
    reduce_scatter x1, waiting for transfers between devices, per_device(): lax.psum_scatter(grad_down.astype(jnp.bfloat16), 'dp', scatter_dimension=...  113 us
    reduce_scatter x1, waiting for transfers between devices, per_device(): lax.psum_scatter(grad_upward.astype(jnp.bfloat16), 'dp', scatter_dimensio...  113 us
    reduce_scatter x1, waiting for transfers between devices, per_device(): lax.psum_scatter(grad_gate.astype(jnp.bfloat16), 'dp', scatter_dimension=...  113 us
    unnamed x19, waiting for transfers between devices  103 us
    all_gather x1, waiting for transfers between devices, per_device(): lax.all_gather(gate_weight.astype(low_type), 'dp', axis=0, tiled=True)  84.4 us
    all_gather x1, waiting for transfers between devices, per_device(): lax.all_gather(down_weight.astype(low_type), 'dp', axis=0, tiled=True)  81.5 us
    reduce_scatter x1, waiting for transfers between devices, per_device(): lax.psum_scatter(grad_query_w.astype(jnp.bfloat16), 'dp', scatter_dimensi...  70.4 us
    reduce_scatter x1, waiting for transfers between devices, per_device(): lax.psum_scatter(grad_output.astype(jnp.bfloat16), 'dp', scatter_dimensio...  69 us
  transfers between devices with their start and end apart: 17, of which 13 were waited for; matrix products, arithmetic and copies ran while one was open for 15% of the time, Pallas kernels for 0%

commit v1 on v0

v1 whole, which is shorter than its diff:
```python
import jax
import jax.numpy as jnp
from jax import lax
from jax.experimental import pallas as pl
from jax.experimental.pallas import tpu as pltpu
from jax.sharding import PartitionSpec as P

D = 1024
H = 16
HD = 64
KVH = 2
LAT = 256
GH = H // KVH
GW = D // KVH
EPS = 1e-06
SCALE = HD ** (-0.5)
LOG2E = 1.4426950408889634
NEG = -1e30

LOW = jnp.bfloat16
F32 = jnp.float32
ALL = ("seq", "dp")
VMEM_LIMIT = 56 * 1024 * 1024


def mm(left, right):
    return jnp.dot(left, right, preferred_element_type=F32)


def tn(left, right):
    return lax.dot_general(left, right, (((0,), (0,)), ((), ())), preferred_element_type=F32)


def nt(left, right):
    return lax.dot_general(left, right, (((1,), (1,)), ((), ())), preferred_element_type=F32)


def block_bias(k0, q0, first, width):
    kpos = k0 + lax.broadcasted_iota(jnp.int32, (width, width), 0)
    qpos = q0 + lax.broadcasted_iota(jnp.int32, (width, width), 1)
    lowest = jnp.where(qpos >= first, first, 0)
    return jnp.where((kpos <= qpos) & (kpos >= lowest), 0.0, NEG)


def block_needed(k0, q0, first, width):
    before = jnp.logical_and(q0 >= first, k0 + (width - 1) < first)
    return jnp.logical_and(k0 <= q0, jnp.logical_not(before))


def forward_kernel(nkb, batch, width, meta, qt, kxt, vxt, c, ct, o_low, o_full, mix_out, lse_out, q_s, acc, m_s, l_s):
    b, qb = pl.program_id(0), pl.program_id(1)
    q0, first, diag = meta[nkb + qb], meta[nkb + 2 + b], meta[nkb + 2 + batch] + qb
    for h in range(GH):
        cols = slice(h * width, (h + 1) * width)
        rows = slice(h * HD, (h + 1) * HD)
        q_s[:, cols] = (tn(kxt[rows, :], qt[0, rows, :]) * (SCALE * LOG2E)).astype(LOW)
    m_s[...] = jnp.full_like(m_s, NEG)
    l_s[...] = jnp.zeros_like(l_s)
    acc[...] = jnp.zeros_like(acc)

    def step(j, carry):
        kb = lax.rem(diag + j, nkb)
        k0 = meta[kb]

        @pl.when(block_needed(k0, q0, first, width))
        def _():
            bias = block_bias(k0, q0, first, width)
            keys, keys_t = c[0, kb], ct[0, kb]
            for h in range(GH):
                cols = slice(h * width, (h + 1) * width)
                s = mm(keys, q_s[:, cols]) + bias
                m_old = m_s[:, cols]
                m_new = jnp.maximum(m_old, jnp.max(s, axis=0, keepdims=True))
                p = jnp.exp2(s - m_new)
                alpha = jnp.exp2(m_old - m_new)
                m_s[:, cols] = m_new
                l_s[:, cols] = l_s[:, cols] * alpha + jnp.sum(p, axis=0, keepdims=True)
                acc[:, cols] = acc[:, cols] * alpha + mm(keys_t, p.astype(LOW))

        return carry

    lax.fori_loop(0, nkb, step, 0)
    for h in range(GH):
        cols = slice(h * width, (h + 1) * width)
        rows = slice(h * HD, (h + 1) * HD)
        total = l_s[:, cols]
        mixed = (acc[:, cols] * (1.0 / total)).astype(LOW)
        mix_out[0, 0, :, cols] = mixed
        out = mm(vxt[rows, :], mixed)
        o_full[0, rows, :] = out
        o_low[0, rows, :] = out.astype(LOW)
        lse_out[0, 0, :, cols] = m_s[:, cols] + jnp.log(total) * LOG2E


def backward_kernel(
    nkb, batch, width, meta, qt, dot_, o_full, mix, lse, kxt, vxt, c, ct, dqt, dc, dkxt, dvxt,
    q_s, q_n, do_t, do_n, delta, dq, ds_s, p_s,
):
    b, qb = pl.program_id(0), pl.program_id(1)
    q0, first, diag = meta[nkb + qb], meta[nkb + 2 + b], meta[nkb + 2 + batch] + qb

    @pl.when(qb == 0)
    def _():
        dc[...] = jnp.zeros_like(dc)

    @pl.when(jnp.logical_and(b == 0, qb == 0))
    def _():
        dkxt[...] = jnp.zeros_like(dkxt)
        dvxt[...] = jnp.zeros_like(dvxt)

    for h in range(GH):
        cols = slice(h * width, (h + 1) * width)
        rows = slice(h * HD, (h + 1) * HD)
        qh, kh, doh, vh = qt[0, rows, :], kxt[rows, :], dot_[0, rows, :], vxt[rows, :]
        q_s[:, cols] = (tn(kh, qh) * (SCALE * LOG2E)).astype(LOW)
        q_n[cols, :] = (tn(qh, kh) * SCALE).astype(LOW)
        do_t[:, cols] = tn(vh, doh).astype(LOW)
        do_n[cols, :] = tn(doh, vh).astype(LOW)
        delta[:, cols] = jnp.sum(doh.astype(F32) * o_full[0, rows, :], axis=0, keepdims=True)
    dq[...] = jnp.zeros_like(dq)

    def step(j, carry):
        kb = lax.rem(diag + j, nkb)
        k0 = meta[kb]

        @pl.when(block_needed(k0, q0, first, width))
        def _():
            bias = block_bias(k0, q0, first, width)
            keys, keys_t = c[0, kb], ct[0, kb]
            for h in range(GH):
                cols = slice(h * width, (h + 1) * width)
                s = mm(keys, q_s[:, cols]) + bias
                p = jnp.exp2(s - lse[0, 0, :, cols])
                dp = mm(keys, do_t[:, cols])
                ds = (p * (dp - delta[:, cols])).astype(LOW)
                p_s[:, cols] = p.astype(LOW)
                ds_s[:, cols] = ds
                dq[:, cols] += mm(keys_t, ds)
            dc[0, kb] += mm(ds_s[...], q_n[...]) + mm(p_s[...], do_n[...])

        return carry

    lax.fori_loop(0, nkb, step, 0)
    for h in range(GH):
        cols = slice(h * width, (h + 1) * width)
        rows = slice(h * HD, (h + 1) * HD)
        dq_low = (dq[:, cols] * SCALE).astype(LOW)
        dqt[0, rows, :] = mm(kxt[rows, :], dq_low).astype(LOW)
        dkxt[rows, :] += nt(qt[0, rows, :], dq_low)
        dvxt[rows, :] += nt(dot_[0, rows, :], mix[0, 0, :, cols])


def attention_specs(nkb, width):
    wide = GH * width
    return {
        "meta": pl.BlockSpec(memory_space=pltpu.SMEM),
        "q": pl.BlockSpec((1, GW, width), lambda b, q: (b, 0, q)),
        "expand": pl.BlockSpec((GW, LAT), lambda b, q: (0, 0)),
        "c": pl.BlockSpec((1, nkb, width, LAT), lambda b, q: (b, 0, 0, 0)),
        "ct": pl.BlockSpec((1, nkb, LAT, width), lambda b, q: (b, 0, 0, 0)),
        "mix": pl.BlockSpec((1, 1, LAT, wide), lambda b, q: (b, q, 0, 0)),
        "lse": pl.BlockSpec((1, 1, 1, wide), lambda b, q: (b, q, 0, 0)),
    }


def attention_forward(meta, qt, kxt, vxt, c, ct):
    batch, nkb, width, _ = c.shape
    wide = GH * width
    sp = attention_specs(nkb, width)
    pairs = batch * 7 * GH * width * width * LAT * 2
    return pl.pallas_call(
        lambda *refs: forward_kernel(nkb, batch, width, *refs),
        grid=(batch, 2),
        in_specs=[sp["meta"], sp["q"], sp["expand"], sp["expand"], sp["c"], sp["ct"]],
        out_specs=[sp["q"], sp["q"], sp["mix"], sp["lse"]],
        out_shape=[
            jax.ShapeDtypeStruct(qt.shape, LOW),
            jax.ShapeDtypeStruct(qt.shape, F32),
            jax.ShapeDtypeStruct((batch, 2, LAT, wide), LOW),
            jax.ShapeDtypeStruct((batch, 2, 1, wide), F32),
        ],
        scratch_shapes=[
            pltpu.VMEM((LAT, wide), LOW),
            pltpu.VMEM((LAT, wide), F32),
            pltpu.VMEM((1, wide), F32),
            pltpu.VMEM((1, wide), F32),
        ],
        compiler_params=pltpu.CompilerParams(
            dimension_semantics=("arbitrary", "arbitrary"), vmem_limit_bytes=VMEM_LIMIT
        ),
        cost_estimate=pl.CostEstimate(
            flops=2 * pairs, bytes_accessed=16 << 20, transcendentals=batch * 7 * GH * width * width
        ),
        name="attention_forward",
    )(meta, qt, kxt, vxt, c, ct)


def attention_backward(meta, qt, dot_, o_full, mix, lse, kxt, vxt, c, ct):
    batch, nkb, width, _ = c.shape
    wide = GH * width
    sp = attention_specs(nkb, width)
    pairs = batch * 7 * GH * width * width * LAT * 2
    return pl.pallas_call(
        lambda *refs: backward_kernel(nkb, batch, width, *refs),
        grid=(batch, 2),
        in_specs=[
            sp["meta"], sp["q"], sp["q"], sp["q"], sp["mix"], sp["lse"],
            sp["expand"], sp["expand"], sp["c"], sp["ct"],
        ],
        out_specs=[sp["q"], sp["c"], sp["expand"], sp["expand"]],
        out_shape=[
            jax.ShapeDtypeStruct(qt.shape, LOW),
            jax.ShapeDtypeStruct(c.shape, F32),
            jax.ShapeDtypeStruct(kxt.shape, F32),
            jax.ShapeDtypeStruct(vxt.shape, F32),
        ],
        scratch_shapes=[
            pltpu.VMEM((LAT, wide), LOW),
            pltpu.VMEM((wide, LAT), LOW),
            pltpu.VMEM((LAT, wide), LOW),
            pltpu.VMEM((wide, LAT), LOW),
            pltpu.VMEM((1, wide), F32),
            pltpu.VMEM((LAT, wide), F32),
            pltpu.VMEM((width, wide), LOW),
            pltpu.VMEM((width, wide), LOW),
        ],
        compiler_params=pltpu.CompilerParams(
            dimension_semantics=("arbitrary", "arbitrary"), vmem_limit_bytes=VMEM_LIMIT
        ),
        cost_estimate=pl.CostEstimate(
            flops=5 * pairs, bytes_accessed=24 << 20, transcendentals=batch * 7 * GH * width * width
        ),
        name="attention_backward",
    )(meta, qt, dot_, o_full, mix, lse, kxt, vxt, c, ct)


class Place:
    def __init__(self):
        self.seq, self.dp = lax.axis_size("seq"), lax.axis_size("dp")
        s, d = lax.axis_index("seq"), lax.axis_index("dp")
        self.core, self.chip = s % 2, s // 2
        self.y, self.x, self.z = s // 2, d % 2, d // 2
        self.square = self.seq == 4 and self.dp == 8

    def pairs(self, move):
        found = []
        for s in range(self.seq):
            for d in range(self.dp):
                target = move(s, d)
                if target is not None:
                    found.append((s * self.dp + d, target[0] * self.dp + target[1]))
        return found

    def send(self, value, move):
        return lax.ppermute(value, ALL, self.pairs(move))

    def to_core(self, value):
        return self.send(value, lambda s, d: (s ^ 1, d))

    def to_y(self, value):
        return self.send(value, lambda s, d: (s ^ 2, d))

    def to_x(self, value):
        return self.send(value, lambda s, d: (s, d ^ 1))

    def to_z(self, value, step):
        return self.send(value, lambda s, d: (s, (d + 2 * step) % 8))

    def up_y(self, value):
        return self.send(value, lambda s, d: (s + 2, d) if s < 2 else None)

    def down_y(self, value):
        return self.send(value, lambda s, d: (s - 2, d) if s >= 2 else None)


def half(value, index, axis, count=2):
    size = value.shape[axis] // count
    return lax.dynamic_slice_in_dim(value, index * size, size, axis)


def ordered(flag, own, other, axis):
    return jnp.where(
        flag == 0, jnp.concatenate([own, other], axis), jnp.concatenate([other, own], axis)
    )


def add_low(own, other):
    return (own.astype(F32) + other.astype(F32)).astype(LOW)


def gather_z(pl_, piece):
    seen = [piece] + [pl_.to_z(piece, k) for k in (1, 2, 3)]
    seen = seen[::-1]
    return lax.dynamic_slice_in_dim(jnp.stack(seen + seen[:3]), 3 - pl_.z, 4, 0)


def gather_xy(pl_, base, x_first):
    if x_first:
        near = pl_.to_x(base)
        far, both = pl_.to_y(base), pl_.to_y(near)
    else:
        far = pl_.to_y(base)
        near, both = pl_.to_x(base), pl_.to_x(far)
    rel = {(0, 0): base, (1, 0): near, (0, 1): far, (1, 1): both}
    out = {}
    for x in range(2):
        for y in range(2):
            a = [jnp.where(pl_.y == y, rel[(r, 0)], rel[(r, 1)]) for r in range(2)]
            out[(x, y)] = jnp.where(pl_.x == x, a[0], a[1])
    return out


def over_x(got, y, cols=slice(None)):
    return jnp.stack([got[(0, y)][..., cols], got[(1, y)][..., cols]], axis=1)


def gather_rows(pl_, piece, x_first):
    got = gather_xy(pl_, gather_z(pl_, piece), x_first)
    block = jnp.concatenate([over_x(got, 0), over_x(got, 1)], axis=-1)
    mine = half(block, pl_.core, 0)
    other = pl_.to_core(half(block, 1 - pl_.core, 0))
    full = ordered(pl_.core, mine, other, -1)
    return full.reshape(-1, full.shape[-1])


def scatter_yx(pl_, keep, send, y_first):
    x, rest = pl_.x, 1 - pl_.x
    if y_first:
        one = add_low(keep, pl_.to_y(send))
        return add_low(half(one, x, 1), pl_.to_x(half(one, rest, 1)))[:, 0]
    one = add_low(half(keep, x, 1), pl_.to_x(half(keep, rest, 1)))
    two = add_low(half(send, x, 1), pl_.to_x(half(send, rest, 1)))
    return add_low(one, pl_.to_y(two))[:, 0]


def scatter_z(pl_, parts):
    total = half(parts, pl_.z, 0, 4)[0].astype(F32)
    for k in (1, 2, 3):
        total = total + pl_.to_z(half(parts, (pl_.z + k) % 4, 0, 4), k)[0].astype(F32)
    return total


def pick(flag, zero, one):
    return jnp.where(flag == 0, zero, one)


def scatter(pl_, zero, one):
    keep, send = pick(pl_.y, zero, one), pick(pl_.y, one, zero)
    a = scatter_yx(pl_, keep[:2], send[:2], True)
    b = scatter_yx(pl_, keep[2:], send[2:], False)
    return scatter_z(pl_, jnp.concatenate([a, b], 0))


def scatter_rows(pl_, grad):
    rows = grad.shape[0] // 4
    grad = grad.reshape(2, 2, rows, 2 * GW)
    mine, other = half(grad, pl_.core, 3), pl_.to_core(half(grad, 1 - pl_.core, 3))
    y = pl_.y
    a = scatter_yx(pl_, half(mine, y, 3), half(mine, 1 - y, 3), True)
    b = scatter_yx(pl_, half(other, y, 3), half(other, 1 - y, 3), False)
    own = scatter_z(pl_, ordered(pl_.core, a, b, 0)).astype(LOW)
    wide = ordered(y, own, pl_.to_y(own), 1)
    return ordered(pl_.core, wide, pl_.to_core(wide), 1).astype(F32)


class Square:
    def __init__(self, place):
        self.p = place

    def gather(self, w):
        p = self.p
        core, y = p.core, p.y
        ff = w["gate"].shape[1] // 2
        quarter = 2 * core + y

        def cols(value, count, index):
            return half(value, index, 1, count).astype(LOW)

        query = cols(w["query"], 4, quarter)
        latent = cols(w["latent"], 4, quarter)
        kv = half(pick(y, w["key"], w["value"]), core, 0).astype(LOW).T
        gains = jnp.stack([w["gain1"], w["gain2"]] + [jnp.zeros_like(w["gain1"])] * 6)
        first_a = jnp.concatenate([query, kv], 1)
        first_b = jnp.concatenate([latent, gains.astype(LOW)], 0)
        za, zb = gather_z(p, first_a), gather_z(p, first_b)
        got_a, got_b = gather_xy(p, za, True), gather_xy(p, zb, False)
        out = {}
        out["query"] = jnp.concatenate(
            [over_x(got_a, 0, slice(0, 256)), over_x(got_a, 1, slice(0, 256))], -1
        ).reshape(D, GW)
        lat = [over_x(got_b, i) for i in range(2)]
        out["latent"] = jnp.concatenate([v[:, :, :128] for v in lat], -1).reshape(D, LAT)
        out["gain1"] = lat[0][:, :, 128].reshape(D)
        out["gain2"] = lat[0][:, :, 129].reshape(D)
        kv_all = jnp.stack([over_x(got_a, i, slice(256, 384)) for i in range(2)])
        mine = half(kv_all, core, 1)
        other = p.to_core(half(kv_all, 1 - core, 1))
        kv_full = ordered(core, mine, other, -1).reshape(2, GW, LAT)
        out["key_t"], out["value_t"] = kv_full[0], kv_full[1]
        out["output"] = gather_rows(p, cols(w["output"], 4, quarter), False)
        gate_up = half(pick(y, w["gate"], w["up"]), core, 1).astype(LOW)
        zg = gather_z(p, gate_up)
        ga, gb = gather_xy(p, zg[:2], True), gather_xy(p, zg[2:], False)
        for i, name in ((0, "gate"), (1, "up")):
            out[name] = jnp.concatenate([over_x(ga, i), over_x(gb, i)], 0).reshape(D, ff)
        out["down"] = gather_rows(p, cols(w["down"], 4, quarter), True)
        return out

    def down(self, grad):
        return scatter_rows(self.p, grad)

    def output(self, grad):
        return scatter_rows(self.p, grad)

    def gate_up(self, gate, up):
        p = self.p
        ff = gate.shape[1]
        own = scatter(p, gate.reshape(4, 2, 128, ff), up.reshape(4, 2, 128, ff)).astype(LOW)
        other = p.to_y(own)
        both = jnp.stack([pick(p.y, own, other), pick(p.y, other, own)])
        full = ordered(p.core, both, p.to_core(both), 2).astype(F32)
        return full[0], full[1]

    def query_kv(self, query, key_t, value_t):
        p = self.p
        kv = jnp.stack([key_t, value_t]).reshape(2, 2, 2, 128, LAT)
        mine, other = half(kv, p.core, 4), p.to_core(half(kv, 1 - p.core, 4))
        kv = ordered(p.core, mine, other, 1)
        query = query.reshape(4, 2, 128, GW)
        own = scatter(
            p,
            jnp.concatenate([query[..., :256], kv[0]], -1),
            jnp.concatenate([query[..., 256:], kv[1]], -1),
        ).astype(LOW)
        other = p.to_y(own)
        zero, one = pick(p.y, own, other), pick(p.y, other, own)
        both = jnp.concatenate([zero[:, :256], one[:, :256], zero[:, 256:], one[:, 256:]], 1)
        far = p.to_core(both)
        grad_query = ordered(p.core, both[:, :GW], far[:, :GW], 1)
        grad_key = ordered(p.core, both[:, GW : GW + 128], far[:, GW : GW + 128], 1)
        grad_value = ordered(p.core, both[:, GW + 128 :], far[:, GW + 128 :], 1)
        return grad_query.astype(F32), grad_key.T.astype(F32), grad_value.T.astype(F32)

    def latent_gains(self, latent, gain1, gain2):
        p = self.p
        latent = latent.reshape(4, 2, 128, LAT)
        rest = jnp.zeros((4, 2, 7, 128), LOW)

        def part(i, gain):
            row = gain.astype(LOW).reshape(4, 2, 1, 128)
            return jnp.concatenate([latent[..., i * 128 : (i + 1) * 128], row, rest], 2)

        own = scatter(p, part(0, gain1), part(1, gain2)).astype(LOW)
        other = p.to_y(own)
        both = ordered(p.y, own, other, 1)
        far = p.to_core(both)
        grad = ordered(p.core, both[:128], far[:128], 1).astype(F32)
        gains = both[128].astype(F32) + far[128].astype(F32)
        return grad, gains[:128], gains[128:]


class Plain:
    def __init__(self, place):
        self.p = place
        count = place.seq // 2
        self.same_core = [[2 * i + c for i in range(count)] for c in range(2)]
        self.chip = [[2 * i, 2 * i + 1] for i in range(count)]

    def gather(self, w):
        core = self.p.core

        def full(value, axis=0):
            return lax.all_gather(value.astype(LOW), "dp", axis=axis, tiled=True)

        out = {name: full(half(w[name], core, 1)) for name in ("query", "latent", "gate", "up")}
        out["key_t"] = half(full(w["key"].T), core, 0)
        out["value_t"] = half(full(w["value"].T), core, 0)
        out["output"] = half(full(w["output"]), core, 0)
        out["down"] = half(full(w["down"]), core, 0)
        out["gain1"], out["gain2"] = full(w["gain1"]), full(w["gain2"])
        return out

    def columns(self, grad):
        share = lax.psum_scatter(grad.astype(LOW), "dp", scatter_dimension=0, tiled=True)
        share = lax.psum(share, "seq", axis_index_groups=self.same_core)
        return lax.all_gather(
            share, "seq", axis=1, tiled=True, axis_index_groups=self.chip
        ).astype(F32)

    def rows(self, grad):
        grad = grad.astype(LOW)
        grad = ordered(self.p.core, grad, jnp.zeros_like(grad), 0)
        share = lax.psum_scatter(grad, "dp", scatter_dimension=0, tiled=True)
        return lax.psum(share, "seq").astype(F32)

    def gain(self, grad):
        share = lax.psum_scatter(grad.astype(LOW), "dp", scatter_dimension=0, tiled=True)
        return lax.psum(share, "seq").astype(F32)

    def down(self, grad):
        return self.rows(grad)

    def output(self, grad):
        return self.rows(grad)

    def gate_up(self, gate, up):
        return self.columns(gate), self.columns(up)

    def query_kv(self, query, key_t, value_t):
        return self.columns(query), self.rows(key_t).T, self.rows(value_t).T

    def latent_gains(self, latent, gain1, gain2):
        return self.columns(latent), self.gain(gain1), self.gain(gain2)


def inverse_rms(values):
    return lax.rsqrt(jnp.mean(values * values, axis=-1, keepdims=True) + EPS)


def norm_back(grad, normed, inverse, gain):
    scaled = grad * gain
    return inverse * (scaled - normed * jnp.mean(scaled * normed, axis=-1, keepdims=True))


def per_device(
    tokens,
    attn_gain,
    query_weight,
    latent_weight,
    key_expand,
    value_expand,
    output_weight,
    mlp_gain,
    gate_weight,
    up_weight,
    down_weight,
    cotangent,
    lengths,
):
    p = Place()
    ways = Square(p) if p.square else Plain(p)
    batch, length, _ = tokens.shape
    count = 2 * batch * length
    w = ways.gather(
        {
            "gain1": attn_gain,
            "query": query_weight,
            "latent": latent_weight,
            "key": key_expand,
            "value": value_expand,
            "output": output_weight,
            "gain2": mlp_gain,
            "gate": gate_weight,
            "up": up_weight,
            "down": down_weight,
        }
    )

    def chip(own):
        return jnp.stack([own, p.to_core(own)], axis=1)

    def chip_sum(partial):
        return partial[:, 0] + p.to_core(partial[:, 1].astype(LOW)).astype(F32)

    gain1, gain2 = w["gain1"].astype(F32), w["gain2"].astype(F32)
    firsts = lengths[:, 0]
    chips = p.seq // 2

    rows = chip(tokens).astype(F32)
    first_low = (rows * inverse_rms(rows) * gain1).astype(LOW)
    first_flat = first_low.reshape(batch, 2 * length, D)
    latent = jnp.einsum(
        "btd,dl->btl", first_flat, w["latent"], preferred_element_type=F32
    ).astype(LOW)
    query_t = jnp.einsum(
        "dn,btd->bnt", w["query"], first_flat, preferred_element_type=F32
    ).astype(LOW)
    blocks = latent.reshape(batch, 2, length, LAT)
    starts = jnp.stack([p.core, 1 - p.core]).astype(jnp.int32) * length
    base = p.chip * 2 * length
    if p.square:
        keys = jnp.concatenate([blocks, p.up_y(blocks)], axis=1)
        far = jnp.where(p.chip == 0, 2 * length, 0)
        key_starts = jnp.concatenate([base + starts, far + starts])
        diag = jnp.zeros((1,), jnp.int32)
    else:
        keys = lax.all_gather(blocks, "seq", axis=1, tiled=True, axis_index_groups=ways.same_core)
        key_starts = (
            2 * length * jnp.arange(chips, dtype=jnp.int32)[:, None] + starts[None, :]
        ).reshape(-1)
        diag = (2 * p.chip).astype(jnp.int32).reshape(1)
    keys_t = jnp.swapaxes(keys, 2, 3)
    meta = jnp.concatenate([key_starts, base + starts, firsts, diag]).astype(jnp.int32)
    out_low, out_full, mixed, lse = attention_forward(
        meta, query_t, w["key_t"], w["value_t"], keys, keys_t
    )
    branch = jnp.einsum("bnt,nd->btd", out_low, w["output"], preferred_element_type=F32)
    middle = tokens.astype(F32) + chip_sum(branch.reshape(batch, 2, length, D))

    inverse2 = inverse_rms(middle)
    normed2 = middle * inverse2
    second = chip((normed2 * gain2).astype(LOW)).reshape(count, D)
    cot = chip(cotangent).reshape(count, D)
    gate = mm(second, w["gate"])
    up = mm(second, w["up"])
    sig = jax.nn.sigmoid(gate)
    act = gate * sig
    hidden = (act * up).astype(LOW)
    layer_out = (middle + chip_sum(mm(hidden, w["down"]).reshape(batch, 2, length, D))).astype(LOW)
    grad_down = ways.down(tn(hidden, cot).astype(LOW))
    d_hidden = nt(cot, w["down"])
    d_gate = (d_hidden * up * sig * (1.0 + gate * (1.0 - sig))).astype(LOW)
    d_up = (d_hidden * act).astype(LOW)
    grad_gate, grad_up = ways.gate_up(tn(second, d_gate).astype(LOW), tn(second, d_up).astype(LOW))
    d_second = chip_sum((nt(d_gate, w["gate"]) + nt(d_up, w["up"])).reshape(batch, 2, length, D))
    gain2_sum = jnp.sum(d_second * normed2, axis=(0, 1))
    d_middle = cotangent.astype(F32) + norm_back(d_second, normed2, inverse2, gain2)

    d_a = chip(d_middle.astype(LOW)).reshape(batch, 2 * length, D)
    grad_output = ways.output(
        jnp.einsum("bnt,btd->nd", out_low, d_a, preferred_element_type=F32).astype(LOW)
    )
    d_out_t = jnp.einsum(
        "nd,btd->bnt", w["output"], d_a, preferred_element_type=F32
    ).astype(LOW)
    dq_t, d_keys, d_key_t, d_value_t = attention_backward(
        meta, query_t, d_out_t, out_full, mixed, lse, w["key_t"], w["value_t"], keys, keys_t
    )
    if p.square:
        d_blocks = d_keys[:, :2] + p.down_y(d_keys[:, 2:].astype(LOW)).astype(F32)
    else:
        d_blocks = lax.psum_scatter(
            d_keys.astype(LOW),
            "seq",
            scatter_dimension=1,
            tiled=True,
            axis_index_groups=ways.same_core,
        )
    d_latent = d_blocks.astype(LOW).reshape(batch, 2 * length, LAT)
    grad_query, grad_key, grad_value = ways.query_kv(
        jnp.einsum("btd,bnt->dn", first_flat, dq_t, preferred_element_type=F32).astype(LOW),
        d_key_t.astype(LOW),
        d_value_t.astype(LOW),
    )
    d_first = jnp.einsum(
        "bnt,dn->btd", dq_t, w["query"], preferred_element_type=F32
    ) + jnp.einsum("btl,dl->btd", d_latent, w["latent"], preferred_element_type=F32)
    d_first = chip_sum(d_first.reshape(batch, 2, length, D))
    own = tokens.astype(F32)
    inverse1 = inverse_rms(own)
    normed1 = own * inverse1
    gain1_sum = jnp.sum(d_first * normed1, axis=(0, 1))
    grad_tokens = d_middle + norm_back(d_first, normed1, inverse1, gain1)
    grad_latent, grad_gain1, grad_gain2 = ways.latent_gains(
        jnp.einsum("btd,btl->dl", first_flat, d_latent, preferred_element_type=F32).astype(LOW),
        gain1_sum,
        gain2_sum,
    )
    return (
        layer_out,
        grad_tokens,
        grad_gain1,
        grad_query,
        grad_latent,
        grad_key,
        grad_value,
        grad_output,
        grad_gain2,
        grad_gate,
        grad_up,
        grad_down,
    )


def solution(mesh):
    rows, gain, weight, across = P("dp", "seq", None), P("dp"), P("dp", None), P(None, "dp")
    return jax.shard_map(
        per_device,
        mesh=mesh,
        in_specs=(
            rows, gain, weight, weight, across, across, weight, gain, weight, weight, weight, rows,
            P("dp", None),
        ),
        out_specs=(
            rows, rows, gain, weight, weight, across, across, weight, gain, weight, weight, weight,
        ),
        check_vma=False,
    )
```

time: 1450 us -> 568 us (0.39)
  waiting for transfers between devices: 878 us -> 193 us
  matrix products: 289 us -> 59.8 us
  starting transfers between devices: 0.88 us -> 158 us
  blocking collectives: 127 us -> 0 us
  Pallas kernels: 0 us -> 48 us
  local copies, waits for them, and re-layouts: 71 us -> 45.1 us
  other arithmetic: 66.6 us -> 51.2 us
    reduce_scatter x7 -> x0, waiting for transfers between devices: 561 us -> none  [the longest x1 113 us: per_device(): lax.psum_scatter(grad_down.astype(jnp.bfloat16), 'dp', scatter_dimension=...]
    dot_general x82 -> x18, matrix products: 289 us -> 59.8 us  [the longest x3 16 us: mm(): return jnp.dot(left, right, preferred_element_type=F32)]
    ppermute x0 -> x99, waiting for transfers between devices: none -> 193 us  [send(): return lax.ppermute(value, ALL, self.pairs(move))]
    all_gather x7 -> x0, waiting for transfers between devices: 185 us -> none  [the longest x1 84.4 us: per_device(): lax.all_gather(gate_weight.astype(low_type), 'dp', axis=0, tiled=True)]
    ppermute x0 -> x99, starting transfers between devices: none -> 158 us  [send(): return lax.ppermute(value, ALL, self.pairs(move))]
    unnamed x19 -> x0, waiting for transfers between devices: 103 us -> none
    all_gather x4 -> x0, blocking collectives: 101 us -> none  [the longest x1 30.5 us: per_device(): lax.all_gather(key_expand.astype(low_type), 'dp', axis=1, tiled=True)]
    pallas_call x0 -> x2, Pallas kernels: none -> 48 us  [the longest x1 35.2 us: attention_backward(): pl.pallas_call(lambda *refs: backward_kernel(nkb, batch, width, *refs), g...]
  transfers between devices with their start and end apart: 17 -> 99, of which waited for: 13 -> 42; matrix products, arithmetic and copies ran while one was open for 15% -> 21% of each run, Pallas kernels for 0% -> 9%
where the time goes in v1:
time: 568 us; the launch traced here: 559 us
  waiting for transfers between devices  193 us (34%)
  starting transfers between devices  158 us (28%)
  matrix products  59.8 us (11%)
  other arithmetic  51.2 us (9%)
  Pallas kernels  48 us (8%)
  local copies, waits for them, and re-layouts  45.1 us (8%)
    ppermute x99, waiting for transfers between devices, send(): return lax.ppermute(value, ALL, self.pairs(move))  193 us
    ppermute x99, starting transfers between devices, send(): return lax.ppermute(value, ALL, self.pairs(move))  158 us
    pallas_call x1, Pallas kernels, attention_backward(): pl.pallas_call(lambda *refs: backward_kernel(nkb, batch, width, *refs), g...  35.2 us
    unnamed x111, local copies, waits for them, and re-layouts  17.1 us
    dot_general x3, matrix products, mm(): return jnp.dot(left, right, preferred_element_type=F32)  16 us
    dot_general x3, matrix products, nt(): lax.dot_general(left, right, (((1,), (1,)), ((), ())), preferred_element_...  16 us
    pallas_call x1, Pallas kernels, attention_forward(): pl.pallas_call(lambda *refs: forward_kernel(nkb, batch, width, *refs), gr...  12.8 us
  transfers between devices with their start and end apart: 99, of which 42 were waited for; matrix products, arithmetic and copies ran while one was open for 21% of the time, Pallas kernels for 9%

profile of v1, /device:TPU:0, one launch (start us, length us, event | category | flops | bytes accessed | tf_op | source)
XLA Modules:
  0.0 558.5 jit_solution(10840541441514352856)
XLA Ops:
  2.1 5.1 collective-permute-start.24
  9.3 2.6 collective-permute-start.2
  19.9 4.4 collective-permute-done.1
  24.2 16.9 %collective-permute-start.26 = (bf16[128,1408]{1,0:T(8,128)(2,1)S(1)}, bf16[128,1408]{1,0:T(8,128)(2,1)S(1)}, u32[]{:S(2)}, u32[]{:S(2)}) collective-permute-start(bf16[128,1408]{1,0:T(8,128)(2,1)S(1)} %fusion.35), channel_id=1, source_target_pairs={{0,2},{1,3},{2,4},{3,5},{4,6},{5,7},{6,0},{7,1},{8,10},{9,11},{10,... | collective-permute-start | bytes 1081352 | tf_op jit(solution)/shard_map/ppermute | solution.py:255
  42.9 2.1 stack.318
  45.2 4.9 collective-permute-done.15
  51.4 4.6 collective-permute-start.7
  59.5 2.5 collective-permute-start.9
  62.1 5.5 collective-permute-done.8
  67.6 3.4 collective-permute-start.33
  74.4 4.2 collective-permute-done.34
  80.1 3.5 collective-permute-done.4
  94.4 5.6 collective-permute-done.18
  103.9 8.1 %collective-permute-done.11 = bf16[4,128,384]{2,1,0:T(8,128)(2,1)S(1)} collective-permute-done((bf16[4,128,384]{2,1,0:T(8,128)(2,1)S(1)}, bf16[4,128,384]{2,1,0:T(8,128)(2,1)S(1)}, u32[]{:S(2)}, u32[]{:S(2)}) %collective-permute-start.11) | collective-permute-done | bytes 393248 | tf_op jit(solution)/shard_map/ppermute | solution.py:255
  113.4 4.1 collective-permute-done.20
  120.9 8.7 %collective-permute-done.12 = bf16[4,128,384]{2,1,0:T(8,128)(2,1)S(1)} collective-permute-done((bf16[4,128,384]{2,1,0:T(8,128)(2,1)S(1)}, bf16[4,128,384]{2,1,0:T(8,128)(2,1)S(1)}, u32[]{:S(2)}, u32[]{:S(2)}) %collective-permute-start.12) | collective-permute-done | bytes 393248 | tf_op jit(solution)/shard_map/ppermute | solution.py:255
  134.1 2.3 fusion.23.refs_1_
  141.7 3.7 collective-permute-start.14
  145.4 2.8 pad_maximum_fusion.1
  151.2 6.5 %collective-permute-done.14 = bf16[2,2,256,256]{2,3,1,0:T(8,128)(2,1)S(1)} collective-permute-done((bf16[2,2,256,256]{2,3,1,0:T(8,128)(2,1)}, bf16[2,2,256,256]{2,3,1,0:T(8,128)(2,1)S(1)}, u32[]{:S(2)}, u32[]{:S(2)}) %collective-permute-start.14) | collective-permute-done | bytes 524320 | tf_op jit(solution)/shard_map/ppermute | solution.py:255
  157.7 2.4 collective-permute-start.38
  162.5 12.8 %attention_forward.1 = (bf16[2,512,512]{2,1,0:T(8,128)(2,1)}, f32[2,512,512]{2,1,0:T(8,128)}, bf16[2,2,256,2048]{3,2,1,0:T(8,128)(2,1)}, f32[2,2,1,2048]{3,2,1,0:T(1,128)}) custom-call(s32[9]{0:T(128)} %concatenate.167.refs_0_, bf16[2,512,512]{2,1,0:T(8,128)(2,1)} %fusion.23.refs_1_, bf16[512,256]{1,0:T(8,128)(2,1)} %bitcast.398, ...), custom_call_target="tpu_custom_call" | custom-call | flops 7516192768 | bytes 16777216 | tf_op jit(solution)/shard_map/attention_forward/pallas_call | solution.py:171
  176.8 6.3 %collective-permute-start.27 = (bf16[2,128,1408]{2,1,0:T(8,128)(2,1)S(1)}, bf16[2,128,1408]{2,1,0:T(8,128)(2,1)S(1)}, u32[]{:S(2)}, u32[]{:S(2)}) collective-permute-start(bf16[2,128,1408]{2,1,0:T(8,128)(2,1)S(1)} %get-tuple-element.147), channel_id=1, source_target_pairs={{0,16},{1,17},{2,18},{3,19},{4,20},{5,21},{6,22},{7,23},{8,24},{9,... | collective-permute-start | bytes 2162696 | tf_op jit(solution)/shard_map/ppermute | solution.py:255
  183.1 2.8 fusion.30
  190.9 13.0 %collective-permute-done.27 = bf16[2,128,1408]{2,1,0:T(8,128)(2,1)S(1)} collective-permute-done((bf16[2,128,1408]{2,1,0:T(8,128)(2,1)S(1)}, bf16[2,128,1408]{2,1,0:T(8,128)(2,1)S(1)}, u32[]{:S(2)}, u32[]{:S(2)}) %collective-permute-start.27) | collective-permute-done | bytes 720928 | tf_op jit(solution)/shard_map/ppermute | solution.py:255
  203.9 15.2 %collective-permute-done.29 = bf16[2,128,1408]{2,1,0:T(8,128)(2,1)S(1)} collective-permute-done((bf16[2,128,1408]{2,1,0:T(8,128)(2,1)}, bf16[2,128,1408]{2,1,0:T(8,128)(2,1)S(1)}, u32[]{:S(2)}, u32[]{:S(2)}) %collective-permute-start.29) | collective-permute-done | bytes 720928 | tf_op jit(solution)/shard_map/ppermute | solution.py:255
  226.1 5.3 fusion.38
  231.8 3.4 fusion.91
  235.2 9.0 %multiply_convert_fusion = (bf16[1024,1408]{1,0:T(8,128)(2,1)}, bf16[1024,1408]{1,0:T(8,128)(2,1)S(1)}, bf16[1024,1408]{1,0:T(8,128)(2,1)S(1)}) fusion(f32[1024,1408]{1,0:T(8,128)} %fusion.38, f32[1024,1408]{1,0:T(8,128)S(1)} %fusion.91, bf16[1024,1024]{1,0:T(8,128)(2,1)S(1)} %bitcast.378, bf16[1024,1408]{1,0:T(8,128)(2,1)S(1)} %bitcast.367), kind=kOutput, calls=%fused_computation | convolution fusion | flops 2974416896 | bytes 25165824 | tf_op jit(solution)/shard_map/dot_general | solution.py:27
  244.3 3.7 convolution_convert_fusion.2
  248.0 5.0 fusion.92
  253.0 3.4 convolution_convert_fusion
  257.2 2.4 collective-permute-start.88
  261.6 3.9 broadcast_select_fusion
  269.1 5.6 convolution_add_fusion.1
  276.0 3.5 fusion.6
  279.8 5.1 collective-permute-done.81
  290.7 15.3 %collective-permute-done.89 = bf16[2,1,352,256]{3,2,0,1:T(8,128)(2,1)S(1)} collective-permute-done((bf16[2,1,352,256]{3,2,0,1:T(8,128)(2,1)S(1)}, bf16[2,1,352,256]{3,2,0,1:T(8,128)(2,1)S(1)}, u32[]{:S(2)}, u32[]{:S(2)}) %collective-permute-start.89) | collective-permute-done | bytes 360480 | tf_op jit(solution)/shard_map/ppermute | solution.py:255
  307.9 11.8 %collective-permute-done.78 = bf16[2,2,128,1408]{3,2,0,1:T(8,128)(2,1)} collective-permute-done((bf16[2,2,128,1408]{3,2,0,1:T(8,128)(2,1)S(1)}, bf16[2,2,128,1408]{3,2,0,1:T(8,128)(2,1)}, u32[]{:S(2)}, u32[]{:S(2)}) %collective-permute-start.78) | collective-permute-done | bytes 1441824 | tf_op jit(solution)/shard_map/ppermute | solution.py:255
  324.4 10.3 %collective-permute-done.82 = bf16[2,1,128,1408]{3,2,0,1:T(8,128)(2,1)S(1)} collective-permute-done((bf16[2,1,128,1408]{3,2,0,1:T(8,128)(2,1)S(1)}, bf16[2,1,128,1408]{3,2,0,1:T(8,128)(2,1)S(1)}, u32[]{:S(2)}, u32[]{:S(2)}) %collective-permute-start.82) | collective-permute-done | bytes 720928 | tf_op jit(solution)/shard_map/ppermute | solution.py:255
  341.0 3.5 fusion.24.refs_2_
  347.9 35.2 %attention_backward.1 = (bf16[2,512,512]{2,1,0:T(8,128)(2,1)}, f32[2,4,256,256]{3,2,1,0:T(8,128)}, f32[512,256]{1,0:T(8,128)}, f32[512,256]{1,0:T(8,128)}) custom-call(s32[9]{0:T(128)} %concatenate.167.refs_0_, bf16[2,512,512]{2,1,0:T(8,128)(2,1)} %fusion.23.refs_1_, bf16[2,512,512]{2,1,0:T(8,128)(2,1)} %fusion.24.refs_2_, ...), custom_call_target="tpu_custom_call" | custom-call | flops 18790481920 | bytes 25165824 | tf_op jit(solution)/shard_map/attention_backward/pallas_call | solution.py:203
  385.3 2.7 bitcast_convert_fusion.1
  394.2 3.3 collective-permute-start.95
  398.5 4.8 collective-permute-done.94
  403.2 7.3 %collective-permute-done.95 = bf16[1,352,256]{2,1,0:T(8,128)(2,1)S(1)} collective-permute-done((bf16[1,352,256]{2,1,0:T(8,128)(2,1)S(1)}, bf16[1,352,256]{2,1,0:T(8,128)(2,1)S(1)}, u32[]{:S(2)}, u32[]{:S(2)}) %collective-permute-start.95) | collective-permute-done | bytes 180256 | tf_op jit(solution)/shard_map/ppermute | solution.py:255
  411.6 3.4 collective-permute-start.84
  419.6 3.6 collective-permute-done.68
  424.9 21.4 %collective-permute-start.97 = (bf16[352,256]{1,0:T(8,128)(2,1)S(1)}, bf16[352,256]{1,0:T(8,128)(2,1)S(1)}, u32[]{:S(2)}, u32[]{:S(2)}) collective-permute-start(bf16[352,256]{1,0:T(8,128)(2,1)S(1)} %fusion.55), channel_id=1, source_target_pairs={{0,16},{1,17},{2,18},{3,19},{4,20},{5,21},{6,22},{7,23},{8,24},{9,... | collective-permute-start | bytes 540680 | tf_op jit(solution)/shard_map/ppermute | solution.py:255
  448.6 11.6 %collective-permute-done.97 = bf16[352,256]{1,0:T(8,128)(2,1)S(1)} collective-permute-done((bf16[352,256]{1,0:T(8,128)(2,1)S(1)}, bf16[352,256]{1,0:T(8,128)(2,1)S(1)}, u32[]{:S(2)}, u32[]{:S(2)}) %collective-permute-start.97) | collective-permute-done | bytes 180256 | tf_op jit(solution)/shard_map/ppermute | solution.py:255
  462.3 5.3 collective-permute-start.86
  474.7 7.9 %collective-permute-done.61 = bf16[2,1,128,384]{3,2,0,1:T(8,128)(2,1)S(1)} collective-permute-done((bf16[2,1,128,384]{3,2,0,1:T(8,128)(2,1)S(1)}, bf16[2,1,128,384]{3,2,0,1:T(8,128)(2,1)S(1)}, u32[]{:S(2)}, u32[]{:S(2)}) %collective-permute-start.61) | collective-permute-done | bytes 196640 | tf_op jit(solution)/shard_map/ppermute | solution.py:255
  485.1 2.5 collective-permute-done.72
  487.8 7.2 %collective-permute-start.73 = (bf16[1,128,256]{2,1,0:T(8,128)(2,1)S(1)}, bf16[1,128,256]{2,1,0:T(8,128)(2,1)S(1)}, u32[]{:S(2)}, u32[]{:S(2)}) collective-permute-start(bf16[1,128,256]{2,1,0:T(8,128)(2,1)S(1)} %get-tuple-element.206), channel_id=1, source_target_pairs={{0,2},{1,3},{2,4},{3,5},{4,6},{5,7},{6,0},{7,1},{8,10},{9,11},{10,... | collective-permute-start | bytes 196616 | tf_op jit(solution)/shard_map/ppermute | solution.py:255
  495.9 2.4 collective-permute-start.75
  502.2 3.2 collective-permute-start.64
  505.6 3.0 collective-permute-done.63
  510.7 2.1 collective-permute-done.76
  532.9 2.1 collective-permute-done.49
  535.7 2.8 collective-permute-done.46
  540.1 2.8 collective-permute-done.47
  543.1 2.2 collective-permute-start.52
  550.9 2.5 collective-permute-done.54
  553.6 3.2 fusion.13
  (451 shorter events, 167.5 us)
Async XLA Ops:
  2.1 89.0 %collective-permute-start.24 = (bf16[128,1408]{1,0:T(8,128)(2,1)S(1)}, bf16[128,1408]{1,0:T(8,128)(2,1)S(1)}, u32[]{:S(2)}, u32[]{:S(2)}) collective-permute-start(bf16[128,1408]{1,0:T(8,128)(2,1)S(1)} %fusion.35), channel_id=1, source_target_pairs={{0,6},{1,7},{2,0},{3,1},{4,2},{5,3},{6,4},{7,5},{8,14},{9,15},{10,... | collective-permute-start | bytes 1081352 | tf_op jit(solution)/shard_map/ppermute | solution.py:255
  7.2 85.5 %collective-permute-start.25 = (bf16[128,1408]{1,0:T(8,128)(2,1)S(1)}, bf16[128,1408]{1,0:T(8,128)(2,1)S(1)}, u32[]{:S(2)}, u32[]{:S(2)}) collective-permute-start(bf16[128,1408]{1,0:T(8,128)(2,1)S(1)} %fusion.35), channel_id=1, source_target_pairs={{0,4},{1,5},{2,6},{3,7},{4,0},{5,1},{6,2},{7,3},{8,12},{9,13},{10,... | collective-permute-start | bytes 1081352 | tf_op jit(solution)/shard_map/ppermute | solution.py:255
  8.8 15.4 %collective-permute-start.1 = (bf16[136,128]{1,0:T(8,128)(2,1)S(1)}, bf16[136,128]{1,0:T(8,128)(2,1)S(1)}, u32[]{:S(2)}, u32[]{:S(2)}) collective-permute-start(bf16[136,128]{1,0:T(8,128)(2,1)S(1)} %concatenate.168), channel_id=1, source_target_pairs={{0,6},{1,7},{2,0},{3,1},{4,2},{5,3},{6,4},{7,5},{8,14},{9,15},{10,... | collective-permute-start | bytes 104456 | tf_op jit(solution)/shard_map/ppermute | solution.py:255
  9.3 31.9 %collective-permute-start.2 = (bf16[136,128]{1,0:T(8,128)(2,1)S(1)}, bf16[136,128]{1,0:T(8,128)(2,1)S(1)}, u32[]{:S(2)}, u32[]{:S(2)}) collective-permute-start(bf16[136,128]{1,0:T(8,128)(2,1)S(1)} %concatenate.168), channel_id=1, source_target_pairs={{0,4},{1,5},{2,6},{3,7},{4,0},{5,1},{6,2},{7,3},{8,12},{9,13},{10,... | collective-permute-start | bytes 104456 | tf_op jit(solution)/shard_map/ppermute | solution.py:255
  11.9 29.5 %collective-permute-start.3 = (bf16[136,128]{1,0:T(8,128)(2,1)S(1)}, bf16[136,128]{1,0:T(8,128)(2,1)S(1)}, u32[]{:S(2)}, u32[]{:S(2)}) collective-permute-start(bf16[136,128]{1,0:T(8,128)(2,1)S(1)} %concatenate.168), channel_id=1, source_target_pairs={{0,2},{1,3},{2,4},{3,5},{4,6},{5,7},{6,0},{7,1},{8,10},{9,11},{10,... | collective-permute-start | bytes 104456 | tf_op jit(solution)/shard_map/ppermute | solution.py:255
  24.2 77.2 %collective-permute-start.26 = (bf16[128,1408]{1,0:T(8,128)(2,1)S(1)}, bf16[128,1408]{1,0:T(8,128)(2,1)S(1)}, u32[]{:S(2)}, u32[]{:S(2)}) collective-permute-start(bf16[128,1408]{1,0:T(8,128)(2,1)S(1)} %fusion.35), channel_id=1, source_target_pairs={{0,2},{1,3},{2,4},{3,5},{4,6},{5,7},{6,0},{7,1},{8,10},{9,11},{10,... | collective-permute-start | bytes 1081352 | tf_op jit(solution)/shard_map/ppermute | solution.py:255
  41.4 10.0 %collective-permute-start.16 = (bf16[128,256]{1,0:T(8,128)(2,1)S(1)}, bf16[128,256]{1,0:T(8,128)(2,1)S(1)}, u32[]{:S(2)}, u32[]{:S(2)}) collective-permute-start(bf16[128,256]{1,0:T(8,128)(2,1)S(1)} %dynamic-slice_convert_fusion.1), channel_id=1, source_target_pairs={{0,4},{1,5},{2,6},{3,7},{4,0},{5,1},{6,2},{7,3},{8,12},{9,13},{10,... | collective-permute-start | bytes 196616 | tf_op jit(solution)/shard_map/ppermute | solution.py:255
  57.5 10.1 %collective-permute-start.8 = (bf16[128,384]{1,0:T(8,128)(2,1)S(1)}, bf16[128,384]{1,0:T(8,128)(2,1)S(1)}, u32[]{:S(2)}, u32[]{:S(2)}) collective-permute-start(bf16[128,384]{1,0:T(8,128)(2,1)S(1)} %pad_maximum_fusion.12), channel_id=1, source_target_pairs={{0,4},{1,5},{2,6},{3,7},{4,0},{5,1},{6,2},{7,3},{8,12},{9,13},{10,... | collective-permute-start | bytes 294920 | tf_op jit(solution)/shard_map/ppermute | solution.py:255
  59.5 11.5 %collective-permute-start.9 = (bf16[128,384]{1,0:T(8,128)(2,1)S(1)}, bf16[128,384]{1,0:T(8,128)(2,1)S(1)}, u32[]{:S(2)}, u32[]{:S(2)}) collective-permute-start(bf16[128,384]{1,0:T(8,128)(2,1)S(1)} %pad_maximum_fusion.12), channel_id=1, source_target_pairs={{0,2},{1,3},{2,4},{3,5},{4,6},{5,7},{6,0},{7,1},{8,10},{9,11},{10,... | collective-permute-start | bytes 294920 | tf_op jit(solution)/shard_map/ppermute | solution.py:255
  74.4 10.7 %collective-permute-start.35 = (bf16[352,256]{1,0:T(8,128)(2,1)}, bf16[352,256]{1,0:T(8,128)(2,1)S(1)}, u32[]{:S(2)}, u32[]{:S(2)}) collective-permute-start(bf16[352,256]{1,0:T(8,128)(2,1)} %dynamic-slice_convert_fusion), channel_id=1, source_target_pairs={{0,2},{1,3},{2,4},{3,5},{4,6},{5,7},{6,0},{7,1},{8,10},{9,11},{10,... | collective-permute-start | bytes 540680 | tf_op jit(solution)/shard_map/ppermute | solution.py:255
  88.7 44.1 %collective-permute-start = (bf16[2,256,1024]{2,1,0:T(8,128)(2,1)S(1)}, bf16[2,256,1024]{2,1,0:T(8,128)(2,1)S(1)}, u32[]{:S(2)}, u32[]{:S(2)}) collective-permute-start(bf16[2,256,1024]{2,1,0:T(8,128)(2,1)S(1)} %copy-done.2), channel_id=1, source_target_pairs={{0,8},{1,9},{2,10},{3,11},{4,12},{5,13},{6,14},{7,15},{8,0},{9,1},... | collective-permute-start | bytes 3145736 | tf_op jit(solution)/shard_map/ppermute | solution.py:255
  90.2 51.6 %collective-permute-start.41 = (bf16[2,256,1024]{2,1,0:T(8,128)(2,1)S(1)}, bf16[2,256,1024]{2,1,0:T(8,128)(2,1)}, u32[]{:S(2)}, u32[]{:S(2)}) collective-permute-start(bf16[2,256,1024]{2,1,0:T(8,128)(2,1)S(1)} %copy-done.6), channel_id=1, source_target_pairs={{0,8},{1,9},{2,10},{3,11},{4,12},{5,13},{6,14},{7,15},{8,0},{9,1},... | collective-permute-start | bytes 3145736 | tf_op jit(solution)/shard_map/ppermute | solution.py:255
  92.8 9.5 %collective-permute-start.19 = (bf16[4,128,256]{2,1,0:T(8,128)(2,1)S(1)}, bf16[4,128,256]{2,1,0:T(8,128)(2,1)S(1)}, u32[]{:S(2)}, u32[]{:S(2)}) collective-permute-start(bf16[4,128,256]{2,1,0:T(8,128)(2,1)S(1)} %constant_dynamic-slice_fusion.32), channel_id=1, source_target_pairs={{0,1},{1,0},{2,3},{3,2},{4,5},{5,4},{6,7},{7,6},{8,9},{9,8},{10,11... | collective-permute-start | bytes 786440 | tf_op jit(solution)/shard_map/ppermute | solution.py:255
  99.9 12.0 %collective-permute-start.11 = (bf16[4,128,384]{2,1,0:T(8,128)(2,1)S(1)}, bf16[4,128,384]{2,1,0:T(8,128)(2,1)S(1)}, u32[]{:S(2)}, u32[]{:S(2)}) collective-permute-start(bf16[4,128,384]{2,1,0:T(8,128)(2,1)S(1)} %constant_dynamic-slice_fusion.33), channel_id=1, source_target_pairs={{0,1},{1,0},{2,3},{3,2},{4,5},{5,4},{6,7},{7,6},{8,9},{9,8},{10,11... | collective-permute-start | bytes 1179656 | tf_op jit(solution)/shard_map/ppermute | solution.py:255
  101.4 16.1 %collective-permute-start.20 = (bf16[4,128,256]{2,1,0:T(8,128)(2,1)S(1)}, bf16[4,128,256]{2,1,0:T(8,128)(2,1)S(1)}, u32[]{:S(2)}, u32[]{:S(2)}) collective-permute-start(bf16[4,128,256]{2,1,0:T(8,128)(2,1)S(1)} %collective-permute-done.18), channel_id=1, source_target_pairs={{0,1},{1,0},{2,3},{3,2},{4,5},{5,4},{6,7},{7,6},{8,9},{9,8},{10,11... | collective-permute-start | bytes 786440 | tf_op jit(solution)/shard_map/ppermute | solution.py:255
  102.3 18.1 %collective-permute-start.10 = (bf16[4,128,384]{2,1,0:T(8,128)(2,1)S(1)}, bf16[4,128,384]{2,1,0:T(8,128)(2,1)S(1)}, u32[]{:S(2)}, u32[]{:S(2)}) collective-permute-start(bf16[4,128,384]{2,1,0:T(8,128)(2,1)S(1)} %constant_dynamic-slice_fusion.33), channel_id=1, source_target_pairs={{0,16},{1,17},{2,18},{3,19},{4,20},{5,21},{6,22},{7,23},{8,24},{9,... | collective-permute-start | bytes 1179656 | tf_op jit(solution)/shard_map/ppermute | solution.py:255
  111.9 39.0 %collective-permute-start.37 = (bf16[4,352,256]{2,1,0:T(8,128)(2,1)}, bf16[4,352,256]{2,1,0:T(8,128)(2,1)}, u32[]{:S(2)}, u32[]{:S(2)}) collective-permute-start(bf16[4,352,256]{2,1,0:T(8,128)(2,1)} %constant_dynamic-slice_fusion.28), channel_id=1, source_target_pairs={{0,1},{1,0},{2,3},{3,2},{4,5},{5,4},{6,7},{7,6},{8,9},{9,8},{10,11... | collective-permute-start | bytes 2162696 | tf_op jit(solution)/shard_map/ppermute | solution.py:255
  117.6 12.1 %collective-permute-start.12 = (bf16[4,128,384]{2,1,0:T(8,128)(2,1)S(1)}, bf16[4,128,384]{2,1,0:T(8,128)(2,1)S(1)}, u32[]{:S(2)}, u32[]{:S(2)}) collective-permute-start(bf16[4,128,384]{2,1,0:T(8,128)(2,1)S(1)} %collective-permute-done.11), channel_id=1, source_target_pairs={{0,16},{1,17},{2,18},{3,19},{4,20},{5,21},{6,22},{7,23},{8,24},{9,... | collective-permute-start | bytes 1179656 | tf_op jit(solution)/shard_map/ppermute | solution.py:255
  120.4 65.7 %collective-permute-start.36 = (bf16[4,352,256]{2,1,0:T(8,128)(2,1)}, bf16[4,352,256]{2,1,0:T(8,128)(2,1)}, u32[]{:S(2)}, u32[]{:S(2)}) collective-permute-start(bf16[4,352,256]{2,1,0:T(8,128)(2,1)} %constant_dynamic-slice_fusion.28), channel_id=1, source_target_pairs={{0,16},{1,17},{2,18},{3,19},{4,20},{5,21},{6,22},{7,23},{8,24},{9,... | collective-permute-start | bytes 2162696 | tf_op jit(solution)/shard_map/ppermute | solution.py:255
  129.6 57.1 %collective-permute-start.28 = (bf16[2,128,1408]{2,1,0:T(8,128)(2,1)S(1)}, bf16[2,128,1408]{2,1,0:T(8,128)(2,1)}, u32[]{:S(2)}, u32[]{:S(2)}) collective-permute-start(bf16[2,128,1408]{2,1,0:T(8,128)(2,1)S(1)} %get-tuple-element.147), channel_id=1, source_target_pairs={{0,1},{1,0},{2,3},{3,2},{4,5},{5,4},{6,7},{7,6},{8,9},{9,8},{10,11... | collective-permute-start | bytes 2162696 | tf_op jit(solution)/shard_map/ppermute | solution.py:255
  132.8 15.5 %collective-permute-start.13 = (bf16[2,2,2,128,128]{4,3,1,2,0:T(8,128)(2,1)}, bf16[2,2,2,128,128]{4,3,1,2,0:T(8,128)(2,1)}, u32[]{:S(2)}, u32[]{:S(2)}) collective-permute-start(bf16[2,2,2,128,128]{4,3,1,2,0:T(8,128)(2,1)} %get-tuple-element.198), channel_id=1, source_target_pairs={{0,8},{1,9},{2,10},{3,11},{4,12},{5,13},{6,14},{7,15},{8,0},{9,1},... | collective-permute-start | bytes 786440 | tf_op jit(solution)/shard_map/ppermute | solution.py:255
  141.7 16.0 %collective-permute-start.14 = (bf16[2,2,256,256]{2,3,1,0:T(8,128)(2,1)}, bf16[2,2,256,256]{2,3,1,0:T(8,128)(2,1)S(1)}, u32[]{:S(2)}, u32[]{:S(2)}) collective-permute-start(bf16[2,2,256,256]{2,3,1,0:T(8,128)(2,1)} %copy.370), channel_id=1, source_target_pairs={{0,16},{1,17},{2,18},{3,19},{4,20},{5,21},{6,22},{7,23},{8,24},{9,... | collective-permute-start | bytes 1572872 | tf_op jit(solution)/shard_map/ppermute | solution.py:255
  148.2 38.5 %collective-permute-start.30 = (bf16[2,128,1408]{2,1,0:T(8,128)(2,1)S(1)}, bf16[2,128,1408]{2,1,0:T(8,128)(2,1)}, u32[]{:S(2)}, u32[]{:S(2)}) collective-permute-start(bf16[2,128,1408]{2,1,0:T(8,128)(2,1)S(1)} %get-tuple-element.148), channel_id=1, source_target_pairs={{0,16},{1,17},{2,18},{3,19},{4,20},{5,21},{6,22},{7,23},{8,24},{9,... | collective-permute-start | bytes 2162696 | tf_op jit(solution)/shard_map/ppermute | solution.py:255
  151.0 25.8 %collective-permute-start.21 = (bf16[2,2,128,512]{3,2,1,0:T(8,128)(2,1)}, bf16[2,2,128,512]{3,2,1,0:T(8,128)(2,1)}, u32[]{:S(2)}, u32[]{:S(2)}) collective-permute-start(bf16[2,2,128,512]{3,2,1,0:T(8,128)(2,1)} %get-tuple-element.167), channel_id=1, source_target_pairs={{0,8},{1,9},{2,10},{3,11},{4,12},{5,13},{6,14},{7,15},{8,0},{9,1},... | collective-permute-start | bytes 1572872 | tf_op jit(solution)/shard_map/ppermute | solution.py:255
  157.7 30.9 %collective-permute-start.38 = (bf16[4,352,256]{2,1,0:T(8,128)(2,1)}, bf16[4,352,256]{2,1,0:T(8,128)(2,1)}, u32[]{:S(2)}, u32[]{:S(2)}) collective-permute-start(bf16[4,352,256]{2,1,0:T(8,128)(2,1)} %collective-permute-done.37), channel_id=1, source_target_pairs={{0,16},{1,17},{2,18},{3,19},{4,20},{5,21},{6,22},{7,23},{8,24},{9,... | collective-permute-start | bytes 2162696 | tf_op jit(solution)/shard_map/ppermute | solution.py:255
  176.8 27.1 %collective-permute-start.27 = (bf16[2,128,1408]{2,1,0:T(8,128)(2,1)S(1)}, bf16[2,128,1408]{2,1,0:T(8,128)(2,1)S(1)}, u32[]{:S(2)}, u32[]{:S(2)}) collective-permute-start(bf16[2,128,1408]{2,1,0:T(8,128)(2,1)S(1)} %get-tuple-element.147), channel_id=1, source_target_pairs={{0,16},{1,17},{2,18},{3,19},{4,20},{5,21},{6,22},{7,23},{8,24},{9,... | collective-permute-start | bytes 2162696 | tf_op jit(solution)/shard_map/ppermute | solution.py:255
  186.1 34.5 %collective-permute-start.31 = (bf16[2,128,1408]{2,1,0:T(8,128)(2,1)S(1)}, bf16[2,128,1408]{2,1,0:T(8,128)(2,1)S(1)}, u32[]{:S(2)}, u32[]{:S(2)}) collective-permute-start(bf16[2,128,1408]{2,1,0:T(8,128)(2,1)S(1)} %get-tuple-element.148), channel_id=1, source_target_pairs={{0,1},{1,0},{2,3},{3,2},{4,5},{5,4},{6,7},{7,6},{8,9},{9,8},{10,11... | collective-permute-start | bytes 2162696 | tf_op jit(solution)/shard_map/ppermute | solution.py:255
  186.7 32.4 %collective-permute-start.29 = (bf16[2,128,1408]{2,1,0:T(8,128)(2,1)}, bf16[2,128,1408]{2,1,0:T(8,128)(2,1)S(1)}, u32[]{:S(2)}, u32[]{:S(2)}) collective-permute-start(bf16[2,128,1408]{2,1,0:T(8,128)(2,1)} %collective-permute-done.28), channel_id=1, source_target_pairs={{0,16},{1,17},{2,18},{3,19},{4,20},{5,21},{6,22},{7,23},{8,24},{9,... | collective-permute-start | bytes 2162696 | tf_op jit(solution)/shard_map/ppermute | solution.py:255
  186.7 33.9 %collective-permute-start.32 = (bf16[2,128,1408]{2,1,0:T(8,128)(2,1)}, bf16[2,128,1408]{2,1,0:T(8,128)(2,1)S(1)}, u32[]{:S(2)}, u32[]{:S(2)}) collective-permute-start(bf16[2,128,1408]{2,1,0:T(8,128)(2,1)} %collective-permute-done.30), channel_id=1, source_target_pairs={{0,1},{1,0},{2,3},{3,2},{4,5},{5,4},{6,7},{7,6},{8,9},{9,8},{10,11... | collective-permute-start | bytes 2162696 | tf_op jit(solution)/shard_map/ppermute | solution.py:255
  188.6 34.5 %collective-permute-start.22 = (bf16[2,256,1024]{2,1,0:T(8,128)(2,1)S(1)}, bf16[2,256,1024]{2,1,0:T(8,128)(2,1)S(1)}, u32[]{:S(2)}, u32[]{:S(2)}) collective-permute-start(bf16[2,256,1024]{2,1,0:T(8,128)(2,1)S(1)} %fusion.26), channel_id=1, source_target_pairs={{0,8},{1,9},{2,10},{3,11},{4,12},{5,13},{6,14},{7,15},{8,0},{9,1},... | collective-permute-start | bytes 3145736 | tf_op jit(solution)/shard_map/ppermute | solution.py:255
  203.9 20.4 %collective-permute-start.39 = (bf16[2,2,352,512]{3,2,1,0:T(8,128)(2,1)S(1)}, bf16[2,2,352,512]{3,2,1,0:T(8,128)(2,1)S(1)}, u32[]{:S(2)}, u32[]{:S(2)}) collective-permute-start(bf16[2,2,352,512]{3,2,1,0:T(8,128)(2,1)S(1)} %get-tuple-element.134), channel_id=1, source_target_pairs={{0,8},{1,9},{2,10},{3,11},{4,12},{5,13},{6,14},{7,15},{8,0},{9,1},... | collective-permute-start | bytes 4325384 | tf_op jit(solution)/shard_map/ppermute | solution.py:255
  257.2 28.0 %collective-permute-start.88 = (bf16[2,2,352,256]{3,2,0,1:T(8,128)(2,1)S(1)}, bf16[2,2,352,256]{3,2,0,1:T(8,128)(2,1)S(1)}, u32[]{:S(2)}, u32[]{:S(2)}) collective-permute-start(bf16[2,2,352,256]{3,2,0,1:T(8,128)(2,1)S(1)} %copy.443), channel_id=1, source_target_pairs={{0,16},{1,17},{2,18},{3,19},{4,20},{5,21},{6,22},{7,23},{8,24},{9,... | collective-permute-start | bytes 2162696 | tf_op jit(solution)/shard_map/ppermute | solution.py:255
  259.9 46.2 %collective-permute-start.90 = (bf16[2,2,352,512]{3,2,0,1:T(8,128)(2,1)S(1)}, bf16[2,2,352,512]{3,2,0,1:T(8,128)(2,1)S(1)}, u32[]{:S(2)}, u32[]{:S(2)}) collective-permute-start(bf16[2,2,352,512]{3,2,0,1:T(8,128)(2,1)S(1)} %copy.444), channel_id=1, source_target_pairs={{0,8},{1,9},{2,10},{3,11},{4,12},{5,13},{6,14},{7,15},{8,0},{9,1},... | collective-permute-start | bytes 4325384 | tf_op jit(solution)/shard_map/ppermute | solution.py:255
  265.8 19.1 %collective-permute-start.81 = (bf16[2,1,128,1408]{3,2,0,1:T(8,128)(2,1)S(1)}, bf16[2,1,128,1408]{3,2,0,1:T(8,128)(2,1)S(1)}, u32[]{:S(2)}, u32[]{:S(2)}) collective-permute-start(bf16[2,1,128,1408]{3,2,0,1:T(8,128)(2,1)S(1)} %dynamic-slice_bitcast_fusion), channel_id=1, source_target_pairs={{0,1},{1,0},{2,3},{3,2},{4,5},{5,4},{6,7},{7,6},{8,9},{9,8},{10,11... | collective-permute-start | bytes 2162696 | tf_op jit(solution)/shard_map/ppermute | solution.py:255
  267.6 55.3 %collective-permute-start.80 = (bf16[2,1,128,1408]{3,2,0,1:T(8,128)(2,1)}, bf16[2,1,128,1408]{3,2,0,1:T(8,128)(2,1)}, u32[]{:S(2)}, u32[]{:S(2)}) collective-permute-start(bf16[2,1,128,1408]{3,2,0,1:T(8,128)(2,1)} %dynamic-slice_bitcast_fusion.1), channel_id=1, source_target_pairs={{0,1},{1,0},{2,3},{3,2},{4,5},{5,4},{6,7},{7,6},{8,9},{9,8},{10,11... | collective-permute-start | bytes 2162696 | tf_op jit(solution)/shard_map/ppermute | solution.py:255
  274.8 10.7 %collective-permute-start.42 = (bf16[2,256,1024]{2,1,0:T(8,128)(2,1)S(1)}, bf16[2,256,1024]{2,1,0:T(8,128)(2,1)S(1)}, u32[]{:S(2)}, u32[]{:S(2)}) collective-permute-start(bf16[2,256,1024]{2,1,0:T(8,128)(2,1)S(1)} %fusion.28), channel_id=1, source_target_pairs={{0,8},{1,9},{2,10},{3,11},{4,12},{5,13},{6,14},{7,15},{8,0},{9,1},... | collective-permute-start | bytes 3145736 | tf_op jit(solution)/shard_map/ppermute | solution.py:255
  285.2 34.6 %collective-permute-start.78 = (bf16[2,2,128,1408]{3,2,0,1:T(8,128)(2,1)S(1)}, bf16[2,2,128,1408]{3,2,0,1:T(8,128)(2,1)}, u32[]{:S(2)}, u32[]{:S(2)}) collective-permute-start(bf16[2,2,128,1408]{3,2,0,1:T(8,128)(2,1)S(1)} %copy.406), channel_id=1, source_target_pairs={{0,16},{1,17},{2,18},{3,19},{4,20},{5,21},{6,22},{7,23},{8,24},{9,... | collective-permute-start | bytes 4325384 | tf_op jit(solution)/shard_map/ppermute | solution.py:255
  285.5 20.5 %collective-permute-start.89 = (bf16[2,1,352,256]{3,2,0,1:T(8,128)(2,1)S(1)}, bf16[2,1,352,256]{3,2,0,1:T(8,128)(2,1)S(1)}, u32[]{:S(2)}, u32[]{:S(2)}) collective-permute-start(bf16[2,1,352,256]{3,2,0,1:T(8,128)(2,1)S(1)} %constant_dynamic-slice_fusion.6), channel_id=1, source_target_pairs={{0,1},{1,0},{2,3},{3,2},{4,5},{5,4},{6,7},{7,6},{8,9},{9,8},{10,11... | collective-permute-start | bytes 1081352 | tf_op jit(solution)/shard_map/ppermute | solution.py:255
  287.6 47.1 %collective-permute-start.82 = (bf16[2,1,128,1408]{3,2,0,1:T(8,128)(2,1)S(1)}, bf16[2,1,128,1408]{3,2,0,1:T(8,128)(2,1)S(1)}, u32[]{:S(2)}, u32[]{:S(2)}) collective-permute-start(bf16[2,1,128,1408]{3,2,0,1:T(8,128)(2,1)S(1)} %add_convert_fusion.2), channel_id=1, source_target_pairs={{0,16},{1,17},{2,18},{3,19},{4,20},{5,21},{6,22},{7,23},{8,24},{9,... | collective-permute-start | bytes 2162696 | tf_op jit(solution)/shard_map/ppermute | solution.py:255
  306.0 31.3 %collective-permute-start.43 = (bf16[2,256,1024]{2,1,0:T(8,128)(2,1)S(1)}, bf16[2,256,1024]{2,1,0:T(8,128)(2,1)S(1)}, u32[]{:S(2)}, u32[]{:S(2)}) collective-permute-start(bf16[2,256,1024]{2,1,0:T(8,128)(2,1)S(1)} %get-tuple-element.116), channel_id=1, source_target_pairs={{0,8},{1,9},{2,10},{3,11},{4,12},{5,13},{6,14},{7,15},{8,0},{9,1},... | collective-permute-start | bytes 3145736 | tf_op jit(solution)/shard_map/ppermute | solution.py:255
  307.4 28.7 %collective-permute-start.92 = (bf16[2,1,352,256]{3,2,0,1:T(8,128)(2,1)S(1)}, bf16[2,1,352,256]{3,2,0,1:T(8,128)(2,1)S(1)}, u32[]{:S(2)}, u32[]{:S(2)}) collective-permute-start(bf16[2,1,352,256]{3,2,0,1:T(8,128)(2,1)S(1)} %get-tuple-element.157), channel_id=1, source_target_pairs={{0,1},{1,0},{2,3},{3,2},{4,5},{5,4},{6,7},{7,6},{8,9},{9,8},{10,11... | collective-permute-start | bytes 1081352 | tf_op jit(solution)/shard_map/ppermute | solution.py:255
  319.7 72.5 %collective-permute-start.91 = (bf16[2,1,352,256]{3,2,0,1:T(8,128)(2,1)}, bf16[2,1,352,256]{3,2,0,1:T(8,128)(2,1)}, u32[]{:S(2)}, u32[]{:S(2)}) collective-permute-start(bf16[2,1,352,256]{3,2,0,1:T(8,128)(2,1)} %get-tuple-element.156), channel_id=1, source_target_pairs={{0,1},{1,0},{2,3},{3,2},{4,5},{5,4},{6,7},{7,6},{8,9},{9,8},{10,11... | collective-permute-start | bytes 1081352 | tf_op jit(solution)/shard_map/ppermute | solution.py:255
  322.9 68.0 %collective-permute-start.79 = (bf16[2,1,128,1408]{3,2,0,1:T(8,128)(2,1)}, bf16[2,1,128,1408]{3,2,0,1:T(8,128)(2,1)}, u32[]{:S(2)}, u32[]{:S(2)}) collective-permute-start(bf16[2,1,128,1408]{3,2,0,1:T(8,128)(2,1)} %constant_dynamic-slice_fusion.9), channel_id=1, source_target_pairs={{0,1},{1,0},{2,3},{3,2},{4,5},{5,4},{6,7},{7,6},{8,9},{9,8},{10,11... | collective-permute-start | bytes 2162696 | tf_op jit(solution)/shard_map/ppermute | solution.py:255
  337.0 55.2 %collective-permute-start.93 = (bf16[2,1,352,256]{3,2,0,1:T(8,128)(2,1)}, bf16[2,1,352,256]{3,2,0,1:T(8,128)(2,1)}, u32[]{:S(2)}, u32[]{:S(2)}) collective-permute-start(bf16[2,1,352,256]{3,2,0,1:T(8,128)(2,1)} %add_convert_fusion.8), channel_id=1, source_target_pairs={{0,16},{1,17},{2,18},{3,19},{4,20},{5,21},{6,22},{7,23},{8,24},{9,... | collective-permute-start | bytes 1081352 | tf_op jit(solution)/shard_map/ppermute | solution.py:255
  345.3 69.8 %collective-permute-start.67 = (bf16[2,2,128,256]{3,2,0,1:T(8,128)(2,1)}, bf16[2,2,128,256]{3,2,0,1:T(8,128)(2,1)}, u32[]{:S(2)}, u32[]{:S(2)}) collective-permute-start(bf16[2,2,128,256]{3,2,0,1:T(8,128)(2,1)} %copy.436), channel_id=1, source_target_pairs={{0,16},{1,17},{2,18},{3,19},{4,20},{5,21},{6,22},{7,23},{8,24},{9,... | collective-permute-start | bytes 786440 | tf_op jit(solution)/shard_map/ppermute | solution.py:255
  347.9 114.3 %collective-permute-start.69 = (bf16[2,2,128,512]{3,2,0,1:T(8,128)(2,1)}, bf16[2,2,128,512]{3,2,0,1:T(8,128)(2,1)S(1)}, u32[]{:S(2)}, u32[]{:S(2)}) collective-permute-start(bf16[2,2,128,512]{3,2,0,1:T(8,128)(2,1)} %copy.437), channel_id=1, source_target_pairs={{0,8},{1,9},{2,10},{3,11},{4,12},{5,13},{6,14},{7,15},{8,0},{9,1},... | collective-permute-start | bytes 1572872 | tf_op jit(solution)/shard_map/ppermute | solution.py:255
  394.2 16.3 %collective-permute-start.95 = (bf16[1,352,256]{2,1,0:T(8,128)(2,1)S(1)}, bf16[1,352,256]{2,1,0:T(8,128)(2,1)S(1)}, u32[]{:S(2)}, u32[]{:S(2)}) collective-permute-start(bf16[1,352,256]{2,1,0:T(8,128)(2,1)S(1)} %get-tuple-element.178), channel_id=1, source_target_pairs={{0,4},{1,5},{2,6},{3,7},{4,0},{5,1},{6,2},{7,3},{8,12},{9,13},{10,... | collective-permute-start | bytes 540680 | tf_op jit(solution)/shard_map/ppermute | solution.py:255
  397.5 14.1 %collective-permute-start.96 = (bf16[1,352,256]{2,1,0:T(8,128)(2,1)S(1)}, bf16[1,352,256]{2,1,0:T(8,128)(2,1)S(1)}, u32[]{:S(2)}, u32[]{:S(2)}) collective-permute-start(bf16[1,352,256]{2,1,0:T(8,128)(2,1)S(1)} %get-tuple-element.177), channel_id=1, source_target_pairs={{0,6},{1,7},{2,0},{3,1},{4,2},{5,3},{6,4},{7,5},{8,14},{9,15},{10,... | collective-permute-start | bytes 540680 | tf_op jit(solution)/shard_map/ppermute | solution.py:255
  403.2 15.0 %collective-permute-start.56 = (bf16[2,2,2,128,128]{4,3,1,2,0:T(8,128)(2,1)S(1)}, bf16[2,2,2,128,128]{4,3,1,2,0:T(8,128)(2,1)S(1)}, u32[]{:S(2)}, u32[]{:S(2)}) collective-permute-start(bf16[2,2,2,128,128]{4,3,1,2,0:T(8,128)(2,1)S(1)} %copy.433), channel_id=1, source_target_pairs={{0,8},{1,9},{2,10},{3,11},{4,12},{5,13},{6,14},{7,15},{8,0},{9,1},... | collective-permute-start | bytes 786440 | tf_op jit(solution)/shard_map/ppermute | solution.py:255
  410.5 14.3 %collective-permute-start.83 = (bf16[1,128,1408]{2,1,0:T(8,128)(2,1)S(1)}, bf16[1,128,1408]{2,1,0:T(8,128)(2,1)S(1)}, u32[]{:S(2)}, u32[]{:S(2)}) collective-permute-start(bf16[1,128,1408]{2,1,0:T(8,128)(2,1)S(1)} %get-tuple-element.158), channel_id=1, source_target_pairs={{0,2},{1,3},{2,4},{3,5},{4,6},{5,7},{6,0},{7,1},{8,10},{9,11},{10,... | collective-permute-start | bytes 1081352 | tf_op jit(solution)/shard_map/ppermute | solution.py:255
  411.6 34.6 %collective-permute-start.84 = (bf16[1,128,1408]{2,1,0:T(8,128)(2,1)S(1)}, bf16[1,128,1408]{2,1,0:T(8,128)(2,1)S(1)}, u32[]{:S(2)}, u32[]{:S(2)}) collective-permute-start(bf16[1,128,1408]{2,1,0:T(8,128)(2,1)S(1)} %get-tuple-element.159), channel_id=1, source_target_pairs={{0,4},{1,5},{2,6},{3,7},{4,0},{5,1},{6,2},{7,3},{8,12},{9,13},{10,... | collective-permute-start | bytes 1081352 | tf_op jit(solution)/shard_map/ppermute | solution.py:255
  415.1 31.7 %collective-permute-start.85 = (bf16[1,128,1408]{2,1,0:T(8,128)(2,1)S(1)}, bf16[1,128,1408]{2,1,0:T(8,128)(2,1)S(1)}, u32[]{:S(2)}, u32[]{:S(2)}) collective-permute-start(bf16[1,128,1408]{2,1,0:T(8,128)(2,1)S(1)} %get-tuple-element.160), channel_id=1, source_target_pairs={{0,6},{1,7},{2,0},{3,1},{4,2},{5,3},{6,4},{7,5},{8,14},{9,15},{10,... | collective-permute-start | bytes 1081352 | tf_op jit(solution)/shard_map/ppermute | solution.py:255
  423.3 44.4 %collective-permute-start.44 = (bf16[2,2,256,256]{3,2,1,0:T(8,128)(2,1)S(1)}, bf16[2,2,256,256]{3,2,1,0:T(8,128)(2,1)S(1)}, u32[]{:S(2)}, u32[]{:S(2)}) collective-permute-start(bf16[2,2,256,256]{3,2,1,0:T(8,128)(2,1)S(1)} %slice.373), channel_id=1, source_target_pairs={{16,0},{17,1},{18,2},{19,3},{20,4},{21,5},{22,6},{23,7},{24,8},{25... | collective-permute-start | bytes 1572872 | tf_op jit(solution)/shard_map/ppermute | solution.py:255
  424.9 35.3 %collective-permute-start.97 = (bf16[352,256]{1,0:T(8,128)(2,1)S(1)}, bf16[352,256]{1,0:T(8,128)(2,1)S(1)}, u32[]{:S(2)}, u32[]{:S(2)}) collective-permute-start(bf16[352,256]{1,0:T(8,128)(2,1)S(1)} %fusion.55), channel_id=1, source_target_pairs={{0,16},{1,17},{2,18},{3,19},{4,20},{5,21},{6,22},{7,23},{8,24},{9,... | collective-permute-start | bytes 540680 | tf_op jit(solution)/shard_map/ppermute | solution.py:255
  446.3 15.8 %collective-permute-start.60 = (bf16[2,1,128,384]{3,2,0,1:T(8,128)(2,1)S(1)}, bf16[2,1,128,384]{3,2,0,1:T(8,128)(2,1)S(1)}, u32[]{:S(2)}, u32[]{:S(2)}) collective-permute-start(bf16[2,1,128,384]{3,2,0,1:T(8,128)(2,1)S(1)} %constant_dynamic-slice_fusion.19), channel_id=1, source_target_pairs={{0,1},{1,0},{2,3},{3,2},{4,5},{5,4},{6,7},{7,6},{8,9},{9,8},{10,11... | collective-permute-start | bytes 589832 | tf_op jit(solution)/shard_map/ppermute | solution.py:255
  446.8 27.8 %collective-permute-start.59 = (bf16[2,1,128,384]{3,2,0,1:T(8,128)(2,1)S(1)}, bf16[2,1,128,384]{3,2,0,1:T(8,128)(2,1)S(1)}, u32[]{:S(2)}, u32[]{:S(2)}) collective-permute-start(bf16[2,1,128,384]{3,2,0,1:T(8,128)(2,1)S(1)} %constant_dynamic-slice_fusion.20), channel_id=1, source_target_pairs={{0,1},{1,0},{2,3},{3,2},{4,5},{5,4},{6,7},{7,6},{8,9},{9,8},{10,11... | collective-permute-start | bytes 589832 | tf_op jit(solution)/shard_map/ppermute | solution.py:255
  460.2 13.7 %collective-permute-start.57 = (bf16[2,2,128,384]{3,2,0,1:T(8,128)(2,1)S(1)}, bf16[2,2,128,384]{3,2,0,1:T(8,128)(2,1)S(1)}, u32[]{:S(2)}, u32[]{:S(2)}) collective-permute-start(bf16[2,2,128,384]{3,2,0,1:T(8,128)(2,1)S(1)} %get-tuple-element.175), channel_id=1, source_target_pairs={{0,16},{1,17},{2,18},{3,19},{4,20},{5,21},{6,22},{7,23},{8,24},{9,... | collective-permute-start | bytes 1179656 | tf_op jit(solution)/shard_map/ppermute | solution.py:255
  462.1 53.0 %collective-permute-start.98 = (bf16[352,512]{1,0:T(8,128)(2,1)S(1)}, bf16[352,512]{1,0:T(8,128)(2,1)S(1)}, u32[]{:S(2)}, u32[]{:S(2)}) collective-permute-start(bf16[352,512]{1,0:T(8,128)(2,1)S(1)} %maximum_select_fusion.9), channel_id=1, source_target_pairs={{0,8},{1,9},{2,10},{3,11},{4,12},{5,13},{6,14},{7,15},{8,0},{9,1},... | collective-permute-start | bytes 1081352 | tf_op jit(solution)/shard_map/ppermute | solution.py:255
  462.3 32.6 %collective-permute-start.86 = (bf16[128,1408]{1,0:T(8,128)(2,1)S(1)}, bf16[128,1408]{1,0:T(8,128)(2,1)S(1)}, u32[]{:S(2)}, u32[]{:S(2)}) collective-permute-start(bf16[128,1408]{1,0:T(8,128)(2,1)S(1)} %fusion.39), channel_id=1, source_target_pairs={{0,16},{1,17},{2,18},{3,19},{4,20},{5,21},{6,22},{7,23},{8,24},{9,... | collective-permute-start | bytes 1081352 | tf_op jit(solution)/shard_map/ppermute | solution.py:255
  473.8 10.6 %collective-permute-start.70 = (bf16[2,1,128,256]{3,2,0,1:T(8,128)(2,1)S(1)}, bf16[2,1,128,256]{3,2,0,1:T(8,128)(2,1)S(1)}, u32[]{:S(2)}, u32[]{:S(2)}) collective-permute-start(bf16[2,1,128,256]{3,2,0,1:T(8,128)(2,1)S(1)} %get-tuple-element.187), channel_id=1, source_target_pairs={{0,1},{1,0},{2,3},{3,2},{4,5},{5,4},{6,7},{7,6},{8,9},{9,8},{10,11... | collective-permute-start | bytes 393224 | tf_op jit(solution)/shard_map/ppermute | solution.py:255
  474.6 53.2 %collective-permute-start.45 = (bf16[2,256,1024]{2,1,0:T(8,128)(2,1)}, bf16[2,256,1024]{2,1,0:T(8,128)(2,1)}, u32[]{:S(2)}, u32[]{:S(2)}) collective-permute-start(bf16[2,256,1024]{2,1,0:T(8,128)(2,1)} %fusion.29), channel_id=1, source_target_pairs={{0,8},{1,9},{2,10},{3,11},{4,12},{5,13},{6,14},{7,15},{8,0},{9,1},... | collective-permute-start | bytes 3145736 | tf_op jit(solution)/shard_map/ppermute | solution.py:255
  484.5 11.5 %collective-permute-start.58 = (bf16[2,1,128,384]{3,2,0,1:T(8,128)(2,1)S(1)}, bf16[2,1,128,384]{3,2,0,1:T(8,128)(2,1)S(1)}, u32[]{:S(2)}, u32[]{:S(2)}) collective-permute-start(bf16[2,1,128,384]{3,2,0,1:T(8,128)(2,1)S(1)} %constant_dynamic-slice_fusion.21), channel_id=1, source_target_pairs={{0,1},{1,0},{2,3},{3,2},{4,5},{5,4},{6,7},{7,6},{8,9},{9,8},{10,11... | collective-permute-start | bytes 589832 | tf_op jit(solution)/shard_map/ppermute | solution.py:255
  487.8 10.8 %collective-permute-start.73 = (bf16[1,128,256]{2,1,0:T(8,128)(2,1)S(1)}, bf16[1,128,256]{2,1,0:T(8,128)(2,1)S(1)}, u32[]{:S(2)}, u32[]{:S(2)}) collective-permute-start(bf16[1,128,256]{2,1,0:T(8,128)(2,1)S(1)} %get-tuple-element.206), channel_id=1, source_target_pairs={{0,2},{1,3},{2,4},{3,5},{4,6},{5,7},{6,0},{7,1},{8,10},{9,11},{10,... | collective-permute-start | bytes 196616 | tf_op jit(solution)/shard_map/ppermute | solution.py:255
  505.6 20.5 %collective-permute-start.87 = (bf16[2,128,1408]{2,1,0:T(8,128)(2,1)}, bf16[2,128,1408]{2,1,0:T(8,128)(2,1)}, u32[]{:S(2)}, u32[]{:S(2)}) collective-permute-start(bf16[2,128,1408]{2,1,0:T(8,128)(2,1)} %pad_maximum_fusion.8), channel_id=1, source_target_pairs={{0,8},{1,9},{2,10},{3,11},{4,12},{5,13},{6,14},{7,15},{8,0},{9,1},... | collective-permute-start | bytes 2162696 | tf_op jit(solution)/shard_map/ppermute | solution.py:255
  (74 other events, 580.7 us)

commit v2 on v1

v2 whole, which is shorter than its diff:
```python
import jax
import jax.numpy as jnp
from jax import lax
from jax.experimental import pallas as pl
from jax.experimental.pallas import tpu as pltpu
from jax.sharding import PartitionSpec as P

D = 1024
H = 16
HD = 64
KVH = 2
LAT = 256
GH = H // KVH
GW = D // KVH
EPS = 1e-06
SCALE = HD ** (-0.5)
LOG2E = 1.4426950408889634
NEG = -1e30

LOW = jnp.bfloat16
F32 = jnp.float32
ALL = ("seq", "dp")
VMEM_LIMIT = 56 * 1024 * 1024


def mm(left, right):
    return jnp.dot(left, right, preferred_element_type=F32)


def tn(left, right):
    return lax.dot_general(left, right, (((0,), (0,)), ((), ())), preferred_element_type=F32)


def nt(left, right):
    return lax.dot_general(left, right, (((1,), (1,)), ((), ())), preferred_element_type=F32)


def block_bias(k0, q0, first, width):
    kpos = k0 + lax.broadcasted_iota(jnp.int32, (width, width), 0)
    qpos = q0 + lax.broadcasted_iota(jnp.int32, (width, width), 1)
    lowest = jnp.where(qpos >= first, first, 0)
    return jnp.where((kpos <= qpos) & (kpos >= lowest), 0.0, NEG)


def block_needed(k0, q0, first, width):
    before = jnp.logical_and(q0 >= first, k0 + (width - 1) < first)
    return jnp.logical_and(k0 <= q0, jnp.logical_not(before))


def forward_kernel(b, nkb, batch, width, meta, qt, kxt, vxt, c, o_low, o_full, mix_out, lse_out, q_s, acc, m_s, l_s):
    qb = pl.program_id(0)
    q0, first, diag = meta[nkb + qb], meta[nkb + 2 + b], meta[nkb + 2 + batch] + qb
    for h in range(GH):
        cols = slice(h * width, (h + 1) * width)
        rows = slice(h * HD, (h + 1) * HD)
        q_s[:, cols] = (tn(kxt[rows, :], qt[0, rows, :]) * (SCALE * LOG2E)).astype(LOW)
    m_s[...] = jnp.full_like(m_s, NEG)
    l_s[...] = jnp.zeros_like(l_s)
    acc[...] = jnp.zeros_like(acc)

    def step(j, carry):
        kb = lax.rem(diag + j, nkb)
        k0 = meta[kb]

        @pl.when(block_needed(k0, q0, first, width))
        def _():
            bias = block_bias(k0, q0, first, width)
            keys = c[0, kb]
            keys_t = keys.T
            for h in range(GH):
                cols = slice(h * width, (h + 1) * width)
                s = mm(keys, q_s[:, cols]) + bias
                m_old = m_s[:, cols]
                m_new = jnp.maximum(m_old, jnp.max(s, axis=0, keepdims=True))
                p = jnp.exp2(s - m_new)
                alpha = jnp.exp2(m_old - m_new)
                m_s[:, cols] = m_new
                l_s[:, cols] = l_s[:, cols] * alpha + jnp.sum(p, axis=0, keepdims=True)
                acc[:, cols] = acc[:, cols] * alpha + mm(keys_t, p.astype(LOW))

        return carry

    lax.fori_loop(0, nkb, step, 0)
    for h in range(GH):
        cols = slice(h * width, (h + 1) * width)
        rows = slice(h * HD, (h + 1) * HD)
        total = l_s[:, cols]
        mixed = (acc[:, cols] * (1.0 / total)).astype(LOW)
        mix_out[0, :, cols] = mixed
        out = mm(vxt[rows, :], mixed)
        o_full[0, rows, :] = out
        o_low[0, rows, :] = out.astype(LOW)
        lse_out[0, :, cols] = m_s[:, cols] + jnp.log(total) * LOG2E


def backward_kernel(
    b, qb, nkb, batch, width, add_dc, add_dw, meta, qt, dot_, o_full, mix, lse, kxt, vxt, c, *refs
):
    refs = list(refs)
    dc_old = refs.pop(0) if add_dc else None
    dk_old, dv_old = (refs.pop(0), refs.pop(0)) if add_dw else (None, None)
    dqt, dc, dkxt, dvxt, q_s, q_n, do_t, do_n, delta, dq, ds_s, p_s = refs
    q0, first, diag = meta[nkb + qb], meta[nkb + 2 + b], meta[nkb + 2 + batch] + qb
    dc[...] = dc_old[...] if add_dc else jnp.zeros_like(dc)

    for h in range(GH):
        cols = slice(h * width, (h + 1) * width)
        rows = slice(h * HD, (h + 1) * HD)
        qh, kh, doh, vh = qt[0, rows, :], kxt[rows, :], dot_[0, rows, :], vxt[rows, :]
        q_s[:, cols] = (tn(kh, qh) * (SCALE * LOG2E)).astype(LOW)
        q_n[cols, :] = (tn(qh, kh) * SCALE).astype(LOW)
        do_t[:, cols] = tn(vh, doh).astype(LOW)
        do_n[cols, :] = tn(doh, vh).astype(LOW)
        delta[:, cols] = jnp.sum(doh.astype(F32) * o_full[0, rows, :], axis=0, keepdims=True)
    dq[...] = jnp.zeros_like(dq)

    def step(j, carry):
        kb = lax.rem(diag + j, nkb)
        k0 = meta[kb]

        @pl.when(block_needed(k0, q0, first, width))
        def _():
            bias = block_bias(k0, q0, first, width)
            keys = c[0, kb]
            keys_t = keys.T
            for h in range(GH):
                cols = slice(h * width, (h + 1) * width)
                s = mm(keys, q_s[:, cols]) + bias
                p = jnp.exp2(s - lse[0, :, cols])
                dp = mm(keys, do_t[:, cols])
                ds = (p * (dp - delta[:, cols])).astype(LOW)
                p_s[:, cols] = p.astype(LOW)
                ds_s[:, cols] = ds
                dq[:, cols] += mm(keys_t, ds)
            dc[kb] += mm(ds_s[...], q_n[...]) + mm(p_s[...], do_n[...])

        return carry

    lax.fori_loop(0, nkb, step, 0)
    for h in range(GH):
        cols = slice(h * width, (h + 1) * width)
        rows = slice(h * HD, (h + 1) * HD)
        dq_low = (dq[:, cols] * SCALE).astype(LOW)
        dqt[rows, :] = mm(kxt[rows, :], dq_low).astype(LOW)
        dk, dv = nt(qt[0, rows, :], dq_low), nt(dot_[0, rows, :], mix[0, :, cols])
        dkxt[rows, :] = dk + dk_old[rows, :] if add_dw else dk
        dvxt[rows, :] = dv + dv_old[rows, :] if add_dw else dv


def attention_forward(b, meta, qt, kxt, vxt, c):
    batch, nkb, width, _ = c.shape
    wide = GH * width
    pairs = 7 * GH * width * width * LAT
    expand = pl.BlockSpec((GW, LAT), lambda q: (0, 0))
    out_spec = pl.BlockSpec((1, GW, width), lambda q: (0, 0, q))
    return pl.pallas_call(
        lambda *refs: forward_kernel(b, nkb, batch, width, *refs),
        grid=(2,),
        in_specs=[
            pl.BlockSpec(memory_space=pltpu.SMEM),
            pl.BlockSpec((1, GW, width), lambda q: (b, 0, q)),
            expand,
            expand,
            pl.BlockSpec((1, nkb, width, LAT), lambda q: (b, 0, 0, 0)),
        ],
        out_specs=[
            out_spec,
            out_spec,
            pl.BlockSpec((1, LAT, wide), lambda q: (q, 0, 0)),
            pl.BlockSpec((1, 1, wide), lambda q: (q, 0, 0)),
        ],
        out_shape=[
            jax.ShapeDtypeStruct((1, GW, 2 * width), LOW),
            jax.ShapeDtypeStruct((1, GW, 2 * width), F32),
            jax.ShapeDtypeStruct((2, LAT, wide), LOW),
            jax.ShapeDtypeStruct((2, 1, wide), F32),
        ],
        scratch_shapes=[
            pltpu.VMEM((LAT, wide), LOW),
            pltpu.VMEM((LAT, wide), F32),
            pltpu.VMEM((1, wide), F32),
            pltpu.VMEM((1, wide), F32),
        ],
        compiler_params=pltpu.CompilerParams(
            dimension_semantics=("arbitrary",), vmem_limit_bytes=VMEM_LIMIT
        ),
        cost_estimate=pl.CostEstimate(
            flops=4 * pairs, bytes_accessed=8 << 20, transcendentals=7 * GH * width * width
        ),
        name="attention_forward",
    )(meta, qt, kxt, vxt, c)


def attention_backward(b, qb, meta, qt, dot_, o_full, mix, lse, kxt, vxt, c, old_dc, old_dw):
    batch, nkb, width, _ = c.shape
    wide = GH * width
    pairs = 4 * GH * width * width * LAT * 2
    q_spec = pl.BlockSpec((1, GW, width), lambda i: (b, 0, qb))
    expand = pl.BlockSpec((GW, LAT), lambda i: (0, 0))
    return pl.pallas_call(
        lambda *refs: backward_kernel(
            b, qb, nkb, batch, width, bool(old_dc), bool(old_dw), *refs
        ),
        grid=(1,),
        in_specs=[
            pl.BlockSpec(memory_space=pltpu.SMEM),
            q_spec,
            q_spec,
            pl.BlockSpec((1, GW, width), lambda i: (0, 0, qb)),
            pl.BlockSpec((1, LAT, wide), lambda i: (qb, 0, 0)),
            pl.BlockSpec((1, 1, wide), lambda i: (qb, 0, 0)),
            expand,
            expand,
            pl.BlockSpec((1, nkb, width, LAT), lambda i: (b, 0, 0, 0)),
        ]
        + [pl.BlockSpec((nkb, width, LAT), lambda i: (0, 0, 0))] * len(old_dc)
        + [expand] * len(old_dw),
        out_specs=[
            pl.BlockSpec((GW, width), lambda i: (0, 0)),
            pl.BlockSpec((nkb, width, LAT), lambda i: (0, 0, 0)),
            expand,
            expand,
        ],
        out_shape=[
            jax.ShapeDtypeStruct((GW, width), LOW),
            jax.ShapeDtypeStruct((nkb, width, LAT), F32),
            jax.ShapeDtypeStruct(kxt.shape, F32),
            jax.ShapeDtypeStruct(vxt.shape, F32),
        ],
        scratch_shapes=[
            pltpu.VMEM((LAT, wide), LOW),
            pltpu.VMEM((wide, LAT), LOW),
            pltpu.VMEM((LAT, wide), LOW),
            pltpu.VMEM((wide, LAT), LOW),
            pltpu.VMEM((1, wide), F32),
            pltpu.VMEM((LAT, wide), F32),
            pltpu.VMEM((width, wide), LOW),
            pltpu.VMEM((width, wide), LOW),
        ],
        compiler_params=pltpu.CompilerParams(
            dimension_semantics=("arbitrary",), vmem_limit_bytes=VMEM_LIMIT
        ),
        cost_estimate=pl.CostEstimate(
            flops=5 * pairs, bytes_accessed=6 << 20, transcendentals=4 * GH * width * width
        ),
        name="attention_backward",
    )(meta, qt, dot_, o_full, mix, lse, kxt, vxt, c, *old_dc, *old_dw)


class Place:
    def __init__(self):
        self.seq, self.dp = lax.axis_size("seq"), lax.axis_size("dp")
        s, d = lax.axis_index("seq"), lax.axis_index("dp")
        self.core, self.chip = s % 2, s // 2
        self.y, self.x, self.z = s // 2, d % 2, d // 2
        self.square = self.seq == 4 and self.dp == 8

    def pairs(self, move):
        found = []
        for s in range(self.seq):
            for d in range(self.dp):
                target = move(s, d)
                if target is not None:
                    found.append((s * self.dp + d, target[0] * self.dp + target[1]))
        return found

    def send(self, value, move):
        return lax.ppermute(value, ALL, self.pairs(move))

    def to_core(self, value):
        return self.send(value, lambda s, d: (s ^ 1, d))

    def to_y(self, value):
        return self.send(value, lambda s, d: (s ^ 2, d))

    def to_x(self, value):
        return self.send(value, lambda s, d: (s, d ^ 1))

    def to_z(self, value, step):
        return self.send(value, lambda s, d: (s, (d + 2 * step) % 8))

    def up_y(self, value):
        return self.send(value, lambda s, d: (s + 2, d) if s < 2 else None)

    def down_y(self, value):
        return self.send(value, lambda s, d: (s - 2, d) if s >= 2 else None)


def half(value, index, axis, count=2):
    size = value.shape[axis] // count
    return lax.dynamic_slice_in_dim(value, index * size, size, axis)


def ordered(flag, own, other, axis):
    return jnp.where(
        flag == 0, jnp.concatenate([own, other], axis), jnp.concatenate([other, own], axis)
    )


def after(value, *others):
    return lax.optimization_barrier((value, others))[0]


def add_low(own, other):
    return (own.astype(F32) + other.astype(F32)).astype(LOW)


class Plain:
    def __init__(self, place):
        self.p = place
        count = place.seq // 2
        self.same_core = [[2 * i + c for i in range(count)] for c in range(2)]
        self.chip = [[2 * i, 2 * i + 1] for i in range(count)]

    def gather(self, w):
        core = self.p.core

        def full(value, axis=0):
            return lax.all_gather(value.astype(LOW), "dp", axis=axis, tiled=True)

        out = {name: full(half(w[name], core, 1)) for name in ("query", "latent", "gate", "up")}
        out["key_t"] = half(full(w["key"].T), core, 0)
        out["value_t"] = half(full(w["value"].T), core, 0)
        out["output"] = half(full(w["output"]), core, 0)
        out["down"] = half(full(w["down"]), core, 0)
        out["gain1"], out["gain2"] = full(w["gain1"]), full(w["gain2"])
        return out

    def columns(self, grad):
        share = lax.psum_scatter(grad.astype(LOW), "dp", scatter_dimension=0, tiled=True)
        share = lax.psum(share, "seq", axis_index_groups=self.same_core)
        return lax.all_gather(
            share, "seq", axis=1, tiled=True, axis_index_groups=self.chip
        ).astype(F32)

    def rows(self, grad):
        grad = grad.astype(LOW)
        grad = ordered(self.p.core, grad, jnp.zeros_like(grad), 0)
        share = lax.psum_scatter(grad, "dp", scatter_dimension=0, tiled=True)
        return lax.psum(share, "seq").astype(F32)

    def gain(self, grad):
        share = lax.psum_scatter(grad.astype(LOW), "dp", scatter_dimension=0, tiled=True)
        return lax.psum(share, "seq").astype(F32)


def inverse_rms(values):
    return lax.rsqrt(jnp.mean(values * values, axis=-1, keepdims=True) + EPS)


def norm_back(grad, normed, inverse, gain):
    scaled = grad * gain
    return inverse * (scaled - normed * jnp.mean(scaled * normed, axis=-1, keepdims=True))


def dots(spec, left, right):
    return jnp.einsum(spec, left, right, preferred_element_type=F32)


def pick(flag, zero, one):
    return jnp.where(flag == 0, zero, one)


def chip(p, own):
    return jnp.stack([own, p.to_core(own)], axis=1)


def chip_sum(p, partial):
    return partial[:, 0] + p.to_core(partial[:, 1].astype(LOW)).astype(F32)


def plain_layer(
    p, tokens, attn_gain, query_weight, latent_weight, key_expand, value_expand, output_weight,
    mlp_gain, gate_weight, up_weight, down_weight, cotangent, lengths,
):
    ways = Plain(p)
    batch, length, _ = tokens.shape
    count = 2 * batch * length
    w = ways.gather(
        {
            "gain1": attn_gain, "query": query_weight, "latent": latent_weight,
            "key": key_expand, "value": value_expand, "output": output_weight,
            "gain2": mlp_gain, "gate": gate_weight, "up": up_weight, "down": down_weight,
        }
    )
    gain1, gain2 = w["gain1"].astype(F32), w["gain2"].astype(F32)
    firsts = lengths[:, 0]
    chips = p.seq // 2
    rows = chip(p, tokens).astype(F32)
    first_low = (rows * inverse_rms(rows) * gain1).astype(LOW)
    first_flat = first_low.reshape(batch, 2 * length, D)
    latent = dots("btd,dl->btl", first_flat, w["latent"]).astype(LOW)
    query_t = dots("dn,btd->bnt", w["query"], first_flat).astype(LOW)
    blocks = latent.reshape(batch, 2, length, LAT)
    starts = jnp.stack([p.core, 1 - p.core]).astype(jnp.int32) * length
    base = p.chip * 2 * length
    keys = lax.all_gather(blocks, "seq", axis=1, tiled=True, axis_index_groups=ways.same_core)
    key_starts = (
        2 * length * jnp.arange(chips, dtype=jnp.int32)[:, None] + starts[None, :]
    ).reshape(-1)
    diag = (2 * p.chip).astype(jnp.int32).reshape(1)
    meta = jnp.concatenate([key_starts, base + starts, firsts, diag]).astype(jnp.int32)
    att = [
        attention_forward(b, meta, query_t, w["key_t"], w["value_t"], keys)
        for b in range(batch)
    ]
    out_low = jnp.concatenate([a[0] for a in att])
    branch = dots("bnt,nd->btd", out_low, w["output"])
    middle = tokens.astype(F32) + chip_sum(p, branch.reshape(batch, 2, length, D))
    inverse2 = inverse_rms(middle)
    normed2 = middle * inverse2
    second = chip(p, (normed2 * gain2).astype(LOW)).reshape(count, D)
    cot = chip(p, cotangent).reshape(count, D)
    gate = mm(second, w["gate"])
    up = mm(second, w["up"])
    sig = jax.nn.sigmoid(gate)
    act = gate * sig
    hidden = (act * up).astype(LOW)
    partial = mm(hidden, w["down"]).reshape(batch, 2, length, D)
    layer_out = (middle + chip_sum(p, partial)).astype(LOW)
    grad_down = ways.rows(tn(hidden, cot))
    d_hidden = nt(cot, w["down"])
    d_gate = (d_hidden * up * sig * (1.0 + gate * (1.0 - sig))).astype(LOW)
    d_up = (d_hidden * act).astype(LOW)
    grad_gate, grad_up = ways.columns(tn(second, d_gate)), ways.columns(tn(second, d_up))
    partial = (nt(d_gate, w["gate"]) + nt(d_up, w["up"])).reshape(batch, 2, length, D)
    d_second = chip_sum(p, partial)
    gain2_sum = jnp.sum(d_second * normed2, axis=(0, 1))
    d_middle = cotangent.astype(F32) + norm_back(d_second, normed2, inverse2, gain2)
    d_a = chip(p, d_middle.astype(LOW)).reshape(batch, 2 * length, D)
    grad_output = ways.rows(dots("bnt,btd->nd", out_low, d_a))
    d_out_t = dots("nd,btd->bnt", w["output"], d_a).astype(LOW)
    d_queries, d_keys, sums = [], [], ()
    for b in range(batch):
        far = ()
        for qb in range(2):
            found = attention_backward(
                b, qb, meta, query_t, d_out_t, *att[b][1:], w["key_t"], w["value_t"], keys,
                far, sums,
            )
            far, sums = found[1:2], found[2:]
            d_queries.append(found[0])
        d_keys.append(far[0])
    dq_t = jnp.stack([jnp.concatenate(d_queries[2 * b : 2 * b + 2], 1) for b in range(batch)])
    d_keys = jnp.stack(d_keys)
    d_key_t, d_value_t = sums
    d_blocks = lax.psum_scatter(
        d_keys.astype(LOW), "seq", scatter_dimension=1, tiled=True,
        axis_index_groups=ways.same_core,
    )
    d_latent = d_blocks.astype(LOW).reshape(batch, 2 * length, LAT)
    grad_query = ways.columns(dots("btd,bnt->dn", first_flat, dq_t))
    grad_latent = ways.columns(dots("btd,btl->dl", first_flat, d_latent))
    d_first = dots("bnt,dn->btd", dq_t, w["query"]) + dots("btl,dl->btd", d_latent, w["latent"])
    d_first = chip_sum(p, d_first.reshape(batch, 2, length, D))
    own = tokens.astype(F32)
    inverse1 = inverse_rms(own)
    normed1 = own * inverse1
    gain1_sum = jnp.sum(d_first * normed1, axis=(0, 1))
    grad_tokens = d_middle + norm_back(d_first, normed1, inverse1, gain1)
    return (
        layer_out, grad_tokens, ways.gain(gain1_sum), grad_query, grad_latent,
        ways.rows(d_key_t).T, ways.rows(d_value_t).T, grad_output, ways.gain(gain2_sum),
        grad_gate, grad_up, grad_down,
    )


class Live:
    def __init__(self, values):
        self.__dict__.update(values)

    @property
    def pop(self):
        return Taken(self)


class Taken:
    def __init__(self, live):
        self.live = live

    def __getattr__(self, name):
        return self.live.__dict__.pop(name)


def sync(v):
    return Live(lax.optimization_barrier(dict(v.__dict__)))


def z_gather(p, piece):
    seen = [piece] + [p.to_z(piece, k) for k in (1, 2, 3)]
    out = []
    for z in range(4):
        back = (p.z - z) % 4
        pair = [jnp.where(back % 2 == 0, seen[k], seen[k + 1]) for k in (0, 2)]
        out.append(jnp.where(back < 2, pair[0], pair[1]))
    return jnp.stack(out)


def z_scatter(p, parts):
    total = half(parts, p.z, 0, 4)[0].astype(F32)
    for k in (1, 2, 3):
        total = total + p.to_z(half(parts, (p.z + k) % 4, 0, 4), k)[0].astype(F32)
    return total.astype(LOW)


def to_xy(p, value):
    return p.send(value, lambda s, d: (s ^ 2, d ^ 1))


def add_all(parts):
    return sum(part.astype(F32) for part in parts).astype(LOW)


def place_kernel(plan, sources, outs, where, *refs):
    src, dst = refs[:sources], refs[sources:]
    spot = where[0], where[1], where[2]
    for make in plan:
        source, there, out, here = make(*spot)
        dst[out][here] = src[source][there].astype(LOW)


def placed(p, plan, sources, shapes):
    where = jnp.stack([p.x, p.y, p.core]).astype(jnp.int32)
    inside = pl.BlockSpec(memory_space=pltpu.VMEM)
    return pl.pallas_call(
        lambda *refs: place_kernel(plan, len(sources), len(shapes), *refs),
        in_specs=[pl.BlockSpec(memory_space=pltpu.SMEM)] + [inside] * len(sources),
        out_specs=[inside] * len(shapes),
        out_shape=[jax.ShapeDtypeStruct(shape, LOW) for shape in shapes],
        compiler_params=pltpu.CompilerParams(vmem_limit_bytes=VMEM_LIMIT),
        name="place",
    )(where, *sources)


def lanes(start, width):
    return pl.ds(pl.multiple_of(start, 128), width)


RELATIVE = [(0, 0), (1, 0), (0, 1), (1, 1)]


def spread(p, parts):
    return parts[0], p.to_x(parts[1]), p.to_y(parts[2]), to_xy(p, parts[3])


def square_layer(
    p, tokens, attn_gain, query_weight, latent_weight, key_expand, value_expand, output_weight,
    mlp_gain, gate_weight, up_weight, down_weight, cotangent, lengths,
):
    batch, length, _ = tokens.shape
    count = 2 * batch * length
    core, x, y = p.core, p.x, p.y
    ff = gate_weight.shape[1] // 2
    quarter = 2 * core + y
    v = Live({})

    def cols(value, parts, index):
        return half(value, index, 1, parts).astype(LOW)

    def x_own(value):
        return half(value, x, 1)

    def x_other(value):
        return half(value, 1 - x, 1)

    v.pgu = jnp.concatenate([cols(gate_weight, 2, core), cols(up_weight, 2, core)], 1)
    v.tok = p.to_core(tokens)
    v = sync(v)
    kv = half(pick(y, key_expand, value_expand), core, 0).astype(LOW).T
    gains = jnp.stack([attn_gain, mlp_gain] + [jnp.zeros_like(attn_gain)] * 6).astype(LOW)
    piece = [
        cols(latent_weight, 4, quarter), cols(output_weight, 4, quarter),
        cols(query_weight, 4, quarter), kv,
    ]
    piece = jnp.concatenate(piece, 1)
    pad = jnp.zeros((8, piece.shape[1] - 128), LOW)
    piece = jnp.concatenate([piece, jnp.concatenate([gains, pad], 1)], 0)
    first = z_gather(p, piece)
    v.a, v.b = first[:, :, :384], first[:, :, 384:]
    rows = jnp.stack([tokens, v.pop.tok], 1).astype(F32)
    v.normed1 = rows * inverse_rms(rows)
    v.pd = cols(down_weight, 4, quarter)
    v = sync(v)

    w_gu = lax.all_gather(v.pop.pgu, "dp", axis=0, tiled=True)
    v.ax, v.by = p.to_x(v.a), p.to_y(v.b)
    v = sync(v)
    v.ay, v.axy = p.to_y(v.a), p.to_y(v.ax)
    v.bx, v.bxy = p.to_x(v.b), p.to_x(v.by)
    v = sync(v)

    v.from_ab = (v.pop.a, v.pop.ax, v.pop.ay, v.pop.axy, v.pop.b, v.pop.bx, v.pop.by, v.pop.bxy)
    plan = []
    for n, (r, k) in enumerate(RELATIVE):
        low = pl.ds(0, 128)
        plan += [
            lambda x, y, c, n=n, r=r, k=k: (
                n, (slice(None), low, pl.ds(0, 128)), 0,
                (slice(None), x ^ r, slice(None), lanes((y ^ k) * 128, 128)),
            ),
            lambda x, y, c, n=n, r=r, k=k: (
                4 + n, (slice(None), low, pl.ds(0, 256)), 1,
                (slice(None), x ^ r, slice(None), lanes((y ^ k) * 256, 256)),
            ),
            lambda x, y, c, n=n: (n, (pl.ds(2 * (1 - c), 2), low, pl.ds(128, 256)), 2, n),
            lambda x, y, c, n=n: (4 + n, (pl.ds(2 * (1 - c), 2), low, pl.ds(256, 128)), 3, n),
        ]
    wl, wq, v.wo_send, v.kv_send = placed(
        p, plan, v.from_ab,
        [(4, 2, 128, LAT), (4, 2, 128, GW), (4, 2, 128, 256), (4, 2, 128, 128)],
    )
    v.wl, v.wq = wl.reshape(D, LAT), wq.reshape(D, GW)
    gains = [part[:, 128:130, :128] for part in v.from_ab[:2]]
    gains = pick(x, jnp.stack(gains, 2), jnp.stack(gains[::-1], 2)).astype(F32)
    v.gain1, v.gain2 = gains[:, 0].reshape(D), gains[:, 1].reshape(D)
    v.first = (v.pop.normed1 * v.gain1).astype(LOW).reshape(batch, 2 * length, D)
    v.keys = dots("btd,dl->btl", v.first, v.wl).astype(LOW).reshape(batch, 2, length, LAT)
    v = sync(v)
    far_keys = p.up_y(v.keys)
    wo_come, kv_come = p.to_core(v.pop.wo_send), p.to_core(v.pop.kv_send)
    v.zd = z_gather(p, v.pop.pd)
    v.qt = dots("dn,btd->bnt", v.wq, v.first).astype(LOW)
    plan = []
    for n, (r, k) in enumerate(RELATIVE):
        for s in range(2):
            plan += [
                lambda x, y, c, n=n, r=r, k=k, s=s: (
                    (n, (pl.ds(2 * c, 2), pl.ds(0, 128), pl.ds(128, 256))) if s == 0 else (8, n)
                ) + (0, (slice(None), x ^ r, slice(None), lanes(((c ^ s) * 2 + (y ^ k)) * 256, 256))),
                lambda x, y, c, n=n, r=r, k=k, s=s: (
                    (4 + n, (pl.ds(2 * c, 2), pl.ds(0, 128), pl.ds(256, 128))) if s == 0 else (9, n)
                ) + (1, (y ^ k, slice(None), x ^ r, slice(None), lanes((c ^ s) * 128, 128))),
            ]
    wo, kv = placed(
        p, plan, (*v.pop.from_ab, wo_come, kv_come), [(2, 2, 128, D), (2, 2, 2, 128, LAT)]
    )
    v.wo, kv = wo.reshape(GW, D), kv.reshape(2, GW, LAT)
    v.kxt, v.vxt = kv[0], kv[1]
    starts = jnp.stack([core, 1 - core]).astype(jnp.int32) * length
    base = p.chip * 2 * length
    far = pick(p.chip, 2 * length, 0)
    meta = [base + starts, far + starts, base + starts, lengths[:, 0], jnp.zeros((1,), jnp.int32)]
    v.meta = jnp.concatenate(meta).astype(jnp.int32)
    v.keys = jnp.concatenate([v.keys, far_keys], axis=1)
    v = sync(v)

    def forward(b):
        return attention_forward(b, v.meta, v.qt, v.kxt, v.vxt, v.keys)

    v.dax, v.dby = p.to_x(v.zd[:2]), p.to_y(v.zd[2:])
    v.cot = chip(p, cotangent).reshape(count, D)
    v.att0 = forward(0)
    v = sync(v)
    v.day, v.daxy = p.to_y(v.zd[:2]), p.to_y(v.dax)
    v.dbx, v.dbxy = p.to_x(v.zd[2:]), p.to_x(v.dby)
    cot = half(v.cot, core, 1)
    v.cot_c = [half(cot, i, 1) for i in (y, 1 - y)] + [half(v.cot, 1 - core, 1)]
    v.att1 = forward(1)
    v = sync(v)

    down = (v.pop.zd, v.pop.dax, v.pop.day, v.pop.daxy, v.pop.dby, v.pop.dbx, v.pop.dbxy)
    fronts = [down[0][:2], down[1], down[2], down[3]]
    backs = [down[0][2:], down[5], down[4], down[6]]
    mine = [pick(core, front, back) for front, back in zip(fronts, backs)]
    come = [p.to_core(pick(core, back, front)) for front, back in zip(fronts, backs)]
    v.down = mine + come
    v.out = jnp.concatenate([v.att0[0], v.att1[0]])
    branch = dots("bnt,nd->btd", v.out, v.wo).reshape(batch, 2, length, D)
    v.middle = tokens.astype(F32) + chip_sum(p, branch)
    v.inv2 = inverse_rms(v.middle)
    second = v.middle * v.inv2 * v.gain2
    v.second = chip(p, second.astype(LOW)).reshape(count, D)
    v = sync(v)

    plan = []
    for n, (r, k) in enumerate(RELATIVE):
        for s in range(2):
            plan += [
                lambda x, y, c, n=n, r=r, k=k, s=s: (
                    4 * s + n, slice(None), 0,
                    (slice(None), x ^ r, slice(None), lanes(((c ^ s) * 2 + (y ^ k)) * 256, 256)),
                )
            ]
    wd = placed(p, plan, v.pop.down, [(2, 2, ff // 4, D)])[0]
    v.wd = wd.reshape(ff, D)
    v.w_gu = w_gu
    v = sync(v)
    v.act = mm(v.second, v.w_gu)
    gate, up = v.act[:, :ff], v.act[:, ff:]
    v.hidden = (gate * jax.nn.sigmoid(gate) * up).astype(LOW)
    cot_y, cot_far, cot_core = v.pop.cot_c
    v.gd_a = tn(v.hidden, cot_y).astype(LOW).reshape(2, 2, -1, 256)
    v.gd_ay = tn(v.hidden, cot_far).astype(LOW).reshape(2, 2, -1, 256)
    v.gd_send = tn(v.hidden, cot_core).astype(LOW).reshape(2, 2, -1, 512)
    v = sync(v)

    v.gd_b = p.to_core(v.pop.gd_send)
    gate, up = v.act[:, :ff], v.pop.act[:, ff:]
    sig = jax.nn.sigmoid(gate)
    d_hidden = nt(v.cot, v.wd)
    d_gate = d_hidden * up * sig * (1.0 + gate * (1.0 - sig))
    d_up = d_hidden * (gate * sig)
    v.d_gu = jnp.concatenate([d_gate, d_up], 1).astype(LOW)
    v = sync(v)
    v.gd_ay, v.gd_bx = p.to_y(v.gd_ay), p.to_x(x_other(v.gd_b))
    v.gg = tn(v.pop.second, v.d_gu).astype(LOW)
    v = sync(v)
    gg = lax.psum_scatter(v.pop.gg, "dp", scatter_dimension=0, tiled=True)
    v.gd_a = add_low(v.gd_a, v.pop.gd_ay)
    v.gd_b = add_low(x_own(v.gd_b), v.pop.gd_bx)
    v.gd_ax, v.gd_by = p.to_x(x_other(v.gd_a)), p.to_y(half(v.gd_b, 1 - y, 3))
    d_second = chip_sum(p, nt(v.pop.d_gu, v.pop.w_gu).reshape(batch, 2, length, D))
    normed2 = v.middle * v.inv2
    v.gain2_sum = jnp.sum(d_second * normed2, axis=(0, 1))
    v.d_middle = cotangent.astype(F32) + norm_back(d_second, normed2, v.pop.inv2, v.pop.gain2)
    v = sync(v)
    v.d_a = chip(p, v.d_middle.astype(LOW)).reshape(batch, 2 * length, D)
    gd_a = add_low(x_own(v.pop.gd_a), v.pop.gd_ax)[:, 0]
    gd_b = add_low(half(v.pop.gd_b, y, 3), v.pop.gd_by)[:, 0]
    v.gd = ordered(core, gd_a, gd_b, 0)
    partial = mm(v.pop.hidden, v.pop.wd).reshape(batch, 2, length, D)
    layer_out = (v.pop.middle + chip_sum(p, partial)).astype(LOW)
    v.out_done = layer_out
    v.dot = dots("nd,btd->bnt", v.pop.wo, v.d_a).astype(LOW)
    v = sync(v)
    layer_out = v.pop.out_done

    def backward(b, qb, old_dc, old_dw):
        att = (v.att0, v.att1)[b][1:]
        return attention_backward(
            b, qb, v.meta, v.qt, v.dot, *att, v.kxt, v.vxt, v.keys, old_dc, old_dw
        )

    v.gd = z_scatter(p, v.gd)
    v.back00 = backward(0, 0, (), ())
    go = dots("bnt,btd->nd", v.pop.out, v.pop.d_a).astype(LOW).reshape(2, 2, 128, D)
    v.go_a, v.go_b = half(go, core, 3), half(go, 1 - core, 3)
    v = sync(v)
    v.gd1, v.go_b = p.to_y(v.gd), p.to_core(v.go_b)
    v.back01 = backward(0, 1, v.back00[1:2], v.back00[2:])
    v = sync(v)
    d_keys = v.back01[1]
    v.dk0, v.dk_far0 = d_keys[:2], p.down_y(d_keys[2:].astype(LOW))
    v.gd = ordered(y, v.gd, v.pop.gd1, 1)
    v.gd1 = p.to_core(v.gd)
    plan = []
    for n, (r, k) in enumerate(RELATIVE):
        for s in range(2):
            plan += [
                lambda x, y, c, n=n, r=r, k=k, s=s: (
                    s, (slice(None), x ^ r, slice(None), lanes((y ^ k) * 256, 256)),
                    n, pl.ds(2 * (c ^ s), 2),
                )
            ]
    v.go = spread(p, placed(p, plan, (v.pop.go_a, v.pop.go_b), [(4, 128, 256)] * 4))
    v.back10 = backward(1, 0, (), v.back01[2:])
    v = sync(v)
    v.go = z_scatter(p, add_all(v.pop.go))
    v.dk0 = (v.dk0 + v.pop.dk_far0.astype(F32)).astype(LOW).reshape(1, 2 * length, LAT)
    grad_down = ordered(core, v.pop.gd, v.pop.gd1, 1).astype(F32)
    v.back11 = backward(1, 1, v.back10[1:2], v.back10[2:])
    v.down_done = grad_down
    v = sync(v)
    grad_down = v.pop.down_done

    back = [[v.pop.back00, v.pop.back01], [v.pop.back10, v.pop.back11]]
    d_keys = back[1][1][1]
    v.far1 = p.down_y(d_keys[2:].astype(LOW))
    v.dk1 = d_keys[:2]
    plan = []
    for n in range(2):
        for s in range(2):
            plan += [
                lambda x, y, c, n=n, s=s: (n, (slice(None), lanes((c ^ s) * 128, 128)), s, n)
            ]
    v.kv_mine, kv_send = placed(p, plan, back[1][1][2:], [(2, GW, 128)] * 2)
    v.kv_come = p.to_core(kv_send)
    dq_t = jnp.stack([jnp.concatenate([part[0] for part in row], 1) for row in back])
    v.gq = dots("btd,bnt->dn", v.first, dq_t).astype(LOW)
    v.d_first = dots("bnt,dn->btd", dq_t, v.wq)
    v = sync(v)
    dk1 = (v.pop.dk1 + v.pop.far1.astype(F32)).astype(LOW).reshape(1, 2 * length, LAT)
    d_latent = jnp.concatenate([v.pop.dk0, dk1])
    gl = dots("btd,btl->dl", v.pop.first, d_latent).astype(LOW).reshape(4, 2, 128, LAT)
    plan = []
    for n, (r, k) in enumerate(RELATIVE):
        full = slice(None)
        plan += [
            lambda x, y, c, n=n, r=r, k=k: (
                0, (full, x ^ r, full, lanes((y ^ k) * 256, 256)), n, (full, full, pl.ds(0, 256)),
            ),
            lambda x, y, c, n=n, r=r, k=k: (
                1, (full, x ^ r, full, lanes((y ^ k) * 128, 128)), n, (full, full, pl.ds(384, 128)),
            ),
        ]
        for s in range(2):
            plan += [
                lambda x, y, c, n=n, r=r, k=k, s=s: (
                    2 + s, (y ^ k, full, x ^ r), n, (pl.ds(2 * (c ^ s), 2), full, pl.ds(256, 128)),
                )
            ]
    kv = [part.reshape(2, 2, 2, 128, 128) for part in (v.pop.kv_mine, v.pop.kv_come)]
    parts = placed(p, plan, (v.pop.gq.reshape(4, 2, 128, GW), gl, *kv), [(4, 128, 512)] * 4)
    v.found = spread(p, parts)
    d_first = v.pop.d_first + dots("btl,dl->btd", d_latent, v.wl)
    d_first = chip_sum(p, d_first.reshape(batch, 2, length, D))
    own = tokens.astype(F32)
    inverse1 = inverse_rms(own)
    normed1 = own * inverse1
    gains = jnp.stack([jnp.sum(d_first * normed1, axis=(0, 1)), v.pop.gain2_sum])
    gains = gains.astype(LOW).reshape(16, 128)
    v.gains = spread(p, [gains] * 4)
    v.tokens_done = v.d_middle + norm_back(d_first, normed1, inverse1, v.gain1)
    v.gg = gg
    v = sync(v)
    grad_tokens = v.pop.tokens_done
    gains = sum(part.astype(F32) for part in v.pop.gains).reshape(2, 4, 2, 128)
    gains = x_own(jnp.moveaxis(gains, 0, 2).reshape(4, 2, 2, 128))[:, 0].astype(LOW)
    gains = jnp.pad(gains, ((0, 0), (0, 6), (0, 384)))
    v.q = z_scatter(p, jnp.concatenate([add_all(v.pop.found), gains], 1))
    v.gg = add_low(v.gg, p.to_y(v.gg))
    v.go1 = p.to_y(v.go)
    v = sync(v)
    v.q1 = p.to_y(v.q)
    v.gg1 = p.to_core(v.gg)
    v.go = ordered(y, v.go, v.pop.go1, 1)
    v.go1 = p.to_core(v.go)
    v = sync(v)
    q0, q1 = pick(y, v.q, v.q1), pick(y, v.pop.q1, v.pop.q)
    mine = jnp.concatenate([q0, q1], 1)
    other = p.to_core(mine)
    grad_gate = ordered(core, v.gg[:, :ff], v.gg1[:, :ff], 1).astype(F32)
    grad_up = ordered(core, v.gg[:, ff:], v.gg1[:, ff:], 1).astype(F32)
    grad_output = ordered(core, v.go, v.go1, 1).astype(F32)
    zero, one = pick(core, mine, other), pick(core, other, mine)

    def columns(start, width):
        found = [part[:128, i : i + width] for part in (zero, one) for i in (start, start + 512)]
        return jnp.concatenate(found, 1).astype(F32)

    def expand_grad(start):
        return jnp.concatenate([p_[:128, start : start + 128] for p_ in (zero, one)], 1)

    gains = mine[128:130, :128].astype(F32) + other[128:130, :128].astype(F32)
    return (
        layer_out, grad_tokens, gains[0], columns(0, 256), columns(384, 128),
        expand_grad(256).T.astype(F32), expand_grad(768).T.astype(F32), grad_output, gains[1],
        grad_gate, grad_up, grad_down,
    )


def per_device(*arguments):
    p = Place()
    return (square_layer if p.square else plain_layer)(p, *arguments)


def solution(mesh):
    rows, gain, weight, across = P("dp", "seq", None), P("dp"), P("dp", None), P(None, "dp")
    return jax.shard_map(
        per_device,
        mesh=mesh,
        in_specs=(
            rows, gain, weight, weight, across, across, weight, gain, weight, weight, weight, rows,
            P("dp", None),
        ),
        out_specs=(
            rows, rows, gain, weight, weight, across, across, weight, gain, weight, weight, weight,
        ),
        check_vma=False,
    )
```

time: 568 us -> 484 us (0.85)
  starting transfers between devices: 158 us -> 97.7 us
  waiting for transfers between devices: 193 us -> 134 us
  Pallas kernels: 48 us -> 78.2 us
  between operations: 3.18 us -> 15.8 us
    ppermute x99 -> x68, starting transfers between devices: 158 us -> 97.6 us  [send(): return lax.ppermute(value, ALL, self.pairs(move))]
    ppermute x99 -> x68, waiting for transfers between devices: 193 us -> 134 us  [send(): return lax.ppermute(value, ALL, self.pairs(move))]
    pallas_call x2 -> x12, Pallas kernels: 48 us -> 78.2 us  [the longest x4 43.7 us: attention_backward(): pl.pallas_call(lambda *refs: backward_kernel(b, qb, nkb, batch, width, bo...]
    dot_general x3 -> x2, matrix products: 16 us -> 12.8 us  [mm(): return jnp.dot(left, right, preferred_element_type=F32)]
    dot_general x3 -> x4, matrix products: 11 us -> 13.7 us  [tn(): lax.dot_general(left, right, (((0,), (0,)), ((), ())), preferred_element_...]
    convert_element_type x17 -> x18, other arithmetic: 16.1 us -> 15.3 us  [the longest x1 2.92 us: square_layer(): (v.pop.normed1 * v.gain1).astype(LOW).reshape(batch, 2 * length, D)]
    unnamed x111 -> x150, local copies, waits for them, and re-layouts: 17.1 us -> 16.4 us
    dot_general x3 -> x2, matrix products: 16 us -> 16.6 us  [nt(): lax.dot_general(left, right, (((1,), (1,)), ((), ())), preferred_element_...]
  transfers between devices with their start and end apart: 99 -> 70, of which waited for: 42 -> 28; matrix products, arithmetic and copies ran while one was open for 21% -> 20% of each run, Pallas kernels for 9% -> 16%
where the time goes in v2:
time: 484 us; the launch traced here: 479 us
  waiting for transfers between devices  134 us (28%)
  starting transfers between devices  97.7 us (20%)
  Pallas kernels  78.2 us (16%)
  matrix products  59.3 us (12%)
  other arithmetic  52.2 us (11%)
  local copies, waits for them, and re-layouts  41.1 us (8%)
  between operations  15.8 us (3%)
    ppermute x68, waiting for transfers between devices, send(): return lax.ppermute(value, ALL, self.pairs(move))  134 us
    ppermute x68, starting transfers between devices, send(): return lax.ppermute(value, ALL, self.pairs(move))  97.6 us
    pallas_call x4, Pallas kernels, attention_backward(): pl.pallas_call(lambda *refs: backward_kernel(b, qb, nkb, batch, width, bo...  43.7 us
    pallas_call x6, Pallas kernels, placed(): pl.pallas_call(lambda *refs: place_kernel(plan, len(sources), len(shapes)...  18.4 us
    dot_general x2, matrix products, nt(): lax.dot_general(left, right, (((1,), (1,)), ((), ())), preferred_element_...  16.6 us
    unnamed x150, local copies, waits for them, and re-layouts  16.4 us
    dot_general x9, matrix products, dots(): return jnp.einsum(spec, left, right, preferred_element_type=F32)  16.1 us
    pallas_call x2, Pallas kernels, attention_forward(): pl.pallas_call(lambda *refs: forward_kernel(b, nkb, batch, width, *refs),...  16.1 us
  transfers between devices with their start and end apart: 70, of which 28 were waited for; matrix products, arithmetic and copies ran while one was open for 20% of the time, Pallas kernels for 16%

profile of v2, /device:TPU:0, one launch (start us, length us, event | category | flops | bytes accessed | tf_op | source)
XLA Modules:
  0.0 478.6 jit_solution(10589453761397456522)
XLA Ops:
  11.3 3.1 collective-permute-start
  14.4 2.6 collective-permute-start.1
  22.5 8.1 %collective-permute-done.1 = bf16[136,768]{1,0:T(8,128)(2,1)S(1)} collective-permute-done((bf16[136,768]{1,0:T(8,128)(2,1)S(1)}, bf16[136,768]{1,0:T(8,128)(2,1)S(1)}, u32[]{:S(2)}, u32[]{:S(2)}) %collective-permute-start.1) | collective-permute-done | bytes 208928 | tf_op jit(solution)/shard_map/ppermute | solution.py:268
  32.7 2.3 convert_multiply_fusion
  38.1 8.7 %collective-permute-done.4.refs_2_ = bf16[4,136,384]{2,1,0:T(8,128)(2,1)S(1)} collective-permute-done((bf16[4,136,384]{2,1,0:T(8,128)(2,1)}, bf16[4,136,384]{2,1,0:T(8,128)(2,1)S(1)}, u32[]{:S(2)}, u32[]{:S(2)}) %collective-permute-start.4) | collective-permute-done | bytes 417824 | tf_op jit(solution)/shard_map/ppermute | solution.py:268
  52.7 8.0 %collective-permute-done.6.refs_4_ = bf16[4,136,384]{2,1,0:T(8,128)(2,1)} collective-permute-done((bf16[4,136,384]{2,1,0:T(8,128)(2,1)S(1)}, bf16[4,136,384]{2,1,0:T(8,128)(2,1)}, u32[]{:S(2)}, u32[]{:S(2)}) %collective-permute-start.6) | collective-permute-done | bytes 417824 | tf_op jit(solution)/shard_map/ppermute | solution.py:268
  60.7 6.7 %collective-permute-done.7.refs_3_ = bf16[4,136,384]{2,1,0:T(8,128)(2,1)} collective-permute-done((bf16[4,136,384]{2,1,0:T(8,128)(2,1)}, bf16[4,136,384]{2,1,0:T(8,128)(2,1)}, u32[]{:S(2)}, u32[]{:S(2)}) %collective-permute-start.7) | collective-permute-done | bytes 417824 | tf_op jit(solution)/shard_map/ppermute | solution.py:268
  67.4 8.0 %collective-permute-done.9.refs_8_ = bf16[4,136,384]{2,1,0:T(8,128)(2,1)} collective-permute-done((bf16[4,136,384]{2,1,0:T(8,128)(2,1)S(1)}, bf16[4,136,384]{2,1,0:T(8,128)(2,1)}, u32[]{:S(2)}, u32[]{:S(2)}) %collective-permute-start.9) | collective-permute-done | bytes 417824 | tf_op jit(solution)/shard_map/ppermute | solution.py:268
  76.2 3.5 place.6
  79.7 2.9 multiply_convert_fusion.2
  85.5 2.1 collective-permute-start.13
  91.8 6.8 %collective-permute-done.13 = bf16[352,256]{1,0:T(8,128)(2,1)S(1)} collective-permute-done((bf16[352,256]{1,0:T(8,128)(2,1)S(1)}, bf16[352,256]{1,0:T(8,128)(2,1)S(1)}, u32[]{:S(2)}, u32[]{:S(2)}) %collective-permute-start.13) | collective-permute-done | bytes 180256 | tf_op jit(solution)/shard_map/ppermute | solution.py:268
  98.6 4.0 collective-permute-start.10
  102.6 3.9 fusion.17.refs_1_
  106.5 5.4 %collective-permute-done.14 = bf16[352,256]{1,0:T(8,128)(2,1)S(1)} collective-permute-done((bf16[352,256]{1,0:T(8,128)(2,1)S(1)}, bf16[352,256]{1,0:T(8,128)(2,1)S(1)}, u32[]{:S(2)}, u32[]{:S(2)}) %collective-permute-start.14) | collective-permute-done | bytes 180256 | tf_op jit(solution)/shard_map/ppermute | solution.py:268
  114.9 3.5 place.7
  124.8 8.3 %attention_forward.2 = (bf16[1,512,512]{2,1,0:T(8,128)(2,1)}, f32[1,512,512]{2,1,0:T(8,128)}, bf16[2,256,2048]{2,1,0:T(8,128)(2,1)}, f32[2,1,2048]{2,1,0:T(1,128)}) custom-call(s32[9]{0:T(128)} %concatenate.99.refs_0_, bf16[2,512,512]{2,1,0:T(8,128)(2,1)} %fusion.17.refs_1_, bf16[512,256]{1,0:T(8,128)(2,1)} %bitcast.253, bf16[512,256]{1,0:T(8,128)(2,1)} %bitcast.247, ...), custom_call_target="tpu_custom_call" | custom-call | flops 3758096384 | bytes 8388608 | tf_op jit(solution)/shard_map/attention_forward/pallas_call | solution.py:156
  133.3 4.8 collective-permute-start.20
  142.7 7.8 %attention_forward.3 = (bf16[1,512,512]{2,1,0:T(8,128)(2,1)}, f32[1,512,512]{2,1,0:T(8,128)}, bf16[2,256,2048]{2,1,0:T(8,128)(2,1)}, f32[2,1,2048]{2,1,0:T(1,128)}) custom-call(s32[9]{0:T(128)} %concatenate.99.refs_0_, bf16[2,512,512]{2,1,0:T(8,128)(2,1)} %fusion.17.refs_1_, bf16[512,256]{1,0:T(8,128)(2,1)} %bitcast.254, bf16[512,256]{1,0:T(8,128)(2,1)} %bitcast.248, ...), custom_call_target="tpu_custom_call" | custom-call | flops 3758096384 | bytes 8388608 | tf_op jit(solution)/shard_map/attention_forward/pallas_call | solution.py:156
  150.5 3.4 collective-permute-done.19
  157.8 2.0 copy-done.6
  162.8 2.5 multiply_reduce_fusion.2
  172.5 3.8 place.8
  176.2 9.4 %fusion.64 = f32[1024,2816]{1,0:T(8,128)S(1)} fusion(bf16[1024,1024]{1,0:T(8,128)(2,1)} %bitcast.217, bf16[1024,2816]{1,0:T(8,128)(2,1)} %all-gather.2.cloned.1.call-done), kind=kOutput, calls=%fused_computation.209 | convolution fusion | flops 5905580032 | bytes 19398656 | tf_op jit(solution)/shard_map/dot_general | solution.py:27
  185.6 2.0 fusion
  195.2 6.3 %multiply_convert_fusion.1 = (bf16[1024,1408]{1,0:T(8,128)(2,1)S(1)}, bf16[1024,1408]{1,0:T(8,128)(2,1)}) fusion(f32[1024,2816]{1,0:T(8,128)S(1)} %fusion.64, bf16[1024,1024]{1,0:T(8,128)(2,1)S(1)} %bitcast.206, bf16[1408,1024]{1,0:T(8,128)(2,1)S(1)} %bitcast.213), kind=kOutput, calls=%fused_computation.4 | convolution fusion | flops 2971533312 | bytes 22282240 | tf_op jit(solution)/shard_map/dot_general | solution.py:35
  201.5 2.2 pad_maximum_fusion
  206.1 2.6 copy.57
  209.5 8.3 %convolution_convert_fusion = bf16[1024,2816]{1,0:T(8,128)(2,1)} fusion(bf16[1024,1024]{1,0:T(8,128)(2,1)S(1)} %bitcast.218, bf16[1024,2816]{1,0:T(8,128)(2,1)S(1)} %pad_maximum_fusion), kind=kOutput, calls=%fused_computation.6 | convolution fusion | flops 5908463616 | bytes 13631488 | tf_op jit(solution)/shard_map/dot_general | solution.py:31
  217.9 6.7 %collective-permute-done.31 = bf16[2,1,352,512]{3,2,0,1:T(8,128)(2,1)} collective-permute-done((bf16[2,1,352,512]{3,2,0,1:T(8,128)(2,1)}, bf16[2,1,352,512]{3,2,0,1:T(8,128)(2,1)}, u32[]{:S(2)}, u32[]{:S(2)}) %collective-permute-start.31) | collective-permute-done | bytes 720928 | tf_op jit(solution)/shard_map/ppermute | solution.py:268
  224.5 2.7 collective-permute-done.30
  227.2 10.3 %fusion.65 = f32[1024,1024]{1,0:T(8,128)S(1)} fusion(bf16[1024,2816]{1,0:T(8,128)(2,1)} %copy-done.13, bf16[1024,2816]{1,0:T(8,128)(2,1)} %all-gather.2.cloned.1.call-done), kind=kOutput, calls=%fused_computation.210 | convolution fusion | flops 5905580032 | bytes 15728640 | tf_op jit(solution)/shard_map/dot_general | solution.py:35
  237.5 2.0 copy-done.11
  248.1 2.8 multiply_reduce_fusion
  251.5 2.0 multiply_add_fusion
  254.1 3.9 collective-permute-done.33
  258.2 3.4 fusion.66
  266.9 2.3 fusion.18.refs_2_
  270.8 14.3 %collective-permute-start.37 = (bf16[1,352,256]{2,1,0:T(8,128)(2,1)S(1)}, bf16[1,352,256]{2,1,0:T(8,128)(2,1)S(1)}, u32[]{:S(2)}, u32[]{:S(2)}) collective-permute-start(bf16[1,352,256]{2,1,0:T(8,128)(2,1)S(1)} %get-tuple-element.985), channel_id=1, source_target_pairs={{0,2},{1,3},{2,4},{3,5},{4,6},{5,7},{6,0},{7,1},{8,10},{9,11},{10,... | collective-permute-start | bytes 540680 | tf_op jit(solution)/shard_map/ppermute | solution.py:268
  287.5 8.9 %attention_backward.4 = (bf16[512,256]{1,0:T(8,128)(2,1)}, f32[4,256,256]{2,1,0:T(8,128)}, f32[512,256]{1,0:T(8,128)}, f32[512,256]{1,0:T(8,128)}) custom-call(s32[9]{0:T(128)} %concatenate.99.refs_0_, bf16[2,512,512]{2,1,0:T(8,128)(2,1)} %fusion.17.refs_1_, bf16[2,512,512]{2,1,0:T(8,128)(2,1)} %fusion.18.refs_2_, ...), custom_call_target="tpu_custom_call" | custom-call | flops 5368709120 | bytes 6291456 | tf_op jit(solution)/shard_map/attention_backward/pallas_call | solution.py:200
  298.7 10.4 %collective-permute-done.38 = bf16[1,352,256]{2,1,0:T(8,128)(2,1)S(1)} collective-permute-done((bf16[1,352,256]{2,1,0:T(8,128)(2,1)S(1)}, bf16[1,352,256]{2,1,0:T(8,128)(2,1)S(1)}, u32[]{:S(2)}, u32[]{:S(2)}) %collective-permute-start.38) | collective-permute-done | bytes 180256 | tf_op jit(solution)/shard_map/ppermute | solution.py:268
  310.8 12.8 %attention_backward.5 = (bf16[512,256]{1,0:T(8,128)(2,1)}, f32[4,256,256]{2,1,0:T(8,128)}, f32[512,256]{1,0:T(8,128)}, f32[512,256]{1,0:T(8,128)}) custom-call(s32[9]{0:T(128)} %concatenate.99.refs_0_, bf16[2,512,512]{2,1,0:T(8,128)(2,1)} %fusion.17.refs_1_, bf16[2,512,512]{2,1,0:T(8,128)(2,1)} %fusion.18.refs_2_, ...), custom_call_target="tpu_custom_call" | custom-call | flops 5368709120 | bytes 6291456 | tf_op jit(solution)/shard_map/attention_backward/pallas_call | solution.py:200
  325.9 2.3 place.9
  329.4 6.3 %collective-permute-start.45 = (bf16[4,128,256]{2,1,0:T(8,128)(2,1)}, bf16[4,128,256]{2,1,0:T(8,128)(2,1)S(1)}, u32[]{:S(2)}, u32[]{:S(2)}) collective-permute-start(bf16[4,128,256]{2,1,0:T(8,128)(2,1)} %get-tuple-element.844), channel_id=1, source_target_pairs={{0,16},{1,17},{2,18},{3,19},{4,20},{5,21},{6,22},{7,23},{8,24},{9,... | collective-permute-start | bytes 786440 | tf_op jit(solution)/shard_map/ppermute | solution.py:268
  338.6 9.3 %attention_backward.6 = (bf16[512,256]{1,0:T(8,128)(2,1)}, f32[4,256,256]{2,1,0:T(8,128)}, f32[512,256]{1,0:T(8,128)}, f32[512,256]{1,0:T(8,128)}) custom-call(s32[9]{0:T(128)} %concatenate.99.refs_0_, bf16[2,512,512]{2,1,0:T(8,128)(2,1)} %fusion.17.refs_1_, bf16[2,512,512]{2,1,0:T(8,128)(2,1)} %fusion.18.refs_2_, ...), custom_call_target="tpu_custom_call" | custom-call | flops 5368709120 | bytes 6291456 | tf_op jit(solution)/shard_map/attention_backward/pallas_call | solution.py:200
  347.9 7.4 %collective-permute-done.46 = bf16[4,128,256]{2,1,0:T(8,128)(2,1)S(1)} collective-permute-done((bf16[4,128,256]{2,1,0:T(8,128)(2,1)}, bf16[4,128,256]{2,1,0:T(8,128)(2,1)S(1)}, u32[]{:S(2)}, u32[]{:S(2)}) %collective-permute-start.46) | collective-permute-done | bytes 262176 | tf_op jit(solution)/shard_map/ppermute | solution.py:268
  355.4 9.7 %collective-permute-start.47 = (bf16[1,128,256]{2,1,0:T(8,128)(2,1)S(1)}, bf16[1,128,256]{2,1,0:T(8,128)(2,1)S(1)}, u32[]{:S(2)}, u32[]{:S(2)}) collective-permute-start(bf16[1,128,256]{2,1,0:T(8,128)(2,1)S(1)} %get-tuple-element.1025), channel_id=1, source_target_pairs={{0,2},{1,3},{2,4},{3,5},{4,6},{5,7},{6,0},{7,1},{8,10},{9,11},{10,... | collective-permute-start | bytes 196616 | tf_op jit(solution)/shard_map/ppermute | solution.py:268
  365.4 2.8 collective-permute-start.49
  368.3 12.8 %attention_backward.7 = (bf16[512,256]{1,0:T(8,128)(2,1)}, f32[4,256,256]{2,1,0:T(8,128)}, f32[512,256]{1,0:T(8,128)}, f32[512,256]{1,0:T(8,128)}) custom-call(s32[9]{0:T(128)} %concatenate.99.refs_0_, bf16[2,512,512]{2,1,0:T(8,128)(2,1)} %fusion.17.refs_1_, bf16[2,512,512]{2,1,0:T(8,128)(2,1)} %fusion.18.refs_2_, ...), custom_call_target="tpu_custom_call" | custom-call | flops 5368709120 | bytes 6291456 | tf_op jit(solution)/shard_map/attention_backward/pallas_call | solution.py:200
  382.6 2.2 place.10
  388.1 2.3 bitcast_convert_fusion
  390.5 10.5 %collective-permute-done.50 = bf16[2,256,256]{2,1,0:T(8,128)(2,1)S(1)} collective-permute-done((bf16[2,256,256]{2,1,0:T(8,128)(2,1)S(1)}, bf16[2,256,256]{2,1,0:T(8,128)(2,1)S(1)}, u32[]{:S(2)}, u32[]{:S(2)}) %collective-permute-start.50) | collective-permute-done | bytes 262176 | tf_op jit(solution)/shard_map/ppermute | solution.py:268
  405.7 3.1 place.11
  408.8 4.2 collective-permute-start.52
  414.5 2.0 fusion.6
  416.6 2.1 collective-permute-start.56
  418.7 7.5 %collective-permute-done.52 = bf16[4,128,512]{2,1,0:T(8,128)(2,1)} collective-permute-done((bf16[4,128,512]{2,1,0:T(8,128)(2,1)}, bf16[4,128,512]{2,1,0:T(8,128)(2,1)}, u32[]{:S(2)}, u32[]{:S(2)}) %collective-permute-start.52) | collective-permute-done | bytes 524320 | tf_op jit(solution)/shard_map/ppermute | solution.py:268
  427.0 3.9 fusion.9
  430.9 7.8 %collective-permute-done.53 = bf16[4,128,512]{2,1,0:T(8,128)(2,1)} collective-permute-done((bf16[4,128,512]{2,1,0:T(8,128)(2,1)}, bf16[4,128,512]{2,1,0:T(8,128)(2,1)}, u32[]{:S(2)}, u32[]{:S(2)}) %collective-permute-start.53) | collective-permute-done | bytes 524320 | tf_op jit(solution)/shard_map/ppermute | solution.py:268
  442.3 2.7 collective-permute-start.63
  446.7 2.9 collective-permute-done.61
  449.6 4.4 collective-permute-done.62
  454.1 3.1 collective-permute-done.59
  460.3 3.7 collective-permute-done.66
  (383 shorter events, 124.8 us)
Async XLA Ops:
  7.2 169.0 %all-gather.2.cloned.1.call-start = ((), (), s32[]{:S(2)}) async-start(), calls=%async_computation.1 | async-start | bytes 6488064 | tf_op jit(solution)/shard_map/all_gather | solution.py:585
  11.3 11.2 %collective-permute-start = (bf16[136,768]{1,0:T(8,128)(2,1)S(1)}, bf16[136,768]{1,0:T(8,128)(2,1)S(1)}, u32[]{:S(2)}, u32[]{:S(2)}) collective-permute-start(bf16[136,768]{1,0:T(8,128)(2,1)S(1)} %fusion.41), channel_id=1, source_target_pairs={{0,2},{1,3},{2,4},{3,5},{4,6},{5,7},{6,0},{7,1},{8,10},{9,11},{10,... | collective-permute-start | bytes 626696 | tf_op jit(solution)/shard_map/ppermute | solution.py:268
  14.4 16.3 %collective-permute-start.1 = (bf16[136,768]{1,0:T(8,128)(2,1)S(1)}, bf16[136,768]{1,0:T(8,128)(2,1)S(1)}, u32[]{:S(2)}, u32[]{:S(2)}) collective-permute-start(bf16[136,768]{1,0:T(8,128)(2,1)S(1)} %fusion.41), channel_id=1, source_target_pairs={{0,4},{1,5},{2,6},{3,7},{4,0},{5,1},{6,2},{7,3},{8,12},{9,13},{10,... | collective-permute-start | bytes 626696 | tf_op jit(solution)/shard_map/ppermute | solution.py:268
  17.0 13.7 %collective-permute-start.2 = (bf16[136,768]{1,0:T(8,128)(2,1)S(1)}, bf16[136,768]{1,0:T(8,128)(2,1)S(1)}, u32[]{:S(2)}, u32[]{:S(2)}) collective-permute-start(bf16[136,768]{1,0:T(8,128)(2,1)S(1)} %fusion.41), channel_id=1, source_target_pairs={{0,6},{1,7},{2,0},{3,1},{4,2},{5,3},{6,4},{7,5},{8,14},{9,15},{10,... | collective-permute-start | bytes 626696 | tf_op jit(solution)/shard_map/ppermute | solution.py:268
  18.3 13.8 %collective-permute-start.3 = (bf16[2,256,1024]{2,1,0:T(8,128)(2,1)}, bf16[2,256,1024]{2,1,0:T(8,128)(2,1)S(1)}, u32[]{:S(2)}, u32[]{:S(2)}) collective-permute-start(bf16[2,256,1024]{2,1,0:T(8,128)(2,1)} %param.13), channel_id=1, source_target_pairs={{0,8},{1,9},{2,10},{3,11},{4,12},{5,13},{6,14},{7,15},{8,0},{9,1},... | collective-permute-start | bytes 3145736 | tf_op jit(solution)/shard_map/ppermute | solution.py:268
  35.0 403.8 %reduce-scatter.2.cloned.1.call-start = ((), (), s32[]{:S(2)}) async-start(), calls=%async_computation.2 | async-start | bytes 6488064 | tf_op jit(solution)/shard_map/reduce_scatter | solution.py:708
  35.1 11.7 %collective-permute-start.4 = (bf16[4,136,384]{2,1,0:T(8,128)(2,1)}, bf16[4,136,384]{2,1,0:T(8,128)(2,1)S(1)}, u32[]{:S(2)}, u32[]{:S(2)}) collective-permute-start(bf16[4,136,384]{2,1,0:T(8,128)(2,1)} %get-tuple-element.505.refs_1_), channel_id=1, source_target_pairs={{0,1},{1,0},{2,3},{3,2},{4,5},{5,4},{6,7},{7,6},{8,9},{9,8},{10,11... | collective-permute-start | bytes 1253384 | tf_op jit(solution)/shard_map/ppermute | solution.py:268
  36.6 11.4 %collective-permute-start.5 = (bf16[4,136,384]{2,1,0:T(8,128)(2,1)}, bf16[4,136,384]{2,1,0:T(8,128)(2,1)S(1)}, u32[]{:S(2)}, u32[]{:S(2)}) collective-permute-start(bf16[4,136,384]{2,1,0:T(8,128)(2,1)} %get-tuple-element.509.refs_5_), channel_id=1, source_target_pairs={{0,16},{1,17},{2,18},{3,19},{4,20},{5,21},{6,22},{7,23},{8,24},{9,... | collective-permute-start | bytes 1253384 | tf_op jit(solution)/shard_map/ppermute | solution.py:268
  48.0 12.7 %collective-permute-start.6 = (bf16[4,136,384]{2,1,0:T(8,128)(2,1)S(1)}, bf16[4,136,384]{2,1,0:T(8,128)(2,1)}, u32[]{:S(2)}, u32[]{:S(2)}) collective-permute-start(bf16[4,136,384]{2,1,0:T(8,128)(2,1)S(1)} %collective-permute-done.4.refs_2_), channel_id=1, source_target_pairs={{0,16},{1,17},{2,18},{3,19},{4,20},{5,21},{6,22},{7,23},{8,24},{9,... | collective-permute-start | bytes 1253384 | tf_op jit(solution)/shard_map/ppermute | solution.py:268
  49.5 17.8 %collective-permute-start.7 = (bf16[4,136,384]{2,1,0:T(8,128)(2,1)}, bf16[4,136,384]{2,1,0:T(8,128)(2,1)}, u32[]{:S(2)}, u32[]{:S(2)}) collective-permute-start(bf16[4,136,384]{2,1,0:T(8,128)(2,1)} %get-tuple-element.505.refs_1_), channel_id=1, source_target_pairs={{0,16},{1,17},{2,18},{3,19},{4,20},{5,21},{6,22},{7,23},{8,24},{9,... | collective-permute-start | bytes 1253384 | tf_op jit(solution)/shard_map/ppermute | solution.py:268
  50.0 17.4 %collective-permute-start.8 = (bf16[4,136,384]{2,1,0:T(8,128)(2,1)}, bf16[4,136,384]{2,1,0:T(8,128)(2,1)}, u32[]{:S(2)}, u32[]{:S(2)}) collective-permute-start(bf16[4,136,384]{2,1,0:T(8,128)(2,1)} %get-tuple-element.509.refs_5_), channel_id=1, source_target_pairs={{0,1},{1,0},{2,3},{3,2},{4,5},{5,4},{6,7},{7,6},{8,9},{9,8},{10,11... | collective-permute-start | bytes 1253384 | tf_op jit(solution)/shard_map/ppermute | solution.py:268
  50.6 24.8 %collective-permute-start.9 = (bf16[4,136,384]{2,1,0:T(8,128)(2,1)S(1)}, bf16[4,136,384]{2,1,0:T(8,128)(2,1)}, u32[]{:S(2)}, u32[]{:S(2)}) collective-permute-start(bf16[4,136,384]{2,1,0:T(8,128)(2,1)S(1)} %collective-permute-done.5.refs_7_), channel_id=1, source_target_pairs={{0,1},{1,0},{2,3},{3,2},{4,5},{5,4},{6,7},{7,6},{8,9},{9,8},{10,11... | collective-permute-start | bytes 1253384 | tf_op jit(solution)/shard_map/ppermute | solution.py:268
  52.1 71.3 %collective-permute-start.16 = (bf16[2,256,1024]{2,1,0:T(8,128)(2,1)S(1)}, bf16[2,256,1024]{2,1,0:T(8,128)(2,1)}, u32[]{:S(2)}, u32[]{:S(2)}) collective-permute-start(bf16[2,256,1024]{2,1,0:T(8,128)(2,1)S(1)} %copy-done.14), channel_id=1, source_target_pairs={{0,8},{1,9},{2,10},{3,11},{4,12},{5,13},{6,14},{7,15},{8,0},{9,1},... | collective-permute-start | bytes 3145736 | tf_op jit(solution)/shard_map/ppermute | solution.py:268
  85.5 13.0 %collective-permute-start.13 = (bf16[352,256]{1,0:T(8,128)(2,1)S(1)}, bf16[352,256]{1,0:T(8,128)(2,1)S(1)}, u32[]{:S(2)}, u32[]{:S(2)}) collective-permute-start(bf16[352,256]{1,0:T(8,128)(2,1)S(1)} %copy-done.39), channel_id=1, source_target_pairs={{0,2},{1,3},{2,4},{3,5},{4,6},{5,7},{6,0},{7,1},{8,10},{9,11},{10,... | collective-permute-start | bytes 540680 | tf_op jit(solution)/shard_map/ppermute | solution.py:268
  88.4 23.4 %collective-permute-start.14 = (bf16[352,256]{1,0:T(8,128)(2,1)S(1)}, bf16[352,256]{1,0:T(8,128)(2,1)S(1)}, u32[]{:S(2)}, u32[]{:S(2)}) collective-permute-start(bf16[352,256]{1,0:T(8,128)(2,1)S(1)} %copy-done.39), channel_id=1, source_target_pairs={{0,4},{1,5},{2,6},{3,7},{4,0},{5,1},{6,2},{7,3},{8,12},{9,13},{10,... | collective-permute-start | bytes 540680 | tf_op jit(solution)/shard_map/ppermute | solution.py:268
  90.3 21.6 %collective-permute-start.15 = (bf16[352,256]{1,0:T(8,128)(2,1)S(1)}, bf16[352,256]{1,0:T(8,128)(2,1)S(1)}, u32[]{:S(2)}, u32[]{:S(2)}) collective-permute-start(bf16[352,256]{1,0:T(8,128)(2,1)S(1)} %copy-done.39), channel_id=1, source_target_pairs={{0,6},{1,7},{2,0},{3,1},{4,2},{5,3},{6,4},{7,5},{8,14},{9,15},{10,... | collective-permute-start | bytes 540680 | tf_op jit(solution)/shard_map/ppermute | solution.py:268
  91.8 21.7 %collective-permute-start.11 = (bf16[4,2,128,256]{3,2,1,0:T(8,128)(2,1)}, bf16[4,2,128,256]{3,2,1,0:T(8,128)(2,1)S(1)}, u32[]{:S(2)}, u32[]{:S(2)}) collective-permute-start(bf16[4,2,128,256]{3,2,1,0:T(8,128)(2,1)} %get-tuple-element.513), channel_id=1, source_target_pairs={{0,8},{1,9},{2,10},{3,11},{4,12},{5,13},{6,14},{7,15},{8,0},{9,1},... | collective-permute-start | bytes 1572872 | tf_op jit(solution)/shard_map/ppermute | solution.py:268
  98.6 19.8 %collective-permute-start.10 = (bf16[2,2,256,256]{3,2,1,0:T(8,128)(2,1)}, bf16[2,2,256,256]{3,2,1,0:T(8,128)(2,1)S(1)}, u32[]{:S(2)}, u32[]{:S(2)}) collective-permute-start(bf16[2,2,256,256]{3,2,1,0:T(8,128)(2,1)} %bitcast.243), channel_id=1, source_target_pairs={{0,16},{1,17},{2,18},{3,19},{4,20},{5,21},{6,22},{7,23},{8,24},{9,... | collective-permute-start | bytes 1572872 | tf_op jit(solution)/shard_map/ppermute | solution.py:268
  120.4 12.8 %collective-permute-start.17 = (bf16[2,352,256]{2,1,0:T(8,128)(2,1)S(1)}, bf16[2,352,256]{2,1,0:T(8,128)(2,1)S(1)}, u32[]{:S(2)}, u32[]{:S(2)}) collective-permute-start(bf16[2,352,256]{2,1,0:T(8,128)(2,1)S(1)} %get-tuple-element.999), channel_id=1, source_target_pairs={{0,1},{1,0},{2,3},{3,2},{4,5},{5,4},{6,7},{7,6},{8,9},{9,8},{10,11... | collective-permute-start | bytes 1081352 | tf_op jit(solution)/shard_map/ppermute | solution.py:268
  121.9 11.2 %collective-permute-start.18 = (bf16[2,352,256]{2,1,0:T(8,128)(2,1)S(1)}, bf16[2,352,256]{2,1,0:T(8,128)(2,1)S(1)}, u32[]{:S(2)}, u32[]{:S(2)}) collective-permute-start(bf16[2,352,256]{2,1,0:T(8,128)(2,1)S(1)} %get-tuple-element.998), channel_id=1, source_target_pairs={{0,16},{1,17},{2,18},{3,19},{4,20},{5,21},{6,22},{7,23},{8,24},{9,... | collective-permute-start | bytes 1081352 | tf_op jit(solution)/shard_map/ppermute | solution.py:268
  133.3 17.2 %collective-permute-start.20 = (bf16[2,352,256]{2,1,0:T(8,128)(2,1)S(1)}, bf16[2,352,256]{2,1,0:T(8,128)(2,1)S(1)}, u32[]{:S(2)}, u32[]{:S(2)}) collective-permute-start(bf16[2,352,256]{2,1,0:T(8,128)(2,1)S(1)} %get-tuple-element.997), channel_id=1, source_target_pairs={{0,16},{1,17},{2,18},{3,19},{4,20},{5,21},{6,22},{7,23},{8,24},{9,... | collective-permute-start | bytes 1081352 | tf_op jit(solution)/shard_map/ppermute | solution.py:268
  138.0 12.5 %collective-permute-start.21 = (bf16[2,352,256]{2,1,0:T(8,128)(2,1)S(1)}, bf16[2,352,256]{2,1,0:T(8,128)(2,1)S(1)}, u32[]{:S(2)}, u32[]{:S(2)}) collective-permute-start(bf16[2,352,256]{2,1,0:T(8,128)(2,1)S(1)} %get-tuple-element.996), channel_id=1, source_target_pairs={{0,1},{1,0},{2,3},{3,2},{4,5},{5,4},{6,7},{7,6},{8,9},{9,8},{10,11... | collective-permute-start | bytes 1081352 | tf_op jit(solution)/shard_map/ppermute | solution.py:268
  138.0 15.9 %collective-permute-start.19 = (bf16[2,352,256]{2,1,0:T(8,128)(2,1)S(1)}, bf16[2,352,256]{2,1,0:T(8,128)(2,1)S(1)}, u32[]{:S(2)}, u32[]{:S(2)}) collective-permute-start(bf16[2,352,256]{2,1,0:T(8,128)(2,1)S(1)} %collective-permute-done.17), channel_id=1, source_target_pairs={{0,16},{1,17},{2,18},{3,19},{4,20},{5,21},{6,22},{7,23},{8,24},{9,... | collective-permute-start | bytes 1081352 | tf_op jit(solution)/shard_map/ppermute | solution.py:268
  138.2 17.2 %collective-permute-start.22 = (bf16[2,352,256]{2,1,0:T(8,128)(2,1)S(1)}, bf16[2,352,256]{2,1,0:T(8,128)(2,1)S(1)}, u32[]{:S(2)}, u32[]{:S(2)}) collective-permute-start(bf16[2,352,256]{2,1,0:T(8,128)(2,1)S(1)} %collective-permute-done.18), channel_id=1, source_target_pairs={{0,1},{1,0},{2,3},{3,2},{4,5},{5,4},{6,7},{7,6},{8,9},{9,8},{10,11... | collective-permute-start | bytes 1081352 | tf_op jit(solution)/shard_map/ppermute | solution.py:268
  160.9 10.5 %collective-permute-start.26 = (bf16[2,352,256]{2,1,0:T(8,128)(2,1)S(1)}, bf16[2,352,256]{2,1,0:T(8,128)(2,1)S(1)}, u32[]{:S(2)}, u32[]{:S(2)}) collective-permute-start(bf16[2,352,256]{2,1,0:T(8,128)(2,1)S(1)} %get-tuple-element.988), channel_id=1, source_target_pairs={{0,8},{1,9},{2,10},{3,11},{4,12},{5,13},{6,14},{7,15},{8,0},{9,1},... | collective-permute-start | bytes 1081352 | tf_op jit(solution)/shard_map/ppermute | solution.py:268
  165.7 4.1 collective-permute-start.28
  167.3 4.1 collective-permute-start.25
  194.3 9.5 %collective-permute-start.29 = (bf16[2,2,352,512]{3,2,0,1:T(8,128)(2,1)}, bf16[2,2,352,512]{3,2,0,1:T(8,128)(2,1)S(1)}, u32[]{:S(2)}, u32[]{:S(2)}) collective-permute-start(bf16[2,2,352,512]{3,2,0,1:T(8,128)(2,1)} %copy.56), channel_id=1, source_target_pairs={{0,8},{1,9},{2,10},{3,11},{4,12},{5,13},{6,14},{7,15},{8,0},{9,1},... | collective-permute-start | bytes 4325384 | tf_op jit(solution)/shard_map/ppermute | solution.py:268
  205.8 18.7 %collective-permute-start.31 = (bf16[2,1,352,512]{3,2,0,1:T(8,128)(2,1)}, bf16[2,1,352,512]{3,2,0,1:T(8,128)(2,1)}, u32[]{:S(2)}, u32[]{:S(2)}) collective-permute-start(bf16[2,1,352,512]{3,2,0,1:T(8,128)(2,1)} %constant_dynamic-slice_fusion.15), channel_id=1, source_target_pairs={{0,1},{1,0},{2,3},{3,2},{4,5},{5,4},{6,7},{7,6},{8,9},{9,8},{10,11... | collective-permute-start | bytes 2162696 | tf_op jit(solution)/shard_map/ppermute | solution.py:268
  208.7 18.6 %collective-permute-start.30 = (bf16[2,2,352,256]{3,2,0,1:T(8,128)(2,1)}, bf16[2,2,352,256]{3,2,0,1:T(8,128)(2,1)}, u32[]{:S(2)}, u32[]{:S(2)}) collective-permute-start(bf16[2,2,352,256]{3,2,0,1:T(8,128)(2,1)} %copy.57), channel_id=1, source_target_pairs={{0,16},{1,17},{2,18},{3,19},{4,20},{5,21},{6,22},{7,23},{8,24},{9,... | collective-permute-start | bytes 2162696 | tf_op jit(solution)/shard_map/ppermute | solution.py:268
  240.6 7.5 %collective-permute-start.32 = (bf16[2,256,1024]{2,1,0:T(8,128)(2,1)}, bf16[2,256,1024]{2,1,0:T(8,128)(2,1)}, u32[]{:S(2)}, u32[]{:S(2)}) collective-permute-start(bf16[2,256,1024]{2,1,0:T(8,128)(2,1)} %fusion.22), channel_id=1, source_target_pairs={{0,8},{1,9},{2,10},{3,11},{4,12},{5,13},{6,14},{7,15},{8,0},{9,1},... | collective-permute-start | bytes 3145736 | tf_op jit(solution)/shard_map/ppermute | solution.py:268
  243.1 11.0 %collective-permute-start.34 = (bf16[2,1,352,256]{3,2,0,1:T(8,128)(2,1)S(1)}, bf16[2,1,352,256]{3,2,0,1:T(8,128)(2,1)}, u32[]{:S(2)}, u32[]{:S(2)}) collective-permute-start(bf16[2,1,352,256]{3,2,0,1:T(8,128)(2,1)S(1)} %constant_dynamic-slice_fusion.13), channel_id=1, source_target_pairs={{0,16},{1,17},{2,18},{3,19},{4,20},{5,21},{6,22},{7,23},{8,24},{9,... | collective-permute-start | bytes 1081352 | tf_op jit(solution)/shard_map/ppermute | solution.py:268
  247.1 10.9 %collective-permute-start.33 = (bf16[2,1,352,256]{3,2,0,1:T(8,128)(2,1)}, bf16[2,1,352,256]{3,2,0,1:T(8,128)(2,1)}, u32[]{:S(2)}, u32[]{:S(2)}) collective-permute-start(bf16[2,1,352,256]{3,2,0,1:T(8,128)(2,1)} %constant_dynamic-slice_fusion.14), channel_id=1, source_target_pairs={{0,1},{1,0},{2,3},{3,2},{4,5},{5,4},{6,7},{7,6},{8,9},{9,8},{10,11... | collective-permute-start | bytes 1081352 | tf_op jit(solution)/shard_map/ppermute | solution.py:268
  258.1 7.1 %collective-permute-start.35 = (bf16[2,256,1024]{2,1,0:T(8,128)(2,1)S(1)}, bf16[2,256,1024]{2,1,0:T(8,128)(2,1)S(1)}, u32[]{:S(2)}, u32[]{:S(2)}) collective-permute-start(bf16[2,256,1024]{2,1,0:T(8,128)(2,1)S(1)} %convert_element_type.350), channel_id=1, source_target_pairs={{0,8},{1,9},{2,10},{3,11},{4,12},{5,13},{6,14},{7,15},{8,0},{9,1},... | collective-permute-start | bytes 3145736 | tf_op jit(solution)/shard_map/ppermute | solution.py:268
  261.8 7.3 %collective-permute-start.36 = (bf16[2,256,1024]{2,1,0:T(8,128)(2,1)S(1)}, bf16[2,256,1024]{2,1,0:T(8,128)(2,1)S(1)}, u32[]{:S(2)}, u32[]{:S(2)}) collective-permute-start(bf16[2,256,1024]{2,1,0:T(8,128)(2,1)S(1)} %fusion.23), channel_id=1, source_target_pairs={{0,8},{1,9},{2,10},{3,11},{4,12},{5,13},{6,14},{7,15},{8,0},{9,1},... | collective-permute-start | bytes 3145736 | tf_op jit(solution)/shard_map/ppermute | solution.py:268
  270.8 27.9 %collective-permute-start.37 = (bf16[1,352,256]{2,1,0:T(8,128)(2,1)S(1)}, bf16[1,352,256]{2,1,0:T(8,128)(2,1)S(1)}, u32[]{:S(2)}, u32[]{:S(2)}) collective-permute-start(bf16[1,352,256]{2,1,0:T(8,128)(2,1)S(1)} %get-tuple-element.985), channel_id=1, source_target_pairs={{0,2},{1,3},{2,4},{3,5},{4,6},{5,7},{6,0},{7,1},{8,10},{9,11},{10,... | collective-permute-start | bytes 540680 | tf_op jit(solution)/shard_map/ppermute | solution.py:268
  285.1 24.0 %collective-permute-start.38 = (bf16[1,352,256]{2,1,0:T(8,128)(2,1)S(1)}, bf16[1,352,256]{2,1,0:T(8,128)(2,1)S(1)}, u32[]{:S(2)}, u32[]{:S(2)}) collective-permute-start(bf16[1,352,256]{2,1,0:T(8,128)(2,1)S(1)} %get-tuple-element.987), channel_id=1, source_target_pairs={{0,4},{1,5},{2,6},{3,7},{4,0},{5,1},{6,2},{7,3},{8,12},{9,13},{10,... | collective-permute-start | bytes 540680 | tf_op jit(solution)/shard_map/ppermute | solution.py:268
  287.1 22.0 %collective-permute-start.39 = (bf16[1,352,256]{2,1,0:T(8,128)(2,1)S(1)}, bf16[1,352,256]{2,1,0:T(8,128)(2,1)S(1)}, u32[]{:S(2)}, u32[]{:S(2)}) collective-permute-start(bf16[1,352,256]{2,1,0:T(8,128)(2,1)S(1)} %get-tuple-element.986), channel_id=1, source_target_pairs={{0,6},{1,7},{2,0},{3,1},{4,2},{5,3},{6,4},{7,5},{8,14},{9,15},{10,... | collective-permute-start | bytes 540680 | tf_op jit(solution)/shard_map/ppermute | solution.py:268
  309.2 14.4 %collective-permute-start.41 = (bf16[2,2,128,512]{3,2,1,0:T(8,128)(2,1)S(1)}, bf16[2,2,128,512]{3,2,1,0:T(8,128)(2,1)S(1)}, u32[]{:S(2)}, u32[]{:S(2)}) collective-permute-start(bf16[2,2,128,512]{3,2,1,0:T(8,128)(2,1)S(1)} %get-tuple-element.813), channel_id=1, source_target_pairs={{0,8},{1,9},{2,10},{3,11},{4,12},{5,13},{6,14},{7,15},{8,0},{9,1},... | collective-permute-start | bytes 1572872 | tf_op jit(solution)/shard_map/ppermute | solution.py:268
  309.2 14.3 %collective-permute-start.40 = (bf16[352,256]{1,0:T(8,128)(2,1)S(1)}, bf16[352,256]{1,0:T(8,128)(2,1)S(1)}, u32[]{:S(2)}, u32[]{:S(2)}) collective-permute-start(bf16[352,256]{1,0:T(8,128)(2,1)S(1)} %fusion.42), channel_id=1, source_target_pairs={{0,16},{1,17},{2,18},{3,19},{4,20},{5,21},{6,22},{7,23},{8,24},{9,... | collective-permute-start | bytes 540680 | tf_op jit(solution)/shard_map/ppermute | solution.py:268
  328.3 19.6 %collective-permute-start.44 = (bf16[4,128,256]{2,1,0:T(8,128)(2,1)}, bf16[4,128,256]{2,1,0:T(8,128)(2,1)S(1)}, u32[]{:S(2)}, u32[]{:S(2)}) collective-permute-start(bf16[4,128,256]{2,1,0:T(8,128)(2,1)} %get-tuple-element.843), channel_id=1, source_target_pairs={{0,1},{1,0},{2,3},{3,2},{4,5},{5,4},{6,7},{7,6},{8,9},{9,8},{10,11... | collective-permute-start | bytes 786440 | tf_op jit(solution)/shard_map/ppermute | solution.py:268
  329.4 18.5 %collective-permute-start.45 = (bf16[4,128,256]{2,1,0:T(8,128)(2,1)}, bf16[4,128,256]{2,1,0:T(8,128)(2,1)S(1)}, u32[]{:S(2)}, u32[]{:S(2)}) collective-permute-start(bf16[4,128,256]{2,1,0:T(8,128)(2,1)} %get-tuple-element.844), channel_id=1, source_target_pairs={{0,16},{1,17},{2,18},{3,19},{4,20},{5,21},{6,22},{7,23},{8,24},{9,... | collective-permute-start | bytes 786440 | tf_op jit(solution)/shard_map/ppermute | solution.py:268
  335.7 19.6 %collective-permute-start.46 = (bf16[4,128,256]{2,1,0:T(8,128)(2,1)}, bf16[4,128,256]{2,1,0:T(8,128)(2,1)S(1)}, u32[]{:S(2)}, u32[]{:S(2)}) collective-permute-start(bf16[4,128,256]{2,1,0:T(8,128)(2,1)} %get-tuple-element.845), channel_id=1, source_target_pairs={{0,17},{1,16},{2,19},{3,18},{4,21},{5,20},{6,23},{7,22},{8,25},{9,... | collective-permute-start | bytes 786440 | tf_op jit(solution)/shard_map/ppermute | solution.py:268
  337.2 18.0 %collective-permute-start.43 = (bf16[352,512]{1,0:T(8,128)(2,1)S(1)}, bf16[352,512]{1,0:T(8,128)(2,1)S(1)}, u32[]{:S(2)}, u32[]{:S(2)}) collective-permute-start(bf16[352,512]{1,0:T(8,128)(2,1)S(1)} %maximum_select_fusion.4), channel_id=1, source_target_pairs={{0,8},{1,9},{2,10},{3,11},{4,12},{5,13},{6,14},{7,15},{8,0},{9,1},... | collective-permute-start | bytes 1081352 | tf_op jit(solution)/shard_map/ppermute | solution.py:268
  337.3 17.9 %collective-permute-start.42 = (bf16[2,256,256]{2,1,0:T(8,128)(2,1)S(1)}, bf16[2,256,256]{2,1,0:T(8,128)(2,1)S(1)}, u32[]{:S(2)}, u32[]{:S(2)}) collective-permute-start(bf16[2,256,256]{2,1,0:T(8,128)(2,1)S(1)} %slice.263), channel_id=1, source_target_pairs={{16,0},{17,1},{18,2},{19,3},{20,4},{21,5},{22,6},{23,7},{24,8},{25... | collective-permute-start | bytes 786440 | tf_op jit(solution)/shard_map/ppermute | solution.py:268
  355.4 27.1 %collective-permute-start.47 = (bf16[1,128,256]{2,1,0:T(8,128)(2,1)S(1)}, bf16[1,128,256]{2,1,0:T(8,128)(2,1)S(1)}, u32[]{:S(2)}, u32[]{:S(2)}) collective-permute-start(bf16[1,128,256]{2,1,0:T(8,128)(2,1)S(1)} %get-tuple-element.1025), channel_id=1, source_target_pairs={{0,2},{1,3},{2,4},{3,5},{4,6},{5,7},{6,0},{7,1},{8,10},{9,11},{10,... | collective-permute-start | bytes 196616 | tf_op jit(solution)/shard_map/ppermute | solution.py:268
  365.1 17.4 %collective-permute-start.48 = (bf16[1,128,256]{2,1,0:T(8,128)(2,1)S(1)}, bf16[1,128,256]{2,1,0:T(8,128)(2,1)S(1)}, u32[]{:S(2)}, u32[]{:S(2)}) collective-permute-start(bf16[1,128,256]{2,1,0:T(8,128)(2,1)S(1)} %get-tuple-element.1027), channel_id=1, source_target_pairs={{0,4},{1,5},{2,6},{3,7},{4,0},{5,1},{6,2},{7,3},{8,12},{9,13},{10,... | collective-permute-start | bytes 196616 | tf_op jit(solution)/shard_map/ppermute | solution.py:268
  365.4 17.1 %collective-permute-start.49 = (bf16[1,128,256]{2,1,0:T(8,128)(2,1)S(1)}, bf16[1,128,256]{2,1,0:T(8,128)(2,1)S(1)}, u32[]{:S(2)}, u32[]{:S(2)}) collective-permute-start(bf16[1,128,256]{2,1,0:T(8,128)(2,1)S(1)} %get-tuple-element.1026), channel_id=1, source_target_pairs={{0,6},{1,7},{2,0},{3,1},{4,2},{5,3},{6,4},{7,5},{8,14},{9,15},{10,... | collective-permute-start | bytes 196616 | tf_op jit(solution)/shard_map/ppermute | solution.py:268
  384.8 5.6 %collective-permute-start.51 = (bf16[2,512,128]{2,1,0:T(8,128)(2,1)}, bf16[2,512,128]{2,1,0:T(8,128)(2,1)S(1)}, u32[]{:S(2)}, u32[]{:S(2)}) collective-permute-start(bf16[2,512,128]{2,1,0:T(8,128)(2,1)} %get-tuple-element.895), channel_id=1, source_target_pairs={{0,8},{1,9},{2,10},{3,11},{4,12},{5,13},{6,14},{7,15},{8,0},{9,1},... | collective-permute-start | bytes 786440 | tf_op jit(solution)/shard_map/ppermute | solution.py:268
  384.8 16.1 %collective-permute-start.50 = (bf16[2,256,256]{2,1,0:T(8,128)(2,1)S(1)}, bf16[2,256,256]{2,1,0:T(8,128)(2,1)S(1)}, u32[]{:S(2)}, u32[]{:S(2)}) collective-permute-start(bf16[2,256,256]{2,1,0:T(8,128)(2,1)S(1)} %slice.262), channel_id=1, source_target_pairs={{16,0},{17,1},{18,2},{19,3},{20,4},{21,5},{22,6},{23,7},{24,8},{25... | collective-permute-start | bytes 786440 | tf_op jit(solution)/shard_map/ppermute | solution.py:268
  404.1 10.4 %collective-permute-start.55 = (bf16[2,256,1024]{2,1,0:T(8,128)(2,1)}, bf16[2,256,1024]{2,1,0:T(8,128)(2,1)}, u32[]{:S(2)}, u32[]{:S(2)}) collective-permute-start(bf16[2,256,1024]{2,1,0:T(8,128)(2,1)} %fusion.24), channel_id=1, source_target_pairs={{0,8},{1,9},{2,10},{3,11},{4,12},{5,13},{6,14},{7,15},{8,0},{9,1},... | collective-permute-start | bytes 3145736 | tf_op jit(solution)/shard_map/ppermute | solution.py:268
  408.8 17.3 %collective-permute-start.52 = (bf16[4,128,512]{2,1,0:T(8,128)(2,1)}, bf16[4,128,512]{2,1,0:T(8,128)(2,1)}, u32[]{:S(2)}, u32[]{:S(2)}) collective-permute-start(bf16[4,128,512]{2,1,0:T(8,128)(2,1)} %get-tuple-element.907), channel_id=1, source_target_pairs={{0,1},{1,0},{2,3},{3,2},{4,5},{5,4},{6,7},{7,6},{8,9},{9,8},{10,11... | collective-permute-start | bytes 1572872 | tf_op jit(solution)/shard_map/ppermute | solution.py:268
  413.0 25.7 %collective-permute-start.53 = (bf16[4,128,512]{2,1,0:T(8,128)(2,1)}, bf16[4,128,512]{2,1,0:T(8,128)(2,1)}, u32[]{:S(2)}, u32[]{:S(2)}) collective-permute-start(bf16[4,128,512]{2,1,0:T(8,128)(2,1)} %get-tuple-element.908), channel_id=1, source_target_pairs={{0,16},{1,17},{2,18},{3,19},{4,20},{5,21},{6,22},{7,23},{8,24},{9,... | collective-permute-start | bytes 1572872 | tf_op jit(solution)/shard_map/ppermute | solution.py:268
  413.0 25.7 %collective-permute-start.54 = (bf16[4,128,512]{2,1,0:T(8,128)(2,1)}, bf16[4,128,512]{2,1,0:T(8,128)(2,1)}, u32[]{:S(2)}, u32[]{:S(2)}) collective-permute-start(bf16[4,128,512]{2,1,0:T(8,128)(2,1)} %get-tuple-element.909), channel_id=1, source_target_pairs={{0,17},{1,16},{2,19},{3,18},{4,21},{5,20},{6,23},{7,22},{8,25},{9,... | collective-permute-start | bytes 1572872 | tf_op jit(solution)/shard_map/ppermute | solution.py:268
  416.6 22.2 %collective-permute-start.56 = (bf16[16,128]{1,0:T(8,128)(2,1)S(1)}, bf16[16,128]{1,0:T(8,128)(2,1)S(1)}, u32[]{:S(2)}, u32[]{:S(2)}) collective-permute-start(bf16[16,128]{1,0:T(8,128)(2,1)S(1)} %convert_element_type.385), channel_id=1, source_target_pairs={{0,1},{1,0},{2,3},{3,2},{4,5},{5,4},{6,7},{7,6},{8,9},{9,8},{10,11... | collective-permute-start | bytes 12296 | tf_op jit(solution)/shard_map/ppermute | solution.py:268
  418.7 20.1 %collective-permute-start.57 = (bf16[16,128]{1,0:T(8,128)(2,1)S(1)}, bf16[16,128]{1,0:T(8,128)(2,1)S(1)}, u32[]{:S(2)}, u32[]{:S(2)}) collective-permute-start(bf16[16,128]{1,0:T(8,128)(2,1)S(1)} %convert_element_type.385), channel_id=1, source_target_pairs={{0,16},{1,17},{2,18},{3,19},{4,20},{5,21},{6,22},{7,23},{8,24},{9,... | collective-permute-start | bytes 12296 | tf_op jit(solution)/shard_map/ppermute | solution.py:268
  426.1 12.7 %collective-permute-start.58 = (bf16[16,128]{1,0:T(8,128)(2,1)S(1)}, bf16[16,128]{1,0:T(8,128)(2,1)S(1)}, u32[]{:S(2)}, u32[]{:S(2)}) collective-permute-start(bf16[16,128]{1,0:T(8,128)(2,1)S(1)} %convert_element_type.385), channel_id=1, source_target_pairs={{0,17},{1,16},{2,19},{3,18},{4,21},{5,20},{6,23},{7,22},{8,25},{9,... | collective-permute-start | bytes 12296 | tf_op jit(solution)/shard_map/ppermute | solution.py:268
  438.8 18.4 %collective-permute-start.59 = (bf16[128,2816]{1,0:T(8,128)(2,1)}, bf16[128,2816]{1,0:T(8,128)(2,1)S(1)}, u32[]{:S(2)}, u32[]{:S(2)}) collective-permute-start(bf16[128,2816]{1,0:T(8,128)(2,1)} %reduce-scatter.2.cloned.1.call-done), channel_id=1, source_target_pairs={{0,16},{1,17},{2,18},{3,19},{4,20},{5,21},{6,22},{7,23},{8,24},{9,... | collective-permute-start | bytes 2162696 | tf_op jit(solution)/shard_map/ppermute | solution.py:268
  441.1 8.5 %collective-permute-start.61 = (bf16[1,136,512]{2,1,0:T(8,128)(2,1)S(1)}, bf16[1,136,512]{2,1,0:T(8,128)(2,1)S(1)}, u32[]{:S(2)}, u32[]{:S(2)}) collective-permute-start(bf16[1,136,512]{2,1,0:T(8,128)(2,1)S(1)} %get-tuple-element.1006), channel_id=1, source_target_pairs={{0,2},{1,3},{2,4},{3,5},{4,6},{5,7},{6,0},{7,1},{8,10},{9,11},{10,... | collective-permute-start | bytes 417800 | tf_op jit(solution)/shard_map/ppermute | solution.py:268
  441.2 12.8 %collective-permute-start.62 = (bf16[1,136,512]{2,1,0:T(8,128)(2,1)S(1)}, bf16[1,136,512]{2,1,0:T(8,128)(2,1)S(1)}, u32[]{:S(2)}, u32[]{:S(2)}) collective-permute-start(bf16[1,136,512]{2,1,0:T(8,128)(2,1)S(1)} %get-tuple-element.1008), channel_id=1, source_target_pairs={{0,4},{1,5},{2,6},{3,7},{4,0},{5,1},{6,2},{7,3},{8,12},{9,13},{10,... | collective-permute-start | bytes 417800 | tf_op jit(solution)/shard_map/ppermute | solution.py:268
  442.3 11.7 %collective-permute-start.63 = (bf16[1,136,512]{2,1,0:T(8,128)(2,1)S(1)}, bf16[1,136,512]{2,1,0:T(8,128)(2,1)S(1)}, u32[]{:S(2)}, u32[]{:S(2)}) collective-permute-start(bf16[1,136,512]{2,1,0:T(8,128)(2,1)S(1)} %get-tuple-element.1007), channel_id=1, source_target_pairs={{0,6},{1,7},{2,0},{3,1},{4,2},{5,3},{6,4},{7,5},{8,14},{9,15},{10,... | collective-permute-start | bytes 417800 | tf_op jit(solution)/shard_map/ppermute | solution.py:268
  445.0 12.9 %collective-permute-start.60 = (bf16[128,256]{1,0:T(8,128)(2,1)S(1)}, bf16[128,256]{1,0:T(8,128)(2,1)S(1)}, u32[]{:S(2)}, u32[]{:S(2)}) collective-permute-start(bf16[128,256]{1,0:T(8,128)(2,1)S(1)} %fusion.44), channel_id=1, source_target_pairs={{0,16},{1,17},{2,18},{3,19},{4,20},{5,21},{6,22},{7,23},{8,24},{9,... | collective-permute-start | bytes 196616 | tf_op jit(solution)/shard_map/ppermute | solution.py:268
  457.9 6.1 %collective-permute-start.64 = (bf16[128,2816]{1,0:T(8,128)(2,1)S(1)}, bf16[128,2816]{1,0:T(8,128)(2,1)S(1)}, u32[]{:S(2)}, u32[]{:S(2)}) collective-permute-start(bf16[128,2816]{1,0:T(8,128)(2,1)S(1)} %add_convert_fusion), channel_id=1, source_target_pairs={{0,8},{1,9},{2,10},{3,11},{4,12},{5,13},{6,14},{7,15},{8,0},{9,1},... | collective-permute-start | bytes 2162696 | tf_op jit(solution)/shard_map/ppermute | solution.py:268
  457.9 6.1 %collective-permute-start.66 = (bf16[136,512]{1,0:T(8,128)(2,1)S(1)}, bf16[136,512]{1,0:T(8,128)(2,1)S(1)}, u32[]{:S(2)}, u32[]{:S(2)}) collective-permute-start(bf16[136,512]{1,0:T(8,128)(2,1)S(1)} %fusion.43), channel_id=1, source_target_pairs={{0,16},{1,17},{2,18},{3,19},{4,20},{5,21},{6,22},{7,23},{8,24},{9,... | collective-permute-start | bytes 417800 | tf_op jit(solution)/shard_map/ppermute | solution.py:268
  (78 other events, 485.6 us)
Sparse Core Ops, SparseCore 0:
  35.1 109.1 all-gather.1
  248.2 147.6 reduce-scatter.1

commit v3 on v2

--- a/solution.py
+++ b/solution.py
@@ -47,7 +47,7 @@
     return jnp.logical_and(k0 <= q0, jnp.logical_not(before))
 
 
-def forward_kernel(b, nkb, batch, width, meta, qt, kxt, vxt, c, o_low, o_full, mix_out, lse_out, q_s, acc, m_s, l_s):
+def forward_kernel(b, nkb, batch, width, meta, qt, kxt, vxt, c, o_low, o_full, mix_out, lse_out, q_s, acc, m_s, l_s, p_s):
     qb = pl.program_id(0)
     q0, first, diag = meta[nkb + qb], meta[nkb + 2 + b], meta[nkb + 2 + batch] + qb
     for h in range(GH):
@@ -67,6 +67,7 @@
             bias = block_bias(k0, q0, first, width)
             keys = c[0, kb]
             keys_t = keys.T
+            alphas = []
             for h in range(GH):
                 cols = slice(h * width, (h + 1) * width)
                 s = mm(keys, q_s[:, cols]) + bias
@@ -76,7 +77,9 @@
                 alpha = jnp.exp2(m_old - m_new)
                 m_s[:, cols] = m_new
                 l_s[:, cols] = l_s[:, cols] * alpha + jnp.sum(p, axis=0, keepdims=True)
-                acc[:, cols] = acc[:, cols] * alpha + mm(keys_t, p.astype(LOW))
+                p_s[:, cols] = p.astype(LOW)
+                alphas.append(alpha)
+            acc[...] = acc[...] * jnp.concatenate(alphas, 1) + mm(keys_t, p_s[...])
 
         return carry
 
@@ -94,23 +97,27 @@
 
 
 def backward_kernel(
-    b, qb, nkb, batch, width, add_dc, add_dw, meta, qt, dot_, o_full, mix, lse, kxt, vxt, c, *refs
+    b, nkb, batch, width, add_dw, meta, qt, dot_, o_full, mix, lse, kxt, vxt, c, *refs
 ):
     refs = list(refs)
-    dc_old = refs.pop(0) if add_dc else None
     dk_old, dv_old = (refs.pop(0), refs.pop(0)) if add_dw else (None, None)
-    dqt, dc, dkxt, dvxt, q_s, q_n, do_t, do_n, delta, dq, ds_s, p_s = refs
+    dqt, dc, dkxt, dvxt, q_s, do_t, delta, dq, ds_s, p_s = refs
+    qb = pl.program_id(0)
     q0, first, diag = meta[nkb + qb], meta[nkb + 2 + b], meta[nkb + 2 + batch] + qb
-    dc[...] = dc_old[...] if add_dc else jnp.zeros_like(dc)
+
+    @pl.when(qb == 0)
+    def _():
+        dc[...] = jnp.zeros_like(dc)
+        dkxt[...] = dk_old[...] if add_dw else jnp.zeros_like(dkxt)
+        dvxt[...] = dv_old[...] if add_dw else jnp.zeros_like(dvxt)
+
 
     for h in range(GH):
         cols = slice(h * width, (h + 1) * width)
         rows = slice(h * HD, (h + 1) * HD)
         qh, kh, doh, vh = qt[0, rows, :], kxt[rows, :], dot_[0, rows, :], vxt[rows, :]
         q_s[:, cols] = (tn(kh, qh) * (SCALE * LOG2E)).astype(LOW)
-        q_n[cols, :] = (tn(qh, kh) * SCALE).astype(LOW)
         do_t[:, cols] = tn(vh, doh).astype(LOW)
-        do_n[cols, :] = tn(doh, vh).astype(LOW)
         delta[:, cols] = jnp.sum(doh.astype(F32) * o_full[0, rows, :], axis=0, keepdims=True)
     dq[...] = jnp.zeros_like(dq)
 
@@ -131,8 +138,8 @@
                 ds = (p * (dp - delta[:, cols])).astype(LOW)
                 p_s[:, cols] = p.astype(LOW)
                 ds_s[:, cols] = ds
-                dq[:, cols] += mm(keys_t, ds)
-            dc[kb] += mm(ds_s[...], q_n[...]) + mm(p_s[...], do_n[...])
+            dq[...] += mm(keys_t, ds_s[...])
+            dc[kb] += nt(ds_s[...], q_s[...]) * (1.0 / LOG2E) + nt(p_s[...], do_t[...])
 
         return carry
 
@@ -142,9 +149,8 @@
         rows = slice(h * HD, (h + 1) * HD)
         dq_low = (dq[:, cols] * SCALE).astype(LOW)
         dqt[rows, :] = mm(kxt[rows, :], dq_low).astype(LOW)
-        dk, dv = nt(qt[0, rows, :], dq_low), nt(dot_[0, rows, :], mix[0, :, cols])
-        dkxt[rows, :] = dk + dk_old[rows, :] if add_dw else dk
-        dvxt[rows, :] = dv + dv_old[rows, :] if add_dw else dv
+        dkxt[rows, :] += nt(qt[0, rows, :], dq_low)
+        dvxt[rows, :] += nt(dot_[0, rows, :], mix[0, :, cols])
 
 
 def attention_forward(b, meta, qt, kxt, vxt, c):
@@ -180,6 +186,7 @@
             pltpu.VMEM((LAT, wide), F32),
             pltpu.VMEM((1, wide), F32),
             pltpu.VMEM((1, wide), F32),
+            pltpu.VMEM((width, wide), LOW),
         ],
         compiler_params=pltpu.CompilerParams(
             dimension_semantics=("arbitrary",), vmem_limit_bytes=VMEM_LIMIT
@@ -191,47 +198,41 @@
     )(meta, qt, kxt, vxt, c)
 
 
-def attention_backward(b, qb, meta, qt, dot_, o_full, mix, lse, kxt, vxt, c, old_dc, old_dw):
+def attention_backward(b, meta, qt, dot_, o_full, mix, lse, kxt, vxt, c, old_dw):
     batch, nkb, width, _ = c.shape
     wide = GH * width
-    pairs = 4 * GH * width * width * LAT * 2
-    q_spec = pl.BlockSpec((1, GW, width), lambda i: (b, 0, qb))
-    expand = pl.BlockSpec((GW, LAT), lambda i: (0, 0))
+    pairs = 7 * GH * width * width * LAT * 2
+    expand = pl.BlockSpec((GW, LAT), lambda q: (0, 0))
     return pl.pallas_call(
-        lambda *refs: backward_kernel(
-            b, qb, nkb, batch, width, bool(old_dc), bool(old_dw), *refs
-        ),
-        grid=(1,),
+        lambda *refs: backward_kernel(b, nkb, batch, width, bool(old_dw), *refs),
+        grid=(2,),
         in_specs=[
             pl.BlockSpec(memory_space=pltpu.SMEM),
-            q_spec,
-            q_spec,
-            pl.BlockSpec((1, GW, width), lambda i: (0, 0, qb)),
-            pl.BlockSpec((1, LAT, wide), lambda i: (qb, 0, 0)),
-            pl.BlockSpec((1, 1, wide), lambda i: (qb, 0, 0)),
+            pl.BlockSpec((1, GW, width), lambda q: (b, 0, q)),
+            pl.BlockSpec((1, GW, width), lambda q: (b, 0, q)),
+            pl.BlockSpec((1, GW, width), lambda q: (0, 0, q)),
+            pl.BlockSpec((1, LAT, wide), lambda q: (q, 0, 0)),
+            pl.BlockSpec((1, 1, wide), lambda q: (q, 0, 0)),
             expand,
             expand,
-            pl.BlockSpec((1, nkb, width, LAT), lambda i: (b, 0, 0, 0)),
+            pl.BlockSpec((1, nkb, width, LAT), lambda q: (b, 0, 0, 0)),
         ]
-        + [pl.BlockSpec((nkb, width, LAT), lambda i: (0, 0, 0))] * len(old_dc)
         + [expand] * len(old_dw),
         out_specs=[
-            pl.BlockSpec((GW, width), lambda i: (0, 0)),
-            pl.BlockSpec((nkb, width, LAT), lambda i: (0, 0, 0)),
+            pl.BlockSpec((GW, width), lambda q: (0, q)),
+            pl.BlockSpec((nkb, width, LAT), lambda q: (0, 0, 0)),
             expand,
             expand,
         ],
         out_shape=[
-            jax.ShapeDtypeStruct((GW, width), LOW),
+            jax.ShapeDtypeStruct((GW, 2 * width), LOW),
             jax.ShapeDtypeStruct((nkb, width, LAT), F32),
             jax.ShapeDtypeStruct(kxt.shape, F32),
             jax.ShapeDtypeStruct(vxt.shape, F32),
         ],
         scratch_shapes=[
             pltpu.VMEM((LAT, wide), LOW),
-            pltpu.VMEM((wide, LAT), LOW),
             pltpu.VMEM((LAT, wide), LOW),
-            pltpu.VMEM((wide, LAT), LOW),
             pltpu.VMEM((1, wide), F32),
             pltpu.VMEM((LAT, wide), F32),
             pltpu.VMEM((width, wide), LOW),
@@ -241,10 +242,92 @@
             dimension_semantics=("arbitrary",), vmem_limit_bytes=VMEM_LIMIT
         ),
         cost_estimate=pl.CostEstimate(
-            flops=5 * pairs, bytes_accessed=6 << 20, transcendentals=4 * GH * width * width
+            flops=5 * pairs, bytes_accessed=10 << 20, transcendentals=7 * GH * width * width
         ),
         name="attention_backward",
-    )(meta, qt, dot_, o_full, mix, lse, kxt, vxt, c, *old_dc, *old_dw)
+    )(meta, qt, dot_, o_full, mix, lse, kxt, vxt, c, *old_dw)
+
+
+def hidden_kernel(x, w, act, hidden):
+    width = hidden.shape[1]
+    both = mm(x[...], w[...])
+    act[...] = both
+    gate, up = both[:, :width], both[:, width:]
+    hidden[...] = (gate * jax.nn.sigmoid(gate) * up).astype(LOW)
+
+
+def hidden_back_kernel(cot, down, w, act, grad, own, other):
+    width = down.shape[0]
+    d_hidden = nt(cot[...], down[...])
+    gate, up = act[:, :width], act[:, width:]
+    sig = jax.nn.sigmoid(gate)
+    grad[:, :width] = (d_hidden * up * sig * (1.0 + gate * (1.0 - sig))).astype(LOW)
+    grad[:, width:] = (d_hidden * (gate * sig)).astype(LOW)
+    back = nt(grad[...], w[...])
+    mine = pl.program_id(0) < pl.num_programs(0) // 2
+
+    @pl.when(mine)
+    def _():
+        own[...] = back
+
+    @pl.when(jnp.logical_not(mine))
+    def _():
+        other[...] = back.astype(LOW)
+
+
+TILE = 256
+
+
+def tiled(width):
+    return pl.BlockSpec((TILE, width), lambda i: (i, 0))
+
+
+def resident(shape):
+    return pl.BlockSpec(shape, lambda i: (0, 0), pipeline_mode=pl.Buffered(1))
+
+
+def feed_forward(x, w):
+    count, both = x.shape[0], w.shape[1]
+    return pl.pallas_call(
+        hidden_kernel,
+        grid=(count // TILE,),
+        in_specs=[tiled(x.shape[1]), resident(w.shape)],
+        out_specs=[tiled(both), tiled(both // 2)],
+        out_shape=[
+            jax.ShapeDtypeStruct((count, both), F32),
+            jax.ShapeDtypeStruct((count, both // 2), LOW),
+        ],
+        compiler_params=pltpu.CompilerParams(vmem_limit_bytes=VMEM_LIMIT),
+        cost_estimate=pl.CostEstimate(
+            flops=2 * x.size * both, bytes_accessed=20 << 20, transcendentals=count * both // 2
+        ),
+        name="feed_forward",
+    )(x, w)
+
+
+def feed_forward_back(cot, down, w, act):
+    count, both = act.shape
+    width, steps = w.shape[0], count // TILE
+    return pl.pallas_call(
+        hidden_back_kernel,
+        grid=(steps,),
+        in_specs=[tiled(cot.shape[1]), resident(down.shape), resident(w.shape), tiled(both)],
+        out_specs=[
+            tiled(both),
+            pl.BlockSpec((TILE, width), lambda i: (jnp.minimum(i, steps // 2 - 1), 0)),
+            pl.BlockSpec((TILE, width), lambda i: (jnp.maximum(i - steps // 2, 0), 0)),
+        ],
+        out_shape=[
+            jax.ShapeDtypeStruct((count, both), LOW),
+            jax.ShapeDtypeStruct((count // 2, width), F32),
+            jax.ShapeDtypeStruct((count // 2, width), LOW),
+        ],
+        compiler_params=pltpu.CompilerParams(vmem_limit_bytes=VMEM_LIMIT),
+        cost_estimate=pl.CostEstimate(
+            flops=3 * cot.size * both, bytes_accessed=30 << 20, transcendentals=count * both // 2
+        ),
+        name="feed_forward_back",
+    )(cot, down, w, act)
 
 
 class Place:
@@ -432,17 +515,13 @@
     d_out_t = dots("nd,btd->bnt", w["output"], d_a).astype(LOW)
     d_queries, d_keys, sums = [], [], ()
     for b in range(batch):
-        far = ()
-        for qb in range(2):
-            found = attention_backward(
-                b, qb, meta, query_t, d_out_t, *att[b][1:], w["key_t"], w["value_t"], keys,
-                far, sums,
-            )
-            far, sums = found[1:2], found[2:]
-            d_queries.append(found[0])
-        d_keys.append(far[0])
-    dq_t = jnp.stack([jnp.concatenate(d_queries[2 * b : 2 * b + 2], 1) for b in range(batch)])
-    d_keys = jnp.stack(d_keys)
+        found = attention_backward(
+            b, meta, query_t, d_out_t, *att[b][1:], w["key_t"], w["value_t"], keys, sums
+        )
+        sums = found[2:]
+        d_queries.append(found[0])
+        d_keys.append(found[1])
+    dq_t, d_keys = jnp.stack(d_queries), jnp.stack(d_keys)
     d_key_t, d_value_t = sums
     d_blocks = lax.psum_scatter(
         d_keys.astype(LOW), "seq", scatter_dimension=1, tiled=True,
@@ -486,8 +565,7 @@
     return Live(lax.optimization_barrier(dict(v.__dict__)))
 
 
-def z_gather(p, piece):
-    seen = [piece] + [p.to_z(piece, k) for k in (1, 2, 3)]
+def in_z(p, seen):
     out = []
     for z in range(4):
         back = (p.z - z) % 4
@@ -496,11 +574,24 @@
     return jnp.stack(out)
 
 
+def z_gather(p, piece):
+    return in_z(p, [piece] + [p.to_z(piece, k) for k in (1, 2, 3)])
+
+
 def z_scatter(p, parts):
     total = half(parts, p.z, 0, 4)[0].astype(F32)
     for k in (1, 2, 3):
         total = total + p.to_z(half(parts, (p.z + k) % 4, 0, 4), k)[0].astype(F32)
     return total.astype(LOW)
+
+
+def summed(p, make):
+    come = p.to_core(make(1).astype(LOW))
+    return make(0) + come.astype(F32)
+
+
+def core_first(p, own):
+    return jnp.concatenate([own, p.to_core(own)], 0)
 
 
 def to_xy(p, value):
@@ -566,6 +657,7 @@
     v.pgu = jnp.concatenate([cols(gate_weight, 2, core), cols(up_weight, 2, core)], 1)
     v.tok = p.to_core(tokens)
     v = sync(v)
+    w_gu = lax.all_gather(v.pop.pgu, "dp", axis=0, tiled=True)
     kv = half(pick(y, key_expand, value_expand), core, 0).astype(LOW).T
     gains = jnp.stack([attn_gain, mlp_gain] + [jnp.zeros_like(attn_gain)] * 6).astype(LOW)
     piece = [
@@ -582,9 +674,10 @@
     v.pd = cols(down_weight, 4, quarter)
     v = sync(v)
 
-    w_gu = lax.all_gather(v.pop.pgu, "dp", axis=0, tiled=True)
     v.ax, v.by = p.to_x(v.a), p.to_y(v.b)
-    v = sync(v)
+    v.zd1 = p.to_z(v.pd, 1)
+    v = sync(v)
+    v.zd2 = p.to_z(v.pd, 2)
     v.ay, v.axy = p.to_y(v.a), p.to_y(v.ax)
     v.bx, v.bxy = p.to_x(v.b), p.to_x(v.by)
     v = sync(v)
@@ -618,7 +711,7 @@
     v = sync(v)
     far_keys = p.up_y(v.keys)
     wo_come, kv_come = p.to_core(v.pop.wo_send), p.to_core(v.pop.kv_send)
-    v.zd = z_gather(p, v.pop.pd)
+    v.zd3 = p.to_z(v.pd, 3)
     v.qt = dots("dn,btd->bnt", v.wq, v.first).astype(LOW)
     plan = []
     for n, (r, k) in enumerate(RELATIVE):
@@ -647,8 +740,9 @@
     def forward(b):
         return attention_forward(b, v.meta, v.qt, v.kxt, v.vxt, v.keys)
 
+    v.zd = in_z(p, [v.pop.pd, v.pop.zd1, v.pop.zd2, v.pop.zd3])
     v.dax, v.dby = p.to_x(v.zd[:2]), p.to_y(v.zd[2:])
-    v.cot = chip(p, cotangent).reshape(count, D)
+    v.cot = core_first(p, cotangent.reshape(count // 2, D))
     v.att0 = forward(0)
     v = sync(v)
     v.day, v.daxy = p.to_y(v.zd[:2]), p.to_y(v.dax)
@@ -658,20 +752,26 @@
     v.att1 = forward(1)
     v = sync(v)
 
-    down = (v.pop.zd, v.pop.dax, v.pop.day, v.pop.daxy, v.pop.dby, v.pop.dbx, v.pop.dbxy)
-    fronts = [down[0][:2], down[1], down[2], down[3]]
-    backs = [down[0][2:], down[5], down[4], down[6]]
+    front, back = v.zd[:2], v.pop.zd[2:]
+    fronts, backs = [front, v.pop.dax, v.pop.day, v.pop.daxy], [back, v.pop.dbx, v.pop.dby, v.pop.dbxy]
     mine = [pick(core, front, back) for front, back in zip(fronts, backs)]
-    come = [p.to_core(pick(core, back, front)) for front, back in zip(fronts, backs)]
-    v.down = mine + come
+    v.down = mine + [p.to_core(pick(core, back, front)) for front, back in zip(fronts, backs)]
     v.out = jnp.concatenate([v.att0[0], v.att1[0]])
-    branch = dots("bnt,nd->btd", v.out, v.wo).reshape(batch, 2, length, D)
-    v.middle = tokens.astype(F32) + chip_sum(p, branch)
+    branch = summed(
+        p, lambda i: dots("bnt,nd->btd", v.out[:, :, i * length : (i + 1) * length], v.wo)
+    )
+    v.middle = tokens.astype(F32) + branch
     v.inv2 = inverse_rms(v.middle)
     second = v.middle * v.inv2 * v.gain2
-    v.second = chip(p, second.astype(LOW)).reshape(count, D)
-    v = sync(v)
-
+    v.second = core_first(p, second.astype(LOW).reshape(count // 2, D))
+    v = sync(v)
+
+    v.w_gu = w_gu
+    v.act, v.hidden = feed_forward(v.second, v.w_gu)
+    cot_y, cot_far, cot_core = v.pop.cot_c
+    v.gd_b = p.to_core(tn(v.hidden, cot_core).astype(LOW).reshape(2, 2, -1, 512))
+    v.gd_a = tn(v.hidden, cot_y).astype(LOW).reshape(2, 2, -1, 256)
+    v.gd_ay = tn(v.hidden, cot_far).astype(LOW).reshape(2, 2, -1, 256)
     plan = []
     for n, (r, k) in enumerate(RELATIVE):
         for s in range(2):
@@ -683,127 +783,118 @@
             ]
     wd = placed(p, plan, v.pop.down, [(2, 2, ff // 4, D)])[0]
     v.wd = wd.reshape(ff, D)
-    v.w_gu = w_gu
-    v = sync(v)
-    v.act = mm(v.second, v.w_gu)
-    gate, up = v.act[:, :ff], v.act[:, ff:]
-    v.hidden = (gate * jax.nn.sigmoid(gate) * up).astype(LOW)
-    cot_y, cot_far, cot_core = v.pop.cot_c
-    v.gd_a = tn(v.hidden, cot_y).astype(LOW).reshape(2, 2, -1, 256)
-    v.gd_ay = tn(v.hidden, cot_far).astype(LOW).reshape(2, 2, -1, 256)
-    v.gd_send = tn(v.hidden, cot_core).astype(LOW).reshape(2, 2, -1, 512)
-    v = sync(v)
-
-    v.gd_b = p.to_core(v.pop.gd_send)
-    gate, up = v.act[:, :ff], v.pop.act[:, ff:]
-    sig = jax.nn.sigmoid(gate)
-    d_hidden = nt(v.cot, v.wd)
-    d_gate = d_hidden * up * sig * (1.0 + gate * (1.0 - sig))
-    d_up = d_hidden * (gate * sig)
-    v.d_gu = jnp.concatenate([d_gate, d_up], 1).astype(LOW)
-    v = sync(v)
+    v = sync(v)
+
     v.gd_ay, v.gd_bx = p.to_y(v.gd_ay), p.to_x(x_other(v.gd_b))
-    v.gg = tn(v.pop.second, v.d_gu).astype(LOW)
-    v = sync(v)
-    gg = lax.psum_scatter(v.pop.gg, "dp", scatter_dimension=0, tiled=True)
+    v.d_gu, v.ds_own, v.ds_other = feed_forward_back(v.cot, v.wd, v.pop.w_gu, v.pop.act)
+    v = sync(v)
     v.gd_a = add_low(v.gd_a, v.pop.gd_ay)
     v.gd_b = add_low(x_own(v.gd_b), v.pop.gd_bx)
     v.gd_ax, v.gd_by = p.to_x(x_other(v.gd_a)), p.to_y(half(v.gd_b, 1 - y, 3))
-    d_second = chip_sum(p, nt(v.pop.d_gu, v.pop.w_gu).reshape(batch, 2, length, D))
+    d_second = (v.pop.ds_own + p.to_core(v.pop.ds_other).astype(F32)).reshape(batch, length, D)
+    v.gg = tn(v.pop.second, v.pop.d_gu).astype(LOW)
     normed2 = v.middle * v.inv2
     v.gain2_sum = jnp.sum(d_second * normed2, axis=(0, 1))
     v.d_middle = cotangent.astype(F32) + norm_back(d_second, normed2, v.pop.inv2, v.pop.gain2)
-    v = sync(v)
     v.d_a = chip(p, v.d_middle.astype(LOW)).reshape(batch, 2 * length, D)
+    v = sync(v)
+    gg = lax.psum_scatter(v.pop.gg, "dp", scatter_dimension=0, tiled=True)
     gd_a = add_low(x_own(v.pop.gd_a), v.pop.gd_ax)[:, 0]
     gd_b = add_low(half(v.pop.gd_b, y, 3), v.pop.gd_by)[:, 0]
     v.gd = ordered(core, gd_a, gd_b, 0)
-    partial = mm(v.pop.hidden, v.pop.wd).reshape(batch, 2, length, D)
-    layer_out = (v.pop.middle + chip_sum(p, partial)).astype(LOW)
-    v.out_done = layer_out
-    v.dot = dots("nd,btd->bnt", v.pop.wo, v.d_a).astype(LOW)
+
+    def gd_step(k):
+        return p.to_z(half(v.gd, (p.z + k) % 4, 0, 4), k)
+
+    v.gd1 = gd_step(1)
+    go = dots("bnt,btd->nd", v.pop.out, v.d_a).astype(LOW).reshape(2, 2, 128, D)
+    v.go_a, v.go_b = half(go, core, 3), p.to_core(half(go, 1 - core, 3))
+    rows = count // 2
+    branch = summed(p, lambda i: mm(v.hidden[i * rows : (i + 1) * rows], v.wd))
+    v.out_done = (v.pop.middle + branch.reshape(batch, length, D)).astype(LOW)
+    del v.hidden, v.wd
+    v.dot = dots("nd,btd->bnt", v.pop.wo, v.pop.d_a).astype(LOW)
     v = sync(v)
     layer_out = v.pop.out_done
 
-    def backward(b, qb, old_dc, old_dw):
-        att = (v.att0, v.att1)[b][1:]
-        return attention_backward(
-            b, qb, v.meta, v.qt, v.dot, *att, v.kxt, v.vxt, v.keys, old_dc, old_dw
-        )
-
-    v.gd = z_scatter(p, v.gd)
-    v.back00 = backward(0, 0, (), ())
-    go = dots("bnt,btd->nd", v.pop.out, v.pop.d_a).astype(LOW).reshape(2, 2, 128, D)
-    v.go_a, v.go_b = half(go, core, 3), half(go, 1 - core, 3)
-    v = sync(v)
-    v.gd1, v.go_b = p.to_y(v.gd), p.to_core(v.go_b)
-    v.back01 = backward(0, 1, v.back00[1:2], v.back00[2:])
-    v = sync(v)
-    d_keys = v.back01[1]
-    v.dk0, v.dk_far0 = d_keys[:2], p.down_y(d_keys[2:].astype(LOW))
-    v.gd = ordered(y, v.gd, v.pop.gd1, 1)
-    v.gd1 = p.to_core(v.gd)
+    full = slice(None)
+    v.gd2 = gd_step(2)
     plan = []
     for n, (r, k) in enumerate(RELATIVE):
         for s in range(2):
             plan += [
                 lambda x, y, c, n=n, r=r, k=k, s=s: (
-                    s, (slice(None), x ^ r, slice(None), lanes((y ^ k) * 256, 256)),
-                    n, pl.ds(2 * (c ^ s), 2),
+                    s, (full, x ^ r, full, lanes((y ^ k) * 256, 256)), n, pl.ds(2 * (c ^ s), 2),
                 )
             ]
     v.go = spread(p, placed(p, plan, (v.pop.go_a, v.pop.go_b), [(4, 128, 256)] * 4))
-    v.back10 = backward(1, 0, (), v.back01[2:])
-    v = sync(v)
-    v.go = z_scatter(p, add_all(v.pop.go))
+    v.back0 = attention_backward(
+        0, v.meta, v.qt, v.dot, *v.att0[1:], v.kxt, v.vxt, v.keys, ()
+    )
+    v = sync(v)
+    v.gd3 = gd_step(3)
+    v.go = z_scatter(p, add_all(v.go))
+    d_keys = v.back0[1]
+    v.dk0, v.dk_far0 = d_keys[:2], p.down_y(d_keys[2:].astype(LOW))
+    v.back1 = attention_backward(
+        1, v.meta, v.qt, v.dot, *v.att1[1:], v.kxt, v.vxt, v.keys, v.back0[2:]
+    )
+    v = sync(v)
+
+    back0, back1 = v.pop.back0, v.pop.back1
+    v.far1 = p.down_y(back1[1][2:].astype(LOW))
+    v.dk1 = back1[1][:2]
     v.dk0 = (v.dk0 + v.pop.dk_far0.astype(F32)).astype(LOW).reshape(1, 2 * length, LAT)
-    grad_down = ordered(core, v.pop.gd, v.pop.gd1, 1).astype(F32)
-    v.back11 = backward(1, 1, v.back10[1:2], v.back10[2:])
-    v.down_done = grad_down
-    v = sync(v)
-    grad_down = v.pop.down_done
-
-    back = [[v.pop.back00, v.pop.back01], [v.pop.back10, v.pop.back11]]
-    d_keys = back[1][1][1]
-    v.far1 = p.down_y(d_keys[2:].astype(LOW))
-    v.dk1 = d_keys[:2]
     plan = []
     for n in range(2):
         for s in range(2):
             plan += [
                 lambda x, y, c, n=n, s=s: (n, (slice(None), lanes((c ^ s) * 128, 128)), s, n)
             ]
-    v.kv_mine, kv_send = placed(p, plan, back[1][1][2:], [(2, GW, 128)] * 2)
+    v.kv_mine, kv_send = placed(p, plan, back1[2:], [(2, GW, 128)] * 2)
     v.kv_come = p.to_core(kv_send)
-    dq_t = jnp.stack([jnp.concatenate([part[0] for part in row], 1) for row in back])
-    v.gq = dots("btd,bnt->dn", v.first, dq_t).astype(LOW)
-    v.d_first = dots("bnt,dn->btd", dq_t, v.wq)
-    v = sync(v)
+    v.gd = add_all([half(v.gd, p.z, 0, 4), v.pop.gd1, v.pop.gd2, v.pop.gd3])[0]
+    v.gd1, v.go1 = p.to_y(v.gd), p.to_y(v.go)
+    v.dq_t = jnp.stack([back0[0], back1[0]])
+    gq = dots("btd,bnt->dn", v.first, v.dq_t).astype(LOW).reshape(4, 2, 128, GW)
+    plan = []
+    for n, (r, k) in enumerate(RELATIVE):
+        plan += [
+            lambda x, y, c, n=n, r=r, k=k: (
+                0, (full, x ^ r, full, lanes((y ^ k) * 256, 256)), n, (full, full, full),
+            )
+        ]
+    v.parts_q = placed(p, plan, (gq,), [(4, 128, 256)] * 4)
+    v = sync(v)
+    v.found_q = spread(p, v.pop.parts_q)
+    v.gd, v.go = ordered(y, v.gd, v.pop.gd1, 1), ordered(y, v.go, v.pop.go1, 1)
+    v.gd1, v.go1 = p.to_core(v.gd), p.to_core(v.go)
     dk1 = (v.pop.dk1 + v.pop.far1.astype(F32)).astype(LOW).reshape(1, 2 * length, LAT)
     d_latent = jnp.concatenate([v.pop.dk0, dk1])
     gl = dots("btd,btl->dl", v.pop.first, d_latent).astype(LOW).reshape(4, 2, 128, LAT)
     plan = []
     for n, (r, k) in enumerate(RELATIVE):
-        full = slice(None)
         plan += [
             lambda x, y, c, n=n, r=r, k=k: (
-                0, (full, x ^ r, full, lanes((y ^ k) * 256, 256)), n, (full, full, pl.ds(0, 256)),
-            ),
-            lambda x, y, c, n=n, r=r, k=k: (
-                1, (full, x ^ r, full, lanes((y ^ k) * 128, 128)), n, (full, full, pl.ds(384, 128)),
-            ),
+                0, (full, x ^ r, full, lanes((y ^ k) * 128, 128)), n, (full, full, pl.ds(128, 128)),
+            )
         ]
         for s in range(2):
             plan += [
                 lambda x, y, c, n=n, r=r, k=k, s=s: (
-                    2 + s, (y ^ k, full, x ^ r), n, (pl.ds(2 * (c ^ s), 2), full, pl.ds(256, 128)),
+                    1 + s, (y ^ k, full, x ^ r), n, (pl.ds(2 * (c ^ s), 2), full, pl.ds(0, 128)),
                 )
             ]
     kv = [part.reshape(2, 2, 2, 128, 128) for part in (v.pop.kv_mine, v.pop.kv_come)]
-    parts = placed(p, plan, (v.pop.gq.reshape(4, 2, 128, GW), gl, *kv), [(4, 128, 512)] * 4)
-    v.found = spread(p, parts)
-    d_first = v.pop.d_first + dots("btl,dl->btd", d_latent, v.wl)
-    d_first = chip_sum(p, d_first.reshape(batch, 2, length, D))
+    v.found = spread(p, placed(p, plan, (gl, *kv), [(4, 128, 256)] * 4))
+    dq_t = v.pop.dq_t
+
+    def first_grad(i):
+        part = slice(i * length, (i + 1) * length)
+        by_q = dots("bnt,dn->btd", dq_t[:, :, part], v.wq)
+        return by_q + dots("btl,dl->btd", d_latent[:, part], v.wl)
+
+    d_first = summed(p, first_grad)
     own = tokens.astype(F32)
     inverse1 = inverse_rms(own)
     normed1 = own * inverse1
@@ -814,24 +905,25 @@
     v.gg = gg
     v = sync(v)
     grad_tokens = v.pop.tokens_done
+    grad_down = ordered(core, v.pop.gd, v.pop.gd1, 1).astype(F32)
+    grad_output = ordered(core, v.pop.go, v.pop.go1, 1).astype(F32)
     gains = sum(part.astype(F32) for part in v.pop.gains).reshape(2, 4, 2, 128)
     gains = x_own(jnp.moveaxis(gains, 0, 2).reshape(4, 2, 2, 128))[:, 0].astype(LOW)
     gains = jnp.pad(gains, ((0, 0), (0, 6), (0, 384)))
-    v.q = z_scatter(p, jnp.concatenate([add_all(v.pop.found), gains], 1))
+    q = jnp.concatenate([add_all(v.pop.found_q), add_all(v.pop.found)], -1)
+    v.q = z_scatter(p, jnp.concatenate([q, gains], 1))
     v.gg = add_low(v.gg, p.to_y(v.gg))
-    v.go1 = p.to_y(v.go)
-    v = sync(v)
+    v.done = grad_down, grad_output
+    v = sync(v)
+    grad_down, grad_output = v.pop.done
     v.q1 = p.to_y(v.q)
     v.gg1 = p.to_core(v.gg)
-    v.go = ordered(y, v.go, v.pop.go1, 1)
-    v.go1 = p.to_core(v.go)
     v = sync(v)
     q0, q1 = pick(y, v.q, v.q1), pick(y, v.pop.q1, v.pop.q)
     mine = jnp.concatenate([q0, q1], 1)
     other = p.to_core(mine)
     grad_gate = ordered(core, v.gg[:, :ff], v.gg1[:, :ff], 1).astype(F32)
     grad_up = ordered(core, v.gg[:, ff:], v.gg1[:, ff:], 1).astype(F32)
-    grad_output = ordered(core, v.go, v.go1, 1).astype(F32)
     zero, one = pick(core, mine, other), pick(core, other, mine)
 
     def columns(start, width):

time: 484 us -> 411 us (0.85)
  waiting for transfers between devices: 134 us -> 85.3 us
  matrix products: 59.3 us -> 44.8 us
  local copies, waits for them, and re-layouts: 41.1 us -> 28.3 us
  Pallas kernels: 78.2 us -> 89.5 us
  starting transfers between devices: 97.7 us -> 91.2 us
    ppermute x68 -> x71, waiting for transfers between devices: 134 us -> 85.2 us  [send(): return lax.ppermute(value, ALL, self.pairs(move))]
    dot_general x2 -> x0, matrix products: 16.6 us -> none  [nt(): lax.dot_general(left, right, (((1,), (1,)), ((), ())), preferred_element_...]
    pallas_call x4, Pallas kernels: 43.7 us -> 53.7 us  [the longest x2 24.5 us: attention_backward(): pl.pallas_call(lambda *refs: backward_kernel(b, nkb, batch, width, bool(o...]
    unnamed x150 -> x164, local copies, waits for them, and re-layouts: 16.4 us -> 7.93 us
    dot_general x2, matrix products: 12.8 us -> 5.98 us  [mm(): return jnp.dot(left, right, preferred_element_type=F32)]
    ppermute x68 -> x71, starting transfers between devices: 97.6 us -> 91.1 us  [send(): return lax.ppermute(value, ALL, self.pairs(move))]
    dot_general x9 -> x12, matrix products: 16.1 us -> 22 us  [dots(): return jnp.einsum(spec, left, right, preferred_element_type=F32)]
    pallas_call x6 -> x7, Pallas kernels: 18.4 us -> 20.3 us  [placed(): pl.pallas_call(lambda *refs: place_kernel(plan, len(sources), len(shapes)...]
  transfers between devices with their start and end apart: 70 -> 73, of which waited for: 28 -> 18; matrix products, arithmetic and copies ran while one was open for 20% -> 26% of each run, Pallas kernels for 16% -> 19%
where the time goes in v3:
time: 411 us; the launch traced here: 405 us
  starting transfers between devices  91.2 us (22%)
  Pallas kernels  89.5 us (22%)
  waiting for transfers between devices  85.3 us (21%)
  other arithmetic  49.7 us (12%)
  matrix products  44.8 us (11%)
  local copies, waits for them, and re-layouts  28.3 us (7%)
  between operations  16 us (4%)
    ppermute x71, starting transfers between devices, send(): return lax.ppermute(value, ALL, self.pairs(move))  91.1 us
    ppermute x71, waiting for transfers between devices, send(): return lax.ppermute(value, ALL, self.pairs(move))  85.2 us
    pallas_call x2, Pallas kernels, attention_backward(): pl.pallas_call(lambda *refs: backward_kernel(b, nkb, batch, width, bool(o...  24.5 us
    dot_general x12, matrix products, dots(): return jnp.einsum(spec, left, right, preferred_element_type=F32)  22 us
    pallas_call x7, Pallas kernels, placed(): pl.pallas_call(lambda *refs: place_kernel(plan, len(sources), len(shapes)...  20.3 us
    pallas_call x1, Pallas kernels, feed_forward_back(): pl.pallas_call(hidden_back_kernel, grid=(steps,), in_specs=[tiled(cot.sha...  17.3 us
    dot_general x4, matrix products, tn(): lax.dot_general(left, right, (((0,), (0,)), ((), ())), preferred_element_...  16.8 us
    pallas_call x2, Pallas kernels, attention_forward(): pl.pallas_call(lambda *refs: forward_kernel(b, nkb, batch, width, *refs),...  15.5 us
  transfers between devices with their start and end apart: 73, of which 18 were waited for; matrix products, arithmetic and copies ran while one was open for 26% of the time, Pallas kernels for 19%

profile of v3, /device:TPU:0, one launch (start us, length us, event | category | flops | bytes accessed | tf_op | source)
XLA Modules:
  0.0 404.9 jit_solution(159167447531759452)
XLA Ops:
  11.7 2.8 collective-permute-start
  14.5 2.6 collective-permute-start.1
  22.7 8.6 %collective-permute-done.1 = bf16[136,768]{1,0:T(8,128)(2,1)S(1)} collective-permute-done((bf16[136,768]{1,0:T(8,128)(2,1)S(1)}, bf16[136,768]{1,0:T(8,128)(2,1)S(1)}, u32[]{:S(2)}, u32[]{:S(2)}) %collective-permute-start.1) | collective-permute-done | bytes 208928 | tf_op jit(solution)/shard_map/ppermute | solution.py:351
  33.3 2.4 convert_multiply_fusion
  38.8 5.0 %collective-permute-start.6 = (bf16[352,256]{1,0:T(8,128)(2,1)S(1)}, bf16[352,256]{1,0:T(8,128)(2,1)S(1)}, u32[]{:S(2)}, u32[]{:S(2)}) collective-permute-start(bf16[352,256]{1,0:T(8,128)(2,1)S(1)} %copy-done.30), channel_id=1, source_target_pairs={{0,2},{1,3},{2,4},{3,5},{4,6},{5,7},{6,0},{7,1},{8,10},{9,11},{10,... | collective-permute-start | bytes 540680 | tf_op jit(solution)/shard_map/ppermute | solution.py:351
  43.7 7.3 %collective-permute-done.6 = bf16[352,256]{1,0:T(8,128)(2,1)S(1)} collective-permute-done((bf16[352,256]{1,0:T(8,128)(2,1)S(1)}, bf16[352,256]{1,0:T(8,128)(2,1)S(1)}, u32[]{:S(2)}, u32[]{:S(2)}) %collective-permute-start.6) | collective-permute-done | bytes 180256 | tf_op jit(solution)/shard_map/ppermute | solution.py:351
  55.3 4.7 %collective-permute-start.11 = (bf16[352,256]{1,0:T(8,128)(2,1)S(1)}, bf16[352,256]{1,0:T(8,128)(2,1)S(1)}, u32[]{:S(2)}, u32[]{:S(2)}) collective-permute-start(bf16[352,256]{1,0:T(8,128)(2,1)S(1)} %copy-done.30), channel_id=1, source_target_pairs={{0,4},{1,5},{2,6},{3,7},{4,0},{5,1},{6,2},{7,3},{8,12},{9,13},{10,... | collective-permute-start | bytes 540680 | tf_op jit(solution)/shard_map/ppermute | solution.py:351
  61.4 16.1 %collective-permute-done.11 = bf16[352,256]{1,0:T(8,128)(2,1)S(1)} collective-permute-done((bf16[352,256]{1,0:T(8,128)(2,1)S(1)}, bf16[352,256]{1,0:T(8,128)(2,1)S(1)}, u32[]{:S(2)}, u32[]{:S(2)}) %collective-permute-start.11) | collective-permute-done | bytes 180256 | tf_op jit(solution)/shard_map/ppermute | solution.py:351
  78.3 3.5 place.7
  81.9 3.0 multiply_convert_fusion
  88.8 2.6 collective-permute-start.12
  91.4 3.7 collective-permute-start.15
  95.1 2.3 fusion.12.refs_1_
  98.8 3.5 place.8
  102.3 1.9 fusion.58
  104.2 2.1 pad_maximum_fusion.4.refs_4_.refs_8_
  108.2 1.8 collective-permute-start.17
  110.1 7.9 %attention_forward.2 = (bf16[1,512,512]{2,1,0:T(8,128)(2,1)}, f32[1,512,512]{2,1,0:T(8,128)}, bf16[2,256,2048]{2,1,0:T(8,128)(2,1)}, f32[2,1,2048]{2,1,0:T(1,128)}) custom-call(s32[9]{0:T(128)} %concatenate.100.refs_0_, bf16[2,512,512]{2,1,0:T(8,128)(2,1)} %fusion.12.refs_1_, bf16[512,256]{1,0:T(8,128)(2,1)} %bitcast.193, bf16[512,256]{1,0:T(8,128)(2,1)} %bitcast.189, ...), custom_call_target="tpu_custom_call" | custom-call | flops 3758096384 | bytes 8388608 | tf_op jit(solution)/shard_map/attention_forward/pallas_call | solution.py:162
  118.0 6.4 %collective-permute-done.17 = bf16[2,352,256]{2,1,0:T(8,128)(2,1)S(1)} collective-permute-done((bf16[2,352,256]{2,1,0:T(8,128)(2,1)S(1)}, bf16[2,352,256]{2,1,0:T(8,128)(2,1)S(1)}, u32[]{:S(2)}, u32[]{:S(2)}) %collective-permute-start.17) | collective-permute-done | bytes 360480 | tf_op jit(solution)/shard_map/ppermute | solution.py:351
  131.1 7.7 %attention_forward.3 = (bf16[1,512,512]{2,1,0:T(8,128)(2,1)}, f32[1,512,512]{2,1,0:T(8,128)}, bf16[2,256,2048]{2,1,0:T(8,128)(2,1)}, f32[2,1,2048]{2,1,0:T(1,128)}) custom-call(s32[9]{0:T(128)} %concatenate.100.refs_0_, bf16[2,512,512]{2,1,0:T(8,128)(2,1)} %fusion.12.refs_1_, bf16[512,256]{1,0:T(8,128)(2,1)} %bitcast.194, bf16[512,256]{1,0:T(8,128)(2,1)} %bitcast.190, ...), custom_call_target="tpu_custom_call" | custom-call | flops 3758096384 | bytes 8388608 | tf_op jit(solution)/shard_map/attention_forward/pallas_call | solution.py:162
  138.9 3.4 collective-permute-done.19
  146.6 2.8 collective-permute-done.27
  149.4 2.6 multiply_reduce_fusion.2
  158.9 11.9 %feed_forward.1 = (f32[1024,2816]{1,0:T(8,128)}, bf16[1024,1408]{1,0:T(8,128)(2,1)}) custom-call(bf16[1024,1024]{1,0:T(8,128)(2,1)} %pad_maximum_fusion.2.x, bf16[1024,2816]{1,0:T(8,128)(2,1)} %all-gather.2.cloned.1.call-done.w), custom_call_target="tpu_custom_call" | custom-call | flops 5905580032 | bytes 20971520 | tf_op jit(solution)/shard_map/feed_forward/pallas_call | solution.py:291
  170.9 3.5 convolution_convert_fusion.1
  175.8 3.8 place.9
  179.6 2.9 convolution_convert_fusion.2
  182.6 1.8 convolution_convert_fusion.3
  186.0 1.8 collective-permute-start.30
  187.8 17.3 %feed_forward_back.1 = (bf16[1024,2816]{1,0:T(8,128)(2,1)}, f32[512,1024]{1,0:T(8,128)}, bf16[512,1024]{1,0:T(8,128)(2,1)}) custom-call(bf16[1024,1024]{1,0:T(8,128)(2,1)} %copy-done.4, bf16[1408,1024]{1,0:T(8,128)(2,1)} %bitcast.160, bf16[1024,2816]{1,0:T(8,128)(2,1)} %all-gather.2.cloned.1.call-done.w, f32[1024,2816]{1,0:T(8,128)} %get-tuple-element.560.act), custom_call_target="tpu_custom_call" | custom-call | flops 8858370048 | bytes 31457280 | tf_op jit(solution)/shard_map/feed_forward_back/pallas_call | solution.py:311
  214.1 2.2 fusion.53
  216.4 8.6 %convolution_convert_fusion = bf16[1024,2816]{1,0:T(8,128)(2,1)} fusion(bf16[1024,1024]{1,0:T(8,128)(2,1)S(1)} %copy-done.17, bf16[1024,2816]{1,0:T(8,128)(2,1)S(1)} %bitcast.213), kind=kOutput, calls=%fused_computation | convolution fusion | flops 5908463616 | bytes 13631488 | tf_op jit(solution)/shard_map/dot_general | solution.py:31
  228.3 4.2 %convolution_convert_fusion.4 = bf16[512,1024]{1,0:T(8,128)(2,1)S(1)} fusion(bf16[1408,1024]{1,0:T(8,128)(2,1)} %bitcast.161, bf16[1024,1408]{1,0:T(8,128)(2,1)} %get-tuple-element.634), kind=kOutput, calls=%fused_computation.36 | convolution fusion | flops 1476919296 | bytes 5373952 | tf_op jit(solution)/shard_map/dot_general | solution.py:27
  239.4 2.3 fusion.13.refs_2_
  241.7 1.8 convert_add_fusion.2
  244.7 6.2 %collective-permute-done.36 = bf16[1,352,256]{2,1,0:T(8,128)(2,1)S(1)} collective-permute-done((bf16[1,352,256]{2,1,0:T(8,128)(2,1)S(1)}, bf16[1,352,256]{2,1,0:T(8,128)(2,1)S(1)}, u32[]{:S(2)}, u32[]{:S(2)}) %collective-permute-start.36) | collective-permute-done | bytes 180256 | tf_op jit(solution)/shard_map/ppermute | solution.py:351
  251.7 2.3 place.10
  257.6 4.2 %collective-permute-start.39 = (bf16[1,352,256]{2,1,0:T(8,128)(2,1)S(1)}, bf16[1,352,256]{2,1,0:T(8,128)(2,1)S(1)}, u32[]{:S(2)}, u32[]{:S(2)}) collective-permute-start(bf16[1,352,256]{2,1,0:T(8,128)(2,1)S(1)} %constant_dynamic-slice_fusion.9), channel_id=1, source_target_pairs={{0,4},{1,5},{2,6},{3,7},{4,0},{5,1},{6,2},{7,3},{8,12},{9,13},{10,... | collective-permute-start | bytes 540680 | tf_op jit(solution)/shard_map/ppermute | solution.py:351
  261.8 12.0 %attention_backward.2 = (bf16[512,512]{1,0:T(8,128)(2,1)}, f32[4,256,256]{2,1,0:T(8,128)}, f32[512,256]{1,0:T(8,128)}, f32[512,256]{1,0:T(8,128)}) custom-call(s32[9]{0:T(128)} %concatenate.100.refs_0_, bf16[2,512,512]{2,1,0:T(8,128)(2,1)} %fusion.12.refs_1_, bf16[2,512,512]{2,1,0:T(8,128)(2,1)} %fusion.13.refs_2_, ...), custom_call_target="tpu_custom_call" | custom-call | flops 9395240960 | bytes 10485760 | tf_op jit(solution)/shard_map/attention_backward/pallas_call | solution.py:206
  273.8 7.4 %collective-permute-done.39 = bf16[1,352,256]{2,1,0:T(8,128)(2,1)S(1)} collective-permute-done((bf16[1,352,256]{2,1,0:T(8,128)(2,1)S(1)}, bf16[1,352,256]{2,1,0:T(8,128)(2,1)S(1)}, u32[]{:S(2)}, u32[]{:S(2)}) %collective-permute-start.39) | collective-permute-done | bytes 180256 | tf_op jit(solution)/shard_map/ppermute | solution.py:351
  283.7 2.2 collective-permute-start.47
  287.9 12.5 %attention_backward.3 = (bf16[512,512]{1,0:T(8,128)(2,1)}, f32[4,256,256]{2,1,0:T(8,128)}, f32[512,256]{1,0:T(8,128)}, f32[512,256]{1,0:T(8,128)}) custom-call(s32[9]{0:T(128)} %concatenate.100.refs_0_, bf16[2,512,512]{2,1,0:T(8,128)(2,1)} %fusion.12.refs_1_, bf16[2,512,512]{2,1,0:T(8,128)(2,1)} %fusion.13.refs_2_, ...), custom_call_target="tpu_custom_call" | custom-call | flops 9395240960 | bytes 10485760 | tf_op jit(solution)/shard_map/attention_backward/pallas_call | solution.py:206
  300.5 2.3 place.11
  304.1 5.8 %collective-permute-start.49 = (bf16[352,256]{1,0:T(8,128)(2,1)S(1)}, bf16[352,256]{1,0:T(8,128)(2,1)}, u32[]{:S(2)}, u32[]{:S(2)}) collective-permute-start(bf16[352,256]{1,0:T(8,128)(2,1)S(1)} %fusion.43), channel_id=1, source_target_pairs={{0,16},{1,17},{2,18},{3,19},{4,20},{5,21},{6,22},{7,23},{8,24},{9,... | collective-permute-start | bytes 540680 | tf_op jit(solution)/shard_map/ppermute | solution.py:351
  311.2 3.3 collective-permute-start.50
  314.6 3.4 bitcast_convert_fusion
  318.2 2.4 place.12
  323.8 1.8 add_convert_fusion
  328.6 2.4 place.13
  331.0 3.5 collective-permute-start.52
  335.9 1.8 maximum_select_fusion.4
  338.3 2.1 collective-permute-start.55
  340.3 3.8 fusion.5
  344.2 2.8 collective-permute-done.52
  348.3 5.9 %collective-permute-done.54 = bf16[4,128,256]{2,1,0:T(8,128)(2,1)} collective-permute-done((bf16[4,128,256]{2,1,0:T(8,128)(2,1)}, bf16[4,128,256]{2,1,0:T(8,128)(2,1)}, u32[]{:S(2)}, u32[]{:S(2)}) %collective-permute-start.54) | collective-permute-done | bytes 262176 | tf_op jit(solution)/shard_map/ppermute | solution.py:351
  354.2 1.8 collective-permute-start.59
  356.0 4.3 %collective-permute-done.55 = bf16[4,128,256]{2,1,0:T(8,128)(2,1)} collective-permute-done((bf16[4,128,256]{2,1,0:T(8,128)(2,1)}, bf16[4,128,256]{2,1,0:T(8,128)(2,1)}, u32[]{:S(2)}, u32[]{:S(2)}) %collective-permute-start.55) | collective-permute-done | bytes 262176 | tf_op jit(solution)/shard_map/ppermute | solution.py:351
  360.4 1.9 collective-permute-start.61
  362.3 3.5 fusion.8
  373.5 2.8 collective-permute-start.67
  376.4 2.0 fusion.41
  379.6 4.5 %collective-permute-done.66 = bf16[1,136,512]{2,1,0:T(8,128)(2,1)S(1)} collective-permute-done((bf16[1,136,512]{2,1,0:T(8,128)(2,1)S(1)}, bf16[1,136,512]{2,1,0:T(8,128)(2,1)S(1)}, u32[]{:S(2)}, u32[]{:S(2)}) %collective-permute-start.66) | collective-permute-done | bytes 139296 | tf_op jit(solution)/shard_map/ppermute | solution.py:351
  384.9 1.8 collective-permute-start.69
  386.7 4.3 %collective-permute-done.69 = bf16[136,512]{1,0:T(8,128)(2,1)S(1)} collective-permute-done((bf16[136,512]{1,0:T(8,128)(2,1)S(1)}, bf16[136,512]{1,0:T(8,128)(2,1)S(1)}, u32[]{:S(2)}, u32[]{:S(2)}) %collective-permute-start.69) | collective-permute-done | bytes 139296 | tf_op jit(solution)/shard_map/ppermute | solution.py:351
  (399 shorter events, 107.2 us)
Async XLA Ops:
  7.2 151.7 %all-gather.2.cloned.1.call-start = ((), (), s32[]{:S(2)}) async-start(), calls=%async_computation.1 | async-start | bytes 6488064 | tf_op jit(solution)/shard_map/all_gather | solution.py:660
  7.2 24.2 %collective-permute-start.3 = (bf16[2,256,1024]{2,1,0:T(8,128)(2,1)}, bf16[2,256,1024]{2,1,0:T(8,128)(2,1)S(1)}, u32[]{:S(2)}, u32[]{:S(2)}) collective-permute-start(bf16[2,256,1024]{2,1,0:T(8,128)(2,1)} %param.13), channel_id=1, source_target_pairs={{0,8},{1,9},{2,10},{3,11},{4,12},{5,13},{6,14},{7,15},{8,0},{9,1},... | collective-permute-start | bytes 3145736 | tf_op jit(solution)/shard_map/ppermute | solution.py:351
  11.7 11.0 %collective-permute-start = (bf16[136,768]{1,0:T(8,128)(2,1)S(1)}, bf16[136,768]{1,0:T(8,128)(2,1)S(1)}, u32[]{:S(2)}, u32[]{:S(2)}) collective-permute-start(bf16[136,768]{1,0:T(8,128)(2,1)S(1)} %fusion.42), channel_id=1, source_target_pairs={{0,2},{1,3},{2,4},{3,5},{4,6},{5,7},{6,0},{7,1},{8,10},{9,11},{10,... | collective-permute-start | bytes 626696 | tf_op jit(solution)/shard_map/ppermute | solution.py:351
  14.5 16.8 %collective-permute-start.1 = (bf16[136,768]{1,0:T(8,128)(2,1)S(1)}, bf16[136,768]{1,0:T(8,128)(2,1)S(1)}, u32[]{:S(2)}, u32[]{:S(2)}) collective-permute-start(bf16[136,768]{1,0:T(8,128)(2,1)S(1)} %fusion.42), channel_id=1, source_target_pairs={{0,4},{1,5},{2,6},{3,7},{4,0},{5,1},{6,2},{7,3},{8,12},{9,13},{10,... | collective-permute-start | bytes 626696 | tf_op jit(solution)/shard_map/ppermute | solution.py:351
  17.1 14.2 %collective-permute-start.2 = (bf16[136,768]{1,0:T(8,128)(2,1)S(1)}, bf16[136,768]{1,0:T(8,128)(2,1)S(1)}, u32[]{:S(2)}, u32[]{:S(2)}) collective-permute-start(bf16[136,768]{1,0:T(8,128)(2,1)S(1)} %fusion.42), channel_id=1, source_target_pairs={{0,6},{1,7},{2,0},{3,1},{4,2},{5,3},{6,4},{7,5},{8,14},{9,15},{10,... | collective-permute-start | bytes 626696 | tf_op jit(solution)/shard_map/ppermute | solution.py:351
  31.5 335.1 %reduce-scatter.2.cloned.1.call-start = ((), (), s32[]{:S(2)}) async-start(), calls=%async_computation.2 | async-start | bytes 6488064 | tf_op jit(solution)/shard_map/reduce_scatter | solution.py:801
  35.7 15.3 %collective-permute-start.4 = (bf16[4,136,384]{2,1,0:T(8,128)(2,1)}, bf16[4,136,384]{2,1,0:T(8,128)(2,1)S(1)}, u32[]{:S(2)}, u32[]{:S(2)}) collective-permute-start(bf16[4,136,384]{2,1,0:T(8,128)(2,1)} %get-tuple-element.426.refs_1_), channel_id=1, source_target_pairs={{0,1},{1,0},{2,3},{3,2},{4,5},{5,4},{6,7},{7,6},{8,9},{9,8},{10,11... | collective-permute-start | bytes 1253384 | tf_op jit(solution)/shard_map/ppermute | solution.py:351
  37.2 13.8 %collective-permute-start.5 = (bf16[4,136,384]{2,1,0:T(8,128)(2,1)}, bf16[4,136,384]{2,1,0:T(8,128)(2,1)S(1)}, u32[]{:S(2)}, u32[]{:S(2)}) collective-permute-start(bf16[4,136,384]{2,1,0:T(8,128)(2,1)} %get-tuple-element.430.refs_5_), channel_id=1, source_target_pairs={{0,16},{1,17},{2,18},{3,19},{4,20},{5,21},{6,22},{7,23},{8,24},{9,... | collective-permute-start | bytes 1253384 | tf_op jit(solution)/shard_map/ppermute | solution.py:351
  38.8 12.3 %collective-permute-start.6 = (bf16[352,256]{1,0:T(8,128)(2,1)S(1)}, bf16[352,256]{1,0:T(8,128)(2,1)S(1)}, u32[]{:S(2)}, u32[]{:S(2)}) collective-permute-start(bf16[352,256]{1,0:T(8,128)(2,1)S(1)} %copy-done.30), channel_id=1, source_target_pairs={{0,2},{1,3},{2,4},{3,5},{4,6},{5,7},{6,0},{7,1},{8,10},{9,11},{10,... | collective-permute-start | bytes 540680 | tf_op jit(solution)/shard_map/ppermute | solution.py:351
  51.0 26.4 %collective-permute-start.10 = (bf16[4,136,384]{2,1,0:T(8,128)(2,1)S(1)}, bf16[4,136,384]{2,1,0:T(8,128)(2,1)}, u32[]{:S(2)}, u32[]{:S(2)}) collective-permute-start(bf16[4,136,384]{2,1,0:T(8,128)(2,1)S(1)} %collective-permute-done.5.refs_7_), channel_id=1, source_target_pairs={{0,1},{1,0},{2,3},{3,2},{4,5},{5,4},{6,7},{7,6},{8,9},{9,8},{10,11... | collective-permute-start | bytes 1253384 | tf_op jit(solution)/shard_map/ppermute | solution.py:351
  52.5 25.0 %collective-permute-start.7 = (bf16[4,136,384]{2,1,0:T(8,128)(2,1)S(1)}, bf16[4,136,384]{2,1,0:T(8,128)(2,1)}, u32[]{:S(2)}, u32[]{:S(2)}) collective-permute-start(bf16[4,136,384]{2,1,0:T(8,128)(2,1)S(1)} %collective-permute-done.4.refs_2_), channel_id=1, source_target_pairs={{0,16},{1,17},{2,18},{3,19},{4,20},{5,21},{6,22},{7,23},{8,24},{9,... | collective-permute-start | bytes 1253384 | tf_op jit(solution)/shard_map/ppermute | solution.py:351
  53.8 23.7 %collective-permute-start.8 = (bf16[4,136,384]{2,1,0:T(8,128)(2,1)}, bf16[4,136,384]{2,1,0:T(8,128)(2,1)}, u32[]{:S(2)}, u32[]{:S(2)}) collective-permute-start(bf16[4,136,384]{2,1,0:T(8,128)(2,1)} %get-tuple-element.426.refs_1_), channel_id=1, source_target_pairs={{0,16},{1,17},{2,18},{3,19},{4,20},{5,21},{6,22},{7,23},{8,24},{9,... | collective-permute-start | bytes 1253384 | tf_op jit(solution)/shard_map/ppermute | solution.py:351
  54.5 23.0 %collective-permute-start.9 = (bf16[4,136,384]{2,1,0:T(8,128)(2,1)}, bf16[4,136,384]{2,1,0:T(8,128)(2,1)}, u32[]{:S(2)}, u32[]{:S(2)}) collective-permute-start(bf16[4,136,384]{2,1,0:T(8,128)(2,1)} %get-tuple-element.430.refs_5_), channel_id=1, source_target_pairs={{0,1},{1,0},{2,3},{3,2},{4,5},{5,4},{6,7},{7,6},{8,9},{9,8},{10,11... | collective-permute-start | bytes 1253384 | tf_op jit(solution)/shard_map/ppermute | solution.py:351
  55.3 22.2 %collective-permute-start.11 = (bf16[352,256]{1,0:T(8,128)(2,1)S(1)}, bf16[352,256]{1,0:T(8,128)(2,1)S(1)}, u32[]{:S(2)}, u32[]{:S(2)}) collective-permute-start(bf16[352,256]{1,0:T(8,128)(2,1)S(1)} %copy-done.30), channel_id=1, source_target_pairs={{0,4},{1,5},{2,6},{3,7},{4,0},{5,1},{6,2},{7,3},{8,12},{9,13},{10,... | collective-permute-start | bytes 540680 | tf_op jit(solution)/shard_map/ppermute | solution.py:351
  77.5 9.7 %collective-permute-start.16 = (bf16[512,1024]{1,0:T(8,128)(2,1)S(1)}, bf16[512,1024]{1,0:T(8,128)(2,1)}, u32[]{:S(2)}, u32[]{:S(2)}) collective-permute-start(bf16[512,1024]{1,0:T(8,128)(2,1)S(1)} %bitcast.151), channel_id=1, source_target_pairs={{0,8},{1,9},{2,10},{3,11},{4,12},{5,13},{6,14},{7,15},{8,0},{9,1},... | collective-permute-start | bytes 3145736 | tf_op jit(solution)/shard_map/ppermute | solution.py:351
  86.5 10.9 %collective-permute-start.13 = (bf16[4,2,128,256]{3,2,1,0:T(8,128)(2,1)S(1)}, bf16[4,2,128,256]{3,2,1,0:T(8,128)(2,1)S(1)}, u32[]{:S(2)}, u32[]{:S(2)}) collective-permute-start(bf16[4,2,128,256]{3,2,1,0:T(8,128)(2,1)S(1)} %copy-done.72), channel_id=1, source_target_pairs={{0,8},{1,9},{2,10},{3,11},{4,12},{5,13},{6,14},{7,15},{8,0},{9,1},... | collective-permute-start | bytes 1572872 | tf_op jit(solution)/shard_map/ppermute | solution.py:351
  88.6 8.7 %collective-permute-start.14 = (bf16[4,2,128,128]{3,2,1,0:T(8,128)(2,1)S(1)}, bf16[4,2,128,128]{3,2,1,0:T(8,128)(2,1)S(1)}, u32[]{:S(2)}, u32[]{:S(2)}) collective-permute-start(bf16[4,2,128,128]{3,2,1,0:T(8,128)(2,1)S(1)} %copy-done.73), channel_id=1, source_target_pairs={{0,8},{1,9},{2,10},{3,11},{4,12},{5,13},{6,14},{7,15},{8,0},{9,1},... | collective-permute-start | bytes 786440 | tf_op jit(solution)/shard_map/ppermute | solution.py:351
  88.8 15.5 %collective-permute-start.12 = (bf16[2,2,256,256]{3,2,1,0:T(8,128)(2,1)}, bf16[2,2,256,256]{3,2,1,0:T(8,128)(2,1)S(1)}, u32[]{:S(2)}, u32[]{:S(2)}) collective-permute-start(bf16[2,2,256,256]{3,2,1,0:T(8,128)(2,1)} %bitcast.19), channel_id=1, source_target_pairs={{0,16},{1,17},{2,18},{3,19},{4,20},{5,21},{6,22},{7,23},{8,24},{9,... | collective-permute-start | bytes 1572872 | tf_op jit(solution)/shard_map/ppermute | solution.py:351
  91.4 15.7 %collective-permute-start.15 = (bf16[352,256]{1,0:T(8,128)(2,1)S(1)}, bf16[352,256]{1,0:T(8,128)(2,1)S(1)}, u32[]{:S(2)}, u32[]{:S(2)}) collective-permute-start(bf16[352,256]{1,0:T(8,128)(2,1)S(1)} %copy-done.30), channel_id=1, source_target_pairs={{0,6},{1,7},{2,0},{3,1},{4,2},{5,3},{6,4},{7,5},{8,14},{9,15},{10,... | collective-permute-start | bytes 540680 | tf_op jit(solution)/shard_map/ppermute | solution.py:351
  107.2 10.8 %collective-permute-start.18 = (bf16[2,352,256]{2,1,0:T(8,128)(2,1)S(1)}, bf16[2,352,256]{2,1,0:T(8,128)(2,1)S(1)}, u32[]{:S(2)}, u32[]{:S(2)}) collective-permute-start(bf16[2,352,256]{2,1,0:T(8,128)(2,1)S(1)} %pad_maximum_fusion.12), channel_id=1, source_target_pairs={{0,16},{1,17},{2,18},{3,19},{4,20},{5,21},{6,22},{7,23},{8,24},{9,... | collective-permute-start | bytes 1081352 | tf_op jit(solution)/shard_map/ppermute | solution.py:351
  108.2 16.2 %collective-permute-start.17 = (bf16[2,352,256]{2,1,0:T(8,128)(2,1)S(1)}, bf16[2,352,256]{2,1,0:T(8,128)(2,1)S(1)}, u32[]{:S(2)}, u32[]{:S(2)}) collective-permute-start(bf16[2,352,256]{2,1,0:T(8,128)(2,1)S(1)} %pad_maximum_fusion.11), channel_id=1, source_target_pairs={{0,1},{1,0},{2,3},{3,2},{4,5},{5,4},{6,7},{7,6},{8,9},{9,8},{10,11... | collective-permute-start | bytes 1081352 | tf_op jit(solution)/shard_map/ppermute | solution.py:351
  124.5 14.3 %collective-permute-start.20 = (bf16[2,352,256]{2,1,0:T(8,128)(2,1)S(1)}, bf16[2,352,256]{2,1,0:T(8,128)(2,1)S(1)}, u32[]{:S(2)}, u32[]{:S(2)}) collective-permute-start(bf16[2,352,256]{2,1,0:T(8,128)(2,1)S(1)} %get-tuple-element.829), channel_id=1, source_target_pairs={{0,16},{1,17},{2,18},{3,19},{4,20},{5,21},{6,22},{7,23},{8,24},{9,... | collective-permute-start | bytes 1081352 | tf_op jit(solution)/shard_map/ppermute | solution.py:351
  126.0 12.8 %collective-permute-start.21 = (bf16[2,352,256]{2,1,0:T(8,128)(2,1)S(1)}, bf16[2,352,256]{2,1,0:T(8,128)(2,1)S(1)}, u32[]{:S(2)}, u32[]{:S(2)}) collective-permute-start(bf16[2,352,256]{2,1,0:T(8,128)(2,1)S(1)} %get-tuple-element.828), channel_id=1, source_target_pairs={{0,1},{1,0},{2,3},{3,2},{4,5},{5,4},{6,7},{7,6},{8,9},{9,8},{10,11... | collective-permute-start | bytes 1081352 | tf_op jit(solution)/shard_map/ppermute | solution.py:351
  126.6 15.6 %collective-permute-start.19 = (bf16[2,352,256]{2,1,0:T(8,128)(2,1)S(1)}, bf16[2,352,256]{2,1,0:T(8,128)(2,1)S(1)}, u32[]{:S(2)}, u32[]{:S(2)}) collective-permute-start(bf16[2,352,256]{2,1,0:T(8,128)(2,1)S(1)} %collective-permute-done.17), channel_id=1, source_target_pairs={{0,16},{1,17},{2,18},{3,19},{4,20},{5,21},{6,22},{7,23},{8,24},{9,... | collective-permute-start | bytes 1081352 | tf_op jit(solution)/shard_map/ppermute | solution.py:351
  126.9 16.6 %collective-permute-start.22 = (bf16[2,352,256]{2,1,0:T(8,128)(2,1)S(1)}, bf16[2,352,256]{2,1,0:T(8,128)(2,1)S(1)}, u32[]{:S(2)}, u32[]{:S(2)}) collective-permute-start(bf16[2,352,256]{2,1,0:T(8,128)(2,1)S(1)} %collective-permute-done.18), channel_id=1, source_target_pairs={{0,1},{1,0},{2,3},{3,2},{4,5},{5,4},{6,7},{7,6},{8,9},{9,8},{10,11... | collective-permute-start | bytes 1081352 | tf_op jit(solution)/shard_map/ppermute | solution.py:351
  175.6 8.8 %collective-permute-start.29 = (bf16[2,2,352,512]{3,2,0,1:T(8,128)(2,1)}, bf16[2,2,352,512]{3,2,0,1:T(8,128)(2,1)}, u32[]{:S(2)}, u32[]{:S(2)}) collective-permute-start(bf16[2,2,352,512]{3,2,0,1:T(8,128)(2,1)} %copy.47), channel_id=1, source_target_pairs={{0,8},{1,9},{2,10},{3,11},{4,12},{5,13},{6,14},{7,15},{8,0},{9,1},... | collective-permute-start | bytes 4325384 | tf_op jit(solution)/shard_map/ppermute | solution.py:351
  185.6 19.6 %collective-permute-start.31 = (bf16[2,1,352,512]{3,2,0,1:T(8,128)(2,1)S(1)}, bf16[2,1,352,512]{3,2,0,1:T(8,128)(2,1)}, u32[]{:S(2)}, u32[]{:S(2)}) collective-permute-start(bf16[2,1,352,512]{3,2,0,1:T(8,128)(2,1)S(1)} %constant_dynamic-slice_fusion.15), channel_id=1, source_target_pairs={{0,1},{1,0},{2,3},{3,2},{4,5},{5,4},{6,7},{7,6},{8,9},{9,8},{10,11... | collective-permute-start | bytes 2162696 | tf_op jit(solution)/shard_map/ppermute | solution.py:351
  186.0 19.1 %collective-permute-start.30 = (bf16[2,2,352,256]{3,2,0,1:T(8,128)(2,1)S(1)}, bf16[2,2,352,256]{3,2,0,1:T(8,128)(2,1)}, u32[]{:S(2)}, u32[]{:S(2)}) collective-permute-start(bf16[2,2,352,256]{3,2,0,1:T(8,128)(2,1)S(1)} %copy.48), channel_id=1, source_target_pairs={{0,16},{1,17},{2,18},{3,19},{4,20},{5,21},{6,22},{7,23},{8,24},{9,... | collective-permute-start | bytes 2162696 | tf_op jit(solution)/shard_map/ppermute | solution.py:351
  206.9 21.2 %collective-permute-start.35 = (bf16[2,1,352,256]{3,2,0,1:T(8,128)(2,1)S(1)}, bf16[2,1,352,256]{3,2,0,1:T(8,128)(2,1)}, u32[]{:S(2)}, u32[]{:S(2)}) collective-permute-start(bf16[2,1,352,256]{3,2,0,1:T(8,128)(2,1)S(1)} %constant_dynamic-slice_fusion.13), channel_id=1, source_target_pairs={{0,16},{1,17},{2,18},{3,19},{4,20},{5,21},{6,22},{7,23},{8,24},{9,... | collective-permute-start | bytes 1081352 | tf_op jit(solution)/shard_map/ppermute | solution.py:351
  209.9 18.3 %collective-permute-start.34 = (bf16[2,1,352,256]{3,2,0,1:T(8,128)(2,1)}, bf16[2,1,352,256]{3,2,0,1:T(8,128)(2,1)}, u32[]{:S(2)}, u32[]{:S(2)}) collective-permute-start(bf16[2,1,352,256]{3,2,0,1:T(8,128)(2,1)} %constant_dynamic-slice_fusion.14), channel_id=1, source_target_pairs={{0,1},{1,0},{2,3},{3,2},{4,5},{5,4},{6,7},{7,6},{8,9},{9,8},{10,11... | collective-permute-start | bytes 1081352 | tf_op jit(solution)/shard_map/ppermute | solution.py:351
  216.3 8.6 %collective-permute-start.33 = (bf16[2,256,1024]{2,1,0:T(8,128)(2,1)}, bf16[2,256,1024]{2,1,0:T(8,128)(2,1)}, u32[]{:S(2)}, u32[]{:S(2)}) collective-permute-start(bf16[2,256,1024]{2,1,0:T(8,128)(2,1)} %get-tuple-element.804), channel_id=1, source_target_pairs={{0,8},{1,9},{2,10},{3,11},{4,12},{5,13},{6,14},{7,15},{8,0},{9,1},... | collective-permute-start | bytes 3145736 | tf_op jit(solution)/shard_map/ppermute | solution.py:351
  232.5 9.2 %collective-permute-start.38 = (bf16[512,1024]{1,0:T(8,128)(2,1)S(1)}, bf16[512,1024]{1,0:T(8,128)(2,1)S(1)}, u32[]{:S(2)}, u32[]{:S(2)}) collective-permute-start(bf16[512,1024]{1,0:T(8,128)(2,1)S(1)} %convolution_convert_fusion.4), channel_id=1, source_target_pairs={{0,8},{1,9},{2,10},{3,11},{4,12},{5,13},{6,14},{7,15},{8,0},{9,1},... | collective-permute-start | bytes 3145736 | tf_op jit(solution)/shard_map/ppermute | solution.py:351
  235.2 15.7 %collective-permute-start.37 = (bf16[2,2,128,512]{3,2,1,0:T(8,128)(2,1)S(1)}, bf16[2,2,128,512]{3,2,1,0:T(8,128)(2,1)S(1)}, u32[]{:S(2)}, u32[]{:S(2)}) collective-permute-start(bf16[2,2,128,512]{3,2,1,0:T(8,128)(2,1)S(1)} %get-tuple-element.808), channel_id=1, source_target_pairs={{0,8},{1,9},{2,10},{3,11},{4,12},{5,13},{6,14},{7,15},{8,0},{9,1},... | collective-permute-start | bytes 1572872 | tf_op jit(solution)/shard_map/ppermute | solution.py:351
  238.1 12.8 %collective-permute-start.36 = (bf16[1,352,256]{2,1,0:T(8,128)(2,1)S(1)}, bf16[1,352,256]{2,1,0:T(8,128)(2,1)S(1)}, u32[]{:S(2)}, u32[]{:S(2)}) collective-permute-start(bf16[1,352,256]{2,1,0:T(8,128)(2,1)S(1)} %constant_dynamic-slice_fusion.12), channel_id=1, source_target_pairs={{0,2},{1,3},{2,4},{3,5},{4,6},{5,7},{6,0},{7,1},{8,10},{9,11},{10,... | collective-permute-start | bytes 540680 | tf_op jit(solution)/shard_map/ppermute | solution.py:351
  254.0 27.2 %collective-permute-start.40 = (bf16[4,128,256]{2,1,0:T(8,128)(2,1)}, bf16[4,128,256]{2,1,0:T(8,128)(2,1)S(1)}, u32[]{:S(2)}, u32[]{:S(2)}) collective-permute-start(bf16[4,128,256]{2,1,0:T(8,128)(2,1)} %get-tuple-element.666), channel_id=1, source_target_pairs={{0,1},{1,0},{2,3},{3,2},{4,5},{5,4},{6,7},{7,6},{8,9},{9,8},{10,11... | collective-permute-start | bytes 786440 | tf_op jit(solution)/shard_map/ppermute | solution.py:351
  255.1 26.1 %collective-permute-start.41 = (bf16[4,128,256]{2,1,0:T(8,128)(2,1)}, bf16[4,128,256]{2,1,0:T(8,128)(2,1)S(1)}, u32[]{:S(2)}, u32[]{:S(2)}) collective-permute-start(bf16[4,128,256]{2,1,0:T(8,128)(2,1)} %get-tuple-element.667), channel_id=1, source_target_pairs={{0,16},{1,17},{2,18},{3,19},{4,20},{5,21},{6,22},{7,23},{8,24},{9,... | collective-permute-start | bytes 786440 | tf_op jit(solution)/shard_map/ppermute | solution.py:351
  256.3 24.9 %collective-permute-start.42 = (bf16[4,128,256]{2,1,0:T(8,128)(2,1)}, bf16[4,128,256]{2,1,0:T(8,128)(2,1)S(1)}, u32[]{:S(2)}, u32[]{:S(2)}) collective-permute-start(bf16[4,128,256]{2,1,0:T(8,128)(2,1)} %get-tuple-element.668), channel_id=1, source_target_pairs={{0,17},{1,16},{2,19},{3,18},{4,21},{5,20},{6,23},{7,22},{8,25},{9,... | collective-permute-start | bytes 786440 | tf_op jit(solution)/shard_map/ppermute | solution.py:351
  257.6 23.6 %collective-permute-start.39 = (bf16[1,352,256]{2,1,0:T(8,128)(2,1)S(1)}, bf16[1,352,256]{2,1,0:T(8,128)(2,1)S(1)}, u32[]{:S(2)}, u32[]{:S(2)}) collective-permute-start(bf16[1,352,256]{2,1,0:T(8,128)(2,1)S(1)} %constant_dynamic-slice_fusion.9), channel_id=1, source_target_pairs={{0,4},{1,5},{2,6},{3,7},{4,0},{5,1},{6,2},{7,3},{8,12},{9,13},{10,... | collective-permute-start | bytes 540680 | tf_op jit(solution)/shard_map/ppermute | solution.py:351
  282.1 18.3 %collective-permute-start.45 = (bf16[1,128,256]{2,1,0:T(8,128)(2,1)}, bf16[1,128,256]{2,1,0:T(8,128)(2,1)S(1)}, u32[]{:S(2)}, u32[]{:S(2)}) collective-permute-start(bf16[1,128,256]{2,1,0:T(8,128)(2,1)} %get-tuple-element.855), channel_id=1, source_target_pairs={{0,2},{1,3},{2,4},{3,5},{4,6},{5,7},{6,0},{7,1},{8,10},{9,11},{10,... | collective-permute-start | bytes 196616 | tf_op jit(solution)/shard_map/ppermute | solution.py:351
  282.1 18.4 %collective-permute-start.46 = (bf16[1,128,256]{2,1,0:T(8,128)(2,1)}, bf16[1,128,256]{2,1,0:T(8,128)(2,1)S(1)}, u32[]{:S(2)}, u32[]{:S(2)}) collective-permute-start(bf16[1,128,256]{2,1,0:T(8,128)(2,1)} %get-tuple-element.857), channel_id=1, source_target_pairs={{0,4},{1,5},{2,6},{3,7},{4,0},{5,1},{6,2},{7,3},{8,12},{9,13},{10,... | collective-permute-start | bytes 196616 | tf_op jit(solution)/shard_map/ppermute | solution.py:351
  283.7 16.7 %collective-permute-start.47 = (bf16[1,128,256]{2,1,0:T(8,128)(2,1)S(1)}, bf16[1,128,256]{2,1,0:T(8,128)(2,1)S(1)}, u32[]{:S(2)}, u32[]{:S(2)}) collective-permute-start(bf16[1,128,256]{2,1,0:T(8,128)(2,1)S(1)} %get-tuple-element.856), channel_id=1, source_target_pairs={{0,6},{1,7},{2,0},{3,1},{4,2},{5,3},{6,4},{7,5},{8,14},{9,15},{10,... | collective-permute-start | bytes 196616 | tf_op jit(solution)/shard_map/ppermute | solution.py:351
  285.9 14.6 %collective-permute-start.44 = (bf16[1,352,256]{2,1,0:T(8,128)(2,1)S(1)}, bf16[1,352,256]{2,1,0:T(8,128)(2,1)}, u32[]{:S(2)}, u32[]{:S(2)}) collective-permute-start(bf16[1,352,256]{2,1,0:T(8,128)(2,1)S(1)} %constant_dynamic-slice_fusion.8), channel_id=1, source_target_pairs={{0,6},{1,7},{2,0},{3,1},{4,2},{5,3},{6,4},{7,5},{8,14},{9,15},{10,... | collective-permute-start | bytes 540680 | tf_op jit(solution)/shard_map/ppermute | solution.py:351
  286.6 13.9 %collective-permute-start.43 = (bf16[2,256,256]{2,1,0:T(8,128)(2,1)S(1)}, bf16[2,256,256]{2,1,0:T(8,128)(2,1)S(1)}, u32[]{:S(2)}, u32[]{:S(2)}) collective-permute-start(bf16[2,256,256]{2,1,0:T(8,128)(2,1)S(1)} %slice.256), channel_id=1, source_target_pairs={{16,0},{17,1},{18,2},{19,3},{20,4},{21,5},{22,6},{23,7},{24,8},{25... | collective-permute-start | bytes 786440 | tf_op jit(solution)/shard_map/ppermute | solution.py:351
  302.9 19.3 %collective-permute-start.51 = (bf16[2,512,128]{2,1,0:T(8,128)(2,1)}, bf16[2,512,128]{2,1,0:T(8,128)(2,1)S(1)}, u32[]{:S(2)}, u32[]{:S(2)}) collective-permute-start(bf16[2,512,128]{2,1,0:T(8,128)(2,1)} %get-tuple-element.717), channel_id=1, source_target_pairs={{0,8},{1,9},{2,10},{3,11},{4,12},{5,13},{6,14},{7,15},{8,0},{9,1},... | collective-permute-start | bytes 786440 | tf_op jit(solution)/shard_map/ppermute | solution.py:351
  304.1 18.1 %collective-permute-start.49 = (bf16[352,256]{1,0:T(8,128)(2,1)S(1)}, bf16[352,256]{1,0:T(8,128)(2,1)}, u32[]{:S(2)}, u32[]{:S(2)}) collective-permute-start(bf16[352,256]{1,0:T(8,128)(2,1)S(1)} %fusion.43), channel_id=1, source_target_pairs={{0,16},{1,17},{2,18},{3,19},{4,20},{5,21},{6,22},{7,23},{8,24},{9,... | collective-permute-start | bytes 540680 | tf_op jit(solution)/shard_map/ppermute | solution.py:351
  309.9 12.2 %collective-permute-start.48 = (bf16[2,256,256]{2,1,0:T(8,128)(2,1)S(1)}, bf16[2,256,256]{2,1,0:T(8,128)(2,1)}, u32[]{:S(2)}, u32[]{:S(2)}) collective-permute-start(bf16[2,256,256]{2,1,0:T(8,128)(2,1)S(1)} %slice.255), channel_id=1, source_target_pairs={{16,0},{17,1},{18,2},{19,3},{20,4},{21,5},{22,6},{23,7},{24,8},{25... | collective-permute-start | bytes 786440 | tf_op jit(solution)/shard_map/ppermute | solution.py:351
  311.2 10.9 %collective-permute-start.50 = (bf16[128,256]{1,0:T(8,128)(2,1)S(1)}, bf16[128,256]{1,0:T(8,128)(2,1)S(1)}, u32[]{:S(2)}, u32[]{:S(2)}) collective-permute-start(bf16[128,256]{1,0:T(8,128)(2,1)S(1)} %fusion.45), channel_id=1, source_target_pairs={{0,16},{1,17},{2,18},{3,19},{4,20},{5,21},{6,22},{7,23},{8,24},{9,... | collective-permute-start | bytes 196616 | tf_op jit(solution)/shard_map/ppermute | solution.py:351
  325.5 12.7 %collective-permute-start.58 = (bf16[2,256,1024]{2,1,0:T(8,128)(2,1)}, bf16[2,256,1024]{2,1,0:T(8,128)(2,1)}, u32[]{:S(2)}, u32[]{:S(2)}) collective-permute-start(bf16[2,256,1024]{2,1,0:T(8,128)(2,1)} %add_convert_fusion), channel_id=1, source_target_pairs={{0,8},{1,9},{2,10},{3,11},{4,12},{5,13},{6,14},{7,15},{8,0},{9,1},... | collective-permute-start | bytes 3145736 | tf_op jit(solution)/shard_map/ppermute | solution.py:351
  326.5 17.6 %collective-permute-start.63 = (bf16[128,512]{1,0:T(8,128)(2,1)}, bf16[128,512]{1,0:T(8,128)(2,1)}, u32[]{:S(2)}, u32[]{:S(2)}) collective-permute-start(bf16[128,512]{1,0:T(8,128)(2,1)} %maximum_select_fusion.6), channel_id=1, source_target_pairs={{0,8},{1,9},{2,10},{3,11},{4,12},{5,13},{6,14},{7,15},{8,0},{9,1},... | collective-permute-start | bytes 393224 | tf_op jit(solution)/shard_map/ppermute | solution.py:351
  331.0 16.0 %collective-permute-start.52 = (bf16[4,128,256]{2,1,0:T(8,128)(2,1)}, bf16[4,128,256]{2,1,0:T(8,128)(2,1)}, u32[]{:S(2)}, u32[]{:S(2)}) collective-permute-start(bf16[4,128,256]{2,1,0:T(8,128)(2,1)} %get-tuple-element.733), channel_id=1, source_target_pairs={{0,1},{1,0},{2,3},{3,2},{4,5},{5,4},{6,7},{7,6},{8,9},{9,8},{10,11... | collective-permute-start | bytes 786440 | tf_op jit(solution)/shard_map/ppermute | solution.py:351
  334.5 12.6 %collective-permute-start.53 = (bf16[4,128,256]{2,1,0:T(8,128)(2,1)}, bf16[4,128,256]{2,1,0:T(8,128)(2,1)}, u32[]{:S(2)}, u32[]{:S(2)}) collective-permute-start(bf16[4,128,256]{2,1,0:T(8,128)(2,1)} %get-tuple-element.734), channel_id=1, source_target_pairs={{0,16},{1,17},{2,18},{3,19},{4,20},{5,21},{6,22},{7,23},{8,24},{9,... | collective-permute-start | bytes 786440 | tf_op jit(solution)/shard_map/ppermute | solution.py:351
  334.5 19.8 %collective-permute-start.54 = (bf16[4,128,256]{2,1,0:T(8,128)(2,1)}, bf16[4,128,256]{2,1,0:T(8,128)(2,1)}, u32[]{:S(2)}, u32[]{:S(2)}) collective-permute-start(bf16[4,128,256]{2,1,0:T(8,128)(2,1)} %get-tuple-element.735), channel_id=1, source_target_pairs={{0,17},{1,16},{2,19},{3,18},{4,21},{5,20},{6,23},{7,22},{8,25},{9,... | collective-permute-start | bytes 786440 | tf_op jit(solution)/shard_map/ppermute | solution.py:351
  338.3 22.0 %collective-permute-start.55 = (bf16[4,128,256]{2,1,0:T(8,128)(2,1)}, bf16[4,128,256]{2,1,0:T(8,128)(2,1)}, u32[]{:S(2)}, u32[]{:S(2)}) collective-permute-start(bf16[4,128,256]{2,1,0:T(8,128)(2,1)} %get-tuple-element.737), channel_id=1, source_target_pairs={{0,1},{1,0},{2,3},{3,2},{4,5},{5,4},{6,7},{7,6},{8,9},{9,8},{10,11... | collective-permute-start | bytes 786440 | tf_op jit(solution)/shard_map/ppermute | solution.py:351
  344.1 16.3 %collective-permute-start.56 = (bf16[4,128,256]{2,1,0:T(8,128)(2,1)}, bf16[4,128,256]{2,1,0:T(8,128)(2,1)}, u32[]{:S(2)}, u32[]{:S(2)}) collective-permute-start(bf16[4,128,256]{2,1,0:T(8,128)(2,1)} %get-tuple-element.738), channel_id=1, source_target_pairs={{0,16},{1,17},{2,18},{3,19},{4,20},{5,21},{6,22},{7,23},{8,24},{9,... | collective-permute-start | bytes 786440 | tf_op jit(solution)/shard_map/ppermute | solution.py:351
  347.0 18.7 %collective-permute-start.62 = (bf16[352,512]{1,0:T(8,128)(2,1)S(1)}, bf16[352,512]{1,0:T(8,128)(2,1)S(1)}, u32[]{:S(2)}, u32[]{:S(2)}) collective-permute-start(bf16[352,512]{1,0:T(8,128)(2,1)S(1)} %copy-done.26), channel_id=1, source_target_pairs={{0,8},{1,9},{2,10},{3,11},{4,12},{5,13},{6,14},{7,15},{8,0},{9,1},... | collective-permute-start | bytes 1081352 | tf_op jit(solution)/shard_map/ppermute | solution.py:351
  347.0 18.7 %collective-permute-start.57 = (bf16[4,128,256]{2,1,0:T(8,128)(2,1)}, bf16[4,128,256]{2,1,0:T(8,128)(2,1)S(1)}, u32[]{:S(2)}, u32[]{:S(2)}) collective-permute-start(bf16[4,128,256]{2,1,0:T(8,128)(2,1)} %get-tuple-element.739), channel_id=1, source_target_pairs={{0,17},{1,16},{2,19},{3,18},{4,21},{5,20},{6,23},{7,22},{8,25},{9,... | collective-permute-start | bytes 786440 | tf_op jit(solution)/shard_map/ppermute | solution.py:351
  354.2 12.3 %collective-permute-start.59 = (bf16[16,128]{1,0:T(8,128)(2,1)S(1)}, bf16[16,128]{1,0:T(8,128)(2,1)S(1)}, u32[]{:S(2)}, u32[]{:S(2)}) collective-permute-start(bf16[16,128]{1,0:T(8,128)(2,1)S(1)} %convert_element_type.385), channel_id=1, source_target_pairs={{0,1},{1,0},{2,3},{3,2},{4,5},{5,4},{6,7},{7,6},{8,9},{9,8},{10,11... | collective-permute-start | bytes 12296 | tf_op jit(solution)/shard_map/ppermute | solution.py:351
  360.2 6.3 %collective-permute-start.60 = (bf16[16,128]{1,0:T(8,128)(2,1)S(1)}, bf16[16,128]{1,0:T(8,128)(2,1)S(1)}, u32[]{:S(2)}, u32[]{:S(2)}) collective-permute-start(bf16[16,128]{1,0:T(8,128)(2,1)S(1)} %convert_element_type.385), channel_id=1, source_target_pairs={{0,16},{1,17},{2,18},{3,19},{4,20},{5,21},{6,22},{7,23},{8,24},{9,... | collective-permute-start | bytes 12296 | tf_op jit(solution)/shard_map/ppermute | solution.py:351
  360.4 6.1 %collective-permute-start.61 = (bf16[16,128]{1,0:T(8,128)(2,1)S(1)}, bf16[16,128]{1,0:T(8,128)(2,1)S(1)}, u32[]{:S(2)}, u32[]{:S(2)}) collective-permute-start(bf16[16,128]{1,0:T(8,128)(2,1)S(1)} %convert_element_type.385), channel_id=1, source_target_pairs={{0,17},{1,16},{2,19},{3,18},{4,21},{5,20},{6,23},{7,22},{8,25},{9,... | collective-permute-start | bytes 12296 | tf_op jit(solution)/shard_map/ppermute | solution.py:351
  366.6 18.1 %collective-permute-start.64 = (bf16[128,2816]{1,0:T(8,128)(2,1)}, bf16[128,2816]{1,0:T(8,128)(2,1)S(1)}, u32[]{:S(2)}, u32[]{:S(2)}) collective-permute-start(bf16[128,2816]{1,0:T(8,128)(2,1)} %reduce-scatter.2.cloned.1.call-done), channel_id=1, source_target_pairs={{0,16},{1,17},{2,18},{3,19},{4,20},{5,21},{6,22},{7,23},{8,24},{9,... | collective-permute-start | bytes 2162696 | tf_op jit(solution)/shard_map/ppermute | solution.py:351
  371.0 8.7 %collective-permute-start.65 = (bf16[1,136,512]{2,1,0:T(8,128)(2,1)S(1)}, bf16[1,136,512]{2,1,0:T(8,128)(2,1)S(1)}, u32[]{:S(2)}, u32[]{:S(2)}) collective-permute-start(bf16[1,136,512]{2,1,0:T(8,128)(2,1)S(1)} %get-tuple-element.836), channel_id=1, source_target_pairs={{0,2},{1,3},{2,4},{3,5},{4,6},{5,7},{6,0},{7,1},{8,10},{9,11},{10,... | collective-permute-start | bytes 417800 | tf_op jit(solution)/shard_map/ppermute | solution.py:351
  372.5 11.7 %collective-permute-start.66 = (bf16[1,136,512]{2,1,0:T(8,128)(2,1)S(1)}, bf16[1,136,512]{2,1,0:T(8,128)(2,1)S(1)}, u32[]{:S(2)}, u32[]{:S(2)}) collective-permute-start(bf16[1,136,512]{2,1,0:T(8,128)(2,1)S(1)} %get-tuple-element.838), channel_id=1, source_target_pairs={{0,4},{1,5},{2,6},{3,7},{4,0},{5,1},{6,2},{7,3},{8,12},{9,13},{10,... | collective-permute-start | bytes 417800 | tf_op jit(solution)/shard_map/ppermute | solution.py:351
  373.5 10.6 %collective-permute-start.67 = (bf16[1,136,512]{2,1,0:T(8,128)(2,1)S(1)}, bf16[1,136,512]{2,1,0:T(8,128)(2,1)S(1)}, u32[]{:S(2)}, u32[]{:S(2)}) collective-permute-start(bf16[1,136,512]{2,1,0:T(8,128)(2,1)S(1)} %get-tuple-element.837), channel_id=1, source_target_pairs={{0,6},{1,7},{2,0},{3,1},{4,2},{5,3},{6,4},{7,5},{8,14},{9,15},{10,... | collective-permute-start | bytes 417800 | tf_op jit(solution)/shard_map/ppermute | solution.py:351
  384.8 6.2 %collective-permute-start.68 = (bf16[128,2816]{1,0:T(8,128)(2,1)S(1)}, bf16[128,2816]{1,0:T(8,128)(2,1)S(1)}, u32[]{:S(2)}, u32[]{:S(2)}) collective-permute-start(bf16[128,2816]{1,0:T(8,128)(2,1)S(1)} %add_convert_fusion.2), channel_id=1, source_target_pairs={{0,8},{1,9},{2,10},{3,11},{4,12},{5,13},{6,14},{7,15},{8,0},{9,1},... | collective-permute-start | bytes 2162696 | tf_op jit(solution)/shard_map/ppermute | solution.py:351
  (88 other events, 667.4 us)
Sparse Core Ops, SparseCore 0:
  31.6 111.3 all-gather.1
  228.3 136.1 reduce-scatter.1

commit v4 on v3

--- a/solution.py
+++ b/solution.py
@@ -47,8 +47,8 @@
     return jnp.logical_and(k0 <= q0, jnp.logical_not(before))
 
 
-def forward_kernel(b, nkb, batch, width, meta, qt, kxt, vxt, c, o_low, o_full, mix_out, lse_out, q_s, acc, m_s, l_s, p_s):
-    qb = pl.program_id(0)
+def forward_kernel(nkb, batch, width, meta, qt, kxt, vxt, c, o_low, o_full, mix_out, lse_out, q_s, acc, m_s, l_s, p_s):
+    b, qb = pl.program_id(0), pl.program_id(1)
     q0, first, diag = meta[nkb + qb], meta[nkb + 2 + b], meta[nkb + 2 + batch] + qb
     for h in range(GH):
         cols = slice(h * width, (h + 1) * width)
@@ -89,11 +89,11 @@
         rows = slice(h * HD, (h + 1) * HD)
         total = l_s[:, cols]
         mixed = (acc[:, cols] * (1.0 / total)).astype(LOW)
-        mix_out[0, :, cols] = mixed
+        mix_out[0, 0, :, cols] = mixed
         out = mm(vxt[rows, :], mixed)
         o_full[0, rows, :] = out
         o_low[0, rows, :] = out.astype(LOW)
-        lse_out[0, :, cols] = m_s[:, cols] + jnp.log(total) * LOG2E
+        lse_out[0, 0, :, cols] = m_s[:, cols] + jnp.log(total) * LOG2E
 
 
 def backward_kernel(
@@ -133,7 +133,7 @@
             for h in range(GH):
                 cols = slice(h * width, (h + 1) * width)
                 s = mm(keys, q_s[:, cols]) + bias
-                p = jnp.exp2(s - lse[0, :, cols])
+                p = jnp.exp2(s - lse[0, 0, :, cols])
                 dp = mm(keys, do_t[:, cols])
                 ds = (p * (dp - delta[:, cols])).astype(LOW)
                 p_s[:, cols] = p.astype(LOW)
@@ -150,36 +150,36 @@
         dq_low = (dq[:, cols] * SCALE).astype(LOW)
         dqt[rows, :] = mm(kxt[rows, :], dq_low).astype(LOW)
         dkxt[rows, :] += nt(qt[0, rows, :], dq_low)
-        dvxt[rows, :] += nt(dot_[0, rows, :], mix[0, :, cols])
-
-
-def attention_forward(b, meta, qt, kxt, vxt, c):
+        dvxt[rows, :] += nt(dot_[0, rows, :], mix[0, 0, :, cols])
+
+
+def attention_forward(meta, qt, kxt, vxt, c):
     batch, nkb, width, _ = c.shape
     wide = GH * width
-    pairs = 7 * GH * width * width * LAT
-    expand = pl.BlockSpec((GW, LAT), lambda q: (0, 0))
-    out_spec = pl.BlockSpec((1, GW, width), lambda q: (0, 0, q))
+    pairs = batch * 7 * GH * width * width * LAT
+    expand = pl.BlockSpec((GW, LAT), lambda b, q: (0, 0))
+    q_spec = pl.BlockSpec((1, GW, width), lambda b, q: (b, 0, q))
     return pl.pallas_call(
-        lambda *refs: forward_kernel(b, nkb, batch, width, *refs),
-        grid=(2,),
+        lambda *refs: forward_kernel(nkb, batch, width, *refs),
+        grid=(batch, 2),
         in_specs=[
             pl.BlockSpec(memory_space=pltpu.SMEM),
-            pl.BlockSpec((1, GW, width), lambda q: (b, 0, q)),
+            q_spec,
             expand,
             expand,
-            pl.BlockSpec((1, nkb, width, LAT), lambda q: (b, 0, 0, 0)),
+            pl.BlockSpec((1, nkb, width, LAT), lambda b, q: (b, 0, 0, 0)),
         ],
         out_specs=[
-            out_spec,
-            out_spec,
-            pl.BlockSpec((1, LAT, wide), lambda q: (q, 0, 0)),
-            pl.BlockSpec((1, 1, wide), lambda q: (q, 0, 0)),
+            q_spec,
+            q_spec,
+            pl.BlockSpec((1, 1, LAT, wide), lambda b, q: (b, q, 0, 0)),
+            pl.BlockSpec((1, 1, 1, wide), lambda b, q: (b, q, 0, 0)),
         ],
         out_shape=[
-            jax.ShapeDtypeStruct((1, GW, 2 * width), LOW),
-            jax.ShapeDtypeStruct((1, GW, 2 * width), F32),
-            jax.ShapeDtypeStruct((2, LAT, wide), LOW),
-            jax.ShapeDtypeStruct((2, 1, wide), F32),
+            jax.ShapeDtypeStruct(qt.shape, LOW),
+            jax.ShapeDtypeStruct(qt.shape, F32),
+            jax.ShapeDtypeStruct((batch, 2, LAT, wide), LOW),
+            jax.ShapeDtypeStruct((batch, 2, 1, wide), F32),
         ],
         scratch_shapes=[
             pltpu.VMEM((LAT, wide), LOW),
@@ -189,10 +189,10 @@
             pltpu.VMEM((width, wide), LOW),
         ],
         compiler_params=pltpu.CompilerParams(
-            dimension_semantics=("arbitrary",), vmem_limit_bytes=VMEM_LIMIT
+            dimension_semantics=("arbitrary", "arbitrary"), vmem_limit_bytes=VMEM_LIMIT
         ),
         cost_estimate=pl.CostEstimate(
-            flops=4 * pairs, bytes_accessed=8 << 20, transcendentals=7 * GH * width * width
+            flops=4 * pairs, bytes_accessed=16 << 20, transcendentals=batch * 7 * GH * width * width
         ),
         name="attention_forward",
     )(meta, qt, kxt, vxt, c)
@@ -210,9 +210,9 @@
             pl.BlockSpec(memory_space=pltpu.SMEM),
             pl.BlockSpec((1, GW, width), lambda q: (b, 0, q)),
             pl.BlockSpec((1, GW, width), lambda q: (b, 0, q)),
-            pl.BlockSpec((1, GW, width), lambda q: (0, 0, q)),
-            pl.BlockSpec((1, LAT, wide), lambda q: (q, 0, 0)),
-            pl.BlockSpec((1, 1, wide), lambda q: (q, 0, 0)),
+            pl.BlockSpec((1, GW, width), lambda q: (b, 0, q)),
+            pl.BlockSpec((1, 1, LAT, wide), lambda q: (b, q, 0, 0)),
+            pl.BlockSpec((1, 1, 1, wide), lambda q: (b, q, 0, 0)),
             expand,
             expand,
             pl.BlockSpec((1, nkb, width, LAT), lambda q: (b, 0, 0, 0)),
@@ -483,11 +483,7 @@
     ).reshape(-1)
     diag = (2 * p.chip).astype(jnp.int32).reshape(1)
     meta = jnp.concatenate([key_starts, base + starts, firsts, diag]).astype(jnp.int32)
-    att = [
-        attention_forward(b, meta, query_t, w["key_t"], w["value_t"], keys)
-        for b in range(batch)
-    ]
-    out_low = jnp.concatenate([a[0] for a in att])
+    out_low, *att = attention_forward(meta, query_t, w["key_t"], w["value_t"], keys)
     branch = dots("bnt,nd->btd", out_low, w["output"])
     middle = tokens.astype(F32) + chip_sum(p, branch.reshape(batch, 2, length, D))
     inverse2 = inverse_rms(middle)
@@ -516,7 +512,7 @@
     d_queries, d_keys, sums = [], [], ()
     for b in range(batch):
         found = attention_backward(
-            b, meta, query_t, d_out_t, *att[b][1:], w["key_t"], w["value_t"], keys, sums
+            b, meta, query_t, d_out_t, *att, w["key_t"], w["value_t"], keys, sums
         )
         sums = found[2:]
         d_queries.append(found[0])
@@ -607,7 +603,15 @@
     spot = where[0], where[1], where[2]
     for make in plan:
         source, there, out, here = make(*spot)
-        dst[out][here] = src[source][there].astype(LOW)
+        if isinstance(source, int):
+            dst[out][here] = src[source][there].astype(LOW)
+            continue
+        flag, sides = source[0], source[1:]
+        for value in range(2):
+
+            @pl.when(flag == value)
+            def _(side=sides[value], there=there, out=out, here=here):
+                dst[out][here] = src[side][there].astype(LOW)
 
 
 def placed(p, plan, sources, shapes):
@@ -657,7 +661,6 @@
     v.pgu = jnp.concatenate([cols(gate_weight, 2, core), cols(up_weight, 2, core)], 1)
     v.tok = p.to_core(tokens)
     v = sync(v)
-    w_gu = lax.all_gather(v.pop.pgu, "dp", axis=0, tiled=True)
     kv = half(pick(y, key_expand, value_expand), core, 0).astype(LOW).T
     gains = jnp.stack([attn_gain, mlp_gain] + [jnp.zeros_like(attn_gain)] * 6).astype(LOW)
     piece = [
@@ -675,13 +678,14 @@
     v = sync(v)
 
     v.ax, v.by = p.to_x(v.a), p.to_y(v.b)
-    v.zd1 = p.to_z(v.pd, 1)
+    w_gu = lax.all_gather(v.pop.pgu, "dp", axis=0, tiled=True)
     v = sync(v)
     v.zd2 = p.to_z(v.pd, 2)
     v.ay, v.axy = p.to_y(v.a), p.to_y(v.ax)
     v.bx, v.bxy = p.to_x(v.b), p.to_x(v.by)
     v = sync(v)
 
+    v.zd1 = p.to_z(v.pd, 1)
     v.from_ab = (v.pop.a, v.pop.ax, v.pop.ay, v.pop.axy, v.pop.b, v.pop.bx, v.pop.by, v.pop.bxy)
     plan = []
     for n, (r, k) in enumerate(RELATIVE):
@@ -737,26 +741,16 @@
     v.keys = jnp.concatenate([v.keys, far_keys], axis=1)
     v = sync(v)
 
-    def forward(b):
-        return attention_forward(b, v.meta, v.qt, v.kxt, v.vxt, v.keys)
-
+    v.cot = core_first(p, cotangent.reshape(count // 2, D))
     v.zd = in_z(p, [v.pop.pd, v.pop.zd1, v.pop.zd2, v.pop.zd3])
     v.dax, v.dby = p.to_x(v.zd[:2]), p.to_y(v.zd[2:])
-    v.cot = core_first(p, cotangent.reshape(count // 2, D))
-    v.att0 = forward(0)
-    v = sync(v)
+    cot = half(v.cot, core, 1)
+    v.cot_c = [half(cot, i, 1) for i in (y, 1 - y)] + [half(v.cot, 1 - core, 1)]
+    v.out, *v.att = attention_forward(v.meta, v.qt, v.kxt, v.vxt, v.keys)
+    v = sync(v)
+
     v.day, v.daxy = p.to_y(v.zd[:2]), p.to_y(v.dax)
     v.dbx, v.dbxy = p.to_x(v.zd[2:]), p.to_x(v.dby)
-    cot = half(v.cot, core, 1)
-    v.cot_c = [half(cot, i, 1) for i in (y, 1 - y)] + [half(v.cot, 1 - core, 1)]
-    v.att1 = forward(1)
-    v = sync(v)
-
-    front, back = v.zd[:2], v.pop.zd[2:]
-    fronts, backs = [front, v.pop.dax, v.pop.day, v.pop.daxy], [back, v.pop.dbx, v.pop.dby, v.pop.dbxy]
-    mine = [pick(core, front, back) for front, back in zip(fronts, backs)]
-    v.down = mine + [p.to_core(pick(core, back, front)) for front, back in zip(fronts, backs)]
-    v.out = jnp.concatenate([v.att0[0], v.att1[0]])
     branch = summed(
         p, lambda i: dots("bnt,nd->btd", v.out[:, :, i * length : (i + 1) * length], v.wo)
     )
@@ -766,31 +760,30 @@
     v.second = core_first(p, second.astype(LOW).reshape(count // 2, D))
     v = sync(v)
 
+    front, back = v.zd[:2], v.pop.zd[2:]
+    sides = (front, v.pop.dax, v.pop.day, v.pop.daxy, back, v.pop.dbx, v.pop.dby, v.pop.dbxy)
+    whole = slice(None)
+    plan = [lambda x, y, c, n=n: ((c, 4 + n, n), whole, 0, n) for n in range(4)]
+    v.come = p.to_core(placed(p, plan, sides, [(4, 2, ff // 4, 256)])[0])
+    v.sides = sides
     v.w_gu = w_gu
     v.act, v.hidden = feed_forward(v.second, v.w_gu)
-    cot_y, cot_far, cot_core = v.pop.cot_c
-    v.gd_b = p.to_core(tn(v.hidden, cot_core).astype(LOW).reshape(2, 2, -1, 512))
-    v.gd_a = tn(v.hidden, cot_y).astype(LOW).reshape(2, 2, -1, 256)
-    v.gd_ay = tn(v.hidden, cot_far).astype(LOW).reshape(2, 2, -1, 256)
+    v = sync(v)
     plan = []
     for n, (r, k) in enumerate(RELATIVE):
         for s in range(2):
             plan += [
                 lambda x, y, c, n=n, r=r, k=k, s=s: (
-                    4 * s + n, slice(None), 0,
-                    (slice(None), x ^ r, slice(None), lanes(((c ^ s) * 2 + (y ^ k)) * 256, 256)),
+                    ((c, n, 4 + n), whole) if s == 0 else (8, n)
+                ) + (
+                    0, (whole, x ^ r, whole, lanes(((c ^ s) * 2 + (y ^ k)) * 256, 256)),
                 )
             ]
-    wd = placed(p, plan, v.pop.down, [(2, 2, ff // 4, D)])[0]
+    wd = placed(p, plan, (*v.pop.sides, v.pop.come), [(2, 2, ff // 4, D)])[0]
     v.wd = wd.reshape(ff, D)
-    v = sync(v)
-
-    v.gd_ay, v.gd_bx = p.to_y(v.gd_ay), p.to_x(x_other(v.gd_b))
+
     v.d_gu, v.ds_own, v.ds_other = feed_forward_back(v.cot, v.wd, v.pop.w_gu, v.pop.act)
     v = sync(v)
-    v.gd_a = add_low(v.gd_a, v.pop.gd_ay)
-    v.gd_b = add_low(x_own(v.gd_b), v.pop.gd_bx)
-    v.gd_ax, v.gd_by = p.to_x(x_other(v.gd_a)), p.to_y(half(v.gd_b, 1 - y, 3))
     d_second = (v.pop.ds_own + p.to_core(v.pop.ds_other).astype(F32)).reshape(batch, length, D)
     v.gg = tn(v.pop.second, v.pop.d_gu).astype(LOW)
     normed2 = v.middle * v.inv2
@@ -799,45 +792,36 @@
     v.d_a = chip(p, v.d_middle.astype(LOW)).reshape(batch, 2 * length, D)
     v = sync(v)
     gg = lax.psum_scatter(v.pop.gg, "dp", scatter_dimension=0, tiled=True)
-    gd_a = add_low(x_own(v.pop.gd_a), v.pop.gd_ax)[:, 0]
-    gd_b = add_low(half(v.pop.gd_b, y, 3), v.pop.gd_by)[:, 0]
-    v.gd = ordered(core, gd_a, gd_b, 0)
-
-    def gd_step(k):
-        return p.to_z(half(v.gd, (p.z + k) % 4, 0, 4), k)
-
-    v.gd1 = gd_step(1)
     go = dots("bnt,btd->nd", v.pop.out, v.d_a).astype(LOW).reshape(2, 2, 128, D)
-    v.go_a, v.go_b = half(go, core, 3), p.to_core(half(go, 1 - core, 3))
+    go_core = half(go, core, 3)
+    go_parts = [half(go_core, y, 3), half(go_core, 1 - y, 3), half(go, 1 - core, 3)]
+    gd_parts = [tn(v.hidden, part).astype(LOW) for part in v.pop.cot_c]
+    v.r_a, v.r_ay, r_send = [
+        jnp.concatenate([gd.reshape(2, 2, -1, gd.shape[-1]), go], 2)
+        for gd, go in zip(gd_parts, go_parts)
+    ]
+    v.r_b = p.to_core(r_send)
+    v.dot = dots("nd,btd->bnt", v.pop.wo, v.pop.d_a).astype(LOW)
+    v = sync(v)
+
+    full = slice(None)
     rows = count // 2
     branch = summed(p, lambda i: mm(v.hidden[i * rows : (i + 1) * rows], v.wd))
     v.out_done = (v.pop.middle + branch.reshape(batch, length, D)).astype(LOW)
     del v.hidden, v.wd
-    v.dot = dots("nd,btd->bnt", v.pop.wo, v.pop.d_a).astype(LOW)
+    v.r_ay, v.r_bx = p.to_y(v.r_ay), p.to_x(x_other(v.r_b))
+    v.back0 = attention_backward(
+        0, v.meta, v.qt, v.dot, *v.att, v.kxt, v.vxt, v.keys, ()
+    )
     v = sync(v)
     layer_out = v.pop.out_done
-
-    full = slice(None)
-    v.gd2 = gd_step(2)
-    plan = []
-    for n, (r, k) in enumerate(RELATIVE):
-        for s in range(2):
-            plan += [
-                lambda x, y, c, n=n, r=r, k=k, s=s: (
-                    s, (full, x ^ r, full, lanes((y ^ k) * 256, 256)), n, pl.ds(2 * (c ^ s), 2),
-                )
-            ]
-    v.go = spread(p, placed(p, plan, (v.pop.go_a, v.pop.go_b), [(4, 128, 256)] * 4))
-    v.back0 = attention_backward(
-        0, v.meta, v.qt, v.dot, *v.att0[1:], v.kxt, v.vxt, v.keys, ()
-    )
-    v = sync(v)
-    v.gd3 = gd_step(3)
-    v.go = z_scatter(p, add_all(v.go))
+    v.r_a = add_low(v.r_a, v.pop.r_ay)
+    v.r_b = add_low(x_own(v.r_b), v.pop.r_bx)
+    v.r_ax, v.r_by = p.to_x(x_other(v.r_a)), p.to_y(half(v.r_b, 1 - y, 3))
     d_keys = v.back0[1]
     v.dk0, v.dk_far0 = d_keys[:2], p.down_y(d_keys[2:].astype(LOW))
     v.back1 = attention_backward(
-        1, v.meta, v.qt, v.dot, *v.att1[1:], v.kxt, v.vxt, v.keys, v.back0[2:]
+        1, v.meta, v.qt, v.dot, *v.att, v.kxt, v.vxt, v.keys, v.back0[2:]
     )
     v = sync(v)
 
@@ -853,22 +837,17 @@
             ]
     v.kv_mine, kv_send = placed(p, plan, back1[2:], [(2, GW, 128)] * 2)
     v.kv_come = p.to_core(kv_send)
-    v.gd = add_all([half(v.gd, p.z, 0, 4), v.pop.gd1, v.pop.gd2, v.pop.gd3])[0]
-    v.gd1, v.go1 = p.to_y(v.gd), p.to_y(v.go)
+    r_a = add_low(x_own(v.pop.r_a), v.pop.r_ax)[:, 0]
+    r_b = add_low(half(v.pop.r_b, y, 3), v.pop.r_by)[:, 0]
+    v.r = ordered(core, r_a, r_b, 0)
+
+    def r_step(k):
+        return p.to_z(half(v.r, (p.z + k) % 4, 0, 4), k)
+
     v.dq_t = jnp.stack([back0[0], back1[0]])
-    gq = dots("btd,bnt->dn", v.first, v.dq_t).astype(LOW).reshape(4, 2, 128, GW)
-    plan = []
-    for n, (r, k) in enumerate(RELATIVE):
-        plan += [
-            lambda x, y, c, n=n, r=r, k=k: (
-                0, (full, x ^ r, full, lanes((y ^ k) * 256, 256)), n, (full, full, full),
-            )
-        ]
-    v.parts_q = placed(p, plan, (gq,), [(4, 128, 256)] * 4)
-    v = sync(v)
-    v.found_q = spread(p, v.pop.parts_q)
-    v.gd, v.go = ordered(y, v.gd, v.pop.gd1, 1), ordered(y, v.go, v.pop.go1, 1)
-    v.gd1, v.go1 = p.to_core(v.gd), p.to_core(v.go)
+    v.gq = dots("btd,bnt->dn", v.first, v.dq_t).astype(LOW).reshape(4, 2, 128, GW)
+    v = sync(v)
+    v.r1, v.r2, v.r3 = r_step(1), r_step(2), r_step(3)
     dk1 = (v.pop.dk1 + v.pop.far1.astype(F32)).astype(LOW).reshape(1, 2 * length, LAT)
     d_latent = jnp.concatenate([v.pop.dk0, dk1])
     gl = dots("btd,btl->dl", v.pop.first, d_latent).astype(LOW).reshape(4, 2, 128, LAT)
@@ -876,17 +855,20 @@
     for n, (r, k) in enumerate(RELATIVE):
         plan += [
             lambda x, y, c, n=n, r=r, k=k: (
-                0, (full, x ^ r, full, lanes((y ^ k) * 128, 128)), n, (full, full, pl.ds(128, 128)),
-            )
+                0, (full, x ^ r, full, lanes((y ^ k) * 256, 256)), n, (full, full, pl.ds(0, 256)),
+            ),
+            lambda x, y, c, n=n, r=r, k=k: (
+                1, (full, x ^ r, full, lanes((y ^ k) * 128, 128)), n, (full, full, pl.ds(384, 128)),
+            ),
         ]
         for s in range(2):
             plan += [
                 lambda x, y, c, n=n, r=r, k=k, s=s: (
-                    1 + s, (y ^ k, full, x ^ r), n, (pl.ds(2 * (c ^ s), 2), full, pl.ds(0, 128)),
+                    2 + s, (y ^ k, full, x ^ r), n, (pl.ds(2 * (c ^ s), 2), full, pl.ds(256, 128)),
                 )
             ]
     kv = [part.reshape(2, 2, 2, 128, 128) for part in (v.pop.kv_mine, v.pop.kv_come)]
-    v.found = spread(p, placed(p, plan, (gl, *kv), [(4, 128, 256)] * 4))
+    v.found = spread(p, placed(p, plan, (v.pop.gq, gl, *kv), [(4, 128, 512)] * 4))
     dq_t = v.pop.dq_t
 
     def first_grad(i):
@@ -899,31 +881,32 @@
     inverse1 = inverse_rms(own)
     normed1 = own * inverse1
     gains = jnp.stack([jnp.sum(d_first * normed1, axis=(0, 1)), v.pop.gain2_sum])
-    gains = gains.astype(LOW).reshape(16, 128)
-    v.gains = spread(p, [gains] * 4)
+    v.gains = gains.astype(LOW).reshape(2, 4, 2, 128)
     v.tokens_done = v.d_middle + norm_back(d_first, normed1, inverse1, v.gain1)
+    v = sync(v)
+    grad_tokens = v.pop.tokens_done
+    v.r = add_all([half(v.r, p.z, 0, 4), v.pop.r1, v.pop.r2, v.pop.r3])[0]
+    gains = jnp.moveaxis(v.pop.gains, 0, 1).reshape(4, 4, 128)
+    gains = jnp.pad(gains, ((0, 0), (0, 4), (0, 384)))
+    v.q = z_scatter(p, jnp.concatenate([add_all(v.pop.found), gains], 1))
     v.gg = gg
-    v = sync(v)
-    grad_tokens = v.pop.tokens_done
-    grad_down = ordered(core, v.pop.gd, v.pop.gd1, 1).astype(F32)
-    grad_output = ordered(core, v.pop.go, v.pop.go1, 1).astype(F32)
-    gains = sum(part.astype(F32) for part in v.pop.gains).reshape(2, 4, 2, 128)
-    gains = x_own(jnp.moveaxis(gains, 0, 2).reshape(4, 2, 2, 128))[:, 0].astype(LOW)
-    gains = jnp.pad(gains, ((0, 0), (0, 6), (0, 384)))
-    q = jnp.concatenate([add_all(v.pop.found_q), add_all(v.pop.found)], -1)
-    v.q = z_scatter(p, jnp.concatenate([q, gains], 1))
     v.gg = add_low(v.gg, p.to_y(v.gg))
-    v.done = grad_down, grad_output
-    v = sync(v)
-    grad_down, grad_output = v.pop.done
+    v = sync(v)
     v.q1 = p.to_y(v.q)
-    v.gg1 = p.to_core(v.gg)
-    v = sync(v)
-    q0, q1 = pick(y, v.q, v.q1), pick(y, v.pop.q1, v.pop.q)
-    mine = jnp.concatenate([q0, q1], 1)
-    other = p.to_core(mine)
+    v.gg1, v.r1 = p.to_core(v.gg), p.to_y(v.r)
+    v = sync(v)
     grad_gate = ordered(core, v.gg[:, :ff], v.gg1[:, :ff], 1).astype(F32)
     grad_up = ordered(core, v.gg[:, ff:], v.gg1[:, ff:], 1).astype(F32)
+    r = ordered(y, v.r, v.r1, 1)
+    grad_rows = ordered(core, r, p.to_core(r), 1).astype(F32)
+    grad_down, grad_output = grad_rows[: ff // 4], grad_rows[ff // 4 :]
+    gains = add_low(v.q[128:132, :128], v.q1[128:132, :128])
+    x_gains = p.to_x(gains)
+    q0, q1 = pick(y, v.q, v.q1), pick(y, v.q1, v.q)
+    mine = jnp.concatenate([q0, q1], 1)
+    mine = lax.dynamic_update_slice(mine, gains, (128, 0))
+    other = p.to_core(mine)
+    x_other_gains = p.send(gains, lambda s, d: (s ^ 1, d ^ 1))
     zero, one = pick(core, mine, other), pick(core, other, mine)
 
     def columns(start, width):
@@ -933,7 +916,10 @@
     def expand_grad(start):
         return jnp.concatenate([p_[:128, start : start + 128] for p_ in (zero, one)], 1)
 
-    gains = mine[128:130, :128].astype(F32) + other[128:130, :128].astype(F32)
+    near_gains = pick(x, gains, x_gains).astype(F32) + pick(x, x_gains, gains).astype(F32)
+    far = other[128:132, :128]
+    far_gains = pick(x, far, x_other_gains).astype(F32) + pick(x, x_other_gains, far).astype(F32)
+    gains = half((near_gains + far_gains).reshape(2, 2, 128), x, 1)[:, 0]
     return (
         layer_out, grad_tokens, gains[0], columns(0, 256), columns(384, 128),
         expand_grad(256).T.astype(F32), expand_grad(768).T.astype(F32), grad_output, gains[1],

time: 411 us -> 411 us (level)
  waiting for transfers between devices: 85.3 us -> 138 us
  starting transfers between devices: 91.2 us -> 54.1 us
  other arithmetic: 49.7 us -> 40 us
  matrix products: 44.8 us -> 39.3 us
    ppermute x71 -> x55, waiting for transfers between devices: 85.2 us -> 129 us  [send(): return lax.ppermute(value, ALL, self.pairs(move))]
    ppermute x71 -> x55, starting transfers between devices: 91.1 us -> 54 us  [send(): return lax.ppermute(value, ALL, self.pairs(move))]
    reduce_scatter x1, waiting for transfers between devices: 0.01 us -> 9.42 us  [square_layer(): gg = lax.psum_scatter(v.pop.gg, 'dp', scatter_dimension=0, tiled=True)]
    unnamed x164 -> x116, local copies, waits for them, and re-layouts: 7.93 us -> 11.4 us
    pallas_call x2 -> x1, Pallas kernels: 15.5 us -> 12.8 us  [attention_forward(): pl.pallas_call(lambda *refs: forward_kernel(nkb, batch, width, *refs), gr...]
    pallas_call x7 -> x6, Pallas kernels: 20.3 us -> 19.8 us  [placed(): pl.pallas_call(lambda *refs: place_kernel(plan, len(sources), len(shapes)...]
  transfers between devices with their start and end apart: 73 -> 57, of which waited for: 18 -> 26; matrix products, arithmetic and copies ran while one was open for 26% -> 20% of each run, Pallas kernels for 19% -> 16%
where the time goes in v4:
time: 411 us; the launch traced here: 404 us
  waiting for transfers between devices  138 us (34%)
  Pallas kernels  85.9 us (21%)
  starting transfers between devices  54.1 us (13%)
  other arithmetic  40 us (10%)
  matrix products  39.3 us (10%)
  local copies, waits for them, and re-layouts  31.2 us (8%)
  between operations  15.4 us (4%)
    ppermute x55, waiting for transfers between devices, send(): return lax.ppermute(value, ALL, self.pairs(move))  129 us
    ppermute x55, starting transfers between devices, send(): return lax.ppermute(value, ALL, self.pairs(move))  54 us
    pallas_call x2, Pallas kernels, attention_backward(): pl.pallas_call(lambda *refs: backward_kernel(b, nkb, batch, width, bool(o...  24.3 us
    pallas_call x6, Pallas kernels, placed(): pl.pallas_call(lambda *refs: place_kernel(plan, len(sources), len(shapes)...  19.8 us
    dot_general x12, matrix products, dots(): return jnp.einsum(spec, left, right, preferred_element_type=F32)  18.6 us
    pallas_call x1, Pallas kernels, feed_forward_back(): pl.pallas_call(hidden_back_kernel, grid=(steps,), in_specs=[tiled(cot.sha...  17.4 us
    dot_general x4, matrix products, tn(): lax.dot_general(left, right, (((0,), (0,)), ((), ())), preferred_element_...  14.6 us
    pallas_call x1, Pallas kernels, attention_forward(): pl.pallas_call(lambda *refs: forward_kernel(nkb, batch, width, *refs), gr...  12.8 us
  transfers between devices with their start and end apart: 57, of which 26 were waited for; matrix products, arithmetic and copies ran while one was open for 20% of the time, Pallas kernels for 16%

profile of v4, /device:TPU:0, one launch (start us, length us, event | category | flops | bytes accessed | tf_op | source)
XLA Modules:
  0.0 404.0 jit_solution(14151927292632267584)
XLA Ops:
  11.3 3.1 collective-permute-start
  14.4 2.6 collective-permute-start.1
  22.5 8.1 %collective-permute-done.1 = bf16[136,768]{1,0:T(8,128)(2,1)S(1)} collective-permute-done((bf16[136,768]{1,0:T(8,128)(2,1)S(1)}, bf16[136,768]{1,0:T(8,128)(2,1)S(1)}, u32[]{:S(2)}, u32[]{:S(2)}) %collective-permute-start.1) | collective-permute-done | bytes 208928 | tf_op jit(solution)/shard_map/ppermute | solution.py:351
  33.9 3.7 convert_multiply_fusion
  40.9 9.2 %collective-permute-done.4.refs_2_ = bf16[4,136,384]{2,1,0:T(8,128)(2,1)} collective-permute-done((bf16[4,136,384]{2,1,0:T(8,128)(2,1)}, bf16[4,136,384]{2,1,0:T(8,128)(2,1)}, u32[]{:S(2)}, u32[]{:S(2)}) %collective-permute-start.4) | collective-permute-done | bytes 417824 | tf_op jit(solution)/shard_map/ppermute | solution.py:351
  56.7 3.9 collective-permute-start.10
  61.6 2.2 fusion.28
  63.8 17.0 %collective-permute-done.10 = bf16[352,256]{1,0:T(8,128)(2,1)S(1)} collective-permute-done((bf16[352,256]{1,0:T(8,128)(2,1)S(1)}, bf16[352,256]{1,0:T(8,128)(2,1)S(1)}, u32[]{:S(2)}, u32[]{:S(2)}) %collective-permute-start.10) | collective-permute-done | bytes 180256 | tf_op jit(solution)/shard_map/ppermute | solution.py:351
  82.4 3.5 place.6
  87.7 2.1 collective-permute-done.11
  91.7 3.4 collective-permute-start.12
  95.2 2.3 collective-permute-start.15
  97.5 2.3 fusion.12.refs_1_
  101.3 3.5 place.7
  104.8 1.8 fusion.61
  107.7 4.4 %collective-permute-done.15 = bf16[352,256]{1,0:T(8,128)(2,1)S(1)} collective-permute-done((bf16[352,256]{1,0:T(8,128)(2,1)S(1)}, bf16[352,256]{1,0:T(8,128)(2,1)S(1)}, u32[]{:S(2)}, u32[]{:S(2)}) %collective-permute-start.15) | collective-permute-done | bytes 180256 | tf_op jit(solution)/shard_map/ppermute | solution.py:351
  113.4 12.8 %attention_forward.1 = (bf16[2,512,512]{2,1,0:T(8,128)(2,1)}, f32[2,512,512]{2,1,0:T(8,128)}, bf16[2,2,256,2048]{3,2,1,0:T(8,128)(2,1)}, f32[2,2,1,2048]{3,2,1,0:T(1,128)}) custom-call(s32[9]{0:T(128)} %concatenate.93.refs_0_, bf16[2,512,512]{2,1,0:T(8,128)(2,1)} %fusion.12.refs_1_, bf16[512,256]{1,0:T(8,128)(2,1)} %bitcast.195, bf16[512,256]{1,0:T(8,128)(2,1)} %bitcast.192, ...), custom_call_target="tpu_custom_call" | custom-call | flops 7516192768 | bytes 16777216 | tf_op jit(solution)/shard_map/attention_forward/pallas_call | solution.py:162
  126.3 5.1 %collective-permute-done.17.refs_2_ = bf16[2,352,256]{2,1,0:T(8,128)(2,1)S(1)} collective-permute-done((bf16[2,352,256]{2,1,0:T(8,128)(2,1)S(1)}, bf16[2,352,256]{2,1,0:T(8,128)(2,1)S(1)}, u32[]{:S(2)}, u32[]{:S(2)}) %collective-permute-start.17) | collective-permute-done | bytes 360480 | tf_op jit(solution)/shard_map/ppermute | solution.py:351
  131.5 1.9 convolution_convert_fusion.7
  133.5 2.6 collective-permute-done.23
  137.6 3.4 collective-permute-start.20
  141.0 1.9 collective-permute-start.21
  144.6 5.6 %collective-permute-done.20.refs_3_ = bf16[2,352,256]{2,1,0:T(8,128)(2,1)S(1)} collective-permute-done((bf16[2,352,256]{2,1,0:T(8,128)(2,1)S(1)}, bf16[2,352,256]{2,1,0:T(8,128)(2,1)S(1)}, u32[]{:S(2)}, u32[]{:S(2)}) %collective-permute-start.20) | collective-permute-done | bytes 360480 | tf_op jit(solution)/shard_map/ppermute | solution.py:351
  150.3 2.0 collective-permute-done.21.refs_6_
  152.2 5.4 %collective-permute-done.19.refs_4_ = bf16[2,352,256]{2,1,0:T(8,128)(2,1)S(1)} collective-permute-done((bf16[2,352,256]{2,1,0:T(8,128)(2,1)S(1)}, bf16[2,352,256]{2,1,0:T(8,128)(2,1)S(1)}, u32[]{:S(2)}, u32[]{:S(2)}) %collective-permute-start.19) | collective-permute-done | bytes 360480 | tf_op jit(solution)/shard_map/ppermute | solution.py:351
  160.3 3.0 place.8
  163.3 11.6 %feed_forward.1 = (f32[1024,2816]{1,0:T(8,128)}, bf16[1024,1408]{1,0:T(8,128)(2,1)}) custom-call(bf16[1024,1024]{1,0:T(8,128)(2,1)} %pad_maximum_fusion.2.x, bf16[1024,2816]{1,0:T(8,128)(2,1)} %all-gather.2.cloned.1.call-done.w), custom_call_target="tpu_custom_call" | custom-call | flops 5905580032 | bytes 20971520 | tf_op jit(solution)/shard_map/feed_forward/pallas_call | solution.py:291
  174.9 4.4 %place.9 = bf16[2,2,352,1024]{3,2,1,0:T(8,128)(2,1)} custom-call(s32[3]{0:T(128)} %pad_add_fusion.refs_0_, bf16[2,352,256]{2,1,0:T(8,128)(2,1)} %get-tuple-element.457.refs_1_, bf16[2,352,256]{2,1,0:T(8,128)(2,1)} %copy-done.23, bf16[2,352,256]{2,1,0:T(8,128)(2,1)} %copy-done.24, bf16[2,352,256]{2,1,0:T(8,128)(2,1)} %copy-done.26, ...), custom_call_target="tpu_custom_call" | custom-call | tf_op jit(solution)/shard_map/place/pallas_call | solution.py:620
  179.3 17.4 %feed_forward_back.1 = (bf16[1024,2816]{1,0:T(8,128)(2,1)}, f32[512,1024]{1,0:T(8,128)}, bf16[512,1024]{1,0:T(8,128)(2,1)}) custom-call(bf16[1024,1024]{1,0:T(8,128)(2,1)} %pad_maximum_fusion.cot, bf16[1408,1024]{1,0:T(8,128)(2,1)} %bitcast.158, bf16[1024,2816]{1,0:T(8,128)(2,1)} %all-gather.2.cloned.1.call-done.w, f32[1024,2816]{1,0:T(8,128)} %get-tuple-element.467.act), custom_call_target="tpu_custom_call" | custom-call | flops 8858370048 | bytes 31457280 | tf_op jit(solution)/shard_map/feed_forward_back/pallas_call | solution.py:311
  197.2 2.5 collective-permute-done.26
  199.7 2.1 convert_add_fusion.3
  203.0 2.2 fusion.55
  205.6 8.8 %convolution_convert_fusion = bf16[1024,2816]{1,0:T(8,128)(2,1)} fusion(bf16[1024,1024]{1,0:T(8,128)(2,1)S(1)} %copy-done.13, bf16[1024,2816]{1,0:T(8,128)(2,1)S(1)} %bitcast.214), kind=kOutput, calls=%fused_computation | convolution fusion | flops 5908463616 | bytes 13631488 | tf_op jit(solution)/shard_map/dot_general | solution.py:31
  214.4 1.7 pad_maximum_fusion.3
  220.8 3.8 convolution_convert_fusion.1
  232.8 2.3 fusion.13.refs_2_
  235.0 2.8 convolution_convert_fusion.4
  238.0 2.2 constant_dynamic-slice_fusion.10
  240.2 1.7 collective-permute-start.31
  242.2 12.1 %attention_backward.2 = (bf16[512,512]{1,0:T(8,128)(2,1)}, f32[4,256,256]{2,1,0:T(8,128)}, f32[512,256]{1,0:T(8,128)}, f32[512,256]{1,0:T(8,128)}) custom-call(s32[9]{0:T(128)} %concatenate.93.refs_0_, bf16[2,512,512]{2,1,0:T(8,128)(2,1)} %fusion.12.refs_1_, bf16[2,512,512]{2,1,0:T(8,128)(2,1)} %fusion.13.refs_2_, ...), custom_call_target="tpu_custom_call" | custom-call | flops 9395240960 | bytes 10485760 | tf_op jit(solution)/shard_map/attention_backward/pallas_call | solution.py:206
  254.3 3.5 convert_add_fusion.2
  259.0 13.3 %collective-permute-done.31 = bf16[2,1,480,512]{3,2,0,1:T(8,128)(2,1)} collective-permute-done((bf16[2,1,480,512]{3,2,0,1:T(8,128)(2,1)}, bf16[2,1,480,512]{3,2,0,1:T(8,128)(2,1)}, u32[]{:S(2)}, u32[]{:S(2)}) %collective-permute-start.31) | collective-permute-done | bytes 983072 | tf_op jit(solution)/shard_map/ppermute | solution.py:351
  274.4 1.8 collective-permute-start.33
  277.6 12.3 %attention_backward.3 = (bf16[512,512]{1,0:T(8,128)(2,1)}, f32[4,256,256]{2,1,0:T(8,128)}, f32[512,256]{1,0:T(8,128)}, f32[512,256]{1,0:T(8,128)}) custom-call(s32[9]{0:T(128)} %concatenate.93.refs_0_, bf16[2,512,512]{2,1,0:T(8,128)(2,1)} %fusion.12.refs_1_, bf16[2,512,512]{2,1,0:T(8,128)(2,1)} %fusion.13.refs_2_, ...), custom_call_target="tpu_custom_call" | custom-call | flops 9395240960 | bytes 10485760 | tf_op jit(solution)/shard_map/attention_backward/pallas_call | solution.py:206
  289.9 2.3 collective-permute-done.32
  292.2 2.2 collective-permute-done.33
  294.4 2.2 place.10
  301.8 2.3 bitcast_convert_fusion
  305.2 4.4 %collective-permute-done.35 = bf16[2,256,256]{2,1,0:T(8,128)(2,1)S(1)} collective-permute-done((bf16[2,256,256]{2,1,0:T(8,128)(2,1)S(1)}, bf16[2,256,256]{2,1,0:T(8,128)(2,1)S(1)}, u32[]{:S(2)}, u32[]{:S(2)}) %collective-permute-start.35) | collective-permute-done | bytes 262176 | tf_op jit(solution)/shard_map/ppermute | solution.py:351
  310.8 1.8 add_convert_fusion
  314.9 3.1 place.11
  319.6 2.5 collective-permute-start.39
  322.0 2.6 fusion.5
  324.7 4.5 %collective-permute-done.41 = bf16[1,480,256]{2,1,0:T(8,128)(2,1)} collective-permute-done((bf16[1,480,256]{2,1,0:T(8,128)(2,1)S(1)}, bf16[1,480,256]{2,1,0:T(8,128)(2,1)}, u32[]{:S(2)}, u32[]{:S(2)}) %collective-permute-start.41) | collective-permute-done | bytes 245792 | tf_op jit(solution)/shard_map/ppermute | solution.py:351
  330.1 1.9 fusion.8
  332.0 13.7 %collective-permute-done.42 = bf16[1,480,256]{2,1,0:T(8,128)(2,1)} collective-permute-done((bf16[1,480,256]{2,1,0:T(8,128)(2,1)S(1)}, bf16[1,480,256]{2,1,0:T(8,128)(2,1)}, u32[]{:S(2)}, u32[]{:S(2)}) %collective-permute-start.42) | collective-permute-done | bytes 245792 | tf_op jit(solution)/shard_map/ppermute | solution.py:351
  346.0 9.4 %reduce-scatter.2.cloned.1.call-done = bf16[128,2816]{1,0:T(8,128)(2,1)} async-done(((bf16[1024,2816]{1,0:T(8,128)(2,1)}), bf16[128,2816]{1,0:T(8,128)(2,1)}) %reduce-scatter.2.cloned.1.call-update) | async-done | bytes 720912 | tf_op jit(solution)/shard_map/reduce_scatter | solution.py:794
  358.6 2.2 collective-permute-start.46
  362.3 3.5 collective-permute-done.45
  365.9 4.1 %collective-permute-done.46 = bf16[1,136,512]{2,1,0:T(8,128)(2,1)S(1)} collective-permute-done((bf16[1,136,512]{2,1,0:T(8,128)(2,1)S(1)}, bf16[1,136,512]{2,1,0:T(8,128)(2,1)S(1)}, u32[]{:S(2)}, u32[]{:S(2)}) %collective-permute-start.46) | collective-permute-done | bytes 139296 | tf_op jit(solution)/shard_map/ppermute | solution.py:351
  370.1 3.1 collective-permute-done.44
  373.4 1.7 collective-permute-start.50
  375.5 9.3 %collective-permute-done.49 = bf16[136,512]{1,0:T(8,128)(2,1)S(1)} collective-permute-done((bf16[136,512]{1,0:T(8,128)(2,1)S(1)}, bf16[136,512]{1,0:T(8,128)(2,1)S(1)}, u32[]{:S(2)}, u32[]{:S(2)}) %collective-permute-start.49) | collective-permute-done | bytes 139296 | tf_op jit(solution)/shard_map/ppermute | solution.py:351
  384.8 2.6 collective-permute-start.51
  (308 shorter events, 85.7 us)
Async XLA Ops:
  7.2 156.1 %all-gather.2.cloned.1.call-start = ((), (), s32[]{:S(2)}) async-start(), calls=%async_computation.1 | async-start | bytes 6488064 | tf_op jit(solution)/shard_map/all_gather | solution.py:681
  11.3 11.2 %collective-permute-start = (bf16[136,768]{1,0:T(8,128)(2,1)S(1)}, bf16[136,768]{1,0:T(8,128)(2,1)S(1)}, u32[]{:S(2)}, u32[]{:S(2)}) collective-permute-start(bf16[136,768]{1,0:T(8,128)(2,1)S(1)} %fusion.45), channel_id=1, source_target_pairs={{0,2},{1,3},{2,4},{3,5},{4,6},{5,7},{6,0},{7,1},{8,10},{9,11},{10,... | collective-permute-start | bytes 626696 | tf_op jit(solution)/shard_map/ppermute | solution.py:351
  14.4 16.3 %collective-permute-start.1 = (bf16[136,768]{1,0:T(8,128)(2,1)S(1)}, bf16[136,768]{1,0:T(8,128)(2,1)S(1)}, u32[]{:S(2)}, u32[]{:S(2)}) collective-permute-start(bf16[136,768]{1,0:T(8,128)(2,1)S(1)} %fusion.45), channel_id=1, source_target_pairs={{0,4},{1,5},{2,6},{3,7},{4,0},{5,1},{6,2},{7,3},{8,12},{9,13},{10,... | collective-permute-start | bytes 626696 | tf_op jit(solution)/shard_map/ppermute | solution.py:351
  17.0 13.7 %collective-permute-start.2 = (bf16[136,768]{1,0:T(8,128)(2,1)S(1)}, bf16[136,768]{1,0:T(8,128)(2,1)S(1)}, u32[]{:S(2)}, u32[]{:S(2)}) collective-permute-start(bf16[136,768]{1,0:T(8,128)(2,1)S(1)} %fusion.45), channel_id=1, source_target_pairs={{0,6},{1,7},{2,0},{3,1},{4,2},{5,3},{6,4},{7,5},{8,14},{9,15},{10,... | collective-permute-start | bytes 626696 | tf_op jit(solution)/shard_map/ppermute | solution.py:351
  18.3 13.8 %collective-permute-start.3 = (bf16[2,256,1024]{2,1,0:T(8,128)(2,1)}, bf16[2,256,1024]{2,1,0:T(8,128)(2,1)}, u32[]{:S(2)}, u32[]{:S(2)}) collective-permute-start(bf16[2,256,1024]{2,1,0:T(8,128)(2,1)} %param.13), channel_id=1, source_target_pairs={{0,8},{1,9},{2,10},{3,11},{4,12},{5,13},{6,14},{7,15},{8,0},{9,1},... | collective-permute-start | bytes 3145736 | tf_op jit(solution)/shard_map/ppermute | solution.py:351
  33.9 22.8 %copy-start.31 = (bf16[352,256]{1,0:T(8,128)(2,1)S(1)}, bf16[352,256]{1,0:T(8,128)(2,1)}, u32[]{:S(2)}) copy-start(bf16[352,256]{1,0:T(8,128)(2,1)} %dynamic-slice_convert_fusion.2) | copy-start | bytes 540676
  37.6 317.9 %reduce-scatter.2.cloned.1.call-start = ((), (), s32[]{:S(2)}) async-start(), calls=%async_computation.2 | async-start | bytes 6488064 | tf_op jit(solution)/shard_map/reduce_scatter | solution.py:794
  37.6 19.0 %collective-permute-start.16 = (bf16[512,1024]{1,0:T(8,128)(2,1)S(1)}, bf16[512,1024]{1,0:T(8,128)(2,1)S(1)}, u32[]{:S(2)}, u32[]{:S(2)}) collective-permute-start(bf16[512,1024]{1,0:T(8,128)(2,1)S(1)} %bitcast.149), channel_id=1, source_target_pairs={{0,8},{1,9},{2,10},{3,11},{4,12},{5,13},{6,14},{7,15},{8,0},{9,1},... | collective-permute-start | bytes 3145736 | tf_op jit(solution)/shard_map/ppermute | solution.py:351
  37.7 12.4 %collective-permute-start.4 = (bf16[4,136,384]{2,1,0:T(8,128)(2,1)}, bf16[4,136,384]{2,1,0:T(8,128)(2,1)}, u32[]{:S(2)}, u32[]{:S(2)}) collective-permute-start(bf16[4,136,384]{2,1,0:T(8,128)(2,1)} %get-tuple-element.360.refs_1_), channel_id=1, source_target_pairs={{0,1},{1,0},{2,3},{3,2},{4,5},{5,4},{6,7},{7,6},{8,9},{9,8},{10,11... | collective-permute-start | bytes 1253384 | tf_op jit(solution)/shard_map/ppermute | solution.py:351
  39.2 12.0 %collective-permute-start.5 = (bf16[4,136,384]{2,1,0:T(8,128)(2,1)}, bf16[4,136,384]{2,1,0:T(8,128)(2,1)}, u32[]{:S(2)}, u32[]{:S(2)}) collective-permute-start(bf16[4,136,384]{2,1,0:T(8,128)(2,1)} %get-tuple-element.364.refs_5_), channel_id=1, source_target_pairs={{0,16},{1,17},{2,18},{3,19},{4,20},{5,21},{6,22},{7,23},{8,24},{9,... | collective-permute-start | bytes 1253384 | tf_op jit(solution)/shard_map/ppermute | solution.py:351
  51.3 29.6 %collective-permute-start.6 = (bf16[4,136,384]{2,1,0:T(8,128)(2,1)}, bf16[4,136,384]{2,1,0:T(8,128)(2,1)}, u32[]{:S(2)}, u32[]{:S(2)}) collective-permute-start(bf16[4,136,384]{2,1,0:T(8,128)(2,1)} %collective-permute-done.4.refs_2_), channel_id=1, source_target_pairs={{0,16},{1,17},{2,18},{3,19},{4,20},{5,21},{6,22},{7,23},{8,24},{9,... | collective-permute-start | bytes 1253384 | tf_op jit(solution)/shard_map/ppermute | solution.py:351
  52.8 28.0 %collective-permute-start.7 = (bf16[4,136,384]{2,1,0:T(8,128)(2,1)}, bf16[4,136,384]{2,1,0:T(8,128)(2,1)}, u32[]{:S(2)}, u32[]{:S(2)}) collective-permute-start(bf16[4,136,384]{2,1,0:T(8,128)(2,1)} %get-tuple-element.360.refs_1_), channel_id=1, source_target_pairs={{0,16},{1,17},{2,18},{3,19},{4,20},{5,21},{6,22},{7,23},{8,24},{9,... | collective-permute-start | bytes 1253384 | tf_op jit(solution)/shard_map/ppermute | solution.py:351
  53.3 27.5 %collective-permute-start.8 = (bf16[4,136,384]{2,1,0:T(8,128)(2,1)}, bf16[4,136,384]{2,1,0:T(8,128)(2,1)}, u32[]{:S(2)}, u32[]{:S(2)}) collective-permute-start(bf16[4,136,384]{2,1,0:T(8,128)(2,1)} %get-tuple-element.364.refs_5_), channel_id=1, source_target_pairs={{0,1},{1,0},{2,3},{3,2},{4,5},{5,4},{6,7},{7,6},{8,9},{9,8},{10,11... | collective-permute-start | bytes 1253384 | tf_op jit(solution)/shard_map/ppermute | solution.py:351
  53.9 27.0 %collective-permute-start.9 = (bf16[4,136,384]{2,1,0:T(8,128)(2,1)}, bf16[4,136,384]{2,1,0:T(8,128)(2,1)}, u32[]{:S(2)}, u32[]{:S(2)}) collective-permute-start(bf16[4,136,384]{2,1,0:T(8,128)(2,1)} %collective-permute-done.5.refs_7_), channel_id=1, source_target_pairs={{0,1},{1,0},{2,3},{3,2},{4,5},{5,4},{6,7},{7,6},{8,9},{9,8},{10,11... | collective-permute-start | bytes 1253384 | tf_op jit(solution)/shard_map/ppermute | solution.py:351
  56.7 24.2 %collective-permute-start.10 = (bf16[352,256]{1,0:T(8,128)(2,1)S(1)}, bf16[352,256]{1,0:T(8,128)(2,1)S(1)}, u32[]{:S(2)}, u32[]{:S(2)}) collective-permute-start(bf16[352,256]{1,0:T(8,128)(2,1)S(1)} %copy-done.31), channel_id=1, source_target_pairs={{0,4},{1,5},{2,6},{3,7},{4,0},{5,1},{6,2},{7,3},{8,12},{9,13},{10,... | collective-permute-start | bytes 540680 | tf_op jit(solution)/shard_map/ppermute | solution.py:351
  61.6 24.3 %copy-start.3 = (f32[2,2,256,1024]{3,2,1,0:T(8,128)S(1)}, f32[2,2,256,1024]{3,2,1,0:T(8,128)}, u32[]{:S(2)}) copy-start(f32[2,2,256,1024]{3,2,1,0:T(8,128)} %convert_multiply_fusion) | copy-start | bytes 12582916
  82.3 7.5 %collective-permute-start.11 = (bf16[352,256]{1,0:T(8,128)(2,1)S(1)}, bf16[352,256]{1,0:T(8,128)(2,1)}, u32[]{:S(2)}, u32[]{:S(2)}) collective-permute-start(bf16[352,256]{1,0:T(8,128)(2,1)S(1)} %copy-done.31), channel_id=1, source_target_pairs={{0,2},{1,3},{2,4},{3,5},{4,6},{5,7},{6,0},{7,1},{8,10},{9,11},{10,... | collective-permute-start | bytes 540680 | tf_op jit(solution)/shard_map/ppermute | solution.py:351
  89.8 10.0 %collective-permute-start.13 = (bf16[4,2,128,256]{3,2,1,0:T(8,128)(2,1)S(1)}, bf16[4,2,128,256]{3,2,1,0:T(8,128)(2,1)S(1)}, u32[]{:S(2)}, u32[]{:S(2)}) collective-permute-start(bf16[4,2,128,256]{3,2,1,0:T(8,128)(2,1)S(1)} %copy-done.48), channel_id=1, source_target_pairs={{0,8},{1,9},{2,10},{3,11},{4,12},{5,13},{6,14},{7,15},{8,0},{9,1},... | collective-permute-start | bytes 1572872 | tf_op jit(solution)/shard_map/ppermute | solution.py:351
  91.2 8.5 %collective-permute-start.14 = (bf16[4,2,128,128]{3,2,1,0:T(8,128)(2,1)S(1)}, bf16[4,2,128,128]{3,2,1,0:T(8,128)(2,1)S(1)}, u32[]{:S(2)}, u32[]{:S(2)}) collective-permute-start(bf16[4,2,128,128]{3,2,1,0:T(8,128)(2,1)S(1)} %copy-done.49), channel_id=1, source_target_pairs={{0,8},{1,9},{2,10},{3,11},{4,12},{5,13},{6,14},{7,15},{8,0},{9,1},... | collective-permute-start | bytes 786440 | tf_op jit(solution)/shard_map/ppermute | solution.py:351
  91.7 14.9 %collective-permute-start.12 = (bf16[2,2,256,256]{3,2,1,0:T(8,128)(2,1)S(1)}, bf16[2,2,256,256]{3,2,1,0:T(8,128)(2,1)S(1)}, u32[]{:S(2)}, u32[]{:S(2)}) collective-permute-start(bf16[2,2,256,256]{3,2,1,0:T(8,128)(2,1)S(1)} %bitcast.186), channel_id=1, source_target_pairs={{0,16},{1,17},{2,18},{3,19},{4,20},{5,21},{6,22},{7,23},{8,24},{9,... | collective-permute-start | bytes 1572872 | tf_op jit(solution)/shard_map/ppermute | solution.py:351
  95.2 16.9 %collective-permute-start.15 = (bf16[352,256]{1,0:T(8,128)(2,1)S(1)}, bf16[352,256]{1,0:T(8,128)(2,1)S(1)}, u32[]{:S(2)}, u32[]{:S(2)}) collective-permute-start(bf16[352,256]{1,0:T(8,128)(2,1)S(1)} %copy-done.31), channel_id=1, source_target_pairs={{0,6},{1,7},{2,0},{3,1},{4,2},{5,3},{6,4},{7,5},{8,14},{9,15},{10,... | collective-permute-start | bytes 540680 | tf_op jit(solution)/shard_map/ppermute | solution.py:351
  113.2 13.2 %collective-permute-start.18 = (bf16[2,352,256]{2,1,0:T(8,128)(2,1)S(1)}, bf16[2,352,256]{2,1,0:T(8,128)(2,1)S(1)}, u32[]{:S(2)}, u32[]{:S(2)}) collective-permute-start(bf16[2,352,256]{2,1,0:T(8,128)(2,1)S(1)} %pad_maximum_fusion.15), channel_id=1, source_target_pairs={{0,16},{1,17},{2,18},{3,19},{4,20},{5,21},{6,22},{7,23},{8,24},{9,... | collective-permute-start | bytes 1081352 | tf_op jit(solution)/shard_map/ppermute | solution.py:351
  113.3 18.2 %copy-start.45 = (bf16[2,2,128,1024]{3,2,1,0:T(8,128)(2,1)S(1)}, bf16[2,2,128,1024]{3,2,1,0:T(8,128)(2,1)}, u32[]{:S(2)}) copy-start(bf16[2,2,128,1024]{3,2,1,0:T(8,128)(2,1)} %get-tuple-element.374) | copy-start | bytes 3145732
  113.3 18.2 %collective-permute-start.17 = (bf16[2,352,256]{2,1,0:T(8,128)(2,1)S(1)}, bf16[2,352,256]{2,1,0:T(8,128)(2,1)S(1)}, u32[]{:S(2)}, u32[]{:S(2)}) collective-permute-start(bf16[2,352,256]{2,1,0:T(8,128)(2,1)S(1)} %pad_maximum_fusion.14), channel_id=1, source_target_pairs={{0,1},{1,0},{2,3},{3,2},{4,5},{5,4},{6,7},{7,6},{8,9},{9,8},{10,11... | collective-permute-start | bytes 1081352 | tf_op jit(solution)/shard_map/ppermute | solution.py:351
  126.3 16.7 %copy-start.22 = (bf16[2,352,256]{2,1,0:T(8,128)(2,1)}, bf16[2,352,256]{2,1,0:T(8,128)(2,1)S(1)}, u32[]{:S(2)}) copy-start(bf16[2,352,256]{2,1,0:T(8,128)(2,1)S(1)} %collective-permute-done.18.refs_7_) | copy-start | bytes 1081348
  133.4 2.7 collective-permute-start.23
  137.3 5.8 %collective-permute-start.24 = (bf16[512,1024]{1,0:T(8,128)(2,1)S(1)}, bf16[512,1024]{1,0:T(8,128)(2,1)S(1)}, u32[]{:S(2)}, u32[]{:S(2)}) collective-permute-start(bf16[512,1024]{1,0:T(8,128)(2,1)S(1)} %bitcast.156), channel_id=1, source_target_pairs={{0,8},{1,9},{2,10},{3,11},{4,12},{5,13},{6,14},{7,15},{8,0},{9,1},... | collective-permute-start | bytes 3145736 | tf_op jit(solution)/shard_map/ppermute | solution.py:351
  137.6 12.7 %collective-permute-start.20 = (bf16[2,352,256]{2,1,0:T(8,128)(2,1)S(1)}, bf16[2,352,256]{2,1,0:T(8,128)(2,1)S(1)}, u32[]{:S(2)}, u32[]{:S(2)}) collective-permute-start(bf16[2,352,256]{2,1,0:T(8,128)(2,1)S(1)} %get-tuple-element.698), channel_id=1, source_target_pairs={{0,16},{1,17},{2,18},{3,19},{4,20},{5,21},{6,22},{7,23},{8,24},{9,... | collective-permute-start | bytes 1081352 | tf_op jit(solution)/shard_map/ppermute | solution.py:351
  141.0 11.2 %collective-permute-start.21 = (bf16[2,352,256]{2,1,0:T(8,128)(2,1)S(1)}, bf16[2,352,256]{2,1,0:T(8,128)(2,1)S(1)}, u32[]{:S(2)}, u32[]{:S(2)}) collective-permute-start(bf16[2,352,256]{2,1,0:T(8,128)(2,1)S(1)} %get-tuple-element.697), channel_id=1, source_target_pairs={{0,1},{1,0},{2,3},{3,2},{4,5},{5,4},{6,7},{7,6},{8,9},{9,8},{10,11... | collective-permute-start | bytes 1081352 | tf_op jit(solution)/shard_map/ppermute | solution.py:351
  143.0 14.7 %collective-permute-start.19 = (bf16[2,352,256]{2,1,0:T(8,128)(2,1)S(1)}, bf16[2,352,256]{2,1,0:T(8,128)(2,1)S(1)}, u32[]{:S(2)}, u32[]{:S(2)}) collective-permute-start(bf16[2,352,256]{2,1,0:T(8,128)(2,1)S(1)} %collective-permute-done.17.refs_2_), channel_id=1, source_target_pairs={{0,16},{1,17},{2,18},{3,19},{4,20},{5,21},{6,22},{7,23},{8,24},{9,... | collective-permute-start | bytes 1081352 | tf_op jit(solution)/shard_map/ppermute | solution.py:351
  143.0 16.3 %collective-permute-start.22 = (bf16[2,352,256]{2,1,0:T(8,128)(2,1)S(1)}, bf16[2,352,256]{2,1,0:T(8,128)(2,1)S(1)}, u32[]{:S(2)}, u32[]{:S(2)}) collective-permute-start(bf16[2,352,256]{2,1,0:T(8,128)(2,1)S(1)} %collective-permute-done.18.refs_7_), channel_id=1, source_target_pairs={{0,1},{1,0},{2,3},{3,2},{4,5},{5,4},{6,7},{7,6},{8,9},{9,8},{10,11... | collective-permute-start | bytes 1081352 | tf_op jit(solution)/shard_map/ppermute | solution.py:351
  163.3 11.6 %collective-permute-start.25 = (bf16[4,2,352,256]{3,2,1,0:T(8,128)(2,1)}, bf16[4,2,352,256]{3,2,1,0:T(8,128)(2,1)}, u32[]{:S(2)}, u32[]{:S(2)}) collective-permute-start(bf16[4,2,352,256]{3,2,1,0:T(8,128)(2,1)} %place.8), channel_id=1, source_target_pairs={{0,8},{1,9},{2,10},{3,11},{4,12},{5,13},{6,14},{7,15},{8,0},{9,1},... | collective-permute-start | bytes 4325384 | tf_op jit(solution)/shard_map/ppermute | solution.py:351
  196.7 3.0 collective-permute-start.26
  205.2 9.2 %collective-permute-start.27 = (bf16[2,256,1024]{2,1,0:T(8,128)(2,1)}, bf16[2,256,1024]{2,1,0:T(8,128)(2,1)}, u32[]{:S(2)}, u32[]{:S(2)}) collective-permute-start(bf16[2,256,1024]{2,1,0:T(8,128)(2,1)} %get-tuple-element.676), channel_id=1, source_target_pairs={{0,8},{1,9},{2,10},{3,11},{4,12},{5,13},{6,14},{7,15},{8,0},{9,1},... | collective-permute-start | bytes 3145736 | tf_op jit(solution)/shard_map/ppermute | solution.py:351
  224.9 10.1 %collective-permute-start.28 = (bf16[2,2,480,512]{3,2,0,1:T(8,128)(2,1)S(1)}, bf16[2,2,480,512]{3,2,0,1:T(8,128)(2,1)S(1)}, u32[]{:S(2)}, u32[]{:S(2)}) collective-permute-start(bf16[2,2,480,512]{3,2,0,1:T(8,128)(2,1)S(1)} %copy.77), channel_id=1, source_target_pairs={{0,8},{1,9},{2,10},{3,11},{4,12},{5,13},{6,14},{7,15},{8,0},{9,1},... | collective-permute-start | bytes 5898248 | tf_op jit(solution)/shard_map/ppermute | solution.py:351
  237.8 16.4 %collective-permute-start.29 = (bf16[512,1024]{1,0:T(8,128)(2,1)}, bf16[512,1024]{1,0:T(8,128)(2,1)}, u32[]{:S(2)}, u32[]{:S(2)}) collective-permute-start(bf16[512,1024]{1,0:T(8,128)(2,1)} %convolution_convert_fusion.4), channel_id=1, source_target_pairs={{0,8},{1,9},{2,10},{3,11},{4,12},{5,13},{6,14},{7,15},{8,0},{9,1},... | collective-permute-start | bytes 3145736 | tf_op jit(solution)/shard_map/ppermute | solution.py:351
  240.2 32.1 %collective-permute-start.31 = (bf16[2,1,480,512]{3,2,0,1:T(8,128)(2,1)}, bf16[2,1,480,512]{3,2,0,1:T(8,128)(2,1)}, u32[]{:S(2)}, u32[]{:S(2)}) collective-permute-start(bf16[2,1,480,512]{3,2,0,1:T(8,128)(2,1)} %constant_dynamic-slice_fusion.10), channel_id=1, source_target_pairs={{0,1},{1,0},{2,3},{3,2},{4,5},{5,4},{6,7},{7,6},{8,9},{9,8},{10,11... | collective-permute-start | bytes 2949128 | tf_op jit(solution)/shard_map/ppermute | solution.py:351
  242.0 30.3 %collective-permute-start.30 = (bf16[2,2,480,256]{3,2,0,1:T(8,128)(2,1)}, bf16[2,2,480,256]{3,2,0,1:T(8,128)(2,1)S(1)}, u32[]{:S(2)}, u32[]{:S(2)}) collective-permute-start(bf16[2,2,480,256]{3,2,0,1:T(8,128)(2,1)} %copy.76), channel_id=1, source_target_pairs={{0,16},{1,17},{2,18},{3,19},{4,20},{5,21},{6,22},{7,23},{8,24},{9,... | collective-permute-start | bytes 2949128 | tf_op jit(solution)/shard_map/ppermute | solution.py:351
  259.0 15.1 %copy-start.9 = (bf16[2,2,480,256]{3,2,0,1:T(8,128)(2,1)S(1)}, bf16[2,2,480,256]{3,2,0,1:T(8,128)(2,1)}, u32[]{:S(2)}) copy-start(bf16[2,2,480,256]{3,2,0,1:T(8,128)(2,1)} %copy.75) | copy-start | bytes 2949124
  273.8 18.4 %collective-permute-start.34 = (bf16[2,1,480,256]{3,2,0,1:T(8,128)(2,1)S(1)}, bf16[2,1,480,256]{3,2,0,1:T(8,128)(2,1)}, u32[]{:S(2)}, u32[]{:S(2)}) collective-permute-start(bf16[2,1,480,256]{3,2,0,1:T(8,128)(2,1)S(1)} %constant_dynamic-slice_fusion.8), channel_id=1, source_target_pairs={{0,16},{1,17},{2,18},{3,19},{4,20},{5,21},{6,22},{7,23},{8,24},{9,... | collective-permute-start | bytes 1474568 | tf_op jit(solution)/shard_map/ppermute | solution.py:351
  274.4 20.0 %collective-permute-start.33 = (bf16[2,1,480,256]{3,2,0,1:T(8,128)(2,1)S(1)}, bf16[2,1,480,256]{3,2,0,1:T(8,128)(2,1)S(1)}, u32[]{:S(2)}, u32[]{:S(2)}) collective-permute-start(bf16[2,1,480,256]{3,2,0,1:T(8,128)(2,1)S(1)} %constant_dynamic-slice_fusion.9), channel_id=1, source_target_pairs={{0,1},{1,0},{2,3},{3,2},{4,5},{5,4},{6,7},{7,6},{8,9},{9,8},{10,11... | collective-permute-start | bytes 1474568 | tf_op jit(solution)/shard_map/ppermute | solution.py:351
  276.3 15.9 %collective-permute-start.32 = (bf16[2,256,256]{2,1,0:T(8,128)(2,1)S(1)}, bf16[2,256,256]{2,1,0:T(8,128)(2,1)S(1)}, u32[]{:S(2)}, u32[]{:S(2)}) collective-permute-start(bf16[2,256,256]{2,1,0:T(8,128)(2,1)S(1)} %slice.264), channel_id=1, source_target_pairs={{16,0},{17,1},{18,2},{19,3},{20,4},{21,5},{22,6},{23,7},{24,8},{25... | collective-permute-start | bytes 786440 | tf_op jit(solution)/shard_map/ppermute | solution.py:351
  296.6 8.5 %collective-permute-start.36 = (bf16[2,512,128]{2,1,0:T(8,128)(2,1)}, bf16[2,512,128]{2,1,0:T(8,128)(2,1)S(1)}, u32[]{:S(2)}, u32[]{:S(2)}) collective-permute-start(bf16[2,512,128]{2,1,0:T(8,128)(2,1)} %get-tuple-element.600), channel_id=1, source_target_pairs={{0,8},{1,9},{2,10},{3,11},{4,12},{5,13},{6,14},{7,15},{8,0},{9,1},... | collective-permute-start | bytes 786440 | tf_op jit(solution)/shard_map/ppermute | solution.py:351
  296.7 12.9 %collective-permute-start.35 = (bf16[2,256,256]{2,1,0:T(8,128)(2,1)S(1)}, bf16[2,256,256]{2,1,0:T(8,128)(2,1)S(1)}, u32[]{:S(2)}, u32[]{:S(2)}) collective-permute-start(bf16[2,256,256]{2,1,0:T(8,128)(2,1)S(1)} %slice.263), channel_id=1, source_target_pairs={{16,0},{17,1},{18,2},{19,3},{20,4},{21,5},{22,6},{23,7},{24,8},{25... | collective-permute-start | bytes 786440 | tf_op jit(solution)/shard_map/ppermute | solution.py:351
  312.6 6.9 %collective-permute-start.40 = (bf16[2,256,1024]{2,1,0:T(8,128)(2,1)}, bf16[2,256,1024]{2,1,0:T(8,128)(2,1)}, u32[]{:S(2)}, u32[]{:S(2)}) collective-permute-start(bf16[2,256,1024]{2,1,0:T(8,128)(2,1)} %add_convert_fusion), channel_id=1, source_target_pairs={{0,8},{1,9},{2,10},{3,11},{4,12},{5,13},{6,14},{7,15},{8,0},{9,1},... | collective-permute-start | bytes 3145736 | tf_op jit(solution)/shard_map/ppermute | solution.py:351
  312.9 16.2 %collective-permute-start.41 = (bf16[1,480,256]{2,1,0:T(8,128)(2,1)S(1)}, bf16[1,480,256]{2,1,0:T(8,128)(2,1)}, u32[]{:S(2)}, u32[]{:S(2)}) collective-permute-start(bf16[1,480,256]{2,1,0:T(8,128)(2,1)S(1)} %get-tuple-element.684), channel_id=1, source_target_pairs={{0,2},{1,3},{2,4},{3,5},{4,6},{5,7},{6,0},{7,1},{8,10},{9,11},{10,... | collective-permute-start | bytes 737288 | tf_op jit(solution)/shard_map/ppermute | solution.py:351
  313.2 32.5 %collective-permute-start.42 = (bf16[1,480,256]{2,1,0:T(8,128)(2,1)S(1)}, bf16[1,480,256]{2,1,0:T(8,128)(2,1)}, u32[]{:S(2)}, u32[]{:S(2)}) collective-permute-start(bf16[1,480,256]{2,1,0:T(8,128)(2,1)S(1)} %get-tuple-element.683), channel_id=1, source_target_pairs={{0,4},{1,5},{2,6},{3,7},{4,0},{5,1},{6,2},{7,3},{8,12},{9,13},{10,... | collective-permute-start | bytes 737288 | tf_op jit(solution)/shard_map/ppermute | solution.py:351
  318.0 27.7 %collective-permute-start.37 = (bf16[4,128,512]{2,1,0:T(8,128)(2,1)}, bf16[4,128,512]{2,1,0:T(8,128)(2,1)S(1)}, u32[]{:S(2)}, u32[]{:S(2)}) collective-permute-start(bf16[4,128,512]{2,1,0:T(8,128)(2,1)} %get-tuple-element.617), channel_id=1, source_target_pairs={{0,1},{1,0},{2,3},{3,2},{4,5},{5,4},{6,7},{7,6},{8,9},{9,8},{10,11... | collective-permute-start | bytes 1572872 | tf_op jit(solution)/shard_map/ppermute | solution.py:351
  318.0 27.7 %collective-permute-start.38 = (bf16[4,128,512]{2,1,0:T(8,128)(2,1)}, bf16[4,128,512]{2,1,0:T(8,128)(2,1)S(1)}, u32[]{:S(2)}, u32[]{:S(2)}) collective-permute-start(bf16[4,128,512]{2,1,0:T(8,128)(2,1)} %get-tuple-element.618), channel_id=1, source_target_pairs={{0,16},{1,17},{2,18},{3,19},{4,20},{5,21},{6,22},{7,23},{8,24},{9,... | collective-permute-start | bytes 1572872 | tf_op jit(solution)/shard_map/ppermute | solution.py:351
  319.6 26.2 %collective-permute-start.39 = (bf16[4,128,512]{2,1,0:T(8,128)(2,1)S(1)}, bf16[4,128,512]{2,1,0:T(8,128)(2,1)S(1)}, u32[]{:S(2)}, u32[]{:S(2)}) collective-permute-start(bf16[4,128,512]{2,1,0:T(8,128)(2,1)S(1)} %copy-done.47), channel_id=1, source_target_pairs={{0,17},{1,16},{2,19},{3,18},{4,21},{5,20},{6,23},{7,22},{8,25},{9,... | collective-permute-start | bytes 1572872 | tf_op jit(solution)/shard_map/ppermute | solution.py:351
  329.2 16.5 %collective-permute-start.43 = (bf16[1,480,256]{2,1,0:T(8,128)(2,1)S(1)}, bf16[1,480,256]{2,1,0:T(8,128)(2,1)S(1)}, u32[]{:S(2)}, u32[]{:S(2)}) collective-permute-start(bf16[1,480,256]{2,1,0:T(8,128)(2,1)S(1)} %get-tuple-element.682), channel_id=1, source_target_pairs={{0,6},{1,7},{2,0},{3,1},{4,2},{5,3},{6,4},{7,5},{8,14},{9,15},{10,... | collective-permute-start | bytes 737288 | tf_op jit(solution)/shard_map/ppermute | solution.py:351
  330.1 15.7 %copy-start.34 = (bf16[4,128,512]{2,1,0:T(8,128)(2,1)S(1)}, bf16[4,128,512]{2,1,0:T(8,128)(2,1)}, u32[]{:S(2)}) copy-start(bf16[4,128,512]{2,1,0:T(8,128)(2,1)} %get-tuple-element.628) | copy-start | bytes 1572868
  355.5 17.7 %copy-start.30 = (bf16[128,2816]{1,0:T(8,128)(2,1)S(1)}, bf16[128,2816]{1,0:T(8,128)(2,1)}, u32[]{:S(2)}) copy-start(bf16[128,2816]{1,0:T(8,128)(2,1)} %reduce-scatter.2.cloned.1.call-done) | copy-start | bytes 2162692
  355.5 17.7 %collective-permute-start.44 = (bf16[128,2816]{1,0:T(8,128)(2,1)}, bf16[128,2816]{1,0:T(8,128)(2,1)S(1)}, u32[]{:S(2)}, u32[]{:S(2)}) collective-permute-start(bf16[128,2816]{1,0:T(8,128)(2,1)} %reduce-scatter.2.cloned.1.call-done), channel_id=1, source_target_pairs={{0,16},{1,17},{2,18},{3,19},{4,20},{5,21},{6,22},{7,23},{8,24},{9,... | collective-permute-start | bytes 2162696 | tf_op jit(solution)/shard_map/ppermute | solution.py:351
  357.3 8.6 %collective-permute-start.45 = (bf16[1,136,512]{2,1,0:T(8,128)(2,1)S(1)}, bf16[1,136,512]{2,1,0:T(8,128)(2,1)S(1)}, u32[]{:S(2)}, u32[]{:S(2)}) collective-permute-start(bf16[1,136,512]{2,1,0:T(8,128)(2,1)S(1)} %get-tuple-element.705), channel_id=1, source_target_pairs={{0,2},{1,3},{2,4},{3,5},{4,6},{5,7},{6,0},{7,1},{8,10},{9,11},{10,... | collective-permute-start | bytes 417800 | tf_op jit(solution)/shard_map/ppermute | solution.py:351
  358.6 11.3 %collective-permute-start.46 = (bf16[1,136,512]{2,1,0:T(8,128)(2,1)S(1)}, bf16[1,136,512]{2,1,0:T(8,128)(2,1)S(1)}, u32[]{:S(2)}, u32[]{:S(2)}) collective-permute-start(bf16[1,136,512]{2,1,0:T(8,128)(2,1)S(1)} %get-tuple-element.707), channel_id=1, source_target_pairs={{0,4},{1,5},{2,6},{3,7},{4,0},{5,1},{6,2},{7,3},{8,12},{9,13},{10,... | collective-permute-start | bytes 417800 | tf_op jit(solution)/shard_map/ppermute | solution.py:351
  360.8 9.2 %collective-permute-start.47 = (bf16[1,136,512]{2,1,0:T(8,128)(2,1)S(1)}, bf16[1,136,512]{2,1,0:T(8,128)(2,1)S(1)}, u32[]{:S(2)}, u32[]{:S(2)}) collective-permute-start(bf16[1,136,512]{2,1,0:T(8,128)(2,1)S(1)} %get-tuple-element.706), channel_id=1, source_target_pairs={{0,6},{1,7},{2,0},{3,1},{4,2},{5,3},{6,4},{7,5},{8,14},{9,15},{10,... | collective-permute-start | bytes 417800 | tf_op jit(solution)/shard_map/ppermute | solution.py:351
  373.3 11.4 %collective-permute-start.48 = (bf16[128,2816]{1,0:T(8,128)(2,1)S(1)}, bf16[128,2816]{1,0:T(8,128)(2,1)S(1)}, u32[]{:S(2)}, u32[]{:S(2)}) collective-permute-start(bf16[128,2816]{1,0:T(8,128)(2,1)S(1)} %add_convert_fusion.4), channel_id=1, source_target_pairs={{0,8},{1,9},{2,10},{3,11},{4,12},{5,13},{6,14},{7,15},{8,0},{9,1},... | collective-permute-start | bytes 2162696 | tf_op jit(solution)/shard_map/ppermute | solution.py:351
  373.4 11.4 %collective-permute-start.50 = (bf16[480,256]{1,0:T(8,128)(2,1)S(1)}, bf16[480,256]{1,0:T(8,128)(2,1)S(1)}, u32[]{:S(2)}, u32[]{:S(2)}) collective-permute-start(bf16[480,256]{1,0:T(8,128)(2,1)S(1)} %fusion.44), channel_id=1, source_target_pairs={{0,16},{1,17},{2,18},{3,19},{4,20},{5,21},{6,22},{7,23},{8,24},{9,... | collective-permute-start | bytes 737288 | tf_op jit(solution)/shard_map/ppermute | solution.py:351
  375.1 9.6 %collective-permute-start.49 = (bf16[136,512]{1,0:T(8,128)(2,1)S(1)}, bf16[136,512]{1,0:T(8,128)(2,1)S(1)}, u32[]{:S(2)}, u32[]{:S(2)}) collective-permute-start(bf16[136,512]{1,0:T(8,128)(2,1)S(1)} %fusion.46), channel_id=1, source_target_pairs={{0,16},{1,17},{2,18},{3,19},{4,20},{5,21},{6,22},{7,23},{8,24},{9,... | collective-permute-start | bytes 417800 | tf_op jit(solution)/shard_map/ppermute | solution.py:351
  384.8 6.1 %collective-permute-start.51 = (bf16[4,128]{1,0:T(4,128)(2,1)S(1)}, bf16[4,128]{1,0:T(4,128)(2,1)S(1)}, u32[]{:S(2)}, u32[]{:S(2)}) collective-permute-start(bf16[4,128]{1,0:T(4,128)(2,1)S(1)} %get-tuple-element.675), channel_id=1, source_target_pairs={{0,1},{1,0},{2,3},{3,2},{4,5},{5,4},{6,7},{7,6},{8,9},{9,8},{10,11... | collective-permute-start | bytes 3080 | tf_op jit(solution)/shard_map/ppermute | solution.py:351
  387.5 3.5 collective-permute-start.53
  387.7 6.9 %collective-permute-start.54 = (bf16[480,512]{1,0:T(8,128)(2,1)S(1)}, bf16[480,512]{1,0:T(8,128)(2,1)S(1)}, u32[]{:S(2)}, u32[]{:S(2)}) collective-permute-start(bf16[480,512]{1,0:T(8,128)(2,1)S(1)} %maximum_select_fusion.4), channel_id=1, source_target_pairs={{0,8},{1,9},{2,10},{3,11},{4,12},{5,13},{6,14},{7,15},{8,0},{9,1},... | collective-permute-start | bytes 1474568 | tf_op jit(solution)/shard_map/ppermute | solution.py:351
  388.0 2.8 collective-permute-start.52
  (49 other events, 219.0 us)
Sparse Core Ops, SparseCore 0:
  37.7 114.8 all-gather.1
  220.9 134.5 reduce-scatter.1

commit v5 on v4

--- a/solution.py
+++ b/solution.py
@@ -570,10 +570,6 @@
     return jnp.stack(out)
 
 
-def z_gather(p, piece):
-    return in_z(p, [piece] + [p.to_z(piece, k) for k in (1, 2, 3)])
-
-
 def z_scatter(p, parts):
     total = half(parts, p.z, 0, 4)[0].astype(F32)
     for k in (1, 2, 3):
@@ -670,7 +666,10 @@
     piece = jnp.concatenate(piece, 1)
     pad = jnp.zeros((8, piece.shape[1] - 128), LOW)
     piece = jnp.concatenate([piece, jnp.concatenate([gains, pad], 1)], 0)
-    first = z_gather(p, piece)
+    seen = [piece] + [p.to_z(piece, k) for k in (1, 2, 3)]
+    w_gu = after(v.pop.pgu, seen[1])
+    w_gu = lax.all_gather(w_gu, "dp", axis=0, tiled=True)
+    first = in_z(p, seen)
     v.a, v.b = first[:, :, :384], first[:, :, 384:]
     rows = jnp.stack([tokens, v.pop.tok], 1).astype(F32)
     v.normed1 = rows * inverse_rms(rows)
@@ -678,14 +677,13 @@
     v = sync(v)
 
     v.ax, v.by = p.to_x(v.a), p.to_y(v.b)
-    w_gu = lax.all_gather(v.pop.pgu, "dp", axis=0, tiled=True)
     v = sync(v)
     v.zd2 = p.to_z(v.pd, 2)
     v.ay, v.axy = p.to_y(v.a), p.to_y(v.ax)
     v.bx, v.bxy = p.to_x(v.b), p.to_x(v.by)
     v = sync(v)
 
-    v.zd1 = p.to_z(v.pd, 1)
+    v.zd1, v.zd3 = p.to_z(v.pd, 1), p.to_z(v.pd, 3)
     v.from_ab = (v.pop.a, v.pop.ax, v.pop.ay, v.pop.axy, v.pop.b, v.pop.bx, v.pop.by, v.pop.bxy)
     plan = []
     for n, (r, k) in enumerate(RELATIVE):
@@ -715,7 +713,8 @@
     v = sync(v)
     far_keys = p.up_y(v.keys)
     wo_come, kv_come = p.to_core(v.pop.wo_send), p.to_core(v.pop.kv_send)
-    v.zd3 = p.to_z(v.pd, 3)
+    v.zd = in_z(p, [v.pop.pd, v.pop.zd1, v.pop.zd2, v.pop.zd3])
+    v.dax, v.dby = p.to_x(v.zd[:2]), p.to_y(v.zd[2:])
     v.qt = dots("dn,btd->bnt", v.wq, v.first).astype(LOW)
     plan = []
     for n, (r, k) in enumerate(RELATIVE):
@@ -742,15 +741,13 @@
     v = sync(v)
 
     v.cot = core_first(p, cotangent.reshape(count // 2, D))
-    v.zd = in_z(p, [v.pop.pd, v.pop.zd1, v.pop.zd2, v.pop.zd3])
-    v.dax, v.dby = p.to_x(v.zd[:2]), p.to_y(v.zd[2:])
+    v.day, v.daxy = p.to_y(v.zd[:2]), p.to_y(v.dax)
+    v.dbx, v.dbxy = p.to_x(v.zd[2:]), p.to_x(v.dby)
     cot = half(v.cot, core, 1)
     v.cot_c = [half(cot, i, 1) for i in (y, 1 - y)] + [half(v.cot, 1 - core, 1)]
     v.out, *v.att = attention_forward(v.meta, v.qt, v.kxt, v.vxt, v.keys)
     v = sync(v)
 
-    v.day, v.daxy = p.to_y(v.zd[:2]), p.to_y(v.dax)
-    v.dbx, v.dbxy = p.to_x(v.zd[2:]), p.to_x(v.dby)
     branch = summed(
         p, lambda i: dots("bnt,nd->btd", v.out[:, :, i * length : (i + 1) * length], v.wo)
     )
@@ -785,13 +782,13 @@
     v.d_gu, v.ds_own, v.ds_other = feed_forward_back(v.cot, v.wd, v.pop.w_gu, v.pop.act)
     v = sync(v)
     d_second = (v.pop.ds_own + p.to_core(v.pop.ds_other).astype(F32)).reshape(batch, length, D)
-    v.gg = tn(v.pop.second, v.pop.d_gu).astype(LOW)
+    gg = tn(v.pop.second, v.pop.d_gu).astype(LOW)
+    gg = lax.psum_scatter(gg, "dp", scatter_dimension=0, tiled=True)
     normed2 = v.middle * v.inv2
     v.gain2_sum = jnp.sum(d_second * normed2, axis=(0, 1))
     v.d_middle = cotangent.astype(F32) + norm_back(d_second, normed2, v.pop.inv2, v.pop.gain2)
     v.d_a = chip(p, v.d_middle.astype(LOW)).reshape(batch, 2 * length, D)
     v = sync(v)
-    gg = lax.psum_scatter(v.pop.gg, "dp", scatter_dimension=0, tiled=True)
     go = dots("bnt,btd->nd", v.pop.out, v.d_a).astype(LOW).reshape(2, 2, 128, D)
     go_core = half(go, core, 3)
     go_parts = [half(go_core, y, 3), half(go_core, 1 - y, 3), half(go, 1 - core, 3)]

time: 411 us -> 402 us (0.978)
  waiting for transfers between devices: 138 us -> 109 us
  starting transfers between devices: 54.1 us -> 80.4 us
  local copies, waits for them, and re-layouts: 31.2 us -> 25.2 us
    ppermute x55, starting transfers between devices: 54 us -> 80.3 us  [send(): return lax.ppermute(value, ALL, self.pairs(move))]
    ppermute x55, waiting for transfers between devices: 129 us -> 103 us  [send(): return lax.ppermute(value, ALL, self.pairs(move))]
  transfers between devices with their start and end apart: 57 -> 57, of which waited for: 26 -> 26; matrix products, arithmetic and copies ran while one was open for 20% -> 22% of each run, Pallas kernels for 16% -> 16%
where the time goes in v5:
time: 402 us; the launch traced here: 396 us
  waiting for transfers between devices  109 us (27%)
  Pallas kernels  86 us (21%)
  starting transfers between devices  80.4 us (20%)
  other arithmetic  42.6 us (11%)
  matrix products  37.4 us (9%)
  local copies, waits for them, and re-layouts  25.2 us (6%)
  between operations  15.5 us (4%)
    ppermute x55, waiting for transfers between devices, send(): return lax.ppermute(value, ALL, self.pairs(move))  103 us
    ppermute x55, starting transfers between devices, send(): return lax.ppermute(value, ALL, self.pairs(move))  80.3 us
    pallas_call x2, Pallas kernels, attention_backward(): pl.pallas_call(lambda *refs: backward_kernel(b, nkb, batch, width, bool(o...  24.4 us
    pallas_call x6, Pallas kernels, placed(): pl.pallas_call(lambda *refs: place_kernel(plan, len(sources), len(shapes)...  19.9 us
    dot_general x12, matrix products, dots(): return jnp.einsum(spec, left, right, preferred_element_type=F32)  18.6 us
    pallas_call x1, Pallas kernels, feed_forward_back(): pl.pallas_call(hidden_back_kernel, grid=(steps,), in_specs=[tiled(cot.sha...  17.4 us
    pallas_call x1, Pallas kernels, attention_forward(): pl.pallas_call(lambda *refs: forward_kernel(nkb, batch, width, *refs), gr...  12.7 us
    dot_general x4, matrix products, tn(): lax.dot_general(left, right, (((0,), (0,)), ((), ())), preferred_element_...  12.4 us
  transfers between devices with their start and end apart: 57, of which 26 were waited for; matrix products, arithmetic and copies ran while one was open for 22% of the time, Pallas kernels for 16%

profile of v5, /device:TPU:0, one launch (start us, length us, event | category | flops | bytes accessed | tf_op | source)
XLA Modules:
  0.0 395.7 jit_solution(3398520688879890166)
XLA Ops:
  11.3 3.1 collective-permute-start
  14.4 2.6 collective-permute-start.1
  22.5 8.1 %collective-permute-done.1 = bf16[136,768]{1,0:T(8,128)(2,1)S(1)} collective-permute-done((bf16[136,768]{1,0:T(8,128)(2,1)S(1)}, bf16[136,768]{1,0:T(8,128)(2,1)S(1)}, u32[]{:S(2)}, u32[]{:S(2)}) %collective-permute-start.1) | collective-permute-done | bytes 208928 | tf_op jit(solution)/shard_map/ppermute | solution.py:351
  34.0 3.7 convert_multiply_fusion
  42.1 11.3 %collective-permute-done.4.refs_2_ = bf16[4,136,384]{2,1,0:T(8,128)(2,1)} collective-permute-done((bf16[4,136,384]{2,1,0:T(8,128)(2,1)S(1)}, bf16[4,136,384]{2,1,0:T(8,128)(2,1)}, u32[]{:S(2)}, u32[]{:S(2)}) %collective-permute-start.4) | collective-permute-done | bytes 417824 | tf_op jit(solution)/shard_map/ppermute | solution.py:351
  55.5 2.6 collective-permute-start.8
  58.1 2.1 fusion.16
  60.2 5.3 %collective-permute-start.10 = (bf16[352,256]{1,0:T(8,128)(2,1)S(1)}, bf16[352,256]{1,0:T(8,128)(2,1)S(1)}, u32[]{:S(2)}, u32[]{:S(2)}) collective-permute-start(bf16[352,256]{1,0:T(8,128)(2,1)S(1)} %dynamic-slice_convert_fusion.2), channel_id=1, source_target_pairs={{0,4},{1,5},{2,6},{3,7},{4,0},{5,1},{6,2},{7,3},{8,12},{9,13},{10,... | collective-permute-start | bytes 540680 | tf_op jit(solution)/shard_map/ppermute | solution.py:351
  65.5 2.9 fusion.28
  68.4 2.8 pad_maximum_fusion.cot
  71.2 8.4 %collective-permute-done.10 = bf16[352,256]{1,0:T(8,128)(2,1)S(1)} collective-permute-done((bf16[352,256]{1,0:T(8,128)(2,1)S(1)}, bf16[352,256]{1,0:T(8,128)(2,1)S(1)}, u32[]{:S(2)}, u32[]{:S(2)}) %collective-permute-start.10) | collective-permute-done | bytes 180256 | tf_op jit(solution)/shard_map/ppermute | solution.py:351
  79.7 2.2 collective-permute-start.11
  84.4 3.6 place.6
  90.0 5.4 %collective-permute-done.12 = bf16[352,256]{1,0:T(8,128)(2,1)S(1)} collective-permute-done((bf16[352,256]{1,0:T(8,128)(2,1)S(1)}, bf16[352,256]{1,0:T(8,128)(2,1)S(1)}, u32[]{:S(2)}, u32[]{:S(2)}) %collective-permute-start.12) | collective-permute-done | bytes 180256 | tf_op jit(solution)/shard_map/ppermute | solution.py:351
  95.9 3.8 collective-permute-start.15
  99.9 2.2 collective-permute-start.13
  102.3 2.3 fusion.12.refs_1_
  106.0 3.5 place.7
  109.5 2.2 collective-permute-done.15
  113.6 4.9 %collective-permute-done.14.refs_7_ = bf16[2,352,256]{2,1,0:T(8,128)(2,1)S(1)} collective-permute-done((bf16[2,352,256]{2,1,0:T(8,128)(2,1)S(1)}, bf16[2,352,256]{2,1,0:T(8,128)(2,1)S(1)}, u32[]{:S(2)}, u32[]{:S(2)}) %collective-permute-start.14) | collective-permute-done | bytes 360480 | tf_op jit(solution)/shard_map/ppermute | solution.py:351
  118.9 2.3 collective-permute-start.20
  121.2 2.2 collective-permute-start.21
  123.5 12.7 %attention_forward.1 = (bf16[2,512,512]{2,1,0:T(8,128)(2,1)}, f32[2,512,512]{2,1,0:T(8,128)}, bf16[2,2,256,2048]{3,2,1,0:T(8,128)(2,1)}, f32[2,2,1,2048]{3,2,1,0:T(1,128)}) custom-call(s32[9]{0:T(128)} %concatenate.93.refs_0_, bf16[2,512,512]{2,1,0:T(8,128)(2,1)} %fusion.12.refs_1_, bf16[512,256]{1,0:T(8,128)(2,1)} %bitcast.195, bf16[512,256]{1,0:T(8,128)(2,1)} %bitcast.192, ...), custom_call_target="tpu_custom_call" | custom-call | flops 7516192768 | bytes 16777216 | tf_op jit(solution)/shard_map/attention_forward/pallas_call | solution.py:162
  136.8 3.0 collective-permute-done.22.refs_8_
  139.9 1.9 convolution_convert_fusion.7
  141.8 2.6 collective-permute-done.23
  146.0 2.5 collective-permute-done.24
  150.9 3.0 place.8
  154.0 11.6 %feed_forward.1 = (f32[1024,2816]{1,0:T(8,128)}, bf16[1024,1408]{1,0:T(8,128)(2,1)}) custom-call(bf16[1024,1024]{1,0:T(8,128)(2,1)} %pad_maximum_fusion.2.x, bf16[1024,2816]{1,0:T(8,128)(2,1)} %all-gather.2.cloned.1.call-done.w), custom_call_target="tpu_custom_call" | custom-call | flops 5905580032 | bytes 20971520 | tf_op jit(solution)/shard_map/feed_forward/pallas_call | solution.py:291
  165.5 4.4 %place.9 = bf16[2,2,352,1024]{3,2,1,0:T(8,128)(2,1)} custom-call(s32[3]{0:T(128)} %pad_add_fusion.refs_0_, bf16[2,352,256]{2,1,0:T(8,128)(2,1)} %get-tuple-element.464.refs_1_, bf16[2,352,256]{2,1,0:T(8,128)(2,1)} %copy-done.24, bf16[2,352,256]{2,1,0:T(8,128)(2,1)} %copy-done.25, bf16[2,352,256]{2,1,0:T(8,128)(2,1)} %copy-done.27, ...), custom_call_target="tpu_custom_call" | custom-call | tf_op jit(solution)/shard_map/place/pallas_call | solution.py:616
  170.0 17.4 %feed_forward_back.1 = (bf16[1024,2816]{1,0:T(8,128)(2,1)}, f32[512,1024]{1,0:T(8,128)}, bf16[512,1024]{1,0:T(8,128)(2,1)}) custom-call(bf16[1024,1024]{1,0:T(8,128)(2,1)} %pad_maximum_fusion.cot, bf16[1408,1024]{1,0:T(8,128)(2,1)} %bitcast.158, bf16[1024,2816]{1,0:T(8,128)(2,1)} %all-gather.2.cloned.1.call-done.w, f32[1024,2816]{1,0:T(8,128)} %get-tuple-element.474.act), custom_call_target="tpu_custom_call" | custom-call | flops 8858370048 | bytes 31457280 | tf_op jit(solution)/shard_map/feed_forward_back/pallas_call | solution.py:311
  187.7 2.5 collective-permute-done.26
  190.2 2.1 convert_add_fusion.3
  193.5 2.2 fusion.55
  196.2 8.8 %convolution_convert_fusion = bf16[1024,2816]{1,0:T(8,128)(2,1)} fusion(bf16[1024,1024]{1,0:T(8,128)(2,1)S(1)} %copy-done.14, bf16[1024,2816]{1,0:T(8,128)(2,1)S(1)} %bitcast.214), kind=kOutput, calls=%fused_computation | convolution fusion | flops 5908463616 | bytes 13631488 | tf_op jit(solution)/shard_map/dot_general | solution.py:31
  217.6 2.3 fusion.13.refs_2_
  219.9 2.8 convolution_convert_fusion.4
  222.8 2.2 constant_dynamic-slice_fusion.10
  225.7 6.5 %collective-permute-start.30 = (bf16[2,2,480,256]{3,2,0,1:T(8,128)(2,1)}, bf16[2,2,480,256]{3,2,0,1:T(8,128)(2,1)S(1)}, u32[]{:S(2)}, u32[]{:S(2)}) collective-permute-start(bf16[2,2,480,256]{3,2,0,1:T(8,128)(2,1)} %copy.76), channel_id=1, source_target_pairs={{0,16},{1,17},{2,18},{3,19},{4,20},{5,21},{6,22},{7,23},{8,24},{9,... | collective-permute-start | bytes 2949128 | tf_op jit(solution)/shard_map/ppermute | solution.py:351
  232.1 12.1 %attention_backward.2 = (bf16[512,512]{1,0:T(8,128)(2,1)}, f32[4,256,256]{2,1,0:T(8,128)}, f32[512,256]{1,0:T(8,128)}, f32[512,256]{1,0:T(8,128)}) custom-call(s32[9]{0:T(128)} %concatenate.93.refs_0_, bf16[2,512,512]{2,1,0:T(8,128)(2,1)} %fusion.12.refs_1_, bf16[2,512,512]{2,1,0:T(8,128)(2,1)} %fusion.13.refs_2_, ...), custom_call_target="tpu_custom_call" | custom-call | flops 9395240960 | bytes 10485760 | tf_op jit(solution)/shard_map/attention_backward/pallas_call | solution.py:206
  244.2 3.6 convert_add_fusion.2
  249.1 8.0 %collective-permute-done.31 = bf16[2,1,480,512]{3,2,0,1:T(8,128)(2,1)} collective-permute-done((bf16[2,1,480,512]{3,2,0,1:T(8,128)(2,1)}, bf16[2,1,480,512]{3,2,0,1:T(8,128)(2,1)}, u32[]{:S(2)}, u32[]{:S(2)}) %collective-permute-start.31) | collective-permute-done | bytes 983072 | tf_op jit(solution)/shard_map/ppermute | solution.py:351
  259.0 5.4 %collective-permute-start.34 = (bf16[2,1,480,256]{3,2,0,1:T(8,128)(2,1)S(1)}, bf16[2,1,480,256]{3,2,0,1:T(8,128)(2,1)}, u32[]{:S(2)}, u32[]{:S(2)}) collective-permute-start(bf16[2,1,480,256]{3,2,0,1:T(8,128)(2,1)S(1)} %constant_dynamic-slice_fusion.8), channel_id=1, source_target_pairs={{0,16},{1,17},{2,18},{3,19},{4,20},{5,21},{6,22},{7,23},{8,24},{9,... | collective-permute-start | bytes 1474568 | tf_op jit(solution)/shard_map/ppermute | solution.py:351
  264.6 1.8 collective-permute-start.33
  267.8 12.3 %attention_backward.3 = (bf16[512,512]{1,0:T(8,128)(2,1)}, f32[4,256,256]{2,1,0:T(8,128)}, f32[512,256]{1,0:T(8,128)}, f32[512,256]{1,0:T(8,128)}) custom-call(s32[9]{0:T(128)} %concatenate.93.refs_0_, bf16[2,512,512]{2,1,0:T(8,128)(2,1)} %fusion.12.refs_1_, bf16[2,512,512]{2,1,0:T(8,128)(2,1)} %fusion.13.refs_2_, ...), custom_call_target="tpu_custom_call" | custom-call | flops 9395240960 | bytes 10485760 | tf_op jit(solution)/shard_map/attention_backward/pallas_call | solution.py:206
  281.0 3.7 collective-permute-done.33
  284.7 2.3 place.10
  292.1 2.3 bitcast_convert_fusion
  295.5 2.1 collective-permute-done.35
  302.3 5.4 %collective-permute-start.42 = (bf16[1,480,256]{2,1,0:T(8,128)(2,1)S(1)}, bf16[1,480,256]{2,1,0:T(8,128)(2,1)}, u32[]{:S(2)}, u32[]{:S(2)}) collective-permute-start(bf16[1,480,256]{2,1,0:T(8,128)(2,1)S(1)} %get-tuple-element.689), channel_id=1, source_target_pairs={{0,4},{1,5},{2,6},{3,7},{4,0},{5,1},{6,2},{7,3},{8,12},{9,13},{10,... | collective-permute-start | bytes 737288 | tf_op jit(solution)/shard_map/ppermute | solution.py:351
  309.3 3.1 place.11
  313.8 2.7 collective-permute-start.39
  316.4 2.6 fusion.5
  319.4 5.3 %collective-permute-start.43 = (bf16[1,480,256]{2,1,0:T(8,128)(2,1)S(1)}, bf16[1,480,256]{2,1,0:T(8,128)(2,1)S(1)}, u32[]{:S(2)}, u32[]{:S(2)}) collective-permute-start(bf16[1,480,256]{2,1,0:T(8,128)(2,1)S(1)} %get-tuple-element.688), channel_id=1, source_target_pairs={{0,6},{1,7},{2,0},{3,1},{4,2},{5,3},{6,4},{7,5},{8,14},{9,15},{10,... | collective-permute-start | bytes 737288 | tf_op jit(solution)/shard_map/ppermute | solution.py:351
  324.7 1.9 fusion.8
  326.6 11.5 %collective-permute-done.42 = bf16[1,480,256]{2,1,0:T(8,128)(2,1)} collective-permute-done((bf16[1,480,256]{2,1,0:T(8,128)(2,1)S(1)}, bf16[1,480,256]{2,1,0:T(8,128)(2,1)}, u32[]{:S(2)}, u32[]{:S(2)}) %collective-permute-start.42) | collective-permute-done | bytes 245792 | tf_op jit(solution)/shard_map/ppermute | solution.py:351
  338.1 2.9 collective-permute-done.43
  341.3 6.0 %reduce-scatter.2.cloned.1.call-done = bf16[128,2816]{1,0:T(8,128)(2,1)} async-done(((bf16[1024,2816]{1,0:T(8,128)(2,1)}), bf16[128,2816]{1,0:T(8,128)(2,1)}) %reduce-scatter.2.cloned.1.call-update) | async-done | bytes 720912 | tf_op jit(solution)/shard_map/reduce_scatter | solution.py:786
  347.3 2.3 collective-permute-start.44
  354.7 3.5 collective-permute-done.45
  358.2 4.1 %collective-permute-done.46 = bf16[1,136,512]{2,1,0:T(8,128)(2,1)S(1)} collective-permute-done((bf16[1,136,512]{2,1,0:T(8,128)(2,1)S(1)}, bf16[1,136,512]{2,1,0:T(8,128)(2,1)S(1)}, u32[]{:S(2)}, u32[]{:S(2)}) %collective-permute-start.46) | collective-permute-done | bytes 139296 | tf_op jit(solution)/shard_map/ppermute | solution.py:351
  362.4 3.2 collective-permute-done.44
  367.9 9.3 %collective-permute-done.49 = bf16[136,512]{1,0:T(8,128)(2,1)S(1)} collective-permute-done((bf16[136,512]{1,0:T(8,128)(2,1)S(1)}, bf16[136,512]{1,0:T(8,128)(2,1)S(1)}, u32[]{:S(2)}, u32[]{:S(2)}) %collective-permute-start.49) | collective-permute-done | bytes 139296 | tf_op jit(solution)/shard_map/ppermute | solution.py:351
  377.3 1.9 collective-permute-start.51
  (308 shorter events, 85.1 us)
Async XLA Ops:
  7.2 146.8 %all-gather.2.cloned.1.call-start = ((), (), s32[]{:S(2)}) async-start(), calls=%async_computation.1 | async-start | bytes 6488064 | tf_op jit(solution)/shard_map/all_gather | solution.py:671
  11.3 11.2 %collective-permute-start = (bf16[136,768]{1,0:T(8,128)(2,1)S(1)}, bf16[136,768]{1,0:T(8,128)(2,1)S(1)}, u32[]{:S(2)}, u32[]{:S(2)}) collective-permute-start(bf16[136,768]{1,0:T(8,128)(2,1)S(1)} %fusion.45), channel_id=1, source_target_pairs={{0,2},{1,3},{2,4},{3,5},{4,6},{5,7},{6,0},{7,1},{8,10},{9,11},{10,... | collective-permute-start | bytes 626696 | tf_op jit(solution)/shard_map/ppermute | solution.py:351
  14.4 16.3 %collective-permute-start.1 = (bf16[136,768]{1,0:T(8,128)(2,1)S(1)}, bf16[136,768]{1,0:T(8,128)(2,1)S(1)}, u32[]{:S(2)}, u32[]{:S(2)}) collective-permute-start(bf16[136,768]{1,0:T(8,128)(2,1)S(1)} %fusion.45), channel_id=1, source_target_pairs={{0,4},{1,5},{2,6},{3,7},{4,0},{5,1},{6,2},{7,3},{8,12},{9,13},{10,... | collective-permute-start | bytes 626696 | tf_op jit(solution)/shard_map/ppermute | solution.py:351
  17.0 13.7 %collective-permute-start.2 = (bf16[136,768]{1,0:T(8,128)(2,1)S(1)}, bf16[136,768]{1,0:T(8,128)(2,1)S(1)}, u32[]{:S(2)}, u32[]{:S(2)}) collective-permute-start(bf16[136,768]{1,0:T(8,128)(2,1)S(1)} %fusion.45), channel_id=1, source_target_pairs={{0,6},{1,7},{2,0},{3,1},{4,2},{5,3},{6,4},{7,5},{8,14},{9,15},{10,... | collective-permute-start | bytes 626696 | tf_op jit(solution)/shard_map/ppermute | solution.py:351
  18.3 12.8 %collective-permute-start.3 = (bf16[2,256,1024]{2,1,0:T(8,128)(2,1)}, bf16[2,256,1024]{2,1,0:T(8,128)(2,1)}, u32[]{:S(2)}, u32[]{:S(2)}) collective-permute-start(bf16[2,256,1024]{2,1,0:T(8,128)(2,1)} %param.13), channel_id=1, source_target_pairs={{0,8},{1,9},{2,10},{3,11},{4,12},{5,13},{6,14},{7,15},{8,0},{9,1},... | collective-permute-start | bytes 3145736 | tf_op jit(solution)/shard_map/ppermute | solution.py:351
  18.3 39.8 %collective-permute-start.18 = (bf16[512,1024]{1,0:T(8,128)(2,1)}, bf16[512,1024]{1,0:T(8,128)(2,1)}, u32[]{:S(2)}, u32[]{:S(2)}) collective-permute-start(bf16[512,1024]{1,0:T(8,128)(2,1)} %bitcast.149), channel_id=1, source_target_pairs={{0,8},{1,9},{2,10},{3,11},{4,12},{5,13},{6,14},{7,15},{8,0},{9,1},... | collective-permute-start | bytes 3145736 | tf_op jit(solution)/shard_map/ppermute | solution.py:351
  31.2 316.1 %reduce-scatter.2.cloned.1.call-start = ((), (), s32[]{:S(2)}) async-start(), calls=%async_computation.2 | async-start | bytes 6488064 | tf_op jit(solution)/shard_map/reduce_scatter | solution.py:786
  31.3 24.2 %copy-start.11 = (bf16[4,136,384]{2,1,0:T(8,128)(2,1)}, bf16[4,136,384]{2,1,0:T(8,128)(2,1)S(1)}, u32[]{:S(2)}) copy-start(bf16[4,136,384]{2,1,0:T(8,128)(2,1)S(1)} %get-tuple-element.370.refs_5_) | copy-start | bytes 1253380
  31.3 53.0 %copy-start.10 = (bf16[4,136,384]{2,1,0:T(8,128)(2,1)}, bf16[4,136,384]{2,1,0:T(8,128)(2,1)S(1)}, u32[]{:S(2)}) copy-start(bf16[4,136,384]{2,1,0:T(8,128)(2,1)S(1)} %get-tuple-element.366.refs_1_) | copy-start | bytes 1253380
  34.0 24.1 %copy-start.4 = (bf16[2,256,1024]{2,1,0:T(8,128)(2,1)S(1)}, bf16[2,256,1024]{2,1,0:T(8,128)(2,1)}, u32[]{:S(2)}) copy-start(bf16[2,256,1024]{2,1,0:T(8,128)(2,1)} %param.24) | copy-start | bytes 3145732
  37.7 15.8 %collective-permute-start.4 = (bf16[4,136,384]{2,1,0:T(8,128)(2,1)S(1)}, bf16[4,136,384]{2,1,0:T(8,128)(2,1)}, u32[]{:S(2)}, u32[]{:S(2)}) collective-permute-start(bf16[4,136,384]{2,1,0:T(8,128)(2,1)S(1)} %get-tuple-element.366.refs_1_), channel_id=1, source_target_pairs={{0,1},{1,0},{2,3},{3,2},{4,5},{5,4},{6,7},{7,6},{8,9},{9,8},{10,11... | collective-permute-start | bytes 1253384 | tf_op jit(solution)/shard_map/ppermute | solution.py:351
  39.1 14.3 %collective-permute-start.5 = (bf16[4,136,384]{2,1,0:T(8,128)(2,1)S(1)}, bf16[4,136,384]{2,1,0:T(8,128)(2,1)}, u32[]{:S(2)}, u32[]{:S(2)}) collective-permute-start(bf16[4,136,384]{2,1,0:T(8,128)(2,1)S(1)} %get-tuple-element.370.refs_5_), channel_id=1, source_target_pairs={{0,16},{1,17},{2,18},{3,19},{4,20},{5,21},{6,22},{7,23},{8,24},{9,... | collective-permute-start | bytes 1253384 | tf_op jit(solution)/shard_map/ppermute | solution.py:351
  53.5 26.2 %collective-permute-start.6 = (bf16[4,136,384]{2,1,0:T(8,128)(2,1)}, bf16[4,136,384]{2,1,0:T(8,128)(2,1)S(1)}, u32[]{:S(2)}, u32[]{:S(2)}) collective-permute-start(bf16[4,136,384]{2,1,0:T(8,128)(2,1)} %collective-permute-done.4.refs_2_), channel_id=1, source_target_pairs={{0,16},{1,17},{2,18},{3,19},{4,20},{5,21},{6,22},{7,23},{8,24},{9,... | collective-permute-start | bytes 1253384 | tf_op jit(solution)/shard_map/ppermute | solution.py:351
  54.9 24.7 %collective-permute-start.7 = (bf16[4,136,384]{2,1,0:T(8,128)(2,1)S(1)}, bf16[4,136,384]{2,1,0:T(8,128)(2,1)S(1)}, u32[]{:S(2)}, u32[]{:S(2)}) collective-permute-start(bf16[4,136,384]{2,1,0:T(8,128)(2,1)S(1)} %get-tuple-element.366.refs_1_), channel_id=1, source_target_pairs={{0,16},{1,17},{2,18},{3,19},{4,20},{5,21},{6,22},{7,23},{8,24},{9,... | collective-permute-start | bytes 1253384 | tf_op jit(solution)/shard_map/ppermute | solution.py:351
  55.5 24.2 %collective-permute-start.8 = (bf16[4,136,384]{2,1,0:T(8,128)(2,1)S(1)}, bf16[4,136,384]{2,1,0:T(8,128)(2,1)S(1)}, u32[]{:S(2)}, u32[]{:S(2)}) collective-permute-start(bf16[4,136,384]{2,1,0:T(8,128)(2,1)S(1)} %get-tuple-element.370.refs_5_), channel_id=1, source_target_pairs={{0,1},{1,0},{2,3},{3,2},{4,5},{5,4},{6,7},{7,6},{8,9},{9,8},{10,11... | collective-permute-start | bytes 1253384 | tf_op jit(solution)/shard_map/ppermute | solution.py:351
  58.1 21.6 %collective-permute-start.9 = (bf16[4,136,384]{2,1,0:T(8,128)(2,1)}, bf16[4,136,384]{2,1,0:T(8,128)(2,1)S(1)}, u32[]{:S(2)}, u32[]{:S(2)}) collective-permute-start(bf16[4,136,384]{2,1,0:T(8,128)(2,1)} %collective-permute-done.5.refs_7_), channel_id=1, source_target_pairs={{0,1},{1,0},{2,3},{3,2},{4,5},{5,4},{6,7},{7,6},{8,9},{9,8},{10,11... | collective-permute-start | bytes 1253384 | tf_op jit(solution)/shard_map/ppermute | solution.py:351
  60.2 19.4 %collective-permute-start.10 = (bf16[352,256]{1,0:T(8,128)(2,1)S(1)}, bf16[352,256]{1,0:T(8,128)(2,1)S(1)}, u32[]{:S(2)}, u32[]{:S(2)}) collective-permute-start(bf16[352,256]{1,0:T(8,128)(2,1)S(1)} %dynamic-slice_convert_fusion.2), channel_id=1, source_target_pairs={{0,4},{1,5},{2,6},{3,7},{4,0},{5,1},{6,2},{7,3},{8,12},{9,13},{10,... | collective-permute-start | bytes 540680 | tf_op jit(solution)/shard_map/ppermute | solution.py:351
  68.4 19.7 %copy-start.3 = (f32[2,2,256,1024]{3,2,1,0:T(8,128)S(1)}, f32[2,2,256,1024]{3,2,1,0:T(8,128)}, u32[]{:S(2)}) copy-start(f32[2,2,256,1024]{3,2,1,0:T(8,128)} %convert_multiply_fusion) | copy-start | bytes 12582916
  79.7 10.3 %collective-permute-start.11 = (bf16[352,256]{1,0:T(8,128)(2,1)S(1)}, bf16[352,256]{1,0:T(8,128)(2,1)S(1)}, u32[]{:S(2)}, u32[]{:S(2)}) collective-permute-start(bf16[352,256]{1,0:T(8,128)(2,1)S(1)} %dynamic-slice_convert_fusion.2), channel_id=1, source_target_pairs={{0,2},{1,3},{2,4},{3,5},{4,6},{5,7},{6,0},{7,1},{8,10},{9,11},{10,... | collective-permute-start | bytes 540680 | tf_op jit(solution)/shard_map/ppermute | solution.py:351
  81.9 13.4 %collective-permute-start.12 = (bf16[352,256]{1,0:T(8,128)(2,1)S(1)}, bf16[352,256]{1,0:T(8,128)(2,1)S(1)}, u32[]{:S(2)}, u32[]{:S(2)}) collective-permute-start(bf16[352,256]{1,0:T(8,128)(2,1)S(1)} %dynamic-slice_convert_fusion.2), channel_id=1, source_target_pairs={{0,6},{1,7},{2,0},{3,1},{4,2},{5,3},{6,4},{7,5},{8,14},{9,15},{10,... | collective-permute-start | bytes 540680 | tf_op jit(solution)/shard_map/ppermute | solution.py:351
  95.4 9.2 %collective-permute-start.16 = (bf16[4,2,128,256]{3,2,1,0:T(8,128)(2,1)S(1)}, bf16[4,2,128,256]{3,2,1,0:T(8,128)(2,1)S(1)}, u32[]{:S(2)}, u32[]{:S(2)}) collective-permute-start(bf16[4,2,128,256]{3,2,1,0:T(8,128)(2,1)S(1)} %copy-done.48), channel_id=1, source_target_pairs={{0,8},{1,9},{2,10},{3,11},{4,12},{5,13},{6,14},{7,15},{8,0},{9,1},... | collective-permute-start | bytes 1572872 | tf_op jit(solution)/shard_map/ppermute | solution.py:351
  95.4 9.2 %collective-permute-start.17 = (bf16[4,2,128,128]{3,2,1,0:T(8,128)(2,1)S(1)}, bf16[4,2,128,128]{3,2,1,0:T(8,128)(2,1)S(1)}, u32[]{:S(2)}, u32[]{:S(2)}) collective-permute-start(bf16[4,2,128,128]{3,2,1,0:T(8,128)(2,1)S(1)} %copy-done.49), channel_id=1, source_target_pairs={{0,8},{1,9},{2,10},{3,11},{4,12},{5,13},{6,14},{7,15},{8,0},{9,1},... | collective-permute-start | bytes 786440 | tf_op jit(solution)/shard_map/ppermute | solution.py:351
  95.9 15.8 %collective-permute-start.15 = (bf16[2,2,256,256]{3,2,1,0:T(8,128)(2,1)S(1)}, bf16[2,2,256,256]{3,2,1,0:T(8,128)(2,1)S(1)}, u32[]{:S(2)}, u32[]{:S(2)}) collective-permute-start(bf16[2,2,256,256]{3,2,1,0:T(8,128)(2,1)S(1)} %bitcast.186), channel_id=1, source_target_pairs={{0,16},{1,17},{2,18},{3,19},{4,20},{5,21},{6,22},{7,23},{8,24},{9,... | collective-permute-start | bytes 1572872 | tf_op jit(solution)/shard_map/ppermute | solution.py:351
  99.8 18.7 %collective-permute-start.14 = (bf16[2,352,256]{2,1,0:T(8,128)(2,1)S(1)}, bf16[2,352,256]{2,1,0:T(8,128)(2,1)S(1)}, u32[]{:S(2)}, u32[]{:S(2)}) collective-permute-start(bf16[2,352,256]{2,1,0:T(8,128)(2,1)S(1)} %pad_maximum_fusion.15), channel_id=1, source_target_pairs={{0,16},{1,17},{2,18},{3,19},{4,20},{5,21},{6,22},{7,23},{8,24},{9,... | collective-permute-start | bytes 1081352 | tf_op jit(solution)/shard_map/ppermute | solution.py:351
  99.9 18.9 %collective-permute-start.13 = (bf16[2,352,256]{2,1,0:T(8,128)(2,1)S(1)}, bf16[2,352,256]{2,1,0:T(8,128)(2,1)S(1)}, u32[]{:S(2)}, u32[]{:S(2)}) collective-permute-start(bf16[2,352,256]{2,1,0:T(8,128)(2,1)S(1)} %pad_maximum_fusion.14), channel_id=1, source_target_pairs={{0,1},{1,0},{2,3},{3,2},{4,5},{5,4},{6,7},{7,6},{8,9},{9,8},{10,11... | collective-permute-start | bytes 1081352 | tf_op jit(solution)/shard_map/ppermute | solution.py:351
  118.9 17.4 %collective-permute-start.20 = (bf16[2,352,256]{2,1,0:T(8,128)(2,1)S(1)}, bf16[2,352,256]{2,1,0:T(8,128)(2,1)S(1)}, u32[]{:S(2)}, u32[]{:S(2)}) collective-permute-start(bf16[2,352,256]{2,1,0:T(8,128)(2,1)S(1)} %get-tuple-element.704), channel_id=1, source_target_pairs={{0,16},{1,17},{2,18},{3,19},{4,20},{5,21},{6,22},{7,23},{8,24},{9,... | collective-permute-start | bytes 1081352 | tf_op jit(solution)/shard_map/ppermute | solution.py:351
  121.2 18.7 %copy-start.45 = (bf16[2,2,128,1024]{3,2,1,0:T(8,128)(2,1)S(1)}, bf16[2,2,128,1024]{3,2,1,0:T(8,128)(2,1)}, u32[]{:S(2)}) copy-start(bf16[2,2,128,1024]{3,2,1,0:T(8,128)(2,1)} %get-tuple-element.379) | copy-start | bytes 3145732
  121.2 15.1 %collective-permute-start.21 = (bf16[2,352,256]{2,1,0:T(8,128)(2,1)S(1)}, bf16[2,352,256]{2,1,0:T(8,128)(2,1)S(1)}, u32[]{:S(2)}, u32[]{:S(2)}) collective-permute-start(bf16[2,352,256]{2,1,0:T(8,128)(2,1)S(1)} %get-tuple-element.703), channel_id=1, source_target_pairs={{0,1},{1,0},{2,3},{3,2},{4,5},{5,4},{6,7},{7,6},{8,9},{9,8},{10,11... | collective-permute-start | bytes 1081352 | tf_op jit(solution)/shard_map/ppermute | solution.py:351
  123.3 13.5 %collective-permute-start.19 = (bf16[2,352,256]{2,1,0:T(8,128)(2,1)S(1)}, bf16[2,352,256]{2,1,0:T(8,128)(2,1)S(1)}, u32[]{:S(2)}, u32[]{:S(2)}) collective-permute-start(bf16[2,352,256]{2,1,0:T(8,128)(2,1)S(1)} %collective-permute-done.13.refs_2_), channel_id=1, source_target_pairs={{0,16},{1,17},{2,18},{3,19},{4,20},{5,21},{6,22},{7,23},{8,24},{9,... | collective-permute-start | bytes 1081352 | tf_op jit(solution)/shard_map/ppermute | solution.py:351
  123.4 16.4 %collective-permute-start.22 = (bf16[2,352,256]{2,1,0:T(8,128)(2,1)S(1)}, bf16[2,352,256]{2,1,0:T(8,128)(2,1)S(1)}, u32[]{:S(2)}, u32[]{:S(2)}) collective-permute-start(bf16[2,352,256]{2,1,0:T(8,128)(2,1)S(1)} %collective-permute-done.14.refs_7_), channel_id=1, source_target_pairs={{0,1},{1,0},{2,3},{3,2},{4,5},{5,4},{6,7},{7,6},{8,9},{9,8},{10,11... | collective-permute-start | bytes 1081352 | tf_op jit(solution)/shard_map/ppermute | solution.py:351
  141.8 2.7 collective-permute-start.23
  145.8 2.7 collective-permute-start.24
  153.8 11.7 %collective-permute-start.25 = (bf16[4,2,352,256]{3,2,1,0:T(8,128)(2,1)}, bf16[4,2,352,256]{3,2,1,0:T(8,128)(2,1)}, u32[]{:S(2)}, u32[]{:S(2)}) collective-permute-start(bf16[4,2,352,256]{3,2,1,0:T(8,128)(2,1)} %place.8), channel_id=1, source_target_pairs={{0,8},{1,9},{2,10},{3,11},{4,12},{5,13},{6,14},{7,15},{8,0},{9,1},... | collective-permute-start | bytes 4325384 | tf_op jit(solution)/shard_map/ppermute | solution.py:351
  187.3 2.9 collective-permute-start.26
  195.8 9.2 %collective-permute-start.27 = (bf16[2,256,1024]{2,1,0:T(8,128)(2,1)}, bf16[2,256,1024]{2,1,0:T(8,128)(2,1)}, u32[]{:S(2)}, u32[]{:S(2)}) collective-permute-start(bf16[2,256,1024]{2,1,0:T(8,128)(2,1)} %get-tuple-element.682), channel_id=1, source_target_pairs={{0,8},{1,9},{2,10},{3,11},{4,12},{5,13},{6,14},{7,15},{8,0},{9,1},... | collective-permute-start | bytes 3145736 | tf_op jit(solution)/shard_map/ppermute | solution.py:351
  212.1 7.8 %collective-permute-start.28 = (bf16[2,2,480,512]{3,2,0,1:T(8,128)(2,1)S(1)}, bf16[2,2,480,512]{3,2,0,1:T(8,128)(2,1)}, u32[]{:S(2)}, u32[]{:S(2)}) collective-permute-start(bf16[2,2,480,512]{3,2,0,1:T(8,128)(2,1)S(1)} %copy.77), channel_id=1, source_target_pairs={{0,8},{1,9},{2,10},{3,11},{4,12},{5,13},{6,14},{7,15},{8,0},{9,1},... | collective-permute-start | bytes 5898248 | tf_op jit(solution)/shard_map/ppermute | solution.py:351
  222.7 21.6 %collective-permute-start.29 = (bf16[512,1024]{1,0:T(8,128)(2,1)}, bf16[512,1024]{1,0:T(8,128)(2,1)}, u32[]{:S(2)}, u32[]{:S(2)}) collective-permute-start(bf16[512,1024]{1,0:T(8,128)(2,1)} %convolution_convert_fusion.4), channel_id=1, source_target_pairs={{0,8},{1,9},{2,10},{3,11},{4,12},{5,13},{6,14},{7,15},{8,0},{9,1},... | collective-permute-start | bytes 3145736 | tf_op jit(solution)/shard_map/ppermute | solution.py:351
  225.0 19.2 %copy-start.13 = (bf16[2,2,352,1024]{3,2,1,0:T(8,128)(2,1)S(1)}, bf16[2,2,352,1024]{3,2,1,0:T(8,128)(2,1)}, u32[]{:S(2)}) copy-start(bf16[2,2,352,1024]{3,2,1,0:T(8,128)(2,1)} %place.9) | copy-start | bytes 8650756
  225.0 32.1 %collective-permute-start.31 = (bf16[2,1,480,512]{3,2,0,1:T(8,128)(2,1)}, bf16[2,1,480,512]{3,2,0,1:T(8,128)(2,1)}, u32[]{:S(2)}, u32[]{:S(2)}) collective-permute-start(bf16[2,1,480,512]{3,2,0,1:T(8,128)(2,1)} %constant_dynamic-slice_fusion.10), channel_id=1, source_target_pairs={{0,1},{1,0},{2,3},{3,2},{4,5},{5,4},{6,7},{7,6},{8,9},{9,8},{10,11... | collective-permute-start | bytes 2949128 | tf_op jit(solution)/shard_map/ppermute | solution.py:351
  225.7 31.4 %collective-permute-start.30 = (bf16[2,2,480,256]{3,2,0,1:T(8,128)(2,1)}, bf16[2,2,480,256]{3,2,0,1:T(8,128)(2,1)S(1)}, u32[]{:S(2)}, u32[]{:S(2)}) collective-permute-start(bf16[2,2,480,256]{3,2,0,1:T(8,128)(2,1)} %copy.76), channel_id=1, source_target_pairs={{0,16},{1,17},{2,18},{3,19},{4,20},{5,21},{6,22},{7,23},{8,24},{9,... | collective-permute-start | bytes 2949128 | tf_op jit(solution)/shard_map/ppermute | solution.py:351
  259.0 22.0 %collective-permute-start.34 = (bf16[2,1,480,256]{3,2,0,1:T(8,128)(2,1)S(1)}, bf16[2,1,480,256]{3,2,0,1:T(8,128)(2,1)}, u32[]{:S(2)}, u32[]{:S(2)}) collective-permute-start(bf16[2,1,480,256]{3,2,0,1:T(8,128)(2,1)S(1)} %constant_dynamic-slice_fusion.8), channel_id=1, source_target_pairs={{0,16},{1,17},{2,18},{3,19},{4,20},{5,21},{6,22},{7,23},{8,24},{9,... | collective-permute-start | bytes 1474568 | tf_op jit(solution)/shard_map/ppermute | solution.py:351
  264.6 20.0 %collective-permute-start.33 = (bf16[2,1,480,256]{3,2,0,1:T(8,128)(2,1)S(1)}, bf16[2,1,480,256]{3,2,0,1:T(8,128)(2,1)S(1)}, u32[]{:S(2)}, u32[]{:S(2)}) collective-permute-start(bf16[2,1,480,256]{3,2,0,1:T(8,128)(2,1)S(1)} %constant_dynamic-slice_fusion.9), channel_id=1, source_target_pairs={{0,1},{1,0},{2,3},{3,2},{4,5},{5,4},{6,7},{7,6},{8,9},{9,8},{10,11... | collective-permute-start | bytes 1474568 | tf_op jit(solution)/shard_map/ppermute | solution.py:351
  266.5 14.5 %collective-permute-start.32 = (bf16[2,256,256]{2,1,0:T(8,128)(2,1)S(1)}, bf16[2,256,256]{2,1,0:T(8,128)(2,1)S(1)}, u32[]{:S(2)}, u32[]{:S(2)}) collective-permute-start(bf16[2,256,256]{2,1,0:T(8,128)(2,1)S(1)} %slice.264), channel_id=1, source_target_pairs={{16,0},{17,1},{18,2},{19,3},{20,4},{21,5},{22,6},{23,7},{24,8},{25... | collective-permute-start | bytes 786440 | tf_op jit(solution)/shard_map/ppermute | solution.py:351
  287.0 8.5 %collective-permute-start.36 = (bf16[2,512,128]{2,1,0:T(8,128)(2,1)}, bf16[2,512,128]{2,1,0:T(8,128)(2,1)S(1)}, u32[]{:S(2)}, u32[]{:S(2)}) collective-permute-start(bf16[2,512,128]{2,1,0:T(8,128)(2,1)} %get-tuple-element.605), channel_id=1, source_target_pairs={{0,8},{1,9},{2,10},{3,11},{4,12},{5,13},{6,14},{7,15},{8,0},{9,1},... | collective-permute-start | bytes 786440 | tf_op jit(solution)/shard_map/ppermute | solution.py:351
  287.0 10.6 %collective-permute-start.35 = (bf16[2,256,256]{2,1,0:T(8,128)(2,1)S(1)}, bf16[2,256,256]{2,1,0:T(8,128)(2,1)S(1)}, u32[]{:S(2)}, u32[]{:S(2)}) collective-permute-start(bf16[2,256,256]{2,1,0:T(8,128)(2,1)S(1)} %slice.263), channel_id=1, source_target_pairs={{16,0},{17,1},{18,2},{19,3},{20,4},{21,5},{22,6},{23,7},{24,8},{25... | collective-permute-start | bytes 786440 | tf_op jit(solution)/shard_map/ppermute | solution.py:351
  300.6 13.2 %collective-permute-start.40 = (bf16[2,256,1024]{2,1,0:T(8,128)(2,1)}, bf16[2,256,1024]{2,1,0:T(8,128)(2,1)}, u32[]{:S(2)}, u32[]{:S(2)}) collective-permute-start(bf16[2,256,1024]{2,1,0:T(8,128)(2,1)} %add_convert_fusion), channel_id=1, source_target_pairs={{0,8},{1,9},{2,10},{3,11},{4,12},{5,13},{6,14},{7,15},{8,0},{9,1},... | collective-permute-start | bytes 3145736 | tf_op jit(solution)/shard_map/ppermute | solution.py:351
  300.9 18.5 %collective-permute-start.41 = (bf16[1,480,256]{2,1,0:T(8,128)(2,1)S(1)}, bf16[1,480,256]{2,1,0:T(8,128)(2,1)}, u32[]{:S(2)}, u32[]{:S(2)}) collective-permute-start(bf16[1,480,256]{2,1,0:T(8,128)(2,1)S(1)} %get-tuple-element.690), channel_id=1, source_target_pairs={{0,2},{1,3},{2,4},{3,5},{4,6},{5,7},{6,0},{7,1},{8,10},{9,11},{10,... | collective-permute-start | bytes 737288 | tf_op jit(solution)/shard_map/ppermute | solution.py:351
  302.3 35.7 %collective-permute-start.42 = (bf16[1,480,256]{2,1,0:T(8,128)(2,1)S(1)}, bf16[1,480,256]{2,1,0:T(8,128)(2,1)}, u32[]{:S(2)}, u32[]{:S(2)}) collective-permute-start(bf16[1,480,256]{2,1,0:T(8,128)(2,1)S(1)} %get-tuple-element.689), channel_id=1, source_target_pairs={{0,4},{1,5},{2,6},{3,7},{4,0},{5,1},{6,2},{7,3},{8,12},{9,13},{10,... | collective-permute-start | bytes 737288 | tf_op jit(solution)/shard_map/ppermute | solution.py:351
  312.4 28.6 %collective-permute-start.37 = (bf16[4,128,512]{2,1,0:T(8,128)(2,1)}, bf16[4,128,512]{2,1,0:T(8,128)(2,1)S(1)}, u32[]{:S(2)}, u32[]{:S(2)}) collective-permute-start(bf16[4,128,512]{2,1,0:T(8,128)(2,1)} %get-tuple-element.622), channel_id=1, source_target_pairs={{0,1},{1,0},{2,3},{3,2},{4,5},{5,4},{6,7},{7,6},{8,9},{9,8},{10,11... | collective-permute-start | bytes 1572872 | tf_op jit(solution)/shard_map/ppermute | solution.py:351
  312.4 28.5 %collective-permute-start.38 = (bf16[4,128,512]{2,1,0:T(8,128)(2,1)}, bf16[4,128,512]{2,1,0:T(8,128)(2,1)S(1)}, u32[]{:S(2)}, u32[]{:S(2)}) collective-permute-start(bf16[4,128,512]{2,1,0:T(8,128)(2,1)} %get-tuple-element.623), channel_id=1, source_target_pairs={{0,16},{1,17},{2,18},{3,19},{4,20},{5,21},{6,22},{7,23},{8,24},{9,... | collective-permute-start | bytes 1572872 | tf_op jit(solution)/shard_map/ppermute | solution.py:351
  313.8 27.2 %collective-permute-start.39 = (bf16[4,128,512]{2,1,0:T(8,128)(2,1)S(1)}, bf16[4,128,512]{2,1,0:T(8,128)(2,1)S(1)}, u32[]{:S(2)}, u32[]{:S(2)}) collective-permute-start(bf16[4,128,512]{2,1,0:T(8,128)(2,1)S(1)} %copy-done.47), channel_id=1, source_target_pairs={{0,17},{1,16},{2,19},{3,18},{4,21},{5,20},{6,23},{7,22},{8,25},{9,... | collective-permute-start | bytes 1572872 | tf_op jit(solution)/shard_map/ppermute | solution.py:351
  319.4 21.5 %collective-permute-start.43 = (bf16[1,480,256]{2,1,0:T(8,128)(2,1)S(1)}, bf16[1,480,256]{2,1,0:T(8,128)(2,1)S(1)}, u32[]{:S(2)}, u32[]{:S(2)}) collective-permute-start(bf16[1,480,256]{2,1,0:T(8,128)(2,1)S(1)} %get-tuple-element.688), channel_id=1, source_target_pairs={{0,6},{1,7},{2,0},{3,1},{4,2},{5,3},{6,4},{7,5},{8,14},{9,15},{10,... | collective-permute-start | bytes 737288 | tf_op jit(solution)/shard_map/ppermute | solution.py:351
  347.3 18.3 %copy-start.30 = (bf16[128,2816]{1,0:T(8,128)(2,1)S(1)}, bf16[128,2816]{1,0:T(8,128)(2,1)}, u32[]{:S(2)}) copy-start(bf16[128,2816]{1,0:T(8,128)(2,1)} %reduce-scatter.2.cloned.1.call-done) | copy-start | bytes 2162692
  347.3 18.3 %collective-permute-start.44 = (bf16[128,2816]{1,0:T(8,128)(2,1)}, bf16[128,2816]{1,0:T(8,128)(2,1)S(1)}, u32[]{:S(2)}, u32[]{:S(2)}) collective-permute-start(bf16[128,2816]{1,0:T(8,128)(2,1)} %reduce-scatter.2.cloned.1.call-done), channel_id=1, source_target_pairs={{0,16},{1,17},{2,18},{3,19},{4,20},{5,21},{6,22},{7,23},{8,24},{9,... | collective-permute-start | bytes 2162696 | tf_op jit(solution)/shard_map/ppermute | solution.py:351
  349.7 8.5 %collective-permute-start.45 = (bf16[1,136,512]{2,1,0:T(8,128)(2,1)S(1)}, bf16[1,136,512]{2,1,0:T(8,128)(2,1)S(1)}, u32[]{:S(2)}, u32[]{:S(2)}) collective-permute-start(bf16[1,136,512]{2,1,0:T(8,128)(2,1)S(1)} %get-tuple-element.711), channel_id=1, source_target_pairs={{0,2},{1,3},{2,4},{3,5},{4,6},{5,7},{6,0},{7,1},{8,10},{9,11},{10,... | collective-permute-start | bytes 417800 | tf_op jit(solution)/shard_map/ppermute | solution.py:351
  350.4 11.9 %collective-permute-start.46 = (bf16[1,136,512]{2,1,0:T(8,128)(2,1)S(1)}, bf16[1,136,512]{2,1,0:T(8,128)(2,1)S(1)}, u32[]{:S(2)}, u32[]{:S(2)}) collective-permute-start(bf16[1,136,512]{2,1,0:T(8,128)(2,1)S(1)} %get-tuple-element.713), channel_id=1, source_target_pairs={{0,4},{1,5},{2,6},{3,7},{4,0},{5,1},{6,2},{7,3},{8,12},{9,13},{10,... | collective-permute-start | bytes 417800 | tf_op jit(solution)/shard_map/ppermute | solution.py:351
  352.2 10.1 %collective-permute-start.47 = (bf16[1,136,512]{2,1,0:T(8,128)(2,1)S(1)}, bf16[1,136,512]{2,1,0:T(8,128)(2,1)S(1)}, u32[]{:S(2)}, u32[]{:S(2)}) collective-permute-start(bf16[1,136,512]{2,1,0:T(8,128)(2,1)S(1)} %get-tuple-element.712), channel_id=1, source_target_pairs={{0,6},{1,7},{2,0},{3,1},{4,2},{5,3},{6,4},{7,5},{8,14},{9,15},{10,... | collective-permute-start | bytes 417800 | tf_op jit(solution)/shard_map/ppermute | solution.py:351
  365.8 11.4 %collective-permute-start.48 = (bf16[128,2816]{1,0:T(8,128)(2,1)S(1)}, bf16[128,2816]{1,0:T(8,128)(2,1)S(1)}, u32[]{:S(2)}, u32[]{:S(2)}) collective-permute-start(bf16[128,2816]{1,0:T(8,128)(2,1)S(1)} %add_convert_fusion.4), channel_id=1, source_target_pairs={{0,8},{1,9},{2,10},{3,11},{4,12},{5,13},{6,14},{7,15},{8,0},{9,1},... | collective-permute-start | bytes 2162696 | tf_op jit(solution)/shard_map/ppermute | solution.py:351
  365.9 11.4 %collective-permute-start.50 = (bf16[480,256]{1,0:T(8,128)(2,1)S(1)}, bf16[480,256]{1,0:T(8,128)(2,1)S(1)}, u32[]{:S(2)}, u32[]{:S(2)}) collective-permute-start(bf16[480,256]{1,0:T(8,128)(2,1)S(1)} %fusion.44), channel_id=1, source_target_pairs={{0,16},{1,17},{2,18},{3,19},{4,20},{5,21},{6,22},{7,23},{8,24},{9,... | collective-permute-start | bytes 737288 | tf_op jit(solution)/shard_map/ppermute | solution.py:351
  367.6 9.6 %collective-permute-start.49 = (bf16[136,512]{1,0:T(8,128)(2,1)S(1)}, bf16[136,512]{1,0:T(8,128)(2,1)S(1)}, u32[]{:S(2)}, u32[]{:S(2)}) collective-permute-start(bf16[136,512]{1,0:T(8,128)(2,1)S(1)} %fusion.46), channel_id=1, source_target_pairs={{0,16},{1,17},{2,18},{3,19},{4,20},{5,21},{6,22},{7,23},{8,24},{9,... | collective-permute-start | bytes 417800 | tf_op jit(solution)/shard_map/ppermute | solution.py:351
  377.3 5.4 %collective-permute-start.51 = (bf16[4,128]{1,0:T(4,128)(2,1)S(1)}, bf16[4,128]{1,0:T(4,128)(2,1)S(1)}, u32[]{:S(2)}, u32[]{:S(2)}) collective-permute-start(bf16[4,128]{1,0:T(4,128)(2,1)S(1)} %get-tuple-element.681), channel_id=1, source_target_pairs={{0,1},{1,0},{2,3},{3,2},{4,5},{5,4},{6,7},{7,6},{8,9},{9,8},{10,11... | collective-permute-start | bytes 3080 | tf_op jit(solution)/shard_map/ppermute | solution.py:351
  379.2 3.5 collective-permute-start.53
  379.4 6.9 %collective-permute-start.54 = (bf16[480,512]{1,0:T(8,128)(2,1)S(1)}, bf16[480,512]{1,0:T(8,128)(2,1)S(1)}, u32[]{:S(2)}, u32[]{:S(2)}) collective-permute-start(bf16[480,512]{1,0:T(8,128)(2,1)S(1)} %maximum_select_fusion.4), channel_id=1, source_target_pairs={{0,8},{1,9},{2,10},{3,11},{4,12},{5,13},{6,14},{7,15},{8,0},{9,1},... | collective-permute-start | bytes 1474568 | tf_op jit(solution)/shard_map/ppermute | solution.py:351
  379.8 2.7 collective-permute-start.52
  (49 other events, 271.8 us)
Sparse Core Ops, SparseCore 0:
  31.3 113.8 all-gather.1
  205.1 142.1 reduce-scatter.1

commit v6 on v5

--- a/solution.py
+++ b/solution.py
@@ -781,14 +781,15 @@
 
     v.d_gu, v.ds_own, v.ds_other = feed_forward_back(v.cot, v.wd, v.pop.w_gu, v.pop.act)
     v = sync(v)
-    d_second = (v.pop.ds_own + p.to_core(v.pop.ds_other).astype(F32)).reshape(batch, length, D)
-    gg = tn(v.pop.second, v.pop.d_gu).astype(LOW)
-    gg = lax.psum_scatter(gg, "dp", scatter_dimension=0, tiled=True)
+    v.ds_other = p.to_core(v.ds_other)
+    v.gg = tn(v.pop.second, v.pop.d_gu).astype(LOW)
+    v = sync(v)
+    gg = lax.psum_scatter(v.pop.gg, "dp", scatter_dimension=0, tiled=True)
+    d_second = (v.pop.ds_own + v.pop.ds_other.astype(F32)).reshape(batch, length, D)
     normed2 = v.middle * v.inv2
     v.gain2_sum = jnp.sum(d_second * normed2, axis=(0, 1))
     v.d_middle = cotangent.astype(F32) + norm_back(d_second, normed2, v.pop.inv2, v.pop.gain2)
     v.d_a = chip(p, v.d_middle.astype(LOW)).reshape(batch, 2 * length, D)
-    v = sync(v)
     go = dots("bnt,btd->nd", v.pop.out, v.d_a).astype(LOW).reshape(2, 2, 128, D)
     go_core = half(go, core, 3)
     go_parts = [half(go_core, y, 3), half(go_core, 1 - y, 3), half(go, 1 - core, 3)]
@@ -844,7 +845,7 @@
     v.dq_t = jnp.stack([back0[0], back1[0]])
     v.gq = dots("btd,bnt->dn", v.first, v.dq_t).astype(LOW).reshape(4, 2, 128, GW)
     v = sync(v)
-    v.r1, v.r2, v.r3 = r_step(1), r_step(2), r_step(3)
+    v.r1, v.r2 = r_step(1), r_step(2)
     dk1 = (v.pop.dk1 + v.pop.far1.astype(F32)).astype(LOW).reshape(1, 2 * length, LAT)
     d_latent = jnp.concatenate([v.pop.dk0, dk1])
     gl = dots("btd,btl->dl", v.pop.first, d_latent).astype(LOW).reshape(4, 2, 128, LAT)
@@ -882,7 +883,7 @@
     v.tokens_done = v.d_middle + norm_back(d_first, normed1, inverse1, v.gain1)
     v = sync(v)
     grad_tokens = v.pop.tokens_done
-    v.r = add_all([half(v.r, p.z, 0, 4), v.pop.r1, v.pop.r2, v.pop.r3])[0]
+    v.r3 = r_step(3)
     gains = jnp.moveaxis(v.pop.gains, 0, 1).reshape(4, 4, 128)
     gains = jnp.pad(gains, ((0, 0), (0, 4), (0, 384)))
     v.q = z_scatter(p, jnp.concatenate([add_all(v.pop.found), gains], 1))
@@ -890,13 +891,12 @@
     v.gg = add_low(v.gg, p.to_y(v.gg))
     v = sync(v)
     v.q1 = p.to_y(v.q)
-    v.gg1, v.r1 = p.to_core(v.gg), p.to_y(v.r)
-    v = sync(v)
+    v.gg1 = p.to_core(v.gg)
+    v.r = add_all([half(v.r, p.z, 0, 4), v.pop.r1, v.pop.r2, v.pop.r3])[0]
+    v = sync(v)
+    v.r1 = p.to_y(v.r)
     grad_gate = ordered(core, v.gg[:, :ff], v.gg1[:, :ff], 1).astype(F32)
     grad_up = ordered(core, v.gg[:, ff:], v.gg1[:, ff:], 1).astype(F32)
-    r = ordered(y, v.r, v.r1, 1)
-    grad_rows = ordered(core, r, p.to_core(r), 1).astype(F32)
-    grad_down, grad_output = grad_rows[: ff // 4], grad_rows[ff // 4 :]
     gains = add_low(v.q[128:132, :128], v.q1[128:132, :128])
     x_gains = p.to_x(gains)
     q0, q1 = pick(y, v.q, v.q1), pick(y, v.q1, v.q)
@@ -904,6 +904,15 @@
     mine = lax.dynamic_update_slice(mine, gains, (128, 0))
     other = p.to_core(mine)
     x_other_gains = p.send(gains, lambda s, d: (s ^ 1, d ^ 1))
+    v.ends = grad_gate, grad_up, gains, mine, other, x_gains, x_other_gains
+    v = sync(v)
+    grad_gate, grad_up, gains, mine, other, x_gains, x_other_gains = v.ends
+    own_rows = ordered(y, v.r, v.r1, 1)
+    other_rows = p.to_core(own_rows)
+    grad_down, grad_output = [
+        ordered(core, own_rows[part], other_rows[part], 1).astype(F32)
+        for part in (slice(0, ff // 4), slice(ff // 4, None))
+    ]
     zero, one = pick(core, mine, other), pick(core, other, mine)
 
     def columns(start, width):

time: 402 us -> 402 us (level)
  starting transfers between devices: 80.4 us -> 72 us
  matrix products: 37.4 us -> 41.9 us
  other arithmetic: 42.6 us -> 46.9 us
    ppermute x55, starting transfers between devices: 80.3 us -> 71.9 us  [send(): return lax.ppermute(value, ALL, self.pairs(move))]
    dot_general x4, matrix products: 12.4 us -> 16.8 us  [tn(): lax.dot_general(left, right, (((0,), (0,)), ((), ())), preferred_element_...]
    unnamed x116 -> x110, local copies, waits for them, and re-layouts: 9.49 us -> 9.68 us
  transfers between devices with their start and end apart: 57 -> 57, of which waited for: 26 -> 26; matrix products, arithmetic and copies ran while one was open for 22% -> 24% of each run, Pallas kernels for 16% -> 16%
where the time goes in v6:
time: 402 us; the launch traced here: 395 us
  waiting for transfers between devices  108 us (27%)
  Pallas kernels  86 us (21%)
  starting transfers between devices  72 us (18%)
  other arithmetic  46.9 us (12%)
  matrix products  41.9 us (10%)
  local copies, waits for them, and re-layouts  24.2 us (6%)
  between operations  15.5 us (4%)
    ppermute x55, waiting for transfers between devices, send(): return lax.ppermute(value, ALL, self.pairs(move))  105 us
    ppermute x55, starting transfers between devices, send(): return lax.ppermute(value, ALL, self.pairs(move))  71.9 us
    pallas_call x2, Pallas kernels, attention_backward(): pl.pallas_call(lambda *refs: backward_kernel(b, nkb, batch, width, bool(o...  24.3 us
    pallas_call x6, Pallas kernels, placed(): pl.pallas_call(lambda *refs: place_kernel(plan, len(sources), len(shapes)...  19.9 us
    dot_general x12, matrix products, dots(): return jnp.einsum(spec, left, right, preferred_element_type=F32)  18.8 us
    pallas_call x1, Pallas kernels, feed_forward_back(): pl.pallas_call(hidden_back_kernel, grid=(steps,), in_specs=[tiled(cot.sha...  17.5 us
    dot_general x4, matrix products, tn(): lax.dot_general(left, right, (((0,), (0,)), ((), ())), preferred_element_...  16.8 us
    pallas_call x1, Pallas kernels, attention_forward(): pl.pallas_call(lambda *refs: forward_kernel(nkb, batch, width, *refs), gr...  12.7 us
  transfers between devices with their start and end apart: 57, of which 26 were waited for; matrix products, arithmetic and copies ran while one was open for 24% of the time, Pallas kernels for 16%

profile of v6, /device:TPU:0, one launch (start us, length us, event | category | flops | bytes accessed | tf_op | source)
XLA Modules:
  0.0 394.6 jit_solution(1887648044312018842)
XLA Ops:
  11.3 3.1 collective-permute-start
  14.4 2.6 collective-permute-start.1
  22.5 8.1 %collective-permute-done.1 = bf16[136,768]{1,0:T(8,128)(2,1)S(1)} collective-permute-done((bf16[136,768]{1,0:T(8,128)(2,1)S(1)}, bf16[136,768]{1,0:T(8,128)(2,1)S(1)}, u32[]{:S(2)}, u32[]{:S(2)}) %collective-permute-start.1) | collective-permute-done | bytes 208928 | tf_op jit(solution)/shard_map/ppermute | solution.py:351
  34.0 3.7 convert_multiply_fusion
  42.2 11.3 %collective-permute-done.4.refs_2_ = bf16[4,136,384]{2,1,0:T(8,128)(2,1)} collective-permute-done((bf16[4,136,384]{2,1,0:T(8,128)(2,1)S(1)}, bf16[4,136,384]{2,1,0:T(8,128)(2,1)}, u32[]{:S(2)}, u32[]{:S(2)}) %collective-permute-start.4) | collective-permute-done | bytes 417824 | tf_op jit(solution)/shard_map/ppermute | solution.py:351
  55.5 2.6 collective-permute-start.8
  58.1 2.1 fusion.16
  60.2 5.3 %collective-permute-start.10 = (bf16[352,256]{1,0:T(8,128)(2,1)S(1)}, bf16[352,256]{1,0:T(8,128)(2,1)S(1)}, u32[]{:S(2)}, u32[]{:S(2)}) collective-permute-start(bf16[352,256]{1,0:T(8,128)(2,1)S(1)} %dynamic-slice_convert_fusion.2), channel_id=1, source_target_pairs={{0,4},{1,5},{2,6},{3,7},{4,0},{5,1},{6,2},{7,3},{8,12},{9,13},{10,... | collective-permute-start | bytes 540680 | tf_op jit(solution)/shard_map/ppermute | solution.py:351
  65.5 2.8 fusion.28
  68.3 2.9 pad_maximum_fusion.cot
  71.2 8.4 %collective-permute-done.10 = bf16[352,256]{1,0:T(8,128)(2,1)S(1)} collective-permute-done((bf16[352,256]{1,0:T(8,128)(2,1)S(1)}, bf16[352,256]{1,0:T(8,128)(2,1)S(1)}, u32[]{:S(2)}, u32[]{:S(2)}) %collective-permute-start.10) | collective-permute-done | bytes 180256 | tf_op jit(solution)/shard_map/ppermute | solution.py:351
  79.7 2.2 collective-permute-start.11
  84.4 3.6 place.6
  90.0 5.4 %collective-permute-done.12 = bf16[352,256]{1,0:T(8,128)(2,1)S(1)} collective-permute-done((bf16[352,256]{1,0:T(8,128)(2,1)S(1)}, bf16[352,256]{1,0:T(8,128)(2,1)S(1)}, u32[]{:S(2)}, u32[]{:S(2)}) %collective-permute-start.12) | collective-permute-done | bytes 180256 | tf_op jit(solution)/shard_map/ppermute | solution.py:351
  95.9 3.8 collective-permute-start.15
  99.9 2.2 collective-permute-start.13
  102.3 2.3 fusion.12.refs_1_
  106.1 3.5 place.7
  109.5 2.1 collective-permute-done.15
  113.6 4.9 %collective-permute-done.14.refs_7_ = bf16[2,352,256]{2,1,0:T(8,128)(2,1)S(1)} collective-permute-done((bf16[2,352,256]{2,1,0:T(8,128)(2,1)S(1)}, bf16[2,352,256]{2,1,0:T(8,128)(2,1)S(1)}, u32[]{:S(2)}, u32[]{:S(2)}) %collective-permute-start.14) | collective-permute-done | bytes 360480 | tf_op jit(solution)/shard_map/ppermute | solution.py:351
  118.9 2.3 collective-permute-start.20
  121.2 2.2 collective-permute-start.21
  123.5 12.7 %attention_forward.1 = (bf16[2,512,512]{2,1,0:T(8,128)(2,1)}, f32[2,512,512]{2,1,0:T(8,128)}, bf16[2,2,256,2048]{3,2,1,0:T(8,128)(2,1)}, f32[2,2,1,2048]{3,2,1,0:T(1,128)}) custom-call(s32[9]{0:T(128)} %concatenate.99.refs_0_, bf16[2,512,512]{2,1,0:T(8,128)(2,1)} %fusion.12.refs_1_, bf16[512,256]{1,0:T(8,128)(2,1)} %bitcast.195, bf16[512,256]{1,0:T(8,128)(2,1)} %bitcast.192, ...), custom_call_target="tpu_custom_call" | custom-call | flops 7516192768 | bytes 16777216 | tf_op jit(solution)/shard_map/attention_forward/pallas_call | solution.py:162
  136.8 3.1 collective-permute-done.22.refs_8_
  139.9 1.9 convolution_convert_fusion.7
  141.8 2.6 collective-permute-done.23
  146.0 2.5 collective-permute-done.24
  150.9 3.0 place.8
  154.0 11.6 %feed_forward.1 = (f32[1024,2816]{1,0:T(8,128)}, bf16[1024,1408]{1,0:T(8,128)(2,1)}) custom-call(bf16[1024,1024]{1,0:T(8,128)(2,1)} %pad_maximum_fusion.2.x, bf16[1024,2816]{1,0:T(8,128)(2,1)} %all-gather.2.cloned.1.call-done.w), custom_call_target="tpu_custom_call" | custom-call | flops 5905580032 | bytes 20971520 | tf_op jit(solution)/shard_map/feed_forward/pallas_call | solution.py:291
  165.6 4.4 %place.9 = bf16[2,2,352,1024]{3,2,1,0:T(8,128)(2,1)} custom-call(s32[3]{0:T(128)} %pad_add_fusion.refs_0_, bf16[2,352,256]{2,1,0:T(8,128)(2,1)} %get-tuple-element.476.refs_1_, bf16[2,352,256]{2,1,0:T(8,128)(2,1)} %copy-done.24, bf16[2,352,256]{2,1,0:T(8,128)(2,1)} %copy-done.25, bf16[2,352,256]{2,1,0:T(8,128)(2,1)} %copy-done.27, ...), custom_call_target="tpu_custom_call" | custom-call | tf_op jit(solution)/shard_map/place/pallas_call | solution.py:616
  170.1 17.5 %feed_forward_back.1 = (bf16[1024,2816]{1,0:T(8,128)(2,1)}, f32[512,1024]{1,0:T(8,128)}, bf16[512,1024]{1,0:T(8,128)(2,1)}) custom-call(bf16[1024,1024]{1,0:T(8,128)(2,1)} %pad_maximum_fusion.cot, bf16[1408,1024]{1,0:T(8,128)(2,1)} %bitcast.158, bf16[1024,2816]{1,0:T(8,128)(2,1)} %all-gather.2.cloned.1.call-done.w, f32[1024,2816]{1,0:T(8,128)} %get-tuple-element.486.act), custom_call_target="tpu_custom_call" | custom-call | flops 8858370048 | bytes 31457280 | tf_op jit(solution)/shard_map/feed_forward_back/pallas_call | solution.py:311
  187.9 11.1 %convolution_convert_fusion = bf16[1024,2816]{1,0:T(8,128)(2,1)} fusion(bf16[1024,1024]{1,0:T(8,128)(2,1)S(1)} %copy-done.14, bf16[1024,2816]{1,0:T(8,128)(2,1)} %get-tuple-element.518), kind=kOutput, calls=%fused_computation | convolution fusion | flops 5908463616 | bytes 13631488 | tf_op jit(solution)/shard_map/dot_general | solution.py:31
  199.1 2.1 convert_add_fusion.3
  202.4 2.2 fusion.56
  204.8 3.8 convolution_convert_fusion.1
  220.0 2.3 fusion.13.refs_2_
  222.2 2.8 convolution_convert_fusion.4
  225.4 2.2 constant_dynamic-slice_fusion.10
  228.2 6.7 %collective-permute-start.30 = (bf16[2,2,480,256]{3,2,0,1:T(8,128)(2,1)}, bf16[2,2,480,256]{3,2,0,1:T(8,128)(2,1)S(1)}, u32[]{:S(2)}, u32[]{:S(2)}) collective-permute-start(bf16[2,2,480,256]{3,2,0,1:T(8,128)(2,1)} %copy.76), channel_id=1, source_target_pairs={{0,16},{1,17},{2,18},{3,19},{4,20},{5,21},{6,22},{7,23},{8,24},{9,... | collective-permute-start | bytes 2949128 | tf_op jit(solution)/shard_map/ppermute | solution.py:351
  234.9 12.1 %attention_backward.2 = (bf16[512,512]{1,0:T(8,128)(2,1)}, f32[4,256,256]{2,1,0:T(8,128)}, f32[512,256]{1,0:T(8,128)}, f32[512,256]{1,0:T(8,128)}) custom-call(s32[9]{0:T(128)} %concatenate.99.refs_0_, bf16[2,512,512]{2,1,0:T(8,128)(2,1)} %fusion.12.refs_1_, bf16[2,512,512]{2,1,0:T(8,128)(2,1)} %fusion.13.refs_2_, ...), custom_call_target="tpu_custom_call" | custom-call | flops 9395240960 | bytes 10485760 | tf_op jit(solution)/shard_map/attention_backward/pallas_call | solution.py:206
  247.0 3.5 convert_add_fusion.2
  251.7 7.7 %collective-permute-done.31 = bf16[2,1,480,512]{3,2,0,1:T(8,128)(2,1)} collective-permute-done((bf16[2,1,480,512]{3,2,0,1:T(8,128)(2,1)}, bf16[2,1,480,512]{3,2,0,1:T(8,128)(2,1)}, u32[]{:S(2)}, u32[]{:S(2)}) %collective-permute-start.31) | collective-permute-done | bytes 983072 | tf_op jit(solution)/shard_map/ppermute | solution.py:351
  259.4 1.8 add_convert_fusion.2
  261.3 5.7 %collective-permute-start.34 = (bf16[2,1,480,256]{3,2,0,1:T(8,128)(2,1)S(1)}, bf16[2,1,480,256]{3,2,0,1:T(8,128)(2,1)}, u32[]{:S(2)}, u32[]{:S(2)}) collective-permute-start(bf16[2,1,480,256]{3,2,0,1:T(8,128)(2,1)S(1)} %constant_dynamic-slice_fusion.8), channel_id=1, source_target_pairs={{0,16},{1,17},{2,18},{3,19},{4,20},{5,21},{6,22},{7,23},{8,24},{9,... | collective-permute-start | bytes 1474568 | tf_op jit(solution)/shard_map/ppermute | solution.py:351
  267.3 1.9 collective-permute-start.33
  270.5 12.2 %attention_backward.3 = (bf16[512,512]{1,0:T(8,128)(2,1)}, f32[4,256,256]{2,1,0:T(8,128)}, f32[512,256]{1,0:T(8,128)}, f32[512,256]{1,0:T(8,128)}) custom-call(s32[9]{0:T(128)} %concatenate.99.refs_0_, bf16[2,512,512]{2,1,0:T(8,128)(2,1)} %fusion.12.refs_1_, bf16[2,512,512]{2,1,0:T(8,128)(2,1)} %fusion.13.refs_2_, ...), custom_call_target="tpu_custom_call" | custom-call | flops 9395240960 | bytes 10485760 | tf_op jit(solution)/shard_map/attention_backward/pallas_call | solution.py:206
  283.5 3.9 collective-permute-done.33
  287.4 2.2 place.10
  295.1 2.3 bitcast_convert_fusion
  298.4 4.1 %collective-permute-done.35 = bf16[2,256,256]{2,1,0:T(8,128)(2,1)S(1)} collective-permute-done((bf16[2,256,256]{2,1,0:T(8,128)(2,1)S(1)}, bf16[2,256,256]{2,1,0:T(8,128)(2,1)S(1)}, u32[]{:S(2)}, u32[]{:S(2)}) %collective-permute-start.35) | collective-permute-done | bytes 262176 | tf_op jit(solution)/shard_map/ppermute | solution.py:351
  303.7 1.8 add_convert_fusion
  306.6 2.4 collective-permute-start.42
  310.5 3.1 place.11
  313.6 3.0 collective-permute-start.37
  318.7 2.8 fusion.5
  321.5 1.9 fusion.8
  323.5 17.2 %collective-permute-done.42 = bf16[1,480,256]{2,1,0:T(8,128)(2,1)} collective-permute-done((bf16[1,480,256]{2,1,0:T(8,128)(2,1)}, bf16[1,480,256]{2,1,0:T(8,128)(2,1)}, u32[]{:S(2)}, u32[]{:S(2)}) %collective-permute-start.42) | collective-permute-done | bytes 245792 | tf_op jit(solution)/shard_map/ppermute | solution.py:351
  341.6 2.6 reduce-scatter.2.cloned.1.call-done
  348.4 2.8 collective-permute-start.46
  352.4 3.4 collective-permute-done.44
  355.8 4.7 %collective-permute-done.45 = bf16[1,136,512]{2,1,0:T(8,128)(2,1)S(1)} collective-permute-done((bf16[1,136,512]{2,1,0:T(8,128)(2,1)S(1)}, bf16[1,136,512]{2,1,0:T(8,128)(2,1)S(1)}, u32[]{:S(2)}, u32[]{:S(2)}) %collective-permute-start.45) | collective-permute-done | bytes 139296 | tf_op jit(solution)/shard_map/ppermute | solution.py:351
  360.6 1.9 collective-permute-done.43
  366.6 4.3 %collective-permute-done.49 = bf16[136,512]{1,0:T(8,128)(2,1)S(1)} collective-permute-done((bf16[136,512]{1,0:T(8,128)(2,1)S(1)}, bf16[136,512]{1,0:T(8,128)(2,1)S(1)}, u32[]{:S(2)}, u32[]{:S(2)}) %collective-permute-start.49) | collective-permute-done | bytes 139296 | tf_op jit(solution)/shard_map/ppermute | solution.py:351
  376.4 4.8 %collective-permute-done.53 = bf16[480,256]{1,0:T(8,128)(2,1)S(1)} collective-permute-done((bf16[480,256]{1,0:T(8,128)(2,1)S(1)}, bf16[480,256]{1,0:T(8,128)(2,1)S(1)}, u32[]{:S(2)}, u32[]{:S(2)}) %collective-permute-start.53) | collective-permute-done | bytes 245792 | tf_op jit(solution)/shard_map/ppermute | solution.py:351
  (305 shorter events, 85.2 us)
Async XLA Ops:
  7.2 146.8 %all-gather.2.cloned.1.call-start = ((), (), s32[]{:S(2)}) async-start(), calls=%async_computation.1 | async-start | bytes 6488064 | tf_op jit(solution)/shard_map/all_gather | solution.py:671
  11.3 11.2 %collective-permute-start = (bf16[136,768]{1,0:T(8,128)(2,1)S(1)}, bf16[136,768]{1,0:T(8,128)(2,1)S(1)}, u32[]{:S(2)}, u32[]{:S(2)}) collective-permute-start(bf16[136,768]{1,0:T(8,128)(2,1)S(1)} %fusion.46), channel_id=1, source_target_pairs={{0,2},{1,3},{2,4},{3,5},{4,6},{5,7},{6,0},{7,1},{8,10},{9,11},{10,... | collective-permute-start | bytes 626696 | tf_op jit(solution)/shard_map/ppermute | solution.py:351
  14.4 16.3 %collective-permute-start.1 = (bf16[136,768]{1,0:T(8,128)(2,1)S(1)}, bf16[136,768]{1,0:T(8,128)(2,1)S(1)}, u32[]{:S(2)}, u32[]{:S(2)}) collective-permute-start(bf16[136,768]{1,0:T(8,128)(2,1)S(1)} %fusion.46), channel_id=1, source_target_pairs={{0,4},{1,5},{2,6},{3,7},{4,0},{5,1},{6,2},{7,3},{8,12},{9,13},{10,... | collective-permute-start | bytes 626696 | tf_op jit(solution)/shard_map/ppermute | solution.py:351
  17.0 13.7 %collective-permute-start.2 = (bf16[136,768]{1,0:T(8,128)(2,1)S(1)}, bf16[136,768]{1,0:T(8,128)(2,1)S(1)}, u32[]{:S(2)}, u32[]{:S(2)}) collective-permute-start(bf16[136,768]{1,0:T(8,128)(2,1)S(1)} %fusion.46), channel_id=1, source_target_pairs={{0,6},{1,7},{2,0},{3,1},{4,2},{5,3},{6,4},{7,5},{8,14},{9,15},{10,... | collective-permute-start | bytes 626696 | tf_op jit(solution)/shard_map/ppermute | solution.py:351
  18.3 12.8 %collective-permute-start.3 = (bf16[2,256,1024]{2,1,0:T(8,128)(2,1)}, bf16[2,256,1024]{2,1,0:T(8,128)(2,1)}, u32[]{:S(2)}, u32[]{:S(2)}) collective-permute-start(bf16[2,256,1024]{2,1,0:T(8,128)(2,1)} %param.13), channel_id=1, source_target_pairs={{0,8},{1,9},{2,10},{3,11},{4,12},{5,13},{6,14},{7,15},{8,0},{9,1},... | collective-permute-start | bytes 3145736 | tf_op jit(solution)/shard_map/ppermute | solution.py:351
  18.3 39.8 %collective-permute-start.18 = (bf16[512,1024]{1,0:T(8,128)(2,1)}, bf16[512,1024]{1,0:T(8,128)(2,1)}, u32[]{:S(2)}, u32[]{:S(2)}) collective-permute-start(bf16[512,1024]{1,0:T(8,128)(2,1)} %bitcast.149), channel_id=1, source_target_pairs={{0,8},{1,9},{2,10},{3,11},{4,12},{5,13},{6,14},{7,15},{8,0},{9,1},... | collective-permute-start | bytes 3145736 | tf_op jit(solution)/shard_map/ppermute | solution.py:351
  31.2 313.1 %reduce-scatter.2.cloned.1.call-start = ((), (), s32[]{:S(2)}) async-start(), calls=%async_computation.2 | async-start | bytes 6488064 | tf_op jit(solution)/shard_map/reduce_scatter | solution.py:787
  31.3 24.2 %copy-start.11 = (bf16[4,136,384]{2,1,0:T(8,128)(2,1)}, bf16[4,136,384]{2,1,0:T(8,128)(2,1)S(1)}, u32[]{:S(2)}) copy-start(bf16[4,136,384]{2,1,0:T(8,128)(2,1)S(1)} %get-tuple-element.382.refs_5_) | copy-start | bytes 1253380
  31.3 53.0 %copy-start.10 = (bf16[4,136,384]{2,1,0:T(8,128)(2,1)}, bf16[4,136,384]{2,1,0:T(8,128)(2,1)S(1)}, u32[]{:S(2)}) copy-start(bf16[4,136,384]{2,1,0:T(8,128)(2,1)S(1)} %get-tuple-element.378.refs_1_) | copy-start | bytes 1253380
  34.0 24.2 %copy-start.4 = (bf16[2,256,1024]{2,1,0:T(8,128)(2,1)S(1)}, bf16[2,256,1024]{2,1,0:T(8,128)(2,1)}, u32[]{:S(2)}) copy-start(bf16[2,256,1024]{2,1,0:T(8,128)(2,1)} %param.24) | copy-start | bytes 3145732
  37.7 15.8 %collective-permute-start.4 = (bf16[4,136,384]{2,1,0:T(8,128)(2,1)S(1)}, bf16[4,136,384]{2,1,0:T(8,128)(2,1)}, u32[]{:S(2)}, u32[]{:S(2)}) collective-permute-start(bf16[4,136,384]{2,1,0:T(8,128)(2,1)S(1)} %get-tuple-element.378.refs_1_), channel_id=1, source_target_pairs={{0,1},{1,0},{2,3},{3,2},{4,5},{5,4},{6,7},{7,6},{8,9},{9,8},{10,11... | collective-permute-start | bytes 1253384 | tf_op jit(solution)/shard_map/ppermute | solution.py:351
  39.1 14.3 %collective-permute-start.5 = (bf16[4,136,384]{2,1,0:T(8,128)(2,1)S(1)}, bf16[4,136,384]{2,1,0:T(8,128)(2,1)}, u32[]{:S(2)}, u32[]{:S(2)}) collective-permute-start(bf16[4,136,384]{2,1,0:T(8,128)(2,1)S(1)} %get-tuple-element.382.refs_5_), channel_id=1, source_target_pairs={{0,16},{1,17},{2,18},{3,19},{4,20},{5,21},{6,22},{7,23},{8,24},{9,... | collective-permute-start | bytes 1253384 | tf_op jit(solution)/shard_map/ppermute | solution.py:351
  53.5 26.2 %collective-permute-start.6 = (bf16[4,136,384]{2,1,0:T(8,128)(2,1)}, bf16[4,136,384]{2,1,0:T(8,128)(2,1)S(1)}, u32[]{:S(2)}, u32[]{:S(2)}) collective-permute-start(bf16[4,136,384]{2,1,0:T(8,128)(2,1)} %collective-permute-done.4.refs_2_), channel_id=1, source_target_pairs={{0,16},{1,17},{2,18},{3,19},{4,20},{5,21},{6,22},{7,23},{8,24},{9,... | collective-permute-start | bytes 1253384 | tf_op jit(solution)/shard_map/ppermute | solution.py:351
  55.0 24.7 %collective-permute-start.7 = (bf16[4,136,384]{2,1,0:T(8,128)(2,1)S(1)}, bf16[4,136,384]{2,1,0:T(8,128)(2,1)S(1)}, u32[]{:S(2)}, u32[]{:S(2)}) collective-permute-start(bf16[4,136,384]{2,1,0:T(8,128)(2,1)S(1)} %get-tuple-element.378.refs_1_), channel_id=1, source_target_pairs={{0,16},{1,17},{2,18},{3,19},{4,20},{5,21},{6,22},{7,23},{8,24},{9,... | collective-permute-start | bytes 1253384 | tf_op jit(solution)/shard_map/ppermute | solution.py:351
  55.5 24.2 %collective-permute-start.8 = (bf16[4,136,384]{2,1,0:T(8,128)(2,1)S(1)}, bf16[4,136,384]{2,1,0:T(8,128)(2,1)S(1)}, u32[]{:S(2)}, u32[]{:S(2)}) collective-permute-start(bf16[4,136,384]{2,1,0:T(8,128)(2,1)S(1)} %get-tuple-element.382.refs_5_), channel_id=1, source_target_pairs={{0,1},{1,0},{2,3},{3,2},{4,5},{5,4},{6,7},{7,6},{8,9},{9,8},{10,11... | collective-permute-start | bytes 1253384 | tf_op jit(solution)/shard_map/ppermute | solution.py:351
  58.1 21.6 %collective-permute-start.9 = (bf16[4,136,384]{2,1,0:T(8,128)(2,1)}, bf16[4,136,384]{2,1,0:T(8,128)(2,1)S(1)}, u32[]{:S(2)}, u32[]{:S(2)}) collective-permute-start(bf16[4,136,384]{2,1,0:T(8,128)(2,1)} %collective-permute-done.5.refs_7_), channel_id=1, source_target_pairs={{0,1},{1,0},{2,3},{3,2},{4,5},{5,4},{6,7},{7,6},{8,9},{9,8},{10,11... | collective-permute-start | bytes 1253384 | tf_op jit(solution)/shard_map/ppermute | solution.py:351
  60.2 19.4 %collective-permute-start.10 = (bf16[352,256]{1,0:T(8,128)(2,1)S(1)}, bf16[352,256]{1,0:T(8,128)(2,1)S(1)}, u32[]{:S(2)}, u32[]{:S(2)}) collective-permute-start(bf16[352,256]{1,0:T(8,128)(2,1)S(1)} %dynamic-slice_convert_fusion.2), channel_id=1, source_target_pairs={{0,4},{1,5},{2,6},{3,7},{4,0},{5,1},{6,2},{7,3},{8,12},{9,13},{10,... | collective-permute-start | bytes 540680 | tf_op jit(solution)/shard_map/ppermute | solution.py:351
  68.3 19.7 %copy-start.3 = (f32[2,2,256,1024]{3,2,1,0:T(8,128)S(1)}, f32[2,2,256,1024]{3,2,1,0:T(8,128)}, u32[]{:S(2)}) copy-start(f32[2,2,256,1024]{3,2,1,0:T(8,128)} %convert_multiply_fusion) | copy-start | bytes 12582916
  79.7 10.3 %collective-permute-start.11 = (bf16[352,256]{1,0:T(8,128)(2,1)S(1)}, bf16[352,256]{1,0:T(8,128)(2,1)S(1)}, u32[]{:S(2)}, u32[]{:S(2)}) collective-permute-start(bf16[352,256]{1,0:T(8,128)(2,1)S(1)} %dynamic-slice_convert_fusion.2), channel_id=1, source_target_pairs={{0,2},{1,3},{2,4},{3,5},{4,6},{5,7},{6,0},{7,1},{8,10},{9,11},{10,... | collective-permute-start | bytes 540680 | tf_op jit(solution)/shard_map/ppermute | solution.py:351
  81.9 13.4 %collective-permute-start.12 = (bf16[352,256]{1,0:T(8,128)(2,1)S(1)}, bf16[352,256]{1,0:T(8,128)(2,1)S(1)}, u32[]{:S(2)}, u32[]{:S(2)}) collective-permute-start(bf16[352,256]{1,0:T(8,128)(2,1)S(1)} %dynamic-slice_convert_fusion.2), channel_id=1, source_target_pairs={{0,6},{1,7},{2,0},{3,1},{4,2},{5,3},{6,4},{7,5},{8,14},{9,15},{10,... | collective-permute-start | bytes 540680 | tf_op jit(solution)/shard_map/ppermute | solution.py:351
  95.4 9.2 %collective-permute-start.16 = (bf16[4,2,128,256]{3,2,1,0:T(8,128)(2,1)S(1)}, bf16[4,2,128,256]{3,2,1,0:T(8,128)(2,1)S(1)}, u32[]{:S(2)}, u32[]{:S(2)}) collective-permute-start(bf16[4,2,128,256]{3,2,1,0:T(8,128)(2,1)S(1)} %copy-done.47), channel_id=1, source_target_pairs={{0,8},{1,9},{2,10},{3,11},{4,12},{5,13},{6,14},{7,15},{8,0},{9,1},... | collective-permute-start | bytes 1572872 | tf_op jit(solution)/shard_map/ppermute | solution.py:351
  95.4 9.2 %collective-permute-start.17 = (bf16[4,2,128,128]{3,2,1,0:T(8,128)(2,1)S(1)}, bf16[4,2,128,128]{3,2,1,0:T(8,128)(2,1)S(1)}, u32[]{:S(2)}, u32[]{:S(2)}) collective-permute-start(bf16[4,2,128,128]{3,2,1,0:T(8,128)(2,1)S(1)} %copy-done.48), channel_id=1, source_target_pairs={{0,8},{1,9},{2,10},{3,11},{4,12},{5,13},{6,14},{7,15},{8,0},{9,1},... | collective-permute-start | bytes 786440 | tf_op jit(solution)/shard_map/ppermute | solution.py:351
  95.9 15.8 %collective-permute-start.15 = (bf16[2,2,256,256]{3,2,1,0:T(8,128)(2,1)S(1)}, bf16[2,2,256,256]{3,2,1,0:T(8,128)(2,1)S(1)}, u32[]{:S(2)}, u32[]{:S(2)}) collective-permute-start(bf16[2,2,256,256]{3,2,1,0:T(8,128)(2,1)S(1)} %bitcast.186), channel_id=1, source_target_pairs={{0,16},{1,17},{2,18},{3,19},{4,20},{5,21},{6,22},{7,23},{8,24},{9,... | collective-permute-start | bytes 1572872 | tf_op jit(solution)/shard_map/ppermute | solution.py:351
  99.8 18.7 %collective-permute-start.14 = (bf16[2,352,256]{2,1,0:T(8,128)(2,1)S(1)}, bf16[2,352,256]{2,1,0:T(8,128)(2,1)S(1)}, u32[]{:S(2)}, u32[]{:S(2)}) collective-permute-start(bf16[2,352,256]{2,1,0:T(8,128)(2,1)S(1)} %pad_maximum_fusion.15), channel_id=1, source_target_pairs={{0,16},{1,17},{2,18},{3,19},{4,20},{5,21},{6,22},{7,23},{8,24},{9,... | collective-permute-start | bytes 1081352 | tf_op jit(solution)/shard_map/ppermute | solution.py:351
  99.9 18.9 %collective-permute-start.13 = (bf16[2,352,256]{2,1,0:T(8,128)(2,1)S(1)}, bf16[2,352,256]{2,1,0:T(8,128)(2,1)S(1)}, u32[]{:S(2)}, u32[]{:S(2)}) collective-permute-start(bf16[2,352,256]{2,1,0:T(8,128)(2,1)S(1)} %pad_maximum_fusion.14), channel_id=1, source_target_pairs={{0,1},{1,0},{2,3},{3,2},{4,5},{5,4},{6,7},{7,6},{8,9},{9,8},{10,11... | collective-permute-start | bytes 1081352 | tf_op jit(solution)/shard_map/ppermute | solution.py:351
  118.9 17.4 %collective-permute-start.20 = (bf16[2,352,256]{2,1,0:T(8,128)(2,1)S(1)}, bf16[2,352,256]{2,1,0:T(8,128)(2,1)S(1)}, u32[]{:S(2)}, u32[]{:S(2)}) collective-permute-start(bf16[2,352,256]{2,1,0:T(8,128)(2,1)S(1)} %get-tuple-element.727), channel_id=1, source_target_pairs={{0,16},{1,17},{2,18},{3,19},{4,20},{5,21},{6,22},{7,23},{8,24},{9,... | collective-permute-start | bytes 1081352 | tf_op jit(solution)/shard_map/ppermute | solution.py:351
  121.2 18.7 %copy-start.44 = (bf16[2,2,128,1024]{3,2,1,0:T(8,128)(2,1)S(1)}, bf16[2,2,128,1024]{3,2,1,0:T(8,128)(2,1)}, u32[]{:S(2)}) copy-start(bf16[2,2,128,1024]{3,2,1,0:T(8,128)(2,1)} %get-tuple-element.391) | copy-start | bytes 3145732
  121.2 15.1 %collective-permute-start.21 = (bf16[2,352,256]{2,1,0:T(8,128)(2,1)S(1)}, bf16[2,352,256]{2,1,0:T(8,128)(2,1)S(1)}, u32[]{:S(2)}, u32[]{:S(2)}) collective-permute-start(bf16[2,352,256]{2,1,0:T(8,128)(2,1)S(1)} %get-tuple-element.726), channel_id=1, source_target_pairs={{0,1},{1,0},{2,3},{3,2},{4,5},{5,4},{6,7},{7,6},{8,9},{9,8},{10,11... | collective-permute-start | bytes 1081352 | tf_op jit(solution)/shard_map/ppermute | solution.py:351
  123.3 13.5 %collective-permute-start.19 = (bf16[2,352,256]{2,1,0:T(8,128)(2,1)S(1)}, bf16[2,352,256]{2,1,0:T(8,128)(2,1)S(1)}, u32[]{:S(2)}, u32[]{:S(2)}) collective-permute-start(bf16[2,352,256]{2,1,0:T(8,128)(2,1)S(1)} %collective-permute-done.13.refs_2_), channel_id=1, source_target_pairs={{0,16},{1,17},{2,18},{3,19},{4,20},{5,21},{6,22},{7,23},{8,24},{9,... | collective-permute-start | bytes 1081352 | tf_op jit(solution)/shard_map/ppermute | solution.py:351
  123.4 16.4 %collective-permute-start.22 = (bf16[2,352,256]{2,1,0:T(8,128)(2,1)S(1)}, bf16[2,352,256]{2,1,0:T(8,128)(2,1)S(1)}, u32[]{:S(2)}, u32[]{:S(2)}) collective-permute-start(bf16[2,352,256]{2,1,0:T(8,128)(2,1)S(1)} %collective-permute-done.14.refs_7_), channel_id=1, source_target_pairs={{0,1},{1,0},{2,3},{3,2},{4,5},{5,4},{6,7},{7,6},{8,9},{9,8},{10,11... | collective-permute-start | bytes 1081352 | tf_op jit(solution)/shard_map/ppermute | solution.py:351
  141.8 2.7 collective-permute-start.23
  145.8 2.7 collective-permute-start.24
  153.9 11.8 %collective-permute-start.25 = (bf16[4,2,352,256]{3,2,1,0:T(8,128)(2,1)}, bf16[4,2,352,256]{3,2,1,0:T(8,128)(2,1)}, u32[]{:S(2)}, u32[]{:S(2)}) collective-permute-start(bf16[4,2,352,256]{3,2,1,0:T(8,128)(2,1)} %place.8), channel_id=1, source_target_pairs={{0,8},{1,9},{2,10},{3,11},{4,12},{5,13},{6,14},{7,15},{8,0},{9,1},... | collective-permute-start | bytes 4325384 | tf_op jit(solution)/shard_map/ppermute | solution.py:351
  187.5 11.5 %collective-permute-start.26 = (bf16[512,1024]{1,0:T(8,128)(2,1)}, bf16[512,1024]{1,0:T(8,128)(2,1)}, u32[]{:S(2)}, u32[]{:S(2)}) collective-permute-start(bf16[512,1024]{1,0:T(8,128)(2,1)} %get-tuple-element.512), channel_id=1, source_target_pairs={{0,8},{1,9},{2,10},{3,11},{4,12},{5,13},{6,14},{7,15},{8,0},{9,1},... | collective-permute-start | bytes 3145736 | tf_op jit(solution)/shard_map/ppermute | solution.py:351
  204.7 3.9 %collective-permute-start.27 = (bf16[2,256,1024]{2,1,0:T(8,128)(2,1)}, bf16[2,256,1024]{2,1,0:T(8,128)(2,1)}, u32[]{:S(2)}, u32[]{:S(2)}) collective-permute-start(bf16[2,256,1024]{2,1,0:T(8,128)(2,1)} %get-tuple-element.706), channel_id=1, source_target_pairs={{0,8},{1,9},{2,10},{3,11},{4,12},{5,13},{6,14},{7,15},{8,0},{9,1},... | collective-permute-start | bytes 3145736 | tf_op jit(solution)/shard_map/ppermute | solution.py:351
  213.3 9.0 %collective-permute-start.28 = (bf16[2,2,480,512]{3,2,0,1:T(8,128)(2,1)S(1)}, bf16[2,2,480,512]{3,2,0,1:T(8,128)(2,1)}, u32[]{:S(2)}, u32[]{:S(2)}) collective-permute-start(bf16[2,2,480,512]{3,2,0,1:T(8,128)(2,1)S(1)} %copy.77), channel_id=1, source_target_pairs={{0,8},{1,9},{2,10},{3,11},{4,12},{5,13},{6,14},{7,15},{8,0},{9,1},... | collective-permute-start | bytes 5898248 | tf_op jit(solution)/shard_map/ppermute | solution.py:351
  225.0 22.0 %collective-permute-start.29 = (bf16[512,1024]{1,0:T(8,128)(2,1)}, bf16[512,1024]{1,0:T(8,128)(2,1)}, u32[]{:S(2)}, u32[]{:S(2)}) collective-permute-start(bf16[512,1024]{1,0:T(8,128)(2,1)} %convolution_convert_fusion.4), channel_id=1, source_target_pairs={{0,8},{1,9},{2,10},{3,11},{4,12},{5,13},{6,14},{7,15},{8,0},{9,1},... | collective-permute-start | bytes 3145736 | tf_op jit(solution)/shard_map/ppermute | solution.py:351
  227.6 19.4 %copy-start.13 = (bf16[2,2,352,1024]{3,2,1,0:T(8,128)(2,1)S(1)}, bf16[2,2,352,1024]{3,2,1,0:T(8,128)(2,1)}, u32[]{:S(2)}) copy-start(bf16[2,2,352,1024]{3,2,1,0:T(8,128)(2,1)} %place.9) | copy-start | bytes 8650756
  227.6 31.8 %collective-permute-start.31 = (bf16[2,1,480,512]{3,2,0,1:T(8,128)(2,1)}, bf16[2,1,480,512]{3,2,0,1:T(8,128)(2,1)}, u32[]{:S(2)}, u32[]{:S(2)}) collective-permute-start(bf16[2,1,480,512]{3,2,0,1:T(8,128)(2,1)} %constant_dynamic-slice_fusion.10), channel_id=1, source_target_pairs={{0,1},{1,0},{2,3},{3,2},{4,5},{5,4},{6,7},{7,6},{8,9},{9,8},{10,11... | collective-permute-start | bytes 2949128 | tf_op jit(solution)/shard_map/ppermute | solution.py:351
  228.2 31.2 %collective-permute-start.30 = (bf16[2,2,480,256]{3,2,0,1:T(8,128)(2,1)}, bf16[2,2,480,256]{3,2,0,1:T(8,128)(2,1)S(1)}, u32[]{:S(2)}, u32[]{:S(2)}) collective-permute-start(bf16[2,2,480,256]{3,2,0,1:T(8,128)(2,1)} %copy.76), channel_id=1, source_target_pairs={{0,16},{1,17},{2,18},{3,19},{4,20},{5,21},{6,22},{7,23},{8,24},{9,... | collective-permute-start | bytes 2949128 | tf_op jit(solution)/shard_map/ppermute | solution.py:351
  261.3 22.2 %collective-permute-start.34 = (bf16[2,1,480,256]{3,2,0,1:T(8,128)(2,1)S(1)}, bf16[2,1,480,256]{3,2,0,1:T(8,128)(2,1)}, u32[]{:S(2)}, u32[]{:S(2)}) collective-permute-start(bf16[2,1,480,256]{3,2,0,1:T(8,128)(2,1)S(1)} %constant_dynamic-slice_fusion.8), channel_id=1, source_target_pairs={{0,16},{1,17},{2,18},{3,19},{4,20},{5,21},{6,22},{7,23},{8,24},{9,... | collective-permute-start | bytes 1474568 | tf_op jit(solution)/shard_map/ppermute | solution.py:351
  267.3 20.1 %collective-permute-start.33 = (bf16[2,1,480,256]{3,2,0,1:T(8,128)(2,1)S(1)}, bf16[2,1,480,256]{3,2,0,1:T(8,128)(2,1)S(1)}, u32[]{:S(2)}, u32[]{:S(2)}) collective-permute-start(bf16[2,1,480,256]{3,2,0,1:T(8,128)(2,1)S(1)} %constant_dynamic-slice_fusion.9), channel_id=1, source_target_pairs={{0,1},{1,0},{2,3},{3,2},{4,5},{5,4},{6,7},{7,6},{8,9},{9,8},{10,11... | collective-permute-start | bytes 1474568 | tf_op jit(solution)/shard_map/ppermute | solution.py:351
  269.2 14.3 %collective-permute-start.32 = (bf16[2,256,256]{2,1,0:T(8,128)(2,1)S(1)}, bf16[2,256,256]{2,1,0:T(8,128)(2,1)S(1)}, u32[]{:S(2)}, u32[]{:S(2)}) collective-permute-start(bf16[2,256,256]{2,1,0:T(8,128)(2,1)S(1)} %slice.273), channel_id=1, source_target_pairs={{16,0},{17,1},{18,2},{19,3},{20,4},{21,5},{22,6},{23,7},{24,8},{25... | collective-permute-start | bytes 786440 | tf_op jit(solution)/shard_map/ppermute | solution.py:351
  289.6 8.7 %collective-permute-start.36 = (bf16[2,512,128]{2,1,0:T(8,128)(2,1)}, bf16[2,512,128]{2,1,0:T(8,128)(2,1)S(1)}, u32[]{:S(2)}, u32[]{:S(2)}) collective-permute-start(bf16[2,512,128]{2,1,0:T(8,128)(2,1)} %get-tuple-element.620), channel_id=1, source_target_pairs={{0,8},{1,9},{2,10},{3,11},{4,12},{5,13},{6,14},{7,15},{8,0},{9,1},... | collective-permute-start | bytes 786440 | tf_op jit(solution)/shard_map/ppermute | solution.py:351
  289.7 12.8 %collective-permute-start.35 = (bf16[2,256,256]{2,1,0:T(8,128)(2,1)S(1)}, bf16[2,256,256]{2,1,0:T(8,128)(2,1)S(1)}, u32[]{:S(2)}, u32[]{:S(2)}) collective-permute-start(bf16[2,256,256]{2,1,0:T(8,128)(2,1)S(1)} %slice.272), channel_id=1, source_target_pairs={{16,0},{17,1},{18,2},{19,3},{20,4},{21,5},{22,6},{23,7},{24,8},{25... | collective-permute-start | bytes 786440 | tf_op jit(solution)/shard_map/ppermute | solution.py:351
  305.5 12.8 %collective-permute-start.40 = (bf16[2,256,1024]{2,1,0:T(8,128)(2,1)}, bf16[2,256,1024]{2,1,0:T(8,128)(2,1)}, u32[]{:S(2)}, u32[]{:S(2)}) collective-permute-start(bf16[2,256,1024]{2,1,0:T(8,128)(2,1)} %add_convert_fusion), channel_id=1, source_target_pairs={{0,8},{1,9},{2,10},{3,11},{4,12},{5,13},{6,14},{7,15},{8,0},{9,1},... | collective-permute-start | bytes 3145736 | tf_op jit(solution)/shard_map/ppermute | solution.py:351
  306.6 16.9 %collective-permute-start.41 = (bf16[1,480,256]{2,1,0:T(8,128)(2,1)}, bf16[1,480,256]{2,1,0:T(8,128)(2,1)}, u32[]{:S(2)}, u32[]{:S(2)}) collective-permute-start(bf16[1,480,256]{2,1,0:T(8,128)(2,1)} %get-tuple-element.713), channel_id=1, source_target_pairs={{0,2},{1,3},{2,4},{3,5},{4,6},{5,7},{6,0},{7,1},{8,10},{9,11},{10,... | collective-permute-start | bytes 737288 | tf_op jit(solution)/shard_map/ppermute | solution.py:351
  306.6 34.1 %collective-permute-start.42 = (bf16[1,480,256]{2,1,0:T(8,128)(2,1)}, bf16[1,480,256]{2,1,0:T(8,128)(2,1)}, u32[]{:S(2)}, u32[]{:S(2)}) collective-permute-start(bf16[1,480,256]{2,1,0:T(8,128)(2,1)} %get-tuple-element.712), channel_id=1, source_target_pairs={{0,4},{1,5},{2,6},{3,7},{4,0},{5,1},{6,2},{7,3},{8,12},{9,13},{10,... | collective-permute-start | bytes 737288 | tf_op jit(solution)/shard_map/ppermute | solution.py:351
  313.6 27.1 %collective-permute-start.37 = (bf16[4,128,512]{2,1,0:T(8,128)(2,1)}, bf16[4,128,512]{2,1,0:T(8,128)(2,1)S(1)}, u32[]{:S(2)}, u32[]{:S(2)}) collective-permute-start(bf16[4,128,512]{2,1,0:T(8,128)(2,1)} %get-tuple-element.637), channel_id=1, source_target_pairs={{0,1},{1,0},{2,3},{3,2},{4,5},{5,4},{6,7},{7,6},{8,9},{9,8},{10,11... | collective-permute-start | bytes 1572872 | tf_op jit(solution)/shard_map/ppermute | solution.py:351
  316.6 25.0 %collective-permute-start.38 = (bf16[4,128,512]{2,1,0:T(8,128)(2,1)}, bf16[4,128,512]{2,1,0:T(8,128)(2,1)}, u32[]{:S(2)}, u32[]{:S(2)}) collective-permute-start(bf16[4,128,512]{2,1,0:T(8,128)(2,1)} %get-tuple-element.638), channel_id=1, source_target_pairs={{0,16},{1,17},{2,18},{3,19},{4,20},{5,21},{6,22},{7,23},{8,24},{9,... | collective-permute-start | bytes 1572872 | tf_op jit(solution)/shard_map/ppermute | solution.py:351
  318.3 23.4 %collective-permute-start.39 = (bf16[4,128,512]{2,1,0:T(8,128)(2,1)S(1)}, bf16[4,128,512]{2,1,0:T(8,128)(2,1)}, u32[]{:S(2)}, u32[]{:S(2)}) collective-permute-start(bf16[4,128,512]{2,1,0:T(8,128)(2,1)S(1)} %copy-done.46), channel_id=1, source_target_pairs={{0,17},{1,16},{2,19},{3,18},{4,21},{5,20},{6,23},{7,22},{8,25},{9,... | collective-permute-start | bytes 1572872 | tf_op jit(solution)/shard_map/ppermute | solution.py:351
  321.5 24.2 %copy-start.32 = (bf16[4,128,512]{2,1,0:T(8,128)(2,1)S(1)}, bf16[4,128,512]{2,1,0:T(8,128)(2,1)}, u32[]{:S(2)}) copy-start(bf16[4,128,512]{2,1,0:T(8,128)(2,1)} %get-tuple-element.648) | copy-start | bytes 1572868
  344.2 18.3 %collective-permute-start.43 = (bf16[128,2816]{1,0:T(8,128)(2,1)}, bf16[128,2816]{1,0:T(8,128)(2,1)}, u32[]{:S(2)}, u32[]{:S(2)}) collective-permute-start(bf16[128,2816]{1,0:T(8,128)(2,1)} %reduce-scatter.2.cloned.1.call-done), channel_id=1, source_target_pairs={{0,16},{1,17},{2,18},{3,19},{4,20},{5,21},{6,22},{7,23},{8,24},{9,... | collective-permute-start | bytes 2162696 | tf_op jit(solution)/shard_map/ppermute | solution.py:351
  347.3 8.5 %collective-permute-start.44 = (bf16[1,136,512]{2,1,0:T(8,128)(2,1)S(1)}, bf16[1,136,512]{2,1,0:T(8,128)(2,1)S(1)}, u32[]{:S(2)}, u32[]{:S(2)}) collective-permute-start(bf16[1,136,512]{2,1,0:T(8,128)(2,1)S(1)} %get-tuple-element.734), channel_id=1, source_target_pairs={{0,2},{1,3},{2,4},{3,5},{4,6},{5,7},{6,0},{7,1},{8,10},{9,11},{10,... | collective-permute-start | bytes 417800 | tf_op jit(solution)/shard_map/ppermute | solution.py:351
  347.9 12.6 %collective-permute-start.45 = (bf16[1,136,512]{2,1,0:T(8,128)(2,1)S(1)}, bf16[1,136,512]{2,1,0:T(8,128)(2,1)S(1)}, u32[]{:S(2)}, u32[]{:S(2)}) collective-permute-start(bf16[1,136,512]{2,1,0:T(8,128)(2,1)S(1)} %get-tuple-element.736), channel_id=1, source_target_pairs={{0,4},{1,5},{2,6},{3,7},{4,0},{5,1},{6,2},{7,3},{8,12},{9,13},{10,... | collective-permute-start | bytes 417800 | tf_op jit(solution)/shard_map/ppermute | solution.py:351
  348.4 12.1 %collective-permute-start.46 = (bf16[1,136,512]{2,1,0:T(8,128)(2,1)S(1)}, bf16[1,136,512]{2,1,0:T(8,128)(2,1)S(1)}, u32[]{:S(2)}, u32[]{:S(2)}) collective-permute-start(bf16[1,136,512]{2,1,0:T(8,128)(2,1)S(1)} %get-tuple-element.735), channel_id=1, source_target_pairs={{0,6},{1,7},{2,0},{3,1},{4,2},{5,3},{6,4},{7,5},{8,14},{9,15},{10,... | collective-permute-start | bytes 417800 | tf_op jit(solution)/shard_map/ppermute | solution.py:351
  351.3 13.5 %collective-permute-start.47 = (bf16[1,480,256]{2,1,0:T(8,128)(2,1)S(1)}, bf16[1,480,256]{2,1,0:T(8,128)(2,1)S(1)}, u32[]{:S(2)}, u32[]{:S(2)}) collective-permute-start(bf16[1,480,256]{2,1,0:T(8,128)(2,1)S(1)} %constant_dynamic-slice_fusion.2), channel_id=1, source_target_pairs={{0,6},{1,7},{2,0},{3,1},{4,2},{5,3},{6,4},{7,5},{8,14},{9,15},{10,... | collective-permute-start | bytes 737288 | tf_op jit(solution)/shard_map/ppermute | solution.py:351
  364.8 6.1 %collective-permute-start.48 = (bf16[128,2816]{1,0:T(8,128)(2,1)S(1)}, bf16[128,2816]{1,0:T(8,128)(2,1)S(1)}, u32[]{:S(2)}, u32[]{:S(2)}) collective-permute-start(bf16[128,2816]{1,0:T(8,128)(2,1)S(1)} %add_convert_fusion.4), channel_id=1, source_target_pairs={{0,8},{1,9},{2,10},{3,11},{4,12},{5,13},{6,14},{7,15},{8,0},{9,1},... | collective-permute-start | bytes 2162696 | tf_op jit(solution)/shard_map/ppermute | solution.py:351
  364.8 6.1 %collective-permute-start.49 = (bf16[136,512]{1,0:T(8,128)(2,1)S(1)}, bf16[136,512]{1,0:T(8,128)(2,1)S(1)}, u32[]{:S(2)}, u32[]{:S(2)}) collective-permute-start(bf16[136,512]{1,0:T(8,128)(2,1)S(1)} %fusion.47), channel_id=1, source_target_pairs={{0,16},{1,17},{2,18},{3,19},{4,20},{5,21},{6,22},{7,23},{8,24},{9,... | collective-permute-start | bytes 417800 | tf_op jit(solution)/shard_map/ppermute | solution.py:351
  370.9 5.5 %collective-permute-start.51 = (bf16[4,128]{1,0:T(4,128)(2,1)S(1)}, bf16[4,128]{1,0:T(4,128)(2,1)S(1)}, u32[]{:S(2)}, u32[]{:S(2)}) collective-permute-start(bf16[4,128]{1,0:T(4,128)(2,1)S(1)} %get-tuple-element.667), channel_id=1, source_target_pairs={{0,1},{1,0},{2,3},{3,2},{4,5},{5,4},{6,7},{7,6},{8,9},{9,8},{10,11... | collective-permute-start | bytes 3080 | tf_op jit(solution)/shard_map/ppermute | solution.py:351
  372.5 4.0 %collective-permute-start.52 = (bf16[4,128]{1,0:T(4,128)(2,1)S(1)}, bf16[4,128]{1,0:T(4,128)(2,1)S(1)}, u32[]{:S(2)}, u32[]{:S(2)}) collective-permute-start(bf16[4,128]{1,0:T(4,128)(2,1)S(1)} %get-tuple-element.667), channel_id=1, source_target_pairs={{0,9},{1,8},{2,11},{3,10},{4,13},{5,12},{6,15},{7,14},{8,1},{9,0},... | collective-permute-start | bytes 3080 | tf_op jit(solution)/shard_map/ppermute | solution.py:351
  372.5 8.7 %collective-permute-start.50 = (bf16[136,1024]{1,0:T(8,128)(2,1)S(1)}, bf16[136,1024]{1,0:T(8,128)(2,1)S(1)}, u32[]{:S(2)}, u32[]{:S(2)}) collective-permute-start(bf16[136,1024]{1,0:T(8,128)(2,1)S(1)} %get-tuple-element.671), channel_id=1, source_target_pairs={{0,8},{1,9},{2,10},{3,11},{4,12},{5,13},{6,14},{7,15},{8,0},{9,1},... | collective-permute-start | bytes 835592 | tf_op jit(solution)/shard_map/ppermute | solution.py:351
  373.3 7.9 %collective-permute-start.53 = (bf16[480,256]{1,0:T(8,128)(2,1)S(1)}, bf16[480,256]{1,0:T(8,128)(2,1)S(1)}, u32[]{:S(2)}, u32[]{:S(2)}) collective-permute-start(bf16[480,256]{1,0:T(8,128)(2,1)S(1)} %fusion.45), channel_id=1, source_target_pairs={{0,16},{1,17},{2,18},{3,19},{4,20},{5,21},{6,22},{7,23},{8,24},{9,... | collective-permute-start | bytes 737288 | tf_op jit(solution)/shard_map/ppermute | solution.py:351
  381.4 3.8 collective-permute-start.54
  (46 other events, 277.9 us)
Sparse Core Ops, SparseCore 0:
  31.3 113.8 all-gather.1
  205.0 139.2 reduce-scatter.1

commit v7 on v6

--- a/solution.py
+++ b/solution.py
@@ -677,13 +677,14 @@
     v = sync(v)
 
     v.ax, v.by = p.to_x(v.a), p.to_y(v.b)
+    v.zd1 = p.to_z(v.pd, 1)
     v = sync(v)
     v.zd2 = p.to_z(v.pd, 2)
     v.ay, v.axy = p.to_y(v.a), p.to_y(v.ax)
     v.bx, v.bxy = p.to_x(v.b), p.to_x(v.by)
     v = sync(v)
 
-    v.zd1, v.zd3 = p.to_z(v.pd, 1), p.to_z(v.pd, 3)
+    v.zd3 = p.to_z(v.pd, 3)
     v.from_ab = (v.pop.a, v.pop.ax, v.pop.ay, v.pop.axy, v.pop.b, v.pop.bx, v.pop.by, v.pop.bxy)
     plan = []
     for n, (r, k) in enumerate(RELATIVE):

time: 402 us -> 398 us (0.990)
  starting transfers between devices: 72 us -> 63.8 us
    ppermute x55, starting transfers between devices: 71.9 us -> 63.7 us  [send(): return lax.ppermute(value, ALL, self.pairs(move))]
  transfers between devices with their start and end apart: 57 -> 57, of which waited for: 26 -> 24; matrix products, arithmetic and copies ran while one was open for 24% -> 24% of each run, Pallas kernels for 16% -> 17%
where the time goes in v7:
time: 398 us; the launch traced here: 391 us
  waiting for transfers between devices  112 us (28%)
  Pallas kernels  86.4 us (22%)
  starting transfers between devices  63.8 us (16%)
  other arithmetic  46.9 us (12%)
  matrix products  41.7 us (10%)
  local copies, waits for them, and re-layouts  24.8 us (6%)
  between operations  15.4 us (4%)
    ppermute x55, waiting for transfers between devices, send(): return lax.ppermute(value, ALL, self.pairs(move))  109 us
    ppermute x55, starting transfers between devices, send(): return lax.ppermute(value, ALL, self.pairs(move))  63.7 us
    pallas_call x2, Pallas kernels, attention_backward(): pl.pallas_call(lambda *refs: backward_kernel(b, nkb, batch, width, bool(o...  24.3 us
    pallas_call x6, Pallas kernels, placed(): pl.pallas_call(lambda *refs: place_kernel(plan, len(sources), len(shapes)...  20.3 us
    dot_general x12, matrix products, dots(): return jnp.einsum(spec, left, right, preferred_element_type=F32)  18.6 us
    pallas_call x1, Pallas kernels, feed_forward_back(): pl.pallas_call(hidden_back_kernel, grid=(steps,), in_specs=[tiled(cot.sha...  17.5 us
    dot_general x4, matrix products, tn(): lax.dot_general(left, right, (((0,), (0,)), ((), ())), preferred_element_...  16.8 us
    pallas_call x1, Pallas kernels, attention_forward(): pl.pallas_call(lambda *refs: forward_kernel(nkb, batch, width, *refs), gr...  12.7 us
  transfers between devices with their start and end apart: 57, of which 24 were waited for; matrix products, arithmetic and copies ran while one was open for 24% of the time, Pallas kernels for 17%

profile of v7, /device:TPU:0, one launch (start us, length us, event | category | flops | bytes accessed | tf_op | source)
XLA Modules:
  0.0 390.8 jit_solution(4273421363022174206)
XLA Ops:
  11.3 3.1 collective-permute-start
  14.4 2.6 collective-permute-start.1
  22.5 8.1 %collective-permute-done.1 = bf16[136,768]{1,0:T(8,128)(2,1)S(1)} collective-permute-done((bf16[136,768]{1,0:T(8,128)(2,1)S(1)}, bf16[136,768]{1,0:T(8,128)(2,1)S(1)}, u32[]{:S(2)}, u32[]{:S(2)}) %collective-permute-start.1) | collective-permute-done | bytes 208928 | tf_op jit(solution)/shard_map/ppermute | solution.py:351
  34.0 3.7 convert_multiply_fusion
  40.8 5.0 %collective-permute-start.6 = (bf16[352,256]{1,0:T(8,128)(2,1)S(1)}, bf16[352,256]{1,0:T(8,128)(2,1)S(1)}, u32[]{:S(2)}, u32[]{:S(2)}) collective-permute-start(bf16[352,256]{1,0:T(8,128)(2,1)S(1)} %dynamic-slice_convert_fusion.2), channel_id=1, source_target_pairs={{0,2},{1,3},{2,4},{3,5},{4,6},{5,7},{6,0},{7,1},{8,10},{9,11},{10,... | collective-permute-start | bytes 540680 | tf_op jit(solution)/shard_map/ppermute | solution.py:351
  47.2 6.8 %collective-permute-done.6 = bf16[352,256]{1,0:T(8,128)(2,1)S(1)} collective-permute-done((bf16[352,256]{1,0:T(8,128)(2,1)S(1)}, bf16[352,256]{1,0:T(8,128)(2,1)S(1)}, u32[]{:S(2)}, u32[]{:S(2)}) %collective-permute-start.6) | collective-permute-done | bytes 180256 | tf_op jit(solution)/shard_map/ppermute | solution.py:351
  54.0 2.2 collective-permute-start.10
  58.2 2.1 fusion.16
  60.3 5.2 %collective-permute-start.11 = (bf16[352,256]{1,0:T(8,128)(2,1)S(1)}, bf16[352,256]{1,0:T(8,128)(2,1)S(1)}, u32[]{:S(2)}, u32[]{:S(2)}) collective-permute-start(bf16[352,256]{1,0:T(8,128)(2,1)S(1)} %dynamic-slice_convert_fusion.2), channel_id=1, source_target_pairs={{0,4},{1,5},{2,6},{3,7},{4,0},{5,1},{6,2},{7,3},{8,12},{9,13},{10,... | collective-permute-start | bytes 540680 | tf_op jit(solution)/shard_map/ppermute | solution.py:351
  65.6 2.8 fusion.28
  68.4 2.9 pad_maximum_fusion.cot
  71.2 9.6 %collective-permute-done.11 = bf16[352,256]{1,0:T(8,128)(2,1)S(1)} collective-permute-done((bf16[352,256]{1,0:T(8,128)(2,1)S(1)}, bf16[352,256]{1,0:T(8,128)(2,1)S(1)}, u32[]{:S(2)}, u32[]{:S(2)}) %collective-permute-start.11) | collective-permute-done | bytes 180256 | tf_op jit(solution)/shard_map/ppermute | solution.py:351
  81.9 2.2 collective-permute-start.12
  84.1 4.1 %place.6 = (bf16[4,2,128,256]{3,2,1,0:T(8,128)(2,1)}, bf16[4,2,128,512]{3,2,1,0:T(8,128)(2,1)}, bf16[4,2,128,256]{3,2,1,0:T(8,128)(2,1)}, bf16[4,2,128,128]{3,2,1,0:T(8,128)(2,1)}) custom-call(s32[3]{0:T(128)} %pad_add_fusion.refs_0_, bf16[4,136,384]{2,1,0:T(8,128)(2,1)} %copy-done.10, bf16[4,136,384]{2,1,0:T(8,128)(2,1)} %collective-permute-done.4.refs_2_, ...), custom_call_target="tpu_custom_call" | custom-call | tf_op jit(solution)/shard_map/place/pallas_call | solution.py:616
  92.2 3.5 collective-permute-start.15
  96.4 2.3 fusion.12.refs_1_
  100.2 3.5 place.7
  103.7 4.1 %collective-permute-done.15 = bf16[2,2,256,256]{3,2,1,0:T(8,128)(2,1)S(1)} collective-permute-done((bf16[2,2,256,256]{3,2,1,0:T(8,128)(2,1)S(1)}, bf16[2,2,256,256]{3,2,1,0:T(8,128)(2,1)S(1)}, u32[]{:S(2)}, u32[]{:S(2)}) %collective-permute-start.15) | collective-permute-done | bytes 524320 | tf_op jit(solution)/shard_map/ppermute | solution.py:351
  109.7 4.9 %collective-permute-done.14.refs_7_ = bf16[2,352,256]{2,1,0:T(8,128)(2,1)S(1)} collective-permute-done((bf16[2,352,256]{2,1,0:T(8,128)(2,1)S(1)}, bf16[2,352,256]{2,1,0:T(8,128)(2,1)S(1)}, u32[]{:S(2)}, u32[]{:S(2)}) %collective-permute-start.14) | collective-permute-done | bytes 360480 | tf_op jit(solution)/shard_map/ppermute | solution.py:351
  114.7 2.5 collective-permute-start.20
  117.5 1.8 collective-permute-start.22
  119.4 12.7 %attention_forward.1 = (bf16[2,512,512]{2,1,0:T(8,128)(2,1)}, f32[2,512,512]{2,1,0:T(8,128)}, bf16[2,2,256,2048]{3,2,1,0:T(8,128)(2,1)}, f32[2,2,1,2048]{3,2,1,0:T(1,128)}) custom-call(s32[9]{0:T(128)} %concatenate.99.refs_0_, bf16[2,512,512]{2,1,0:T(8,128)(2,1)} %fusion.12.refs_1_, bf16[512,256]{1,0:T(8,128)(2,1)} %bitcast.195, bf16[512,256]{1,0:T(8,128)(2,1)} %bitcast.192, ...), custom_call_target="tpu_custom_call" | custom-call | flops 7516192768 | bytes 16777216 | tf_op jit(solution)/shard_map/attention_forward/pallas_call | solution.py:162
  132.1 2.1 collective-permute-done.21.refs_6_
  134.2 7.1 %collective-permute-done.22.refs_8_ = bf16[2,352,256]{2,1,0:T(8,128)(2,1)S(1)} collective-permute-done((bf16[2,352,256]{2,1,0:T(8,128)(2,1)S(1)}, bf16[2,352,256]{2,1,0:T(8,128)(2,1)S(1)}, u32[]{:S(2)}, u32[]{:S(2)}) %collective-permute-start.22) | collective-permute-done | bytes 360480 | tf_op jit(solution)/shard_map/ppermute | solution.py:351
  141.3 1.9 convolution_convert_fusion.7
  143.3 2.6 collective-permute-done.23
  147.5 2.5 collective-permute-done.24
  152.4 3.0 place.8
  155.5 11.6 %feed_forward.1 = (f32[1024,2816]{1,0:T(8,128)}, bf16[1024,1408]{1,0:T(8,128)(2,1)}) custom-call(bf16[1024,1024]{1,0:T(8,128)(2,1)} %pad_maximum_fusion.2.x, bf16[1024,2816]{1,0:T(8,128)(2,1)} %all-gather.2.cloned.1.call-done.w), custom_call_target="tpu_custom_call" | custom-call | flops 5905580032 | bytes 20971520 | tf_op jit(solution)/shard_map/feed_forward/pallas_call | solution.py:291
  167.1 4.4 %place.9 = bf16[2,2,352,1024]{3,2,1,0:T(8,128)(2,1)} custom-call(s32[3]{0:T(128)} %pad_add_fusion.refs_0_, bf16[2,352,256]{2,1,0:T(8,128)(2,1)} %get-tuple-element.480.refs_1_, bf16[2,352,256]{2,1,0:T(8,128)(2,1)} %copy-done.24, bf16[2,352,256]{2,1,0:T(8,128)(2,1)} %copy-done.25, bf16[2,352,256]{2,1,0:T(8,128)(2,1)} %copy-done.27, ...), custom_call_target="tpu_custom_call" | custom-call | tf_op jit(solution)/shard_map/place/pallas_call | solution.py:616
  171.5 17.5 %feed_forward_back.1 = (bf16[1024,2816]{1,0:T(8,128)(2,1)}, f32[512,1024]{1,0:T(8,128)}, bf16[512,1024]{1,0:T(8,128)(2,1)}) custom-call(bf16[1024,1024]{1,0:T(8,128)(2,1)} %pad_maximum_fusion.cot, bf16[1408,1024]{1,0:T(8,128)(2,1)} %bitcast.158, bf16[1024,2816]{1,0:T(8,128)(2,1)} %all-gather.2.cloned.1.call-done.w, f32[1024,2816]{1,0:T(8,128)} %get-tuple-element.490.act), custom_call_target="tpu_custom_call" | custom-call | flops 8858370048 | bytes 31457280 | tf_op jit(solution)/shard_map/feed_forward_back/pallas_call | solution.py:311
  189.4 11.1 %convolution_convert_fusion = bf16[1024,2816]{1,0:T(8,128)(2,1)} fusion(bf16[1024,1024]{1,0:T(8,128)(2,1)S(1)} %copy-done.14, bf16[1024,2816]{1,0:T(8,128)(2,1)} %get-tuple-element.522), kind=kOutput, calls=%fused_computation | convolution fusion | flops 5908463616 | bytes 13631488 | tf_op jit(solution)/shard_map/dot_general | solution.py:31
  200.5 2.1 convert_add_fusion.3
  203.9 2.2 fusion.56
  206.3 3.8 convolution_convert_fusion.1
  210.1 1.7 pad_maximum_fusion.3
  221.5 2.3 fusion.13.refs_2_
  223.7 2.8 convolution_convert_fusion.4
  226.9 2.2 constant_dynamic-slice_fusion.10
  231.2 12.1 %attention_backward.2 = (bf16[512,512]{1,0:T(8,128)(2,1)}, f32[4,256,256]{2,1,0:T(8,128)}, f32[512,256]{1,0:T(8,128)}, f32[512,256]{1,0:T(8,128)}) custom-call(s32[9]{0:T(128)} %concatenate.99.refs_0_, bf16[2,512,512]{2,1,0:T(8,128)(2,1)} %fusion.12.refs_1_, bf16[2,512,512]{2,1,0:T(8,128)(2,1)} %fusion.13.refs_2_, ...), custom_call_target="tpu_custom_call" | custom-call | flops 9395240960 | bytes 10485760 | tf_op jit(solution)/shard_map/attention_backward/pallas_call | solution.py:206
  243.3 3.5 convert_add_fusion.2
  248.0 13.3 %collective-permute-done.31 = bf16[2,1,480,512]{3,2,0,1:T(8,128)(2,1)} collective-permute-done((bf16[2,1,480,512]{3,2,0,1:T(8,128)(2,1)}, bf16[2,1,480,512]{3,2,0,1:T(8,128)(2,1)}, u32[]{:S(2)}, u32[]{:S(2)}) %collective-permute-start.31) | collective-permute-done | bytes 983072 | tf_op jit(solution)/shard_map/ppermute | solution.py:351
  261.3 1.8 add_convert_fusion.2
  266.7 12.2 %attention_backward.3 = (bf16[512,512]{1,0:T(8,128)(2,1)}, f32[4,256,256]{2,1,0:T(8,128)}, f32[512,256]{1,0:T(8,128)}, f32[512,256]{1,0:T(8,128)}) custom-call(s32[9]{0:T(128)} %concatenate.99.refs_0_, bf16[2,512,512]{2,1,0:T(8,128)(2,1)} %fusion.12.refs_1_, bf16[2,512,512]{2,1,0:T(8,128)(2,1)} %fusion.13.refs_2_, ...), custom_call_target="tpu_custom_call" | custom-call | flops 9395240960 | bytes 10485760 | tf_op jit(solution)/shard_map/attention_backward/pallas_call | solution.py:206
  279.0 1.9 collective-permute-done.32
  280.9 3.0 collective-permute-done.33
  283.9 2.2 place.10
  291.6 2.3 bitcast_convert_fusion
  294.9 1.9 collective-permute-done.35
  298.3 1.8 add_convert_fusion
  301.2 2.4 collective-permute-start.41
  303.6 3.4 collective-permute-start.42
  308.5 3.1 place.11
  313.5 2.2 collective-permute-start.39
  315.7 2.6 fusion.5
  318.3 1.9 fusion.8
  320.3 16.9 %collective-permute-done.42 = bf16[1,480,256]{2,1,0:T(8,128)(2,1)} collective-permute-done((bf16[1,480,256]{2,1,0:T(8,128)(2,1)}, bf16[1,480,256]{2,1,0:T(8,128)(2,1)}, u32[]{:S(2)}, u32[]{:S(2)}) %collective-permute-start.42) | collective-permute-done | bytes 245792 | tf_op jit(solution)/shard_map/ppermute | solution.py:351
  337.3 3.1 reduce-scatter.2.cloned.1.call-done
  344.6 2.8 collective-permute-start.46
  348.1 3.9 %collective-permute-done.44 = bf16[1,136,512]{2,1,0:T(8,128)(2,1)S(1)} collective-permute-done((bf16[1,136,512]{2,1,0:T(8,128)(2,1)S(1)}, bf16[1,136,512]{2,1,0:T(8,128)(2,1)S(1)}, u32[]{:S(2)}, u32[]{:S(2)}) %collective-permute-start.44) | collective-permute-done | bytes 139296 | tf_op jit(solution)/shard_map/ppermute | solution.py:351
  352.0 4.6 %collective-permute-done.45 = bf16[1,136,512]{2,1,0:T(8,128)(2,1)S(1)} collective-permute-done((bf16[1,136,512]{2,1,0:T(8,128)(2,1)S(1)}, bf16[1,136,512]{2,1,0:T(8,128)(2,1)S(1)}, u32[]{:S(2)}, u32[]{:S(2)}) %collective-permute-start.45) | collective-permute-done | bytes 139296 | tf_op jit(solution)/shard_map/ppermute | solution.py:351
  356.8 2.0 collective-permute-done.43
  362.8 4.3 %collective-permute-done.49 = bf16[136,512]{1,0:T(8,128)(2,1)S(1)} collective-permute-done((bf16[136,512]{1,0:T(8,128)(2,1)S(1)}, bf16[136,512]{1,0:T(8,128)(2,1)S(1)}, u32[]{:S(2)}, u32[]{:S(2)}) %collective-permute-start.49) | collective-permute-done | bytes 139296 | tf_op jit(solution)/shard_map/ppermute | solution.py:351
  372.6 4.8 %collective-permute-done.53 = bf16[480,256]{1,0:T(8,128)(2,1)S(1)} collective-permute-done((bf16[480,256]{1,0:T(8,128)(2,1)S(1)}, bf16[480,256]{1,0:T(8,128)(2,1)S(1)}, u32[]{:S(2)}, u32[]{:S(2)}) %collective-permute-start.53) | collective-permute-done | bytes 245792 | tf_op jit(solution)/shard_map/ppermute | solution.py:351
  (305 shorter events, 84.7 us)
Async XLA Ops:
  7.2 148.3 %all-gather.2.cloned.1.call-start = ((), (), s32[]{:S(2)}) async-start(), calls=%async_computation.1 | async-start | bytes 6488064 | tf_op jit(solution)/shard_map/all_gather | solution.py:671
  11.3 11.2 %collective-permute-start = (bf16[136,768]{1,0:T(8,128)(2,1)S(1)}, bf16[136,768]{1,0:T(8,128)(2,1)S(1)}, u32[]{:S(2)}, u32[]{:S(2)}) collective-permute-start(bf16[136,768]{1,0:T(8,128)(2,1)S(1)} %fusion.46), channel_id=1, source_target_pairs={{0,2},{1,3},{2,4},{3,5},{4,6},{5,7},{6,0},{7,1},{8,10},{9,11},{10,... | collective-permute-start | bytes 626696 | tf_op jit(solution)/shard_map/ppermute | solution.py:351
  14.4 16.3 %collective-permute-start.1 = (bf16[136,768]{1,0:T(8,128)(2,1)S(1)}, bf16[136,768]{1,0:T(8,128)(2,1)S(1)}, u32[]{:S(2)}, u32[]{:S(2)}) collective-permute-start(bf16[136,768]{1,0:T(8,128)(2,1)S(1)} %fusion.46), channel_id=1, source_target_pairs={{0,4},{1,5},{2,6},{3,7},{4,0},{5,1},{6,2},{7,3},{8,12},{9,13},{10,... | collective-permute-start | bytes 626696 | tf_op jit(solution)/shard_map/ppermute | solution.py:351
  17.0 13.7 %collective-permute-start.2 = (bf16[136,768]{1,0:T(8,128)(2,1)S(1)}, bf16[136,768]{1,0:T(8,128)(2,1)S(1)}, u32[]{:S(2)}, u32[]{:S(2)}) collective-permute-start(bf16[136,768]{1,0:T(8,128)(2,1)S(1)} %fusion.46), channel_id=1, source_target_pairs={{0,6},{1,7},{2,0},{3,1},{4,2},{5,3},{6,4},{7,5},{8,14},{9,15},{10,... | collective-permute-start | bytes 626696 | tf_op jit(solution)/shard_map/ppermute | solution.py:351
  18.3 12.8 %collective-permute-start.3 = (bf16[2,256,1024]{2,1,0:T(8,128)(2,1)}, bf16[2,256,1024]{2,1,0:T(8,128)(2,1)}, u32[]{:S(2)}, u32[]{:S(2)}) collective-permute-start(bf16[2,256,1024]{2,1,0:T(8,128)(2,1)} %param.13), channel_id=1, source_target_pairs={{0,8},{1,9},{2,10},{3,11},{4,12},{5,13},{6,14},{7,15},{8,0},{9,1},... | collective-permute-start | bytes 3145736 | tf_op jit(solution)/shard_map/ppermute | solution.py:351
  18.3 39.9 %collective-permute-start.18 = (bf16[512,1024]{1,0:T(8,128)(2,1)}, bf16[512,1024]{1,0:T(8,128)(2,1)}, u32[]{:S(2)}, u32[]{:S(2)}) collective-permute-start(bf16[512,1024]{1,0:T(8,128)(2,1)} %bitcast.149), channel_id=1, source_target_pairs={{0,8},{1,9},{2,10},{3,11},{4,12},{5,13},{6,14},{7,15},{8,0},{9,1},... | collective-permute-start | bytes 3145736 | tf_op jit(solution)/shard_map/ppermute | solution.py:351
  31.2 309.3 %reduce-scatter.2.cloned.1.call-start = ((), (), s32[]{:S(2)}) async-start(), calls=%async_computation.2 | async-start | bytes 6488064 | tf_op jit(solution)/shard_map/reduce_scatter | solution.py:788
  31.3 26.9 %copy-start.11 = (bf16[4,136,384]{2,1,0:T(8,128)(2,1)}, bf16[4,136,384]{2,1,0:T(8,128)(2,1)S(1)}, u32[]{:S(2)}) copy-start(bf16[4,136,384]{2,1,0:T(8,128)(2,1)S(1)} %get-tuple-element.386.refs_5_) | copy-start | bytes 1253380
  31.3 50.3 %copy-start.10 = (bf16[4,136,384]{2,1,0:T(8,128)(2,1)}, bf16[4,136,384]{2,1,0:T(8,128)(2,1)S(1)}, u32[]{:S(2)}) copy-start(bf16[4,136,384]{2,1,0:T(8,128)(2,1)S(1)} %get-tuple-element.382.refs_1_) | copy-start | bytes 1253380
  34.0 24.2 %copy-start.4 = (bf16[2,256,1024]{2,1,0:T(8,128)(2,1)S(1)}, bf16[2,256,1024]{2,1,0:T(8,128)(2,1)}, u32[]{:S(2)}) copy-start(bf16[2,256,1024]{2,1,0:T(8,128)(2,1)} %param.24) | copy-start | bytes 3145732
  37.7 16.3 %collective-permute-start.4 = (bf16[4,136,384]{2,1,0:T(8,128)(2,1)S(1)}, bf16[4,136,384]{2,1,0:T(8,128)(2,1)}, u32[]{:S(2)}, u32[]{:S(2)}) collective-permute-start(bf16[4,136,384]{2,1,0:T(8,128)(2,1)S(1)} %get-tuple-element.382.refs_1_), channel_id=1, source_target_pairs={{0,1},{1,0},{2,3},{3,2},{4,5},{5,4},{6,7},{7,6},{8,9},{9,8},{10,11... | collective-permute-start | bytes 1253384 | tf_op jit(solution)/shard_map/ppermute | solution.py:351
  39.1 14.8 %collective-permute-start.5 = (bf16[4,136,384]{2,1,0:T(8,128)(2,1)S(1)}, bf16[4,136,384]{2,1,0:T(8,128)(2,1)}, u32[]{:S(2)}, u32[]{:S(2)}) collective-permute-start(bf16[4,136,384]{2,1,0:T(8,128)(2,1)S(1)} %get-tuple-element.386.refs_5_), channel_id=1, source_target_pairs={{0,16},{1,17},{2,18},{3,19},{4,20},{5,21},{6,22},{7,23},{8,24},{9,... | collective-permute-start | bytes 1253384 | tf_op jit(solution)/shard_map/ppermute | solution.py:351
  40.8 13.2 %collective-permute-start.6 = (bf16[352,256]{1,0:T(8,128)(2,1)S(1)}, bf16[352,256]{1,0:T(8,128)(2,1)S(1)}, u32[]{:S(2)}, u32[]{:S(2)}) collective-permute-start(bf16[352,256]{1,0:T(8,128)(2,1)S(1)} %dynamic-slice_convert_fusion.2), channel_id=1, source_target_pairs={{0,2},{1,3},{2,4},{3,5},{4,6},{5,7},{6,0},{7,1},{8,10},{9,11},{10,... | collective-permute-start | bytes 540680 | tf_op jit(solution)/shard_map/ppermute | solution.py:351
  54.0 26.9 %collective-permute-start.10 = (bf16[4,136,384]{2,1,0:T(8,128)(2,1)}, bf16[4,136,384]{2,1,0:T(8,128)(2,1)S(1)}, u32[]{:S(2)}, u32[]{:S(2)}) collective-permute-start(bf16[4,136,384]{2,1,0:T(8,128)(2,1)} %collective-permute-done.5.refs_7_), channel_id=1, source_target_pairs={{0,1},{1,0},{2,3},{3,2},{4,5},{5,4},{6,7},{7,6},{8,9},{9,8},{10,11... | collective-permute-start | bytes 1253384 | tf_op jit(solution)/shard_map/ppermute | solution.py:351
  56.2 24.7 %collective-permute-start.7 = (bf16[4,136,384]{2,1,0:T(8,128)(2,1)}, bf16[4,136,384]{2,1,0:T(8,128)(2,1)S(1)}, u32[]{:S(2)}, u32[]{:S(2)}) collective-permute-start(bf16[4,136,384]{2,1,0:T(8,128)(2,1)} %collective-permute-done.4.refs_2_), channel_id=1, source_target_pairs={{0,16},{1,17},{2,18},{3,19},{4,20},{5,21},{6,22},{7,23},{8,24},{9,... | collective-permute-start | bytes 1253384 | tf_op jit(solution)/shard_map/ppermute | solution.py:351
  57.5 23.4 %collective-permute-start.8 = (bf16[4,136,384]{2,1,0:T(8,128)(2,1)S(1)}, bf16[4,136,384]{2,1,0:T(8,128)(2,1)S(1)}, u32[]{:S(2)}, u32[]{:S(2)}) collective-permute-start(bf16[4,136,384]{2,1,0:T(8,128)(2,1)S(1)} %get-tuple-element.382.refs_1_), channel_id=1, source_target_pairs={{0,16},{1,17},{2,18},{3,19},{4,20},{5,21},{6,22},{7,23},{8,24},{9,... | collective-permute-start | bytes 1253384 | tf_op jit(solution)/shard_map/ppermute | solution.py:351
  58.2 22.7 %collective-permute-start.9 = (bf16[4,136,384]{2,1,0:T(8,128)(2,1)S(1)}, bf16[4,136,384]{2,1,0:T(8,128)(2,1)S(1)}, u32[]{:S(2)}, u32[]{:S(2)}) collective-permute-start(bf16[4,136,384]{2,1,0:T(8,128)(2,1)S(1)} %get-tuple-element.386.refs_5_), channel_id=1, source_target_pairs={{0,1},{1,0},{2,3},{3,2},{4,5},{5,4},{6,7},{7,6},{8,9},{9,8},{10,11... | collective-permute-start | bytes 1253384 | tf_op jit(solution)/shard_map/ppermute | solution.py:351
  60.3 20.5 %collective-permute-start.11 = (bf16[352,256]{1,0:T(8,128)(2,1)S(1)}, bf16[352,256]{1,0:T(8,128)(2,1)S(1)}, u32[]{:S(2)}, u32[]{:S(2)}) collective-permute-start(bf16[352,256]{1,0:T(8,128)(2,1)S(1)} %dynamic-slice_convert_fusion.2), channel_id=1, source_target_pairs={{0,4},{1,5},{2,6},{3,7},{4,0},{5,1},{6,2},{7,3},{8,12},{9,13},{10,... | collective-permute-start | bytes 540680 | tf_op jit(solution)/shard_map/ppermute | solution.py:351
  68.4 19.8 %copy-start.3 = (f32[2,2,256,1024]{3,2,1,0:T(8,128)S(1)}, f32[2,2,256,1024]{3,2,1,0:T(8,128)}, u32[]{:S(2)}) copy-start(f32[2,2,256,1024]{3,2,1,0:T(8,128)} %convert_multiply_fusion) | copy-start | bytes 12582916
  81.9 9.8 %collective-permute-start.12 = (bf16[352,256]{1,0:T(8,128)(2,1)S(1)}, bf16[352,256]{1,0:T(8,128)(2,1)S(1)}, u32[]{:S(2)}, u32[]{:S(2)}) collective-permute-start(bf16[352,256]{1,0:T(8,128)(2,1)S(1)} %dynamic-slice_convert_fusion.2), channel_id=1, source_target_pairs={{0,6},{1,7},{2,0},{3,1},{4,2},{5,3},{6,4},{7,5},{8,14},{9,15},{10,... | collective-permute-start | bytes 540680 | tf_op jit(solution)/shard_map/ppermute | solution.py:351
  91.7 7.0 %collective-permute-start.16 = (bf16[4,2,128,256]{3,2,1,0:T(8,128)(2,1)S(1)}, bf16[4,2,128,256]{3,2,1,0:T(8,128)(2,1)S(1)}, u32[]{:S(2)}, u32[]{:S(2)}) collective-permute-start(bf16[4,2,128,256]{3,2,1,0:T(8,128)(2,1)S(1)} %copy-done.47), channel_id=1, source_target_pairs={{0,8},{1,9},{2,10},{3,11},{4,12},{5,13},{6,14},{7,15},{8,0},{9,1},... | collective-permute-start | bytes 1572872 | tf_op jit(solution)/shard_map/ppermute | solution.py:351
  91.7 7.0 %collective-permute-start.17 = (bf16[4,2,128,128]{3,2,1,0:T(8,128)(2,1)S(1)}, bf16[4,2,128,128]{3,2,1,0:T(8,128)(2,1)S(1)}, u32[]{:S(2)}, u32[]{:S(2)}) collective-permute-start(bf16[4,2,128,128]{3,2,1,0:T(8,128)(2,1)S(1)} %copy-done.48), channel_id=1, source_target_pairs={{0,8},{1,9},{2,10},{3,11},{4,12},{5,13},{6,14},{7,15},{8,0},{9,1},... | collective-permute-start | bytes 786440 | tf_op jit(solution)/shard_map/ppermute | solution.py:351
  92.2 15.6 %collective-permute-start.15 = (bf16[2,2,256,256]{3,2,1,0:T(8,128)(2,1)S(1)}, bf16[2,2,256,256]{3,2,1,0:T(8,128)(2,1)S(1)}, u32[]{:S(2)}, u32[]{:S(2)}) collective-permute-start(bf16[2,2,256,256]{3,2,1,0:T(8,128)(2,1)S(1)} %bitcast.186), channel_id=1, source_target_pairs={{0,16},{1,17},{2,18},{3,19},{4,20},{5,21},{6,22},{7,23},{8,24},{9,... | collective-permute-start | bytes 1572872 | tf_op jit(solution)/shard_map/ppermute | solution.py:351
  95.9 18.7 %collective-permute-start.14 = (bf16[2,352,256]{2,1,0:T(8,128)(2,1)S(1)}, bf16[2,352,256]{2,1,0:T(8,128)(2,1)S(1)}, u32[]{:S(2)}, u32[]{:S(2)}) collective-permute-start(bf16[2,352,256]{2,1,0:T(8,128)(2,1)S(1)} %pad_maximum_fusion.15), channel_id=1, source_target_pairs={{0,16},{1,17},{2,18},{3,19},{4,20},{5,21},{6,22},{7,23},{8,24},{9,... | collective-permute-start | bytes 1081352 | tf_op jit(solution)/shard_map/ppermute | solution.py:351
  96.0 18.6 %collective-permute-start.13 = (bf16[2,352,256]{2,1,0:T(8,128)(2,1)S(1)}, bf16[2,352,256]{2,1,0:T(8,128)(2,1)S(1)}, u32[]{:S(2)}, u32[]{:S(2)}) collective-permute-start(bf16[2,352,256]{2,1,0:T(8,128)(2,1)S(1)} %pad_maximum_fusion.14), channel_id=1, source_target_pairs={{0,1},{1,0},{2,3},{3,2},{4,5},{5,4},{6,7},{7,6},{8,9},{9,8},{10,11... | collective-permute-start | bytes 1081352 | tf_op jit(solution)/shard_map/ppermute | solution.py:351
  114.7 17.4 %collective-permute-start.20 = (bf16[2,352,256]{2,1,0:T(8,128)(2,1)S(1)}, bf16[2,352,256]{2,1,0:T(8,128)(2,1)S(1)}, u32[]{:S(2)}, u32[]{:S(2)}) collective-permute-start(bf16[2,352,256]{2,1,0:T(8,128)(2,1)S(1)} %get-tuple-element.731), channel_id=1, source_target_pairs={{0,16},{1,17},{2,18},{3,19},{4,20},{5,21},{6,22},{7,23},{8,24},{9,... | collective-permute-start | bytes 1081352 | tf_op jit(solution)/shard_map/ppermute | solution.py:351
  117.2 24.1 %copy-start.44 = (bf16[2,2,128,1024]{3,2,1,0:T(8,128)(2,1)S(1)}, bf16[2,2,128,1024]{3,2,1,0:T(8,128)(2,1)}, u32[]{:S(2)}) copy-start(bf16[2,2,128,1024]{3,2,1,0:T(8,128)(2,1)} %get-tuple-element.395) | copy-start | bytes 3145732
  117.3 17.0 %collective-permute-start.21 = (bf16[2,352,256]{2,1,0:T(8,128)(2,1)S(1)}, bf16[2,352,256]{2,1,0:T(8,128)(2,1)S(1)}, u32[]{:S(2)}, u32[]{:S(2)}) collective-permute-start(bf16[2,352,256]{2,1,0:T(8,128)(2,1)S(1)} %get-tuple-element.730), channel_id=1, source_target_pairs={{0,1},{1,0},{2,3},{3,2},{4,5},{5,4},{6,7},{7,6},{8,9},{9,8},{10,11... | collective-permute-start | bytes 1081352 | tf_op jit(solution)/shard_map/ppermute | solution.py:351
  117.5 16.8 %collective-permute-start.19 = (bf16[2,352,256]{2,1,0:T(8,128)(2,1)S(1)}, bf16[2,352,256]{2,1,0:T(8,128)(2,1)S(1)}, u32[]{:S(2)}, u32[]{:S(2)}) collective-permute-start(bf16[2,352,256]{2,1,0:T(8,128)(2,1)S(1)} %collective-permute-done.13.refs_2_), channel_id=1, source_target_pairs={{0,16},{1,17},{2,18},{3,19},{4,20},{5,21},{6,22},{7,23},{8,24},{9,... | collective-permute-start | bytes 1081352 | tf_op jit(solution)/shard_map/ppermute | solution.py:351
  117.5 23.8 %collective-permute-start.22 = (bf16[2,352,256]{2,1,0:T(8,128)(2,1)S(1)}, bf16[2,352,256]{2,1,0:T(8,128)(2,1)S(1)}, u32[]{:S(2)}, u32[]{:S(2)}) collective-permute-start(bf16[2,352,256]{2,1,0:T(8,128)(2,1)S(1)} %collective-permute-done.14.refs_7_), channel_id=1, source_target_pairs={{0,1},{1,0},{2,3},{3,2},{4,5},{5,4},{6,7},{7,6},{8,9},{9,8},{10,11... | collective-permute-start | bytes 1081352 | tf_op jit(solution)/shard_map/ppermute | solution.py:351
  143.2 2.7 collective-permute-start.23
  147.3 2.7 collective-permute-start.24
  155.3 11.8 %collective-permute-start.25 = (bf16[4,2,352,256]{3,2,1,0:T(8,128)(2,1)}, bf16[4,2,352,256]{3,2,1,0:T(8,128)(2,1)}, u32[]{:S(2)}, u32[]{:S(2)}) collective-permute-start(bf16[4,2,352,256]{3,2,1,0:T(8,128)(2,1)} %place.8), channel_id=1, source_target_pairs={{0,8},{1,9},{2,10},{3,11},{4,12},{5,13},{6,14},{7,15},{8,0},{9,1},... | collective-permute-start | bytes 4325384 | tf_op jit(solution)/shard_map/ppermute | solution.py:351
  171.5 17.9 %copy-start.14 = (bf16[1024,1024]{1,0:T(8,128)(2,1)S(1)}, bf16[1024,1024]{1,0:T(8,128)(2,1)}, u32[]{:S(2)}) copy-start(bf16[1024,1024]{1,0:T(8,128)(2,1)} %pad_maximum_fusion.2.x) | copy-start | bytes 6291460
  189.0 11.5 %collective-permute-start.26 = (bf16[512,1024]{1,0:T(8,128)(2,1)}, bf16[512,1024]{1,0:T(8,128)(2,1)}, u32[]{:S(2)}, u32[]{:S(2)}) collective-permute-start(bf16[512,1024]{1,0:T(8,128)(2,1)} %get-tuple-element.516), channel_id=1, source_target_pairs={{0,8},{1,9},{2,10},{3,11},{4,12},{5,13},{6,14},{7,15},{8,0},{9,1},... | collective-permute-start | bytes 3145736 | tf_op jit(solution)/shard_map/ppermute | solution.py:351
  206.2 3.9 %collective-permute-start.27 = (bf16[2,256,1024]{2,1,0:T(8,128)(2,1)}, bf16[2,256,1024]{2,1,0:T(8,128)(2,1)}, u32[]{:S(2)}, u32[]{:S(2)}) collective-permute-start(bf16[2,256,1024]{2,1,0:T(8,128)(2,1)} %get-tuple-element.710), channel_id=1, source_target_pairs={{0,8},{1,9},{2,10},{3,11},{4,12},{5,13},{6,14},{7,15},{8,0},{9,1},... | collective-permute-start | bytes 3145736 | tf_op jit(solution)/shard_map/ppermute | solution.py:351
  214.7 9.0 %collective-permute-start.28 = (bf16[2,2,480,512]{3,2,0,1:T(8,128)(2,1)S(1)}, bf16[2,2,480,512]{3,2,0,1:T(8,128)(2,1)}, u32[]{:S(2)}, u32[]{:S(2)}) collective-permute-start(bf16[2,2,480,512]{3,2,0,1:T(8,128)(2,1)S(1)} %copy.77), channel_id=1, source_target_pairs={{0,8},{1,9},{2,10},{3,11},{4,12},{5,13},{6,14},{7,15},{8,0},{9,1},... | collective-permute-start | bytes 5898248 | tf_op jit(solution)/shard_map/ppermute | solution.py:351
  226.5 16.8 %collective-permute-start.29 = (bf16[512,1024]{1,0:T(8,128)(2,1)}, bf16[512,1024]{1,0:T(8,128)(2,1)}, u32[]{:S(2)}, u32[]{:S(2)}) collective-permute-start(bf16[512,1024]{1,0:T(8,128)(2,1)} %convolution_convert_fusion.4), channel_id=1, source_target_pairs={{0,8},{1,9},{2,10},{3,11},{4,12},{5,13},{6,14},{7,15},{8,0},{9,1},... | collective-permute-start | bytes 3145736 | tf_op jit(solution)/shard_map/ppermute | solution.py:351
  229.1 32.2 %collective-permute-start.31 = (bf16[2,1,480,512]{3,2,0,1:T(8,128)(2,1)}, bf16[2,1,480,512]{3,2,0,1:T(8,128)(2,1)}, u32[]{:S(2)}, u32[]{:S(2)}) collective-permute-start(bf16[2,1,480,512]{3,2,0,1:T(8,128)(2,1)} %constant_dynamic-slice_fusion.10), channel_id=1, source_target_pairs={{0,1},{1,0},{2,3},{3,2},{4,5},{5,4},{6,7},{7,6},{8,9},{9,8},{10,11... | collective-permute-start | bytes 2949128 | tf_op jit(solution)/shard_map/ppermute | solution.py:351
  229.6 31.7 %collective-permute-start.30 = (bf16[2,2,480,256]{3,2,0,1:T(8,128)(2,1)}, bf16[2,2,480,256]{3,2,0,1:T(8,128)(2,1)S(1)}, u32[]{:S(2)}, u32[]{:S(2)}) collective-permute-start(bf16[2,2,480,256]{3,2,0,1:T(8,128)(2,1)} %copy.76), channel_id=1, source_target_pairs={{0,16},{1,17},{2,18},{3,19},{4,20},{5,21},{6,22},{7,23},{8,24},{9,... | collective-permute-start | bytes 2949128 | tf_op jit(solution)/shard_map/ppermute | solution.py:351
  263.1 17.8 %collective-permute-start.34 = (bf16[2,1,480,256]{3,2,0,1:T(8,128)(2,1)S(1)}, bf16[2,1,480,256]{3,2,0,1:T(8,128)(2,1)}, u32[]{:S(2)}, u32[]{:S(2)}) collective-permute-start(bf16[2,1,480,256]{3,2,0,1:T(8,128)(2,1)S(1)} %constant_dynamic-slice_fusion.8), channel_id=1, source_target_pairs={{0,16},{1,17},{2,18},{3,19},{4,20},{5,21},{6,22},{7,23},{8,24},{9,... | collective-permute-start | bytes 1474568 | tf_op jit(solution)/shard_map/ppermute | solution.py:351
  265.2 18.7 %collective-permute-start.33 = (bf16[2,1,480,256]{3,2,0,1:T(8,128)(2,1)S(1)}, bf16[2,1,480,256]{3,2,0,1:T(8,128)(2,1)S(1)}, u32[]{:S(2)}, u32[]{:S(2)}) collective-permute-start(bf16[2,1,480,256]{3,2,0,1:T(8,128)(2,1)S(1)} %constant_dynamic-slice_fusion.9), channel_id=1, source_target_pairs={{0,1},{1,0},{2,3},{3,2},{4,5},{5,4},{6,7},{7,6},{8,9},{9,8},{10,11... | collective-permute-start | bytes 1474568 | tf_op jit(solution)/shard_map/ppermute | solution.py:351
  265.4 15.5 %collective-permute-start.32 = (bf16[2,256,256]{2,1,0:T(8,128)(2,1)S(1)}, bf16[2,256,256]{2,1,0:T(8,128)(2,1)S(1)}, u32[]{:S(2)}, u32[]{:S(2)}) collective-permute-start(bf16[2,256,256]{2,1,0:T(8,128)(2,1)S(1)} %slice.273), channel_id=1, source_target_pairs={{16,0},{17,1},{18,2},{19,3},{20,4},{21,5},{22,6},{23,7},{24,8},{25... | collective-permute-start | bytes 786440 | tf_op jit(solution)/shard_map/ppermute | solution.py:351
  286.1 8.7 %collective-permute-start.36 = (bf16[2,512,128]{2,1,0:T(8,128)(2,1)}, bf16[2,512,128]{2,1,0:T(8,128)(2,1)S(1)}, u32[]{:S(2)}, u32[]{:S(2)}) collective-permute-start(bf16[2,512,128]{2,1,0:T(8,128)(2,1)} %get-tuple-element.624), channel_id=1, source_target_pairs={{0,8},{1,9},{2,10},{3,11},{4,12},{5,13},{6,14},{7,15},{8,0},{9,1},... | collective-permute-start | bytes 786440 | tf_op jit(solution)/shard_map/ppermute | solution.py:351
  286.2 10.6 %collective-permute-start.35 = (bf16[2,256,256]{2,1,0:T(8,128)(2,1)S(1)}, bf16[2,256,256]{2,1,0:T(8,128)(2,1)S(1)}, u32[]{:S(2)}, u32[]{:S(2)}) collective-permute-start(bf16[2,256,256]{2,1,0:T(8,128)(2,1)S(1)} %slice.272), channel_id=1, source_target_pairs={{16,0},{17,1},{18,2},{19,3},{20,4},{21,5},{22,6},{23,7},{24,8},{25... | collective-permute-start | bytes 786440 | tf_op jit(solution)/shard_map/ppermute | solution.py:351
  300.0 13.4 %collective-permute-start.40 = (bf16[2,256,1024]{2,1,0:T(8,128)(2,1)}, bf16[2,256,1024]{2,1,0:T(8,128)(2,1)}, u32[]{:S(2)}, u32[]{:S(2)}) collective-permute-start(bf16[2,256,1024]{2,1,0:T(8,128)(2,1)} %add_convert_fusion), channel_id=1, source_target_pairs={{0,8},{1,9},{2,10},{3,11},{4,12},{5,13},{6,14},{7,15},{8,0},{9,1},... | collective-permute-start | bytes 3145736 | tf_op jit(solution)/shard_map/ppermute | solution.py:351
  301.2 19.1 %collective-permute-start.41 = (bf16[1,480,256]{2,1,0:T(8,128)(2,1)}, bf16[1,480,256]{2,1,0:T(8,128)(2,1)}, u32[]{:S(2)}, u32[]{:S(2)}) collective-permute-start(bf16[1,480,256]{2,1,0:T(8,128)(2,1)} %get-tuple-element.717), channel_id=1, source_target_pairs={{0,2},{1,3},{2,4},{3,5},{4,6},{5,7},{6,0},{7,1},{8,10},{9,11},{10,... | collective-permute-start | bytes 737288 | tf_op jit(solution)/shard_map/ppermute | solution.py:351
  303.6 33.6 %collective-permute-start.42 = (bf16[1,480,256]{2,1,0:T(8,128)(2,1)}, bf16[1,480,256]{2,1,0:T(8,128)(2,1)}, u32[]{:S(2)}, u32[]{:S(2)}) collective-permute-start(bf16[1,480,256]{2,1,0:T(8,128)(2,1)} %get-tuple-element.716), channel_id=1, source_target_pairs={{0,4},{1,5},{2,6},{3,7},{4,0},{5,1},{6,2},{7,3},{8,12},{9,13},{10,... | collective-permute-start | bytes 737288 | tf_op jit(solution)/shard_map/ppermute | solution.py:351
  311.6 25.6 %collective-permute-start.37 = (bf16[4,128,512]{2,1,0:T(8,128)(2,1)}, bf16[4,128,512]{2,1,0:T(8,128)(2,1)S(1)}, u32[]{:S(2)}, u32[]{:S(2)}) collective-permute-start(bf16[4,128,512]{2,1,0:T(8,128)(2,1)} %get-tuple-element.641), channel_id=1, source_target_pairs={{0,1},{1,0},{2,3},{3,2},{4,5},{5,4},{6,7},{7,6},{8,9},{9,8},{10,11... | collective-permute-start | bytes 1572872 | tf_op jit(solution)/shard_map/ppermute | solution.py:351
  311.8 25.4 %collective-permute-start.38 = (bf16[4,128,512]{2,1,0:T(8,128)(2,1)}, bf16[4,128,512]{2,1,0:T(8,128)(2,1)}, u32[]{:S(2)}, u32[]{:S(2)}) collective-permute-start(bf16[4,128,512]{2,1,0:T(8,128)(2,1)} %get-tuple-element.642), channel_id=1, source_target_pairs={{0,16},{1,17},{2,18},{3,19},{4,20},{5,21},{6,22},{7,23},{8,24},{9,... | collective-permute-start | bytes 1572872 | tf_op jit(solution)/shard_map/ppermute | solution.py:351
  313.5 23.9 %collective-permute-start.39 = (bf16[4,128,512]{2,1,0:T(8,128)(2,1)S(1)}, bf16[4,128,512]{2,1,0:T(8,128)(2,1)}, u32[]{:S(2)}, u32[]{:S(2)}) collective-permute-start(bf16[4,128,512]{2,1,0:T(8,128)(2,1)S(1)} %copy-done.46), channel_id=1, source_target_pairs={{0,17},{1,16},{2,19},{3,18},{4,21},{5,20},{6,23},{7,22},{8,25},{9,... | collective-permute-start | bytes 1572872 | tf_op jit(solution)/shard_map/ppermute | solution.py:351
  318.3 23.6 %copy-start.32 = (bf16[4,128,512]{2,1,0:T(8,128)(2,1)S(1)}, bf16[4,128,512]{2,1,0:T(8,128)(2,1)}, u32[]{:S(2)}) copy-start(bf16[4,128,512]{2,1,0:T(8,128)(2,1)} %get-tuple-element.652) | copy-start | bytes 1572868
  340.5 18.3 %collective-permute-start.43 = (bf16[128,2816]{1,0:T(8,128)(2,1)}, bf16[128,2816]{1,0:T(8,128)(2,1)}, u32[]{:S(2)}, u32[]{:S(2)}) collective-permute-start(bf16[128,2816]{1,0:T(8,128)(2,1)} %reduce-scatter.2.cloned.1.call-done), channel_id=1, source_target_pairs={{0,16},{1,17},{2,18},{3,19},{4,20},{5,21},{6,22},{7,23},{8,24},{9,... | collective-permute-start | bytes 2162696 | tf_op jit(solution)/shard_map/ppermute | solution.py:351
  343.5 8.5 %collective-permute-start.44 = (bf16[1,136,512]{2,1,0:T(8,128)(2,1)S(1)}, bf16[1,136,512]{2,1,0:T(8,128)(2,1)S(1)}, u32[]{:S(2)}, u32[]{:S(2)}) collective-permute-start(bf16[1,136,512]{2,1,0:T(8,128)(2,1)S(1)} %get-tuple-element.738), channel_id=1, source_target_pairs={{0,2},{1,3},{2,4},{3,5},{4,6},{5,7},{6,0},{7,1},{8,10},{9,11},{10,... | collective-permute-start | bytes 417800 | tf_op jit(solution)/shard_map/ppermute | solution.py:351
  343.6 13.1 %collective-permute-start.45 = (bf16[1,136,512]{2,1,0:T(8,128)(2,1)S(1)}, bf16[1,136,512]{2,1,0:T(8,128)(2,1)S(1)}, u32[]{:S(2)}, u32[]{:S(2)}) collective-permute-start(bf16[1,136,512]{2,1,0:T(8,128)(2,1)S(1)} %get-tuple-element.740), channel_id=1, source_target_pairs={{0,4},{1,5},{2,6},{3,7},{4,0},{5,1},{6,2},{7,3},{8,12},{9,13},{10,... | collective-permute-start | bytes 417800 | tf_op jit(solution)/shard_map/ppermute | solution.py:351
  344.6 12.1 %collective-permute-start.46 = (bf16[1,136,512]{2,1,0:T(8,128)(2,1)S(1)}, bf16[1,136,512]{2,1,0:T(8,128)(2,1)S(1)}, u32[]{:S(2)}, u32[]{:S(2)}) collective-permute-start(bf16[1,136,512]{2,1,0:T(8,128)(2,1)S(1)} %get-tuple-element.739), channel_id=1, source_target_pairs={{0,6},{1,7},{2,0},{3,1},{4,2},{5,3},{6,4},{7,5},{8,14},{9,15},{10,... | collective-permute-start | bytes 417800 | tf_op jit(solution)/shard_map/ppermute | solution.py:351
  347.4 13.5 %collective-permute-start.47 = (bf16[1,480,256]{2,1,0:T(8,128)(2,1)S(1)}, bf16[1,480,256]{2,1,0:T(8,128)(2,1)S(1)}, u32[]{:S(2)}, u32[]{:S(2)}) collective-permute-start(bf16[1,480,256]{2,1,0:T(8,128)(2,1)S(1)} %constant_dynamic-slice_fusion.2), channel_id=1, source_target_pairs={{0,6},{1,7},{2,0},{3,1},{4,2},{5,3},{6,4},{7,5},{8,14},{9,15},{10,... | collective-permute-start | bytes 737288 | tf_op jit(solution)/shard_map/ppermute | solution.py:351
  361.0 6.1 %collective-permute-start.48 = (bf16[128,2816]{1,0:T(8,128)(2,1)S(1)}, bf16[128,2816]{1,0:T(8,128)(2,1)S(1)}, u32[]{:S(2)}, u32[]{:S(2)}) collective-permute-start(bf16[128,2816]{1,0:T(8,128)(2,1)S(1)} %add_convert_fusion.4), channel_id=1, source_target_pairs={{0,8},{1,9},{2,10},{3,11},{4,12},{5,13},{6,14},{7,15},{8,0},{9,1},... | collective-permute-start | bytes 2162696 | tf_op jit(solution)/shard_map/ppermute | solution.py:351
  361.0 6.1 %collective-permute-start.49 = (bf16[136,512]{1,0:T(8,128)(2,1)S(1)}, bf16[136,512]{1,0:T(8,128)(2,1)S(1)}, u32[]{:S(2)}, u32[]{:S(2)}) collective-permute-start(bf16[136,512]{1,0:T(8,128)(2,1)S(1)} %fusion.47), channel_id=1, source_target_pairs={{0,16},{1,17},{2,18},{3,19},{4,20},{5,21},{6,22},{7,23},{8,24},{9,... | collective-permute-start | bytes 417800 | tf_op jit(solution)/shard_map/ppermute | solution.py:351
  367.1 5.5 %collective-permute-start.51 = (bf16[4,128]{1,0:T(4,128)(2,1)S(1)}, bf16[4,128]{1,0:T(4,128)(2,1)S(1)}, u32[]{:S(2)}, u32[]{:S(2)}) collective-permute-start(bf16[4,128]{1,0:T(4,128)(2,1)S(1)} %get-tuple-element.671), channel_id=1, source_target_pairs={{0,1},{1,0},{2,3},{3,2},{4,5},{5,4},{6,7},{7,6},{8,9},{9,8},{10,11... | collective-permute-start | bytes 3080 | tf_op jit(solution)/shard_map/ppermute | solution.py:351
  368.7 3.9 %collective-permute-start.52 = (bf16[4,128]{1,0:T(4,128)(2,1)S(1)}, bf16[4,128]{1,0:T(4,128)(2,1)S(1)}, u32[]{:S(2)}, u32[]{:S(2)}) collective-permute-start(bf16[4,128]{1,0:T(4,128)(2,1)S(1)} %get-tuple-element.671), channel_id=1, source_target_pairs={{0,9},{1,8},{2,11},{3,10},{4,13},{5,12},{6,15},{7,14},{8,1},{9,0},... | collective-permute-start | bytes 3080 | tf_op jit(solution)/shard_map/ppermute | solution.py:351
  368.7 8.7 %collective-permute-start.50 = (bf16[136,1024]{1,0:T(8,128)(2,1)S(1)}, bf16[136,1024]{1,0:T(8,128)(2,1)S(1)}, u32[]{:S(2)}, u32[]{:S(2)}) collective-permute-start(bf16[136,1024]{1,0:T(8,128)(2,1)S(1)} %get-tuple-element.675), channel_id=1, source_target_pairs={{0,8},{1,9},{2,10},{3,11},{4,12},{5,13},{6,14},{7,15},{8,0},{9,1},... | collective-permute-start | bytes 835592 | tf_op jit(solution)/shard_map/ppermute | solution.py:351
  369.5 7.9 %collective-permute-start.53 = (bf16[480,256]{1,0:T(8,128)(2,1)S(1)}, bf16[480,256]{1,0:T(8,128)(2,1)S(1)}, u32[]{:S(2)}, u32[]{:S(2)}) collective-permute-start(bf16[480,256]{1,0:T(8,128)(2,1)S(1)} %fusion.45), channel_id=1, source_target_pairs={{0,16},{1,17},{2,18},{3,19},{4,20},{5,21},{6,22},{7,23},{8,24},{9,... | collective-permute-start | bytes 737288 | tf_op jit(solution)/shard_map/ppermute | solution.py:351
  377.6 3.8 collective-permute-start.54
  (46 other events, 256.0 us)
Sparse Core Ops, SparseCore 0:
  31.3 123.0 all-gather.1
  206.4 133.9 reduce-scatter.1
